TPU v7x, 32 devices: a whole 2x2x4 slice. The times are simulated.
32 devices in a mesh: dp: 8 (over y, x, core), tensor: 4 (over z).
Axes of the slice: x: 2, y: 2, z: 4, core: 2. Of those that a mesh axis runs over, the one named last changes fastest.
Arguments:
- attn_out: bfloat16 [4096, 8192], P('dp', 'tensor'), may hold values from -6 to 6
- out_weight: bfloat16 [8192, 3584], P('tensor', 'dp'), may hold values from -0.0625 to 0.0625
- residual: bfloat16 [4096, 3584], P(('dp', 'tensor')), may hold values from -101 to 101
- norm_gain: float32 [3584], replicated, may hold values from 0.5 to 1.5
- expert_ids: int32 [4096, 8], P(('dp', 'tensor')), may hold values from 0 to 31, all different within a row; in each aligned block of 128 rows (0 to 127, 128 to 255, ...) at most 48 rows name the same one
- route_weight: float32 [4096, 8], P(('dp', 'tensor')), may hold values from 0.05 to 0.35
- w_gate: bfloat16 [32, 3584, 1024], P(('dp', 'tensor')), may hold values from -1 to 1
- w_up: bfloat16 [32, 3584, 1024], P(('dp', 'tensor')), may hold values from -1 to 1
- w_down: bfloat16 [32, 1024, 3584], P(('dp', 'tensor')), may hold values from -0.1875 to 0.1875
- history_x: float32 [16], replicated, may hold values from 8 to 40
- history_h: float32 [16], replicated, may hold values from 4 to 16
Outputs:
- layer_out: bfloat16 [4096, 3584], P(('dp', 'tensor'))
- new_history_x: float32 [16], replicated
- new_history_h: float32 [16], replicated
Inputs may be any that keep to these rules, and one draw needn't show every extreme that they name: `expert_ids`: among the routes of one device's 128 tokens no expert is named more than 48 times, a bound that some block reaches.
All inputs are finite; a program needn't handle non-finite values.
Results may differ from a plain program's by a relative error of at most 0.02.
Values may be sent and summed in bfloat16 or wider, within the bound.
No kernel may reach another device: no remote copies, remote signals or barrier semaphores. Data moves between devices by JAX's collectives and lax.ppermute only.
A program may use at most 128 MiB of HBM per device.

v0:
```python
import jax
import jax.numpy as jnp
from jax import lax
from jax.sharding import PartitionSpec as P

FP8_LIMIT = 448.0


def body(
    attn_out,
    out_weight,
    residual,
    norm_gain,
    expert_ids,
    route_weight,
    w_gate,
    w_up,
    w_down,
    history_x,
    history_h,
):
    data_count = lax.axis_size("dp")
    tensor_count = lax.axis_size("tensor")
    experts = data_count * tensor_count
    local_rows = residual.shape[0]
    width = residual.shape[1]
    top_count = expert_ids.shape[1]
    capacity = max(2, 3 * local_rows * top_count // (2 * experts))
    head_terms = jnp.dot(
        attn_out,
        lax.all_gather(out_weight, "dp", axis=1, tiled=True),
        preferred_element_type=jnp.float32,
    )
    projected = lax.psum_scatter(
        head_terms.astype(jnp.bfloat16), "tensor", scatter_dimension=0, tiled=True
    ).astype(jnp.float32)
    stream = residual.astype(jnp.float32) + projected
    normed = (
        stream * lax.rsqrt(jnp.mean(stream * stream, axis=-1, keepdims=True) + 1e-06) * norm_gain
    )
    local_peak_x = jnp.max(jnp.abs(normed))
    amax_x = lax.pmax(local_peak_x, ("dp", "tensor"))
    scale_x = FP8_LIMIT / jnp.max(history_x)
    inv_x = jnp.max(history_x) / FP8_LIMIT
    scale_h = FP8_LIMIT / jnp.max(history_h)
    inv_h = jnp.max(history_h) / FP8_LIMIT
    quantized = jnp.clip(normed * scale_x, -FP8_LIMIT, FP8_LIMIT).astype(jnp.bfloat16)
    flat_ids = expert_ids.reshape(-1)
    onehot = (flat_ids[:, None] == jnp.arange(experts, dtype=jnp.int32)[None, :]).astype(jnp.int32)
    before = jnp.cumsum(onehot, axis=0) - onehot
    slot_index = jnp.sum(before * onehot, axis=-1)
    position = flat_ids * capacity + slot_index
    matches = (
        position.reshape(local_rows, top_count)[:, :, None]
        == jnp.arange(experts * capacity, dtype=jnp.int32)[None, None, :]
    )
    placing = jnp.sum(matches.astype(jnp.int32), axis=1).astype(jnp.bfloat16)
    outgoing = lax.dot_general(
        placing, quantized, (((0,), (0,)), ((), ())), preferred_element_type=jnp.float32
    )
    outgoing = outgoing.astype(jnp.bfloat16).reshape(experts, capacity, width)
    gate_matrix = w_gate[0]
    up_matrix = w_up[0]
    down_matrix = w_down[0]
    token_block = lax.all_to_all(
        outgoing, ("dp", "tensor"), split_axis=0, concat_axis=0, tiled=True
    )
    source_count = token_block.shape[0]
    slot_count = token_block.shape[1]
    flat_rows = token_block.reshape(source_count * slot_count, width)
    gate = jnp.dot(flat_rows, gate_matrix, preferred_element_type=jnp.float32) * inv_x
    upper = jnp.dot(flat_rows, up_matrix, preferred_element_type=jnp.float32) * inv_x
    hidden = jax.nn.silu(gate) * upper
    row_peaks = jnp.max(jnp.abs(hidden), axis=1).reshape(source_count, slot_count)
    hidden_q = jnp.clip(hidden * scale_h, -FP8_LIMIT, FP8_LIMIT).astype(jnp.bfloat16)
    expert_out = (
        jnp.dot(hidden_q, down_matrix, preferred_element_type=jnp.float32) * inv_h
    ).astype(jnp.bfloat16)
    expert_out, row_peaks = (expert_out.reshape(source_count, slot_count, width), row_peaks)
    returned = lax.all_to_all(expert_out, ("dp", "tensor"), split_axis=0, concat_axis=0, tiled=True)
    returned_flat = returned.reshape(experts * capacity, width)
    picked = returned_flat[position].reshape(local_rows, top_count, width)
    mixture = jnp.sum(picked.astype(jnp.float32) * route_weight[:, :, None], axis=1)
    layer_out = (stream + mixture).astype(jnp.bfloat16)
    local_peak_h = jnp.max(row_peaks)
    amax_h = lax.pmax(local_peak_h, ("dp", "tensor"))
    new_history_x = jnp.concatenate([amax_x[None], history_x[:-1]])
    new_history_h = jnp.concatenate([amax_h[None], history_h[:-1]])
    return (layer_out, new_history_x, new_history_h)


def solution(mesh):
    in_specs = (
        P("dp", "tensor"),
        P("tensor", "dp"),
        P(("dp", "tensor"), None),
        P(),
        P(("dp", "tensor"), None),
        P(("dp", "tensor"), None),
        P(("dp", "tensor"), None, None),
        P(("dp", "tensor"), None, None),
        P(("dp", "tensor"), None, None),
        P(),
        P(),
    )
    out_specs = (P(("dp", "tensor"), None), P(), P())
    return jax.shard_map(body, mesh=mesh, in_specs=in_specs, out_specs=out_specs, check_vma=False)
```

profile of v0, /device:TPU:0, one launch (start us, length us, event | category | flops | bytes accessed | tf_op | source)
XLA Modules:
  0.0 813.5 jit_solution(15337353336985178591)
XLA Ops:
  7.2 0.7 all-gather.2.cloned.1.call-update
  8.0 85.6 %all-gather.2.cloned.1.call-done = bf16[2048,3584]{0,1:T(8,128)(2,1)} async-done(((bf16[2048,448]{0,1:T(8,128)(2,1)}), bf16[2048,3584]{0,1:T(8,128)(2,1)}) %all-gather.2.cloned.1.call-update) | async-done | bytes 14680080 | tf_op jit(solution)/shard_map/all_gather | solution.py:31
  93.6 12.4 %convolution_convert_fusion.1 = bf16[512,3584]{1,0:T(8,128)(2,1)} fusion(bf16[512,2048]{1,0:T(8,128)(2,1)S(1)} %copy-done, bf16[2048,3584]{0,1:T(8,128)(2,1)} %all-gather.2.cloned.1.call-done), kind=kOutput, calls=%fused_computation.15 | convolution fusion | flops 7518027776 | bytes 20447232 | tf_op jit(solution)/shard_map/dot_general | solution.py:29
  106.3 9.0 %reduce-window.6 = s32[32,8,128]{2,1,0:T(8,128)S(1)} reduce-window(s32[32,8,128]{2,1,0:T(8,128)S(1)} %fusion.20, s32[]{:T(128)} %constant.8.clone.1), window={size=1x1x128 pad=0_0x0_0x127_0}, to_apply=%region_1.0 | reduce-window | flops 4161536 | bytes 262148 | tf_op jit(solution)/shard_map/reduce-window
  115.5 0.1 copy.25
  115.7 0.1 broadcast_add_fusion
  116.0 0.6 reduce_max.35
  117.3 2.5 convert_reduce_fusion
  119.7 55.0 %reduce-scatter.2.cloned.1.call-done = bf16[128,3584]{1,0:T(8,128)(2,1)} async-done(((bf16[512,3584]{1,0:T(8,128)(2,1)}), bf16[128,3584]{1,0:T(8,128)(2,1)}) %reduce-scatter.2.cloned.1.call-update) | async-done | bytes 917520 | tf_op jit(solution)/shard_map/reduce_scatter | solution.py:34
  174.8 1.6 multiply_reduce_fusion
  176.3 7.1 convolution_convert_fusion
  183.4 5.3 all-to-all-start
  189.3 0.6 reduce_max.36
  191.3 234.6 %all-to-all-done = bf16[32,48,3584]{2,1,0:T(8,128)(2,1)} async-done(((bf16[32,48,3584]{2,1,0:T(8,128)(2,1)}), bf16[32,48,3584]{2,1,0:T(8,128)(2,1)}, u32[]{:S(2)}, u32[]{:S(2)}) %all-to-all-start) | async-done | bytes 11010080 | tf_op jit(solution)/shard_map/all_to_all | solution.py:65
  425.9 16.5 %fusion.2 = f32[1536,1024]{1,0:T(8,128)S(1)} fusion(bf16[1536,3584]{1,0:T(8,128)(2,1)} %bitcast.3, bf16[1,3584,1024]{2,1,0:T(8,128)(2,1)} %param.18), kind=kOutput, calls=%fused_computation.6 | convolution fusion | flops 11274289152 | bytes 24641536 | tf_op jit(solution)/shard_map/dot_general | solution.py:72
  442.5 19.3 %abs_reduce_fusion = (f32[]{:T(128)}, f32[1536,1024]{1,0:T(8,128)}) fusion(f32[1536,1024]{1,0:T(8,128)S(1)} %fusion.2, f32[]{:T(128)S(6)} %div.25, bf16[1536,3584]{1,0:T(8,128)(2,1)} %bitcast.3, bf16[1,3584,1024]{2,1,0:T(8,128)(2,1)} %param.17), kind=kOutput, calls=%fused_computation.10 | convolution fusion | flops 11288444928 | bytes 30933000 | tf_op jit(solution)/shard_map/dot_general | solution.py:71
  461.7 17.3 %multiply_convert_fusion = bf16[1536,3584]{1,0:T(8,128)(2,1)} fusion(f32[]{:T(128)S(6)} %div.28, bf16[1,1024,3584]{2,1,0:T(8,128)(2,1)S(1)} %bitcast.57, f32[1536,1024]{1,0:T(8,128)} %get-tuple-element.10, f32[]{:T(128)S(6)} %div.27), kind=kOutput, calls=%fused_computation.1 | convolution fusion | flops 11290017792 | bytes 24641544 | tf_op jit(solution)/shard_map/dot_general | solution.py:77
  479.0 10.2 %all-to-all-start.1 = ((bf16[32,48,3584]{2,1,0:T(8,128)(2,1)}), bf16[32,48,3584]{2,1,0:T(8,128)(2,1)}, u32[]{:S(2)}, u32[]{:S(2)}) async-start(bf16[32,48,3584]{2,1,0:T(8,128)(2,1)} %bitcast.49), calls=%async_computation.2 | async-start | bytes 22020096 | tf_op jit(solution)/shard_map/all_to_all | solution.py:80
  489.5 237.2 %all-to-all-done.1 = bf16[32,48,3584]{2,1,0:T(8,128)(2,1)} async-done(((bf16[32,48,3584]{2,1,0:T(8,128)(2,1)}), bf16[32,48,3584]{2,1,0:T(8,128)(2,1)}, u32[]{:S(2)}, u32[]{:S(2)}) %all-to-all-start.1) | async-done | bytes 11010080 | tf_op jit(solution)/shard_map/all_to_all | solution.py:80
  726.6 19.5 %gather_fusion = bf16[1024,3584]{1,0:T(8,128)(2,1)} fusion(bf16[1536,3584]{1,0:T(8,128)(2,1)} %bitcast.8, s32[1024]{0:T(1024)S(1)} %broadcast_clamp_fusion), kind=kCustom, calls=%fused_computation | custom fusion | bytes 14684160 | tf_op jit(solution)/shard_map/gather | solution.py:82
  746.1 9.9 %fusion = f32[128,3584]{1,0:T(8,128)S(1)} fusion(bf16[1024,3584]{1,0:T(8,128)(2,1)} %gather_fusion, f32[128,8]{1,0:T(8,128)S(1)} %copy.27), kind=kLoop, calls=%fused_computation.4 | loop fusion | flops 10551296 | bytes 9179136 | tf_op jit(solution)/shard_map/reduce_sum | solution.py:83
  756.0 2.0 abs_reduce_fusion.1
  758.0 46.8 %all-reduce = (f32[1]{0:T(128)}, f32[1]{0:T(128)}) all-reduce(f32[1]{0:T(128)} %bitcast.12, f32[1]{0:T(128)} %bitcast.13), channel_id=1, replica_groups=mesh['dp'=8,'tensor'=4] {'dp','tensor'}, use_global_device_ids=true, to_apply=%region_10.11 | all-reduce | flops 2 | bytes 16 | tf_op jit(solution)/shard_map/pmax | solution.py:42
  804.8 1.8 pad_maximum_fusion
  (42 shorter events, 1.0 us)
Async XLA Ops:
  7.2 86.5 %copy-start = (bf16[512,2048]{1,0:T(8,128)(2,1)S(1)}, bf16[512,2048]{1,0:T(8,128)(2,1)}, u32[]{:S(2)}) copy-start(bf16[512,2048]{1,0:T(8,128)(2,1)} %param.11) | copy-start | bytes 6291460
  7.2 86.4 %all-gather.2.cloned.1.call-start = ((), (), s32[]{:S(2)}) async-start(), calls=%async_computation.3 | async-start | bytes 16515072 | tf_op jit(solution)/shard_map/all_gather | solution.py:31
  7.9 98.1 %copy-start.5 = (s32[128,8]{0,1:T(8,128)S(1)}, s32[128,8]{0,1:T(8,128)}, u32[]{:S(2)}) copy-start(s32[128,8]{0,1:T(8,128)} %param.15) | copy-start | bytes 12292
  7.9 108.0 %copy-start.8 = (f32[16]{0:T(128)S(1)}, f32[16]{0:T(128)}, u32[]{:S(2)}) copy-start(f32[16]{0:T(128)} %param.20) | copy-start | bytes 196
  7.9 166.8 %reduce-scatter.2.cloned.1.call-start = ((), (), s32[]{:S(2)}) async-start(), calls=%async_computation.4 | async-start | bytes 4587520 | tf_op jit(solution)/shard_map/reduce_scatter | solution.py:34
  106.0 68.8 %copy-start.2 = (bf16[128,3584]{1,0:T(8,128)(2,1)S(1)}, bf16[128,3584]{1,0:T(8,128)(2,1)}, u32[]{:S(2)}) copy-start(bf16[128,3584]{1,0:T(8,128)(2,1)} %param.13) | copy-start | bytes 2752516
  106.0 70.3 %copy-start.4 = (f32[3584]{0:T(1024)S(1)}, f32[3584]{0:T(1024)}, u32[]{:S(2)}) copy-start(f32[3584]{0:T(1024)} %param.14) | copy-start | bytes 43012
  183.4 5.9 copy-start.7
  183.4 242.5 %all-to-all-start = ((bf16[32,48,3584]{2,1,0:T(8,128)(2,1)}), bf16[32,48,3584]{2,1,0:T(8,128)(2,1)}, u32[]{:S(2)}, u32[]{:S(2)}) async-start(bf16[32,48,3584]{2,1,0:T(8,128)(2,1)} %bitcast.48), calls=%async_computation.1 | async-start | bytes 22020096 | tf_op jit(solution)/shard_map/all_to_all | solution.py:65
  425.9 35.9 %slice-start = ((s8[7340032]{0:T(1024)(128)(4,1)}), s8[4194304]{0:T(1024)(128)(4,1)S(1)}, s32[]{:S(2)}) async-start(s8[7340032]{0:T(1024)(128)(4,1)} %bitcast.56), calls=%async_computation.5 | async-start | bytes 8388608
  442.4 19.3 %slice-start.1 = ((s8[7340032]{0:T(1024)(128)(4,1)}), s8[3145728]{0:T(1024)(128)(4,1)S(1)}, s32[]{:S(2)}) async-start(s8[7340032]{0:T(1024)(128)(4,1)} %bitcast.56), calls=%async_computation.6 | async-start | bytes 6291456
  479.0 10.3 %copy-start.6 = (f32[128,8]{0,1:T(8,128)S(1)}, f32[128,8]{0,1:T(8,128)}, u32[]{:S(2)}) copy-start(f32[128,8]{0,1:T(8,128)} %param.16) | copy-start | bytes 12292
  479.0 247.6 %all-to-all-start.1 = ((bf16[32,48,3584]{2,1,0:T(8,128)(2,1)}), bf16[32,48,3584]{2,1,0:T(8,128)(2,1)}, u32[]{:S(2)}, u32[]{:S(2)}) async-start(bf16[32,48,3584]{2,1,0:T(8,128)(2,1)} %bitcast.49), calls=%async_computation.2 | async-start | bytes 22020096 | tf_op jit(solution)/shard_map/all_to_all | solution.py:80
  726.6 80.0 %copy-start.1 = (bf16[512,2048]{1,0:T(8,128)(2,1)S(1)}, bf16[512,2048]{1,0:T(8,128)(2,1)}, u32[]{:S(2)}) copy-start(bf16[512,2048]{1,0:T(8,128)(2,1)} %param.11) | copy-start | bytes 6291460
  746.1 9.9 %copy-start.3 = (bf16[128,3584]{1,0:T(8,128)(2,1)S(1)}, bf16[128,3584]{1,0:T(8,128)(2,1)}, u32[]{:S(2)}) copy-start(bf16[128,3584]{1,0:T(8,128)(2,1)} %reduce-scatter.2.cloned.1.call-done) | copy-start | bytes 2752516
Sparse Core Ops, SparseCore 0:
  9.9 83.6 all-gather.1
  106.2 68.5 reduce-scatter.1
where the time goes:
time: 814 us; the launch traced here: 813 us
  waiting for transfers between devices  613 us (75%)
  matrix products  72.5 us (9%)
  blocking collectives  46.8 us (6%)
  other arithmetic  28.2 us (3%)
  local copies, waits for them, and re-layouts  20.4 us (3%)
  between operations  16.9 us (2%)
  starting transfers between devices  15.5 us (2%)
    all_to_all x1, waiting for transfers between devices, body(): lax.all_to_all(expert_out, ('dp', 'tensor'), split_axis=0, concat_axis=0,...  237 us
    all_to_all x1, waiting for transfers between devices, body(): lax.all_to_all(outgoing, ('dp', 'tensor'), split_axis=0, concat_axis=0, t...  235 us
    all_gather x1, waiting for transfers between devices, body(): lax.all_gather(out_weight, 'dp', axis=1, tiled=True)  85.6 us
    reduce_scatter x1, waiting for transfers between devices, body(): lax.psum_scatter(head_terms.astype(jnp.bfloat16), 'tensor', scatter_dimen...  55 us
    pmax x1, blocking collectives, body(): amax_x = lax.pmax(local_peak_x, ('dp', 'tensor'))  46.8 us
    gather x1, local copies, waits for them, and re-layouts, body(): picked = returned_flat[position].reshape(local_rows, top_count, width)  19.5 us
    dot_general x1, matrix products, body(): jnp.dot(flat_rows, gate_matrix, preferred_element_type=jnp.float32) * inv_x  19.3 us
    dot_general x1, matrix products, body(): jnp.dot(hidden_q, down_matrix, preferred_element_type=jnp.float32) * inv_h  17.3 us
  transfers between devices with their start and end apart: 4, of which 4 were waited for; matrix products, arithmetic and copies ran while one was open for 2% of the time, Pallas kernels for 0%

commit v1 on v0

v1 whole, which is shorter than its diff:
```python
import jax
import jax.numpy as jnp
from jax import lax
from jax.sharding import PartitionSpec as P

FP8_LIMIT = 448.0
AXES = ("dp", "tensor")
CHUNKS = 2


def project(attn_out, out_weight):
    head_terms = jnp.dot(
        attn_out,
        lax.all_gather(out_weight, "dp", axis=1, tiled=True),
        preferred_element_type=jnp.float32,
    )
    return lax.psum_scatter(
        head_terms.astype(jnp.bfloat16), "tensor", scatter_dimension=0, tiled=True
    ).astype(jnp.float32)


def peaks_over_all(peaks):
    for axis in AXES:
        count = lax.axis_size(axis)
        shift = 1
        while shift < count:
            pairs = [(i, (i + shift) % count) for i in range(count)]
            peaks = jnp.maximum(peaks, lax.ppermute(peaks, axis, pairs))
            shift *= 2
    return peaks


def slots_of(ids, experts, capacity):
    flat_ids = ids.reshape(-1)
    onehot = (flat_ids[:, None] == jnp.arange(experts, dtype=jnp.int32)[None, :]).astype(jnp.int32)
    before = jnp.cumsum(onehot, axis=0) - onehot
    return flat_ids * capacity + jnp.sum(before * onehot, axis=-1)


def exchange_plan(
    quantized, stream, expert_ids, route_weight, weights, inv_x, scale_h, inv_h, capacity, experts
):
    w_gate, w_up, w_down = weights
    local_rows, width = quantized.shape
    top_count = expert_ids.shape[1]
    position = slots_of(expert_ids, experts, capacity)
    matches = (
        position.reshape(local_rows, top_count)[:, :, None]
        == jnp.arange(experts * capacity, dtype=jnp.int32)[None, None, :]
    )
    placing = jnp.sum(matches.astype(jnp.int32), axis=1).astype(jnp.bfloat16)
    outgoing = lax.dot_general(
        placing, quantized, (((0,), (0,)), ((), ())), preferred_element_type=jnp.float32
    )
    outgoing = outgoing.astype(jnp.bfloat16).reshape(experts, capacity, width)
    token_block = lax.all_to_all(outgoing, AXES, split_axis=0, concat_axis=0, tiled=True)
    flat_rows = token_block.reshape(-1, width)
    gate = jnp.dot(flat_rows, w_gate, preferred_element_type=jnp.float32) * inv_x
    upper = jnp.dot(flat_rows, w_up, preferred_element_type=jnp.float32) * inv_x
    hidden = jax.nn.silu(gate) * upper
    hidden_q = jnp.clip(hidden * scale_h, -FP8_LIMIT, FP8_LIMIT).astype(jnp.bfloat16)
    expert_out = (jnp.dot(hidden_q, w_down, preferred_element_type=jnp.float32) * inv_h).astype(
        jnp.bfloat16
    )
    returned = lax.all_to_all(
        expert_out.reshape(experts, capacity, width), AXES, split_axis=0, concat_axis=0, tiled=True
    )
    picked = returned.reshape(-1, width)[position].reshape(local_rows, top_count, width)
    mixture = jnp.sum(picked.astype(jnp.float32) * route_weight[:, :, None], axis=1)
    return (stream + mixture).astype(jnp.bfloat16), jnp.max(jnp.abs(hidden))


def gather_plan(
    quantized, stream, expert_ids, route_weight, weights, inv_x, scale_h, inv_h, capacity, experts
):
    w_gate, w_up, w_down = weights
    local_rows, width = quantized.shape
    mine = lax.axis_index("dp") * lax.axis_size("tensor") + lax.axis_index("tensor")
    all_ids = lax.all_gather(expert_ids, AXES, axis=0, tiled=True)
    all_weights = lax.all_gather(route_weight, AXES, axis=0, tiled=True)
    hit = all_ids == mine
    named = jnp.any(hit, axis=1).reshape(experts, local_rows)
    weight = jnp.sum(jnp.where(hit, all_weights, 0.0), axis=1).reshape(experts, local_rows)
    earlier = jnp.triu(jnp.ones((local_rows, local_rows), jnp.bfloat16), 1)
    slot = jnp.dot(named.astype(jnp.bfloat16), earlier, preferred_element_type=jnp.float32)
    slot = slot.astype(jnp.int32)
    chosen = (
        slot[:, None, :] == jnp.arange(capacity, dtype=jnp.int32)[None, :, None]
    ) & named[:, None, :]
    slot_weight = jnp.sum(jnp.where(chosen, weight[:, None, :], 0.0), axis=2)
    chosen = chosen.astype(jnp.bfloat16)
    step = width // CHUNKS
    gate = up = 0.0
    for c in range(CHUNKS):
        part = slice(c * step, (c + 1) * step)
        tokens = lax.all_gather(quantized[:, part], AXES, axis=0, tiled=True)
        rows = lax.dot_general(
            chosen,
            tokens.reshape(experts, local_rows, step),
            (((2,), (1,)), ((0,), (0,))),
            preferred_element_type=jnp.float32,
        )
        rows = rows.astype(jnp.bfloat16).reshape(experts * capacity, step)
        gate += jnp.dot(rows, w_gate[part], preferred_element_type=jnp.float32)
        up += jnp.dot(rows, w_up[part], preferred_element_type=jnp.float32)
    hidden = jax.nn.silu(gate * inv_x) * (up * inv_x)
    peak_h = jnp.max(jnp.abs(hidden))
    hidden_q = jnp.clip(hidden * scale_h, -FP8_LIMIT, FP8_LIMIT).astype(jnp.bfloat16)
    factor = slot_weight.reshape(-1, 1) * inv_h
    pieces = []
    for c in range(CHUNKS):
        part = slice(c * step, (c + 1) * step)
        terms = jnp.dot(hidden_q, w_down[:, part], preferred_element_type=jnp.float32) * factor
        spread = lax.dot_general(
            chosen,
            terms.astype(jnp.bfloat16).reshape(experts, capacity, step),
            (((1,), (1,)), ((0,), (0,))),
            preferred_element_type=jnp.float32,
        )
        spread = spread.astype(jnp.bfloat16).reshape(experts * local_rows, step)
        mixed = lax.psum_scatter(spread, AXES, scatter_dimension=0, tiled=True)
        pieces.append((stream[:, part] + mixed.astype(jnp.float32)).astype(jnp.bfloat16))
    return jnp.concatenate(pieces, axis=1), peak_h


def body(
    attn_out,
    out_weight,
    residual,
    norm_gain,
    expert_ids,
    route_weight,
    w_gate,
    w_up,
    w_down,
    history_x,
    history_h,
):
    experts = lax.axis_size("dp") * lax.axis_size("tensor")
    local_rows = residual.shape[0]
    top_count = expert_ids.shape[1]
    capacity = max(2, 3 * local_rows * top_count // (2 * experts))
    stream = residual.astype(jnp.float32) + project(attn_out, out_weight)
    normed = (
        stream * lax.rsqrt(jnp.mean(stream * stream, axis=-1, keepdims=True) + 1e-06) * norm_gain
    )
    peak_x = jnp.max(jnp.abs(normed))
    top_x, top_h = jnp.max(history_x), jnp.max(history_h)
    quantized = jnp.clip(normed * (FP8_LIMIT / top_x), -FP8_LIMIT, FP8_LIMIT).astype(jnp.bfloat16)
    plan = gather_plan if local_rows < 4 * capacity else exchange_plan
    layer_out, peak_h = plan(
        quantized,
        stream,
        expert_ids,
        route_weight,
        (w_gate[0], w_up[0], w_down[0]),
        top_x / FP8_LIMIT,
        FP8_LIMIT / top_h,
        top_h / FP8_LIMIT,
        capacity,
        experts,
    )
    peaks = peaks_over_all(jnp.stack([peak_x, peak_h]))
    new_history_x = jnp.concatenate([peaks[:1], history_x[:-1]])
    new_history_h = jnp.concatenate([peaks[1:], history_h[:-1]])
    return (layer_out, new_history_x, new_history_h)


def solution(mesh):
    in_specs = (
        P("dp", "tensor"),
        P("tensor", "dp"),
        P(AXES, None),
        P(),
        P(AXES, None),
        P(AXES, None),
        P(AXES, None, None),
        P(AXES, None, None),
        P(AXES, None, None),
        P(),
        P(),
    )
    out_specs = (P(AXES, None), P(), P())
    return jax.shard_map(body, mesh=mesh, in_specs=in_specs, out_specs=out_specs, check_vma=False)
```

time: 814 us -> 1110 us (1.36)
  waiting for transfers between devices: 613 us -> 823 us
  blocking collectives: 46.8 us -> 135 us
  matrix products: 72.5 us -> 116 us
  local copies, waits for them, and re-layouts: 20.4 us -> 1.76 us
  starting transfers between devices: 15.5 us -> 3 us
  other arithmetic: 28.2 us -> 15.8 us
    reduce_scatter x1 -> x3, waiting for transfers between devices: 55 us -> 652 us  [the longest x2 585 us: gather_plan(): mixed = lax.psum_scatter(spread, AXES, scatter_dimension=0, tiled=True)]
    all_to_all x2 -> x0, waiting for transfers between devices: 472 us -> none  [the longest x1 237 us: body(): lax.all_to_all(expert_out, ('dp', 'tensor'), split_axis=0, concat_axis=0,...]
    all_gather x0 -> x2, blocking collectives: none -> 135 us  [the longest x1 69.9 us: gather_plan(): all_ids = lax.all_gather(expert_ids, AXES, axis=0, tiled=True)]
    all_gather x1 -> x3, waiting for transfers between devices: 85.6 us -> 150 us  [the longest x1 85.6 us: project(): lax.all_gather(out_weight, 'dp', axis=1, tiled=True)]
    pmax x1 -> x0, blocking collectives: 46.8 us -> none  [body(): amax_x = lax.pmax(local_peak_x, ('dp', 'tensor'))]
    dot_general x5 -> x12, matrix products: 72.5 us -> 116 us  [the longest x2 23.5 us: gather_plan(): up += jnp.dot(rows, w_up[part], preferred_element_type=jnp.float32)]
    ppermute x0 -> x5, waiting for transfers between devices: none -> 19.5 us  [peaks_over_all(): peaks = jnp.maximum(peaks, lax.ppermute(peaks, axis, pairs))]
    gather x1 -> x0, local copies, waits for them, and re-layouts: 19.5 us -> none  [body(): picked = returned_flat[position].reshape(local_rows, top_count, width)]
  transfers between devices with their start and end apart: 4 -> 11, of which waited for: 4 -> 10; matrix products, arithmetic and copies ran while one was open for 2% -> 4% of each run, Pallas kernels for 0% -> 0%
where the time goes in v1:
time: 1110 us
  waiting for transfers between devices  823 us (74%)
  blocking collectives  135 us (12%)
  matrix products  116 us (10%)
  between operations  16.9 us (2%)
  other arithmetic  15.8 us (1%)
    reduce_scatter x2, waiting for transfers between devices, gather_plan(): mixed = lax.psum_scatter(spread, AXES, scatter_dimension=0, tiled=True)  585 us
    all_gather x1, waiting for transfers between devices, project(): lax.all_gather(out_weight, 'dp', axis=1, tiled=True)  85.6 us
    all_gather x1, blocking collectives, gather_plan(): all_ids = lax.all_gather(expert_ids, AXES, axis=0, tiled=True)  69.9 us
    reduce_scatter x1, waiting for transfers between devices, project(): lax.psum_scatter(head_terms.astype(jnp.bfloat16), 'tensor', scatter_dimen...  67.2 us
    all_gather x1, blocking collectives, gather_plan(): all_weights = lax.all_gather(route_weight, AXES, axis=0, tiled=True)  65.6 us
    all_gather x2, waiting for transfers between devices, gather_plan(): tokens = lax.all_gather(quantized[:, part], AXES, axis=0, tiled=True)  64.8 us
    dot_general x2, matrix products, gather_plan(): up += jnp.dot(rows, w_up[part], preferred_element_type=jnp.float32)  23.5 us
    dot_general x2, matrix products, gather_plan(): lax.dot_general(chosen, terms.astype(jnp.bfloat16).reshape(experts, capac...  23.5 us
  transfers between devices with their start and end apart: 11, of which 10 were waited for; matrix products, arithmetic and copies ran while one was open for 4% of the time, Pallas kernels for 0%

profile of v1, /device:TPU:0, one launch (start us, length us, event | category | flops | bytes accessed | tf_op | source)
XLA Modules:
  0.0 1111.5 jit_solution(2366547069174613488)
XLA Ops:
  8.0 85.6 %all-gather.4.cloned.1.call-done = bf16[2048,3584]{0,1:T(8,128)(2,1)} async-done(((bf16[2048,448]{0,1:T(8,128)(2,1)}), bf16[2048,3584]{0,1:T(8,128)(2,1)}) %all-gather.4.cloned.1.call-update) | async-done | bytes 14680080 | tf_op jit(solution)/shard_map/all_gather | solution.py:14
  93.6 12.4 %convolution_convert_fusion.2 = bf16[512,3584]{1,0:T(8,128)(2,1)} fusion(bf16[512,2048]{1,0:T(8,128)(2,1)S(1)} %copy-done, bf16[2048,3584]{0,1:T(8,128)(2,1)} %all-gather.4.cloned.1.call-done), kind=kOutput, calls=%fused_computation.7 | convolution fusion | flops 7518027776 | bytes 20447232 | tf_op jit(solution)/shard_map/dot_general | solution.py:12
  107.4 67.2 %reduce-scatter.4.cloned.1.call-done = bf16[128,3584]{1,0:T(8,128)(2,1)} async-done(((bf16[512,3584]{1,0:T(8,128)(2,1)}), bf16[128,3584]{1,0:T(8,128)(2,1)}) %reduce-scatter.4.cloned.1.call-update) | async-done | bytes 917520 | tf_op jit(solution)/shard_map/reduce_scatter | solution.py:17
  176.2 3.5 abs_reduce_fusion.1
  184.0 69.9 %all_gather.16 = s32[4096,8]{0,1:T(8,128)S(1)} all-gather(s32[128,8]{0,1:T(8,128)S(1)} %copy-done.4), channel_id=1, replica_groups=mesh['dp'=8,'tensor'=4] {'dp','tensor'}, dimensions={0}, use_global_device_ids=true | all-gather | bytes 135168 | tf_op jit(solution)/shard_map/all_gather | solution.py:79
  253.9 65.6 %all_gather.19 = f32[4096,8]{0,1:T(8,128)S(1)} all-gather(f32[128,8]{0,1:T(8,128)S(1)} %copy-done.5), channel_id=1, replica_groups=mesh['dp'=8,'tensor'=4] {'dp','tensor'}, dimensions={0}, use_global_device_ids=true | all-gather | bytes 135168 | tf_op jit(solution)/shard_map/all_gather | solution.py:80
  320.1 9.7 convolution_convert_fusion.3
  329.8 64.8 %all-gather.6.cloned.1.call-done = bf16[4096,1792]{1,0:T(8,128)(2,1)} async-done(((bf16[128,1792]{1,0:T(8,128)(2,1)}), bf16[4096,1792]{1,0:T(8,128)(2,1)}) %all-gather.6.cloned.1.call-update) | async-done | bytes 14680080 | tf_op jit(solution)/shard_map/all_gather | solution.py:96
  394.6 7.2 convolution_convert_fusion.4
  401.9 9.8 fusion.3
  411.6 9.6 fusion.7
  421.3 8.2 fusion.5
  429.5 13.8 %abs_reduce_fusion = (f32[]{:T(128)}, f32[1536,1024]{1,0:T(8,128)}) fusion(f32[1536,1024]{1,0:T(8,128)} %fusion.3, bf16[1536,1792]{1,0:T(8,128)(2,1)S(1)} %bitcast.48, bf16[1,3584,1024]{2,1,0:T(8,128)(2,1)S(1)} %bitcast.64, f32[]{:T(128)S(6)} %div.25, f32[1536,1024]{1,0:T(8,128)} %fusion.7, f32[1536,1024]{1,0:T(8,128)} %fusion.5), kind=kOutput, calls=%fused_computation.4 | convolution fusion | flops 5654446080 | bytes 34340872 | tf_op jit(solution)/shard_map/dot_general | solution.py:105
  443.3 10.7 multiply_convert_fusion
  453.9 11.8 %convolution_convert_fusion = bf16[32,128,1792]{2,1,0:T(8,128)(2,1)} fusion(bf16[32,48,1792]{2,1,0:T(8,128)(2,1)} %bitcast.52, s32[32,128]{1,0:T(8,128)S(1)} %convolution_convert_fusion.5, pred[32,128]{1,0:T(8,128)(4,1)S(1)} %bitcast.56), kind=kOutput, calls=%fused_computation | convolution fusion | flops 712376320 | bytes 20205568 | tf_op jit(solution)/shard_map/dot_general | solution.py:114
  465.8 10.6 multiply_convert_fusion.1
  476.3 11.7 %convolution_convert_fusion.1 = bf16[32,128,1792]{2,1,0:T(8,128)(2,1)} fusion(bf16[32,48,1792]{2,1,0:T(8,128)(2,1)} %bitcast.51, s32[32,128]{1,0:T(8,128)S(1)} %convolution_convert_fusion.5, pred[32,128]{1,0:T(8,128)(4,1)S(1)} %bitcast.57), kind=kOutput, calls=%fused_computation.1 | convolution fusion | flops 712376320 | bytes 20205568 | tf_op jit(solution)/shard_map/dot_general | solution.py:114
  489.9 3.6 collective-permute-done
  495.4 4.0 collective-permute-done.1
  502.1 2.1 collective-permute-done.2
  504.8 4.9 collective-permute-done.3
  509.8 4.9 collective-permute-done.4
  517.2 264.0 %reduce-scatter.8.cloned.1.call-done = bf16[128,1792]{1,0:T(8,128)(2,1)} async-done(((bf16[4096,1792]{1,0:T(8,128)(2,1)}), bf16[128,1792]{1,0:T(8,128)(2,1)}) %reduce-scatter.8.cloned.1.call-update) | async-done | bytes 458768 | tf_op jit(solution)/shard_map/reduce_scatter | solution.py:121
  781.2 320.6 %reduce-scatter.6.cloned.1.call-done = bf16[128,1792]{1,0:T(8,128)(2,1)} async-done(((bf16[4096,1792]{1,0:T(8,128)(2,1)}), bf16[128,1792]{1,0:T(8,128)(2,1)}) %reduce-scatter.6.cloned.1.call-update) | async-done | bytes 458768 | tf_op jit(solution)/shard_map/reduce_scatter | solution.py:121
  (70 shorter events, 18.5 us)
Async XLA Ops:
  7.2 86.5 %copy-start = (bf16[512,2048]{1,0:T(8,128)(2,1)S(1)}, bf16[512,2048]{1,0:T(8,128)(2,1)}, u32[]{:S(2)}) copy-start(bf16[512,2048]{1,0:T(8,128)(2,1)} %param.11) | copy-start | bytes 6291460
  7.2 86.5 %all-gather.4.cloned.1.call-start = ((), (), s32[]{:S(2)}) async-start(), calls=%async_computation.3 | async-start | bytes 16515072 | tf_op jit(solution)/shard_map/all_gather | solution.py:14
  7.9 98.2 %copy-start.6 = (f32[16]{0:T(128)S(1)}, f32[16]{0:T(128)}, u32[]{:S(2)}) copy-start(f32[16]{0:T(128)} %param.20) | copy-start | bytes 196
  7.9 166.7 %copy-start.2 = (bf16[128,3584]{1,0:T(8,128)(2,1)S(1)}, bf16[128,3584]{1,0:T(8,128)(2,1)}, u32[]{:S(2)}) copy-start(bf16[128,3584]{1,0:T(8,128)(2,1)} %param.13) | copy-start | bytes 2752516
  7.9 168.2 %copy-start.3 = (f32[3584]{0:T(1024)S(1)}, f32[3584]{0:T(1024)}, u32[]{:S(2)}) copy-start(f32[3584]{0:T(1024)} %param.14) | copy-start | bytes 43012
  7.9 166.6 %reduce-scatter.4.cloned.1.call-start = ((), (), s32[]{:S(2)}) async-start(), calls=%async_computation.4 | async-start | bytes 4587520 | tf_op jit(solution)/shard_map/reduce_scatter | solution.py:17
  106.0 75.3 %copy-start.7 = (f32[16]{0:T(128)S(1)}, f32[16]{0:T(128)}, u32[]{:S(2)}) copy-start(f32[16]{0:T(128)} %param.21) | copy-start | bytes 196
  106.0 77.9 %copy-start.4 = (s32[128,8]{0,1:T(8,128)S(1)}, s32[128,8]{0,1:T(8,128)}, u32[]{:S(2)}) copy-start(s32[128,8]{0,1:T(8,128)} %param.15) | copy-start | bytes 12292
  106.0 147.8 %copy-start.5 = (f32[128,8]{0,1:T(8,128)S(1)}, f32[128,8]{0,1:T(8,128)}, u32[]{:S(2)}) copy-start(f32[128,8]{0,1:T(8,128)} %param.16) | copy-start | bytes 12292
  106.0 214.1 %all-gather.8.cloned.1.call-start = ((), (), s32[]{:S(2)}) async-start(), calls=%async_computation.6 | async-start | bytes 15138816 | tf_op jit(solution)/shard_map/all_gather | solution.py:96
  180.7 213.9 %all-gather.6.cloned.1.call-start = ((), (), s32[]{:S(2)}) async-start(), calls=%async_computation.5 | async-start | bytes 15138816 | tf_op jit(solution)/shard_map/all_gather | solution.py:96
  181.3 599.9 %reduce-scatter.8.cloned.1.call-start = ((), (), s32[]{:S(2)}) async-start(), calls=%async_computation.8 | async-start | bytes 15138816 | tf_op jit(solution)/shard_map/reduce_scatter | solution.py:121
  401.8 19.4 %slice-start = ((s8[5505024]{0:T(1024)(128)(4,1)}), s8[4194304]{0:T(1024)(128)(4,1)S(1)}, s32[]{:S(2)}) async-start(s8[5505024]{0:T(1024)(128)(4,1)} %bitcast.45), calls=%async_computation.9 | async-start | bytes 8388608
  401.9 19.4 %slice-start.2 = ((s8[7340032]{0:T(1024)(128)(4,1)}), s8[4194304]{0:T(1024)(128)(4,1)S(1)}, s32[]{:S(2)}) async-start(s8[7340032]{0:T(1024)(128)(4,1)} %bitcast.61), calls=%async_computation.11 | async-start | bytes 8388608
  411.6 9.7 slice-start.1
  411.6 9.7 slice-start.3
  411.6 17.8 %slice-start.4 = ((s8[7340032]{0:T(1024)(128)(4,1)}), s8[3145728]{0:T(1024)(128)(4,1)S(1)}, s32[]{:S(2)}) async-start(s8[7340032]{0:T(1024)(128)(4,1)} %bitcast.63), calls=%async_computation.13 | async-start | bytes 6291456
  465.7 636.1 %reduce-scatter.6.cloned.1.call-start = ((), (), s32[]{:S(2)}) async-start(), calls=%async_computation.7 | async-start | bytes 15138816 | tf_op jit(solution)/shard_map/reduce_scatter | solution.py:121
  488.1 616.5 %copy-start.1 = (bf16[512,2048]{1,0:T(8,128)(2,1)S(1)}, bf16[512,2048]{1,0:T(8,128)(2,1)}, u32[]{:S(2)}) copy-start(bf16[512,2048]{1,0:T(8,128)(2,1)} %param.11) | copy-start | bytes 6291460
  489.6 3.9 collective-permute-start
  494.9 4.4 collective-permute-start.1
  500.7 3.5 collective-permute-start.2
  504.2 5.5 collective-permute-start.3
  509.8 4.9 collective-permute-start.4
  (1 other events, 8.2 us)
Sparse Core Ops, SparseCore 0:
  9.9 83.6 all-gather.3
  106.2 68.3 reduce-scatter.3
  180.8 106.9 all-gather.7
  290.5 104.0 all-gather.5
  465.8 315.3 reduce-scatter.7
  783.4 318.3 reduce-scatter.5

commit v2 on v1

--- a/solution.py
+++ b/solution.py
@@ -1,11 +1,16 @@
+import functools
+
 import jax
 import jax.numpy as jnp
 from jax import lax
+from jax.experimental import pallas as pl
+from jax.experimental.pallas import tpu as pltpu
 from jax.sharding import PartitionSpec as P
 
 FP8_LIMIT = 448.0
 AXES = ("dp", "tensor")
 CHUNKS = 2
+VMEM_LIMIT = 40 * 2**20
 
 
 def project(attn_out, out_weight):
@@ -40,7 +45,7 @@
 def exchange_plan(
     quantized, stream, expert_ids, route_weight, weights, inv_x, scale_h, inv_h, capacity, experts
 ):
-    w_gate, w_up, w_down = weights
+    w_gate, w_up, w_down = (weight[0] for weight in weights)
     local_rows, width = quantized.shape
     top_count = expert_ids.shape[1]
     position = slots_of(expert_ids, experts, capacity)
@@ -70,57 +75,206 @@
     return (stream + mixture).astype(jnp.bfloat16), jnp.max(jnp.abs(hidden))
 
 
+def swap(value, bits):
+    count = lax.axis_size("dp")
+    return lax.ppermute(value, "dp", [(i, i ^ bits) for i in range(count)])
+
+
+def route_table(expert_ids, route_weight, experts):
+    rows = expert_ids.shape[0]
+    names = jnp.arange(experts, dtype=jnp.int32)[:, None, None]
+    table = jnp.sum(jnp.where(expert_ids[None] == names, route_weight[None], 0.0), axis=2)
+    count = lax.axis_size("tensor")
+    here = lax.axis_index("tensor")
+    parts = [table]
+    for shift in range(1, count):
+        pairs = [(i, (i + shift) % count) for i in range(count)]
+        parts.append(lax.ppermute(table, "tensor", pairs))
+    order = (here - jnp.arange(count)) % count
+    table = jnp.stack(parts)[order]
+    bit = 1
+    while bit < lax.axis_size("dp"):
+        table = jnp.concatenate([table, swap(table, bit)])
+        bit *= 2
+    mine = lax.axis_index("dp") * count + here
+    table = lax.dynamic_index_in_dim(table, mine, axis=1, keepdims=False)
+    return table.reshape(-1, count, rows)
+
+
+def gate_up_kernel(counts, first, last, *refs):
+    refs = list(refs)
+    scale_ref, chosen_ref = refs.pop(0), refs.pop(0)
+    pieces = [refs.pop(0) for _ in counts]
+    gate_w, up_w = refs.pop(0), refs.pop(0)
+    before = [] if first else [refs.pop(0), refs.pop(0)]
+    rows = refs.pop()
+    capacity = chosen_ref.shape[1]
+
+    @pl.when(pl.program_id(0) == 0)
+    def _():
+        source = 0
+        for piece, count in zip(pieces, counts):
+            for i in range(count):
+                picked = jnp.dot(chosen_ref[source], piece[i], preferred_element_type=jnp.float32)
+                rows[source * capacity : (source + 1) * capacity] = picked.astype(rows.dtype)
+                source += 1
+
+    gate = jnp.dot(rows[...], gate_w[0], preferred_element_type=jnp.float32)
+    up = jnp.dot(rows[...], up_w[0], preferred_element_type=jnp.float32)
+    if not first:
+        gate += before[0][...]
+        up += before[1][...]
+    if not last:
+        refs[0][...] = gate
+        refs[1][...] = up
+        return
+    inv_x, scale_h = scale_ref[0], scale_ref[1]
+    gate, up = gate * inv_x, up * inv_x
+    hidden = gate / (1.0 + jnp.exp(-gate)) * up
+    refs[0][...] = jnp.clip(hidden * scale_h, -FP8_LIMIT, FP8_LIMIT).astype(jnp.bfloat16)
+    peak = jnp.max(jnp.abs(hidden), axis=0, keepdims=True)
+    refs[1][...] = jnp.broadcast_to(peak, refs[1].shape)
+
+
+def gate_up(scales, chosen, pieces, w_gate, w_up, c, before, last):
+    sources, capacity, tokens = chosen.shape
+    step = pieces[0].shape[-1]
+    hidden = w_gate.shape[2]
+    tile = min(256, hidden)
+    rows = sources * capacity
+    whole = lambda shape: pl.BlockSpec(shape, lambda n: (0,) * len(shape))
+    column = lambda height: pl.BlockSpec((height, tile), lambda n: (0, n))
+    weight = pl.BlockSpec((1, step, tile), lambda n: (0, c, n))
+    if last:
+        out_shape = [
+            jax.ShapeDtypeStruct((rows, hidden), jnp.bfloat16),
+            jax.ShapeDtypeStruct((8, hidden), jnp.float32),
+        ]
+        out_specs = [column(rows), column(8)]
+    else:
+        out_shape = [jax.ShapeDtypeStruct((rows, hidden), jnp.float32)] * 2
+        out_specs = [column(rows)] * 2
+    return pl.pallas_call(
+        functools.partial(gate_up_kernel, [p.shape[0] for p in pieces], not before, last),
+        grid=(hidden // tile,),
+        in_specs=[pl.BlockSpec(memory_space=pltpu.SMEM), whole(chosen.shape)]
+        + [whole(p.shape) for p in pieces]
+        + [weight] * 2
+        + [column(rows)] * len(before),
+        out_specs=out_specs,
+        out_shape=out_shape,
+        scratch_shapes=[pltpu.VMEM((rows, step), jnp.bfloat16)],
+        compiler_params=pltpu.CompilerParams(vmem_limit_bytes=VMEM_LIMIT),
+        cost_estimate=pl.CostEstimate(
+            flops=2 * rows * step * (2 * hidden + tokens),
+            bytes_accessed=2 * step * (2 * hidden + sources * tokens) + 16 * rows * hidden,
+            transcendentals=rows * hidden if last else 0,
+        ),
+        name="gate_up",
+    )(scales, chosen, *pieces, w_gate, w_up, *before)
+
+
+def down_kernel(hidden_ref, down_w, factor_ref, spread_ref, own_ref, other_ref):
+    sources, tokens, capacity = spread_ref.shape
+    terms = jnp.dot(hidden_ref[...], down_w[0], preferred_element_type=jnp.float32)
+    terms = (terms * factor_ref[...]).astype(jnp.bfloat16)
+    half = sources // 2
+    for source in range(sources):
+        spread = jnp.dot(
+            spread_ref[source],
+            terms[source * capacity : (source + 1) * capacity],
+            preferred_element_type=jnp.float32,
+        ).astype(jnp.bfloat16)
+        if source < half:
+            own_ref[source] = spread
+        else:
+            other_ref[source - half] = spread
+
+
+def down(hidden_q, w_down, factor, spread, c, step):
+    rows, hidden = hidden_q.shape
+    sources, tokens, capacity = spread.shape
+    tile = 256 if step % 256 == 0 else 128
+    tiles = step // tile
+    whole = lambda shape: pl.BlockSpec(shape, lambda j: (0,) * len(shape))
+    return pl.pallas_call(
+        down_kernel,
+        grid=(tiles,),
+        in_specs=[
+            whole(hidden_q.shape),
+            pl.BlockSpec((1, hidden, tile), lambda j: (0, 0, c * tiles + j)),
+            whole(factor.shape),
+            whole(spread.shape),
+        ],
+        out_specs=[pl.BlockSpec((sources // 2, tokens, tile), lambda j: (0, 0, j))] * 2,
+        out_shape=[jax.ShapeDtypeStruct((sources // 2, tokens, step), jnp.bfloat16)] * 2,
+        compiler_params=pltpu.CompilerParams(vmem_limit_bytes=VMEM_LIMIT),
+        cost_estimate=pl.CostEstimate(
+            flops=2 * rows * step * (hidden + tokens),
+            bytes_accessed=2 * step * (hidden + sources * tokens),
+            transcendentals=0,
+        ),
+        name="down",
+    )(hidden_q, w_down, factor, spread)
+
+
+def add(*terms):
+    return sum(t.astype(jnp.float32) for t in terms).astype(jnp.bfloat16)
+
+
 def gather_plan(
     quantized, stream, expert_ids, route_weight, weights, inv_x, scale_h, inv_h, capacity, experts
 ):
     w_gate, w_up, w_down = weights
     local_rows, width = quantized.shape
-    mine = lax.axis_index("dp") * lax.axis_size("tensor") + lax.axis_index("tensor")
-    all_ids = lax.all_gather(expert_ids, AXES, axis=0, tiled=True)
-    all_weights = lax.all_gather(route_weight, AXES, axis=0, tiled=True)
-    hit = all_ids == mine
-    named = jnp.any(hit, axis=1).reshape(experts, local_rows)
-    weight = jnp.sum(jnp.where(hit, all_weights, 0.0), axis=1).reshape(experts, local_rows)
+    layers = lax.axis_size("tensor")
+    half = layers // 2
+    weight = route_table(expert_ids, route_weight, experts)
+    named = weight > 0.0
     earlier = jnp.triu(jnp.ones((local_rows, local_rows), jnp.bfloat16), 1)
-    slot = jnp.dot(named.astype(jnp.bfloat16), earlier, preferred_element_type=jnp.float32)
-    slot = slot.astype(jnp.int32)
+    slot = lax.dot_general(
+        named.astype(jnp.bfloat16), earlier, (((2,), (0,)), ((), ())),
+        preferred_element_type=jnp.float32,
+    ).astype(jnp.int32)
     chosen = (
-        slot[:, None, :] == jnp.arange(capacity, dtype=jnp.int32)[None, :, None]
-    ) & named[:, None, :]
-    slot_weight = jnp.sum(jnp.where(chosen, weight[:, None, :], 0.0), axis=2)
-    chosen = chosen.astype(jnp.bfloat16)
+        slot[:, :, None, :] == jnp.arange(capacity, dtype=jnp.int32)[:, None]
+    ) & named[:, :, None, :]
+    factor = jnp.sum(jnp.where(chosen, weight[:, :, None, :], 0.0), axis=3) * inv_h
+    chosen = chosen.astype(jnp.bfloat16).reshape(4, 2 * layers, capacity, local_rows)
+    factor = factor.reshape(4, 2 * layers * capacity, 1)
+    spread = chosen.transpose(0, 1, 3, 2)
+    scales = jnp.stack([inv_x, scale_h])
     step = width // CHUNKS
-    gate = up = 0.0
+
+    sums = [[] for _ in range(4)]
     for c in range(CHUNKS):
         part = slice(c * step, (c + 1) * step)
-        tokens = lax.all_gather(quantized[:, part], AXES, axis=0, tiled=True)
-        rows = lax.dot_general(
-            chosen,
-            tokens.reshape(experts, local_rows, step),
-            (((2,), (1,)), ((0,), (0,))),
-            preferred_element_type=jnp.float32,
-        )
-        rows = rows.astype(jnp.bfloat16).reshape(experts * capacity, step)
-        gate += jnp.dot(rows, w_gate[part], preferred_element_type=jnp.float32)
-        up += jnp.dot(rows, w_up[part], preferred_element_type=jnp.float32)
-    hidden = jax.nn.silu(gate * inv_x) * (up * inv_x)
-    peak_h = jnp.max(jnp.abs(hidden))
-    hidden_q = jnp.clip(hidden * scale_h, -FP8_LIMIT, FP8_LIMIT).astype(jnp.bfloat16)
-    factor = slot_weight.reshape(-1, 1) * inv_h
-    pieces = []
+        own = lax.all_gather(quantized[:, part], "tensor", axis=0).reshape(layers, local_rows, step)
+        along_x, along_y = swap(own, 2), swap(own, 4)
+        diagonal = [swap(along_x[:half], 4), swap(along_y[half:], 2)]
+        groups = [[own], [along_x], [along_y], diagonal]
+        for r, group in enumerate(groups):
+            pieces = group + [swap(piece, 1) for piece in group]
+            sums[r] = gate_up(
+                scales, chosen[r], pieces, w_gate, w_up, c, sums[r], c == CHUNKS - 1
+            )
+    peak_h = jnp.max(jnp.stack([jnp.max(s[1]) for s in sums]))
+
+    outputs = []
     for c in range(CHUNKS):
         part = slice(c * step, (c + 1) * step)
-        terms = jnp.dot(hidden_q, w_down[:, part], preferred_element_type=jnp.float32) * factor
-        spread = lax.dot_general(
-            chosen,
-            terms.astype(jnp.bfloat16).reshape(experts, capacity, step),
-            (((1,), (1,)), ((0,), (0,))),
-            preferred_element_type=jnp.float32,
-        )
-        spread = spread.astype(jnp.bfloat16).reshape(experts * local_rows, step)
-        mixed = lax.psum_scatter(spread, AXES, scatter_dimension=0, tiled=True)
-        pieces.append((stream[:, part] + mixed.astype(jnp.float32)).astype(jnp.bfloat16))
-    return jnp.concatenate(pieces, axis=1), peak_h
+        to = []
+        for r in range(4):
+            kept, given = down(sums[r][0], w_down, factor[r], spread[r], c, step)
+            taken = swap(given, 1)
+            to.append([add(kept[:half], taken[:half]), add(kept[half:], taken[half:])])
+        over_x, over_y = swap(to[3][0], 2), swap(to[3][1], 4)
+        low = add(to[0][0], swap(to[1][0], 2), swap(add(to[2][0], over_x), 4))
+        high = add(to[0][1], swap(add(to[1][1], over_y), 2), swap(to[2][1], 4))
+        mixed = jnp.concatenate([low, high]).reshape(layers * local_rows, step)
+        mixed = lax.psum_scatter(mixed, "tensor", scatter_dimension=0, tiled=True)
+        outputs.append((stream[:, part] + mixed.astype(jnp.float32)).astype(jnp.bfloat16))
+    return jnp.concatenate(outputs, axis=1), peak_h
 
 
 def body(
@@ -147,13 +301,14 @@
     peak_x = jnp.max(jnp.abs(normed))
     top_x, top_h = jnp.max(history_x), jnp.max(history_h)
     quantized = jnp.clip(normed * (FP8_LIMIT / top_x), -FP8_LIMIT, FP8_LIMIT).astype(jnp.bfloat16)
-    plan = gather_plan if local_rows < 4 * capacity else exchange_plan
+    gathers = lax.axis_size("dp") == 8 and local_rows < 4 * capacity
+    plan = gather_plan if gathers else exchange_plan
     layer_out, peak_h = plan(
         quantized,
         stream,
         expert_ids,
         route_weight,
-        (w_gate[0], w_up[0], w_down[0]),
+        (w_gate, w_up, w_down),
         top_x / FP8_LIMIT,
         FP8_LIMIT / top_h,
         top_h / FP8_LIMIT,

time: 1110 us -> 665 us (0.60)
  waiting for transfers between devices: 823 us -> 405 us
  blocking collectives: 135 us -> 0 us
  Pallas kernels: 0 us -> 114 us
  matrix products: 116 us -> 12.5 us
  local copies, waits for them, and re-layouts: 1.76 us -> 42.1 us
  starting transfers between devices: 3 us -> 29.8 us
  other arithmetic: 15.8 us -> 40.9 us
    reduce_scatter x2, waiting for transfers between devices: 585 us -> 5.87 us  [gather_plan(): mixed = lax.psum_scatter(mixed, 'tensor', scatter_dimension=0, tiled=True)]
    ppermute x0 -> x44, waiting for transfers between devices: none -> 146 us  [the longest x41 132 us: swap(): return lax.ppermute(value, 'dp', [(i, i ^ bits) for i in range(count)])]
    all_gather x2 -> x0, blocking collectives: 135 us -> none  [the longest x1 69.9 us: gather_plan(): all_ids = lax.all_gather(expert_ids, AXES, axis=0, tiled=True)]
    pallas_call x0 -> x16, Pallas kernels: none -> 114 us  [the longest x8 60.9 us: gate_up(): pl.pallas_call(functools.partial(gate_up_kernel, [p.shape[0] for p in pie...]
    dot_general x11 -> x1, matrix products: 103 us -> 0.13 us  [gather_plan(): lax.dot_general(named.astype(jnp.bfloat16), earlier, (((2,), (0,)), ((),...]
    unnamed x28 -> x125, local copies, waits for them, and re-layouts: 0.07 us -> 28.3 us
    ppermute x0 -> x44, starting transfers between devices: none -> 27.5 us  [the longest x41 27.1 us: swap(): return lax.ppermute(value, 'dp', [(i, i ^ bits) for i in range(count)])]
    convert_element_type x0 -> x10, other arithmetic: none -> 22.9 us  [the longest x8 21.3 us: add(): return sum((t.astype(jnp.float32) for t in terms)).astype(jnp.bfloat16)]
  transfers between devices with their start and end apart: 11 -> 55, of which waited for: 10 -> 25; matrix products, arithmetic and copies ran while one was open for 4% -> 7% of each run, Pallas kernels for 0% -> 17%
where the time goes in v2:
time: 665 us; the launch traced here: 664 us
  waiting for transfers between devices  405 us (61%)
  Pallas kernels  114 us (17%)
  local copies, waits for them, and re-layouts  42.1 us (6%)
  other arithmetic  40.9 us (6%)
  starting transfers between devices  29.8 us (4%)
  between operations  20 us (3%)
  matrix products  12.5 us (2%)
    ppermute x41, waiting for transfers between devices, swap(): return lax.ppermute(value, 'dp', [(i, i ^ bits) for i in range(count)])  132 us
    all_gather x1, waiting for transfers between devices, project(): lax.all_gather(out_weight, 'dp', axis=1, tiled=True)  85.7 us
    all_gather x2, waiting for transfers between devices, gather_plan(): lax.all_gather(quantized[:, part], 'tensor', axis=0)  80.1 us
    reduce_scatter x1, waiting for transfers between devices, project(): lax.psum_scatter(head_terms.astype(jnp.bfloat16), 'tensor', scatter_dimen...  66.6 us
    pallas_call x8, Pallas kernels, gate_up(): pl.pallas_call(functools.partial(gate_up_kernel, [p.shape[0] for p in pie...  60.9 us
    pallas_call x8, Pallas kernels, down(): pl.pallas_call(down_kernel, grid=(tiles,), in_specs=[whole(hidden_q.shape...  52.9 us
    unnamed x125, local copies, waits for them, and re-layouts  28.3 us
    ppermute x41, starting transfers between devices, swap(): return lax.ppermute(value, 'dp', [(i, i ^ bits) for i in range(count)])  27.1 us
  transfers between devices with their start and end apart: 55, of which 25 were waited for; matrix products, arithmetic and copies ran while one was open for 7% of the time, Pallas kernels for 17%

profile of v2, /device:TPU:0, one launch (start us, length us, event | category | flops | bytes accessed | tf_op | source)
XLA Modules:
  0.0 664.3 jit_solution(15412698233688100792)
XLA Ops:
  8.0 85.7 %all-gather.6.cloned.1.call-done = bf16[2048,3584]{0,1:T(8,128)(2,1)} async-done(((bf16[2048,448]{0,1:T(8,128)(2,1)}), bf16[2048,3584]{0,1:T(8,128)(2,1)}) %all-gather.6.cloned.1.call-update) | async-done | bytes 14680080 | tf_op jit(solution)/shard_map/all_gather | solution.py:19
  93.6 12.3 %convolution_convert_fusion = bf16[512,3584]{1,0:T(8,128)(2,1)} fusion(bf16[512,2048]{1,0:T(8,128)(2,1)S(1)} %copy-done, bf16[2048,3584]{0,1:T(8,128)(2,1)} %all-gather.6.cloned.1.call-done), kind=kOutput, calls=%fused_computation.1 | convolution fusion | flops 7518027776 | bytes 20447232 | tf_op jit(solution)/shard_map/dot_general | solution.py:17
  107.9 66.6 %reduce-scatter.4.cloned.1.call-done = bf16[128,3584]{1,0:T(8,128)(2,1)} async-done(((bf16[512,3584]{1,0:T(8,128)(2,1)}), bf16[128,3584]{1,0:T(8,128)(2,1)}) %reduce-scatter.4.cloned.1.call-update) | async-done | bytes 917520 | tf_op jit(solution)/shard_map/reduce_scatter | solution.py:22
  180.2 41.3 %all-gather.10.cloned.1.call-done = bf16[512,1792]{1,0:T(8,128)(2,1)} async-done(((bf16[128,1792]{1,0:T(8,128)(2,1)}), bf16[512,1792]{1,0:T(8,128)(2,1)}) %all-gather.10.cloned.1.call-update) | async-done | bytes 1835024 | tf_op jit(solution)/shard_map/all_gather | solution.py:252
  224.4 38.8 %all-gather.8.cloned.1.call-done = bf16[512,1792]{1,0:T(8,128)(2,1)} async-done(((bf16[128,1792]{1,0:T(8,128)(2,1)}), bf16[512,1792]{1,0:T(8,128)(2,1)}) %all-gather.8.cloned.1.call-update) | async-done | bytes 1835024 | tf_op jit(solution)/shard_map/all_gather | solution.py:252
  284.2 23.8 %collective-permute-done.4 = f32[8,32,128]{2,1,0:T(8,128)S(1)} collective-permute-done((f32[8,32,128]{2,1,0:T(8,128)S(1)}, f32[8,32,128]{2,1,0:T(8,128)S(1)}, u32[]{:S(2)}, u32[]{:S(2)}) %collective-permute-start.4) | collective-permute-done | bytes 131104 | tf_op jit(solution)/shard_map/ppermute | solution.py:80
  315.9 15.8 %collective-permute-done.5 = f32[16,32,128]{2,1,0:T(8,128)S(1)} collective-permute-done((f32[16,32,128]{2,1,0:T(8,128)S(1)}, f32[16,32,128]{2,1,0:T(8,128)S(1)}, u32[]{:S(2)}, u32[]{:S(2)}) %collective-permute-start.5) | collective-permute-done | bytes 262176 | tf_op jit(solution)/shard_map/ppermute | solution.py:80
  338.3 16.8 %collective-permute-done.20.refs_2_ = bf16[2,128,1792]{2,1,0:T(8,128)(2,1)S(1)} collective-permute-done((bf16[2,128,1792]{2,1,0:T(8,128)(2,1)}, bf16[2,128,1792]{2,1,0:T(8,128)(2,1)S(1)}, u32[]{:S(2)}, u32[]{:S(2)}) %collective-permute-start.20) | collective-permute-done | bytes 917536 | tf_op jit(solution)/shard_map/ppermute | solution.py:80
  364.4 7.4 %gate_up.14 = (f32[384,1024]{1,0:T(8,128)S(1)}, f32[384,1024]{1,0:T(8,128)S(1)}) custom-call(f32[2]{0:T(128)S(1)} %pad_maximum_fusion.6.refs_0_, bf16[8,48,128]{2,1,0:T(8,128)(2,1)S(1)} %bitcast.53, bf16[2,128,1792]{2,1,0:T(8,128)(2,1)} %collective-permute-done.24.refs_2_, bf16[2,128,1792]{2,1,0:T(8,128)(2,1)} %collective-permute-done.25.refs_3_, ...), custom_call_target="tpu_custom_call" | custom-call | flops 2994733056 | bytes 17301504 | tf_op jit(solution)/shard_map/gate_up/pallas_call | solution.py:157
  379.2 7.2 %gate_up.15 = (bf16[384,1024]{1,0:T(8,128)(2,1)S(1)}, f32[8,1024]{1,0:T(8,128)S(1)}) custom-call(f32[2]{0:T(128)S(1)} %pad_maximum_fusion.6.refs_0_, bf16[8,48,128]{2,1,0:T(8,128)(2,1)S(1)} %bitcast.54, bf16[2,128,1792]{2,1,0:T(8,128)(2,1)S(1)} %copy-done.34, bf16[2,128,1792]{2,1,0:T(8,128)(2,1)} %collective-permute-done.21.refs_3_, ...), custom_call_target="tpu_custom_call" | custom-call | flops 2994733056 | bytes 17301504 | tf_op jit(solution)/shard_map/gate_up/pallas_call | solution.py:157
  386.4 6.7 %down.15 = (bf16[4,128,1792]{2,1,0:T(8,128)(2,1)S(1)}, bf16[4,128,1792]{2,1,0:T(8,128)(2,1)}) custom-call(bf16[384,1024]{1,0:T(8,128)(2,1)S(1)} %get-tuple-element.52.hidden_ref, bf16[1,1024,3584]{2,1,0:T(8,128)(2,1)S(1)} %bitcast.44, f32[384,1]{1,0:T(8,128)S(1)} %squeeze.65.factor_ref, bf16[8,128,48]{2,1,0:T(8,128)(2,1)S(1)} %get-tuple-element.91.spread_ref), custom_call_target="tpu_custom_call" | custom-call | flops 1585446912 | bytes 7340032 | tf_op jit(solution)/shard_map/down/pallas_call | solution.py:200
  400.5 7.4 %gate_up.8 = (f32[384,1024]{1,0:T(8,128)S(1)}, f32[384,1024]{1,0:T(8,128)S(1)}) custom-call(f32[2]{0:T(128)S(1)} %pad_maximum_fusion.6.refs_0_, bf16[8,48,128]{2,1,0:T(8,128)(2,1)S(1)} %bitcast.47, bf16[4,128,1792]{2,1,0:T(8,128)(2,1)} %bitcast.11.refs_2_, bf16[4,128,1792]{2,1,0:T(8,128)(2,1)} %collective-permute-done.7.refs_3_, ...), custom_call_target="tpu_custom_call" | custom-call | flops 2994733056 | bytes 17301504 | tf_op jit(solution)/shard_map/gate_up/pallas_call | solution.py:157
  410.2 7.4 %gate_up.10 = (f32[384,1024]{1,0:T(8,128)S(1)}, f32[384,1024]{1,0:T(8,128)S(1)}) custom-call(f32[2]{0:T(128)S(1)} %pad_maximum_fusion.6.refs_0_, bf16[8,48,128]{2,1,0:T(8,128)(2,1)S(1)} %bitcast.51, bf16[4,128,1792]{2,1,0:T(8,128)(2,1)} %collective-permute-done.11.refs_2_, bf16[4,128,1792]{2,1,0:T(8,128)(2,1)} %collective-permute-done.12.refs_3_, ...), custom_call_target="tpu_custom_call" | custom-call | flops 2994733056 | bytes 17301504 | tf_op jit(solution)/shard_map/gate_up/pallas_call | solution.py:157
  418.7 8.3 %gate_up.11 = (bf16[384,1024]{1,0:T(8,128)(2,1)S(1)}, f32[8,1024]{1,0:T(8,128)S(1)}) custom-call(f32[2]{0:T(128)S(1)} %pad_maximum_fusion.6.refs_0_, bf16[8,48,128]{2,1,0:T(8,128)(2,1)S(1)} %bitcast.52, bf16[4,128,1792]{2,1,0:T(8,128)(2,1)} %collective-permute-done.9.refs_2_, bf16[4,128,1792]{2,1,0:T(8,128)(2,1)} %collective-permute-done.10.refs_3_, ...), custom_call_target="tpu_custom_call" | custom-call | flops 2994733056 | bytes 17301504 | tf_op jit(solution)/shard_map/gate_up/pallas_call | solution.py:157
  438.6 7.4 %gate_up.12 = (f32[384,1024]{1,0:T(8,128)S(1)}, f32[384,1024]{1,0:T(8,128)S(1)}) custom-call(f32[2]{0:T(128)S(1)} %pad_maximum_fusion.6.refs_0_, bf16[8,48,128]{2,1,0:T(8,128)(2,1)S(1)} %bitcast.49, bf16[4,128,1792]{2,1,0:T(8,128)(2,1)} %collective-permute-done.17.refs_2_, bf16[4,128,1792]{2,1,0:T(8,128)(2,1)} %collective-permute-done.18.refs_3_, ...), custom_call_target="tpu_custom_call" | custom-call | flops 2994733056 | bytes 17301504 | tf_op jit(solution)/shard_map/gate_up/pallas_call | solution.py:157
  446.1 7.6 %gate_up.13 = (bf16[384,1024]{1,0:T(8,128)(2,1)S(1)}, f32[8,1024]{1,0:T(8,128)S(1)}) custom-call(f32[2]{0:T(128)S(1)} %pad_maximum_fusion.6.refs_0_, bf16[8,48,128]{2,1,0:T(8,128)(2,1)S(1)} %bitcast.50, bf16[4,128,1792]{2,1,0:T(8,128)(2,1)S(1)} %collective-permute-done.15.refs_2_, bf16[4,128,1792]{2,1,0:T(8,128)(2,1)} %collective-permute-done.16.refs_3_, ...), custom_call_target="tpu_custom_call" | custom-call | flops 2994733056 | bytes 17301504 | tf_op jit(solution)/shard_map/gate_up/pallas_call | solution.py:157
  453.7 6.9 %down.14 = (bf16[4,128,1792]{2,1,0:T(8,128)(2,1)S(1)}, bf16[4,128,1792]{2,1,0:T(8,128)(2,1)}) custom-call(bf16[384,1024]{1,0:T(8,128)(2,1)S(1)} %get-tuple-element.47.hidden_ref, bf16[1,1024,3584]{2,1,0:T(8,128)(2,1)S(1)} %bitcast.46, f32[384,1]{1,0:T(8,128)S(1)} %copy-done.24, bf16[8,128,48]{2,1,0:T(8,128)(2,1)S(1)} %copy-done.7), custom_call_target="tpu_custom_call" | custom-call | flops 1585446912 | bytes 7340032 | tf_op jit(solution)/shard_map/down/pallas_call | solution.py:200
  465.2 8.1 %gate_up.9 = (bf16[384,1024]{1,0:T(8,128)(2,1)S(1)}, f32[8,1024]{1,0:T(8,128)S(1)}) custom-call(f32[2]{0:T(128)S(1)} %pad_maximum_fusion.6.refs_0_, bf16[8,48,128]{2,1,0:T(8,128)(2,1)S(1)} %bitcast.48, bf16[4,128,1792]{2,1,0:T(8,128)(2,1)} %bitcast.10.refs_2_, bf16[4,128,1792]{2,1,0:T(8,128)(2,1)} %collective-permute-done.6.refs_3_, ...), custom_call_target="tpu_custom_call" | custom-call | flops 2994733056 | bytes 17301504 | tf_op jit(solution)/shard_map/gate_up/pallas_call | solution.py:157
  473.3 6.7 %down.12 = (bf16[4,128,1792]{2,1,0:T(8,128)(2,1)S(1)}, bf16[4,128,1792]{2,1,0:T(8,128)(2,1)}) custom-call(bf16[384,1024]{1,0:T(8,128)(2,1)S(1)} %get-tuple-element.37.hidden_ref, bf16[1,1024,3584]{2,1,0:T(8,128)(2,1)S(1)} %bitcast.46, f32[384,1]{1,0:T(8,128)S(1)} %copy-done.20, bf16[8,128,48]{2,1,0:T(8,128)(2,1)S(1)} %copy-done.6), custom_call_target="tpu_custom_call" | custom-call | flops 1585446912 | bytes 7340032 | tf_op jit(solution)/shard_map/down/pallas_call | solution.py:200
  492.9 10.8 %collective-permute-done.39 = bf16[2,128,1792]{2,1,0:T(8,128)(2,1)} collective-permute-done((bf16[2,128,1792]{2,1,0:T(8,128)(2,1)}, bf16[2,128,1792]{2,1,0:T(8,128)(2,1)}, u32[]{:S(2)}, u32[]{:S(2)}) %collective-permute-start.39) | collective-permute-done | bytes 917536 | tf_op jit(solution)/shard_map/ppermute | solution.py:80
  526.2 16.1 %collective-permute-done.42 = bf16[2,128,1792]{2,1,0:T(8,128)(2,1)S(1)} collective-permute-done((bf16[2,128,1792]{2,1,0:T(8,128)(2,1)}, bf16[2,128,1792]{2,1,0:T(8,128)(2,1)S(1)}, u32[]{:S(2)}, u32[]{:S(2)}) %collective-permute-start.42) | collective-permute-done | bytes 917536 | tf_op jit(solution)/shard_map/ppermute | solution.py:80
  543.7 6.7 %collective-permute-done.43 = bf16[2,128,1792]{2,1,0:T(8,128)(2,1)S(1)} collective-permute-done((bf16[2,128,1792]{2,1,0:T(8,128)(2,1)}, bf16[2,128,1792]{2,1,0:T(8,128)(2,1)S(1)}, u32[]{:S(2)}, u32[]{:S(2)}) %collective-permute-start.43) | collective-permute-done | bytes 917536 | tf_op jit(solution)/shard_map/ppermute | solution.py:80
  578.4 15.5 %collective-permute-done.14 = bf16[2,128,1792]{2,1,0:T(8,128)(2,1)S(1)} collective-permute-done((bf16[2,128,1792]{2,1,0:T(8,128)(2,1)S(1)}, bf16[2,128,1792]{2,1,0:T(8,128)(2,1)S(1)}, u32[]{:S(2)}, u32[]{:S(2)}) %collective-permute-start.14) | collective-permute-done | bytes 917536 | tf_op jit(solution)/shard_map/ppermute | solution.py:80
  594.0 18.1 %collective-permute-done.32 = bf16[2,128,1792]{2,1,0:T(8,128)(2,1)S(1)} collective-permute-done((bf16[2,128,1792]{2,1,0:T(8,128)(2,1)S(1)}, bf16[2,128,1792]{2,1,0:T(8,128)(2,1)S(1)}, u32[]{:S(2)}, u32[]{:S(2)}) %collective-permute-start.32) | collective-permute-done | bytes 917536 | tf_op jit(solution)/shard_map/ppermute | solution.py:80
  (295 shorter events, 194.7 us)
Async XLA Ops:
  7.2 86.5 %all-gather.6.cloned.1.call-start = ((), (), s32[]{:S(2)}) async-start(), calls=%async_computation.3 | async-start | bytes 16515072 | tf_op jit(solution)/shard_map/all_gather | solution.py:19
  7.9 166.6 %reduce-scatter.4.cloned.1.call-start = ((), (), s32[]{:S(2)}) async-start(), calls=%async_computation.4 | async-start | bytes 4587520 | tf_op jit(solution)/shard_map/reduce_scatter | solution.py:22
  106.0 115.5 %all-gather.10.cloned.1.call-start = ((), (), s32[]{:S(2)}) async-start(), calls=%async_computation.8 | async-start | bytes 2293760 | tf_op jit(solution)/shard_map/all_gather | solution.py:252
  179.6 83.7 %all-gather.8.cloned.1.call-start = ((), (), s32[]{:S(2)}) async-start(), calls=%async_computation.7 | async-start | bytes 2293760 | tf_op jit(solution)/shard_map/all_gather | solution.py:252
  180.1 468.4 %reduce-scatter.8.cloned.1.call-start = ((), (), s32[]{:S(2)}) async-start(), calls=%async_computation.6 | async-start | bytes 2293760 | tf_op jit(solution)/shard_map/reduce_scatter | solution.py:275
  221.5 59.4 %collective-permute-start.11 = (bf16[4,128,1792]{2,1,0:T(8,128)(2,1)}, bf16[4,128,1792]{2,1,0:T(8,128)(2,1)}, u32[]{:S(2)}, u32[]{:S(2)}) collective-permute-start(bf16[4,128,1792]{2,1,0:T(8,128)(2,1)} %bitcast.11.refs_2_), channel_id=1, source_target_pairs={{0,8},{4,12},{8,0},{12,4},{16,24},{20,28},{24,16},{28,20},{1,9},{5... | collective-permute-start | bytes 5505032 | tf_op jit(solution)/shard_map/ppermute | solution.py:80
  223.0 86.6 %collective-permute-start.17 = (bf16[4,128,1792]{2,1,0:T(8,128)(2,1)}, bf16[4,128,1792]{2,1,0:T(8,128)(2,1)}, u32[]{:S(2)}, u32[]{:S(2)}) collective-permute-start(bf16[4,128,1792]{2,1,0:T(8,128)(2,1)} %bitcast.11.refs_2_), channel_id=1, source_target_pairs={{0,16},{4,20},{8,24},{12,28},{16,0},{20,4},{24,8},{28,12},{1,17},{... | collective-permute-start | bytes 5505032 | tf_op jit(solution)/shard_map/ppermute | solution.py:80
  263.2 68.5 %collective-permute-start.9 = (bf16[4,128,1792]{2,1,0:T(8,128)(2,1)}, bf16[4,128,1792]{2,1,0:T(8,128)(2,1)}, u32[]{:S(2)}, u32[]{:S(2)}) collective-permute-start(bf16[4,128,1792]{2,1,0:T(8,128)(2,1)} %bitcast.10.refs_2_), channel_id=1, source_target_pairs={{0,8},{4,12},{8,0},{12,4},{16,24},{20,28},{24,16},{28,20},{1,9},{5... | collective-permute-start | bytes 5505032 | tf_op jit(solution)/shard_map/ppermute | solution.py:80
  264.7 70.7 %collective-permute-start.15 = (bf16[4,128,1792]{2,1,0:T(8,128)(2,1)}, bf16[4,128,1792]{2,1,0:T(8,128)(2,1)S(1)}, u32[]{:S(2)}, u32[]{:S(2)}) collective-permute-start(bf16[4,128,1792]{2,1,0:T(8,128)(2,1)} %bitcast.10.refs_2_), channel_id=1, source_target_pairs={{0,16},{4,20},{8,24},{12,28},{16,0},{20,4},{24,8},{28,12},{1,17},{... | collective-permute-start | bytes 5505032 | tf_op jit(solution)/shard_map/ppermute | solution.py:80
  283.0 53.9 %collective-permute-start.24 = (bf16[2,128,1792]{2,1,0:T(8,128)(2,1)}, bf16[2,128,1792]{2,1,0:T(8,128)(2,1)}, u32[]{:S(2)}, u32[]{:S(2)}) collective-permute-start(bf16[2,128,1792]{2,1,0:T(8,128)(2,1)} %slice.264), channel_id=1, source_target_pairs={{0,16},{4,20},{8,24},{12,28},{16,0},{20,4},{24,8},{28,12},{1,17},{... | collective-permute-start | bytes 2752520 | tf_op jit(solution)/shard_map/ppermute | solution.py:80
  338.0 56.4 %collective-permute-start.7 = (bf16[4,128,1792]{2,1,0:T(8,128)(2,1)}, bf16[4,128,1792]{2,1,0:T(8,128)(2,1)}, u32[]{:S(2)}, u32[]{:S(2)}) collective-permute-start(bf16[4,128,1792]{2,1,0:T(8,128)(2,1)} %bitcast.11.refs_2_), channel_id=1, source_target_pairs={{0,4},{4,0},{8,12},{12,8},{16,20},{20,16},{24,28},{28,24},{1,5},{5... | collective-permute-start | bytes 5505032 | tf_op jit(solution)/shard_map/ppermute | solution.py:80
  357.4 52.8 %collective-permute-start.12 = (bf16[4,128,1792]{2,1,0:T(8,128)(2,1)}, bf16[4,128,1792]{2,1,0:T(8,128)(2,1)}, u32[]{:S(2)}, u32[]{:S(2)}) collective-permute-start(bf16[4,128,1792]{2,1,0:T(8,128)(2,1)} %collective-permute-done.11.refs_2_), channel_id=1, source_target_pairs={{0,4},{4,0},{8,12},{12,8},{16,20},{20,16},{24,28},{28,24},{1,5},{5... | collective-permute-start | bytes 5505032 | tf_op jit(solution)/shard_map/ppermute | solution.py:80
  358.1 59.6 %collective-permute-start.10 = (bf16[4,128,1792]{2,1,0:T(8,128)(2,1)}, bf16[4,128,1792]{2,1,0:T(8,128)(2,1)}, u32[]{:S(2)}, u32[]{:S(2)}) collective-permute-start(bf16[4,128,1792]{2,1,0:T(8,128)(2,1)} %collective-permute-done.9.refs_2_), channel_id=1, source_target_pairs={{0,4},{4,0},{8,12},{12,8},{16,20},{20,16},{24,28},{28,24},{1,5},{5... | collective-permute-start | bytes 5505032 | tf_op jit(solution)/shard_map/ppermute | solution.py:80
  360.8 77.7 %collective-permute-start.18 = (bf16[4,128,1792]{2,1,0:T(8,128)(2,1)}, bf16[4,128,1792]{2,1,0:T(8,128)(2,1)}, u32[]{:S(2)}, u32[]{:S(2)}) collective-permute-start(bf16[4,128,1792]{2,1,0:T(8,128)(2,1)} %collective-permute-done.17.refs_2_), channel_id=1, source_target_pairs={{0,4},{4,0},{8,12},{12,8},{16,20},{20,16},{24,28},{28,24},{1,5},{5... | collective-permute-start | bytes 5505032 | tf_op jit(solution)/shard_map/ppermute | solution.py:80
  373.9 72.2 %collective-permute-start.16 = (bf16[4,128,1792]{2,1,0:T(8,128)(2,1)S(1)}, bf16[4,128,1792]{2,1,0:T(8,128)(2,1)}, u32[]{:S(2)}, u32[]{:S(2)}) collective-permute-start(bf16[4,128,1792]{2,1,0:T(8,128)(2,1)S(1)} %collective-permute-done.15.refs_2_), channel_id=1, source_target_pairs={{0,4},{4,0},{8,12},{12,8},{16,20},{20,16},{24,28},{28,24},{1,5},{5... | collective-permute-start | bytes 5505032 | tf_op jit(solution)/shard_map/ppermute | solution.py:80
  394.4 66.2 %collective-permute-start.38 = (bf16[4,128,1792]{2,1,0:T(8,128)(2,1)}, bf16[4,128,1792]{2,1,0:T(8,128)(2,1)}, u32[]{:S(2)}, u32[]{:S(2)}) collective-permute-start(bf16[4,128,1792]{2,1,0:T(8,128)(2,1)} %get-tuple-element.62), channel_id=1, source_target_pairs={{0,4},{4,0},{8,12},{12,8},{16,20},{20,16},{24,28},{28,24},{1,5},{5... | collective-permute-start | bytes 5505032 | tf_op jit(solution)/shard_map/ppermute | solution.py:80
  410.2 54.9 %collective-permute-start.6 = (bf16[4,128,1792]{2,1,0:T(8,128)(2,1)}, bf16[4,128,1792]{2,1,0:T(8,128)(2,1)}, u32[]{:S(2)}, u32[]{:S(2)}) collective-permute-start(bf16[4,128,1792]{2,1,0:T(8,128)(2,1)} %bitcast.10.refs_2_), channel_id=1, source_target_pairs={{0,4},{4,0},{8,12},{12,8},{16,20},{20,16},{24,28},{28,24},{1,5},{5... | collective-permute-start | bytes 5505032 | tf_op jit(solution)/shard_map/ppermute | solution.py:80
  438.1 49.4 %collective-permute-start.35 = (bf16[4,128,1792]{2,1,0:T(8,128)(2,1)}, bf16[4,128,1792]{2,1,0:T(8,128)(2,1)}, u32[]{:S(2)}, u32[]{:S(2)}) collective-permute-start(bf16[4,128,1792]{2,1,0:T(8,128)(2,1)} %get-tuple-element.58), channel_id=1, source_target_pairs={{0,4},{4,0},{8,12},{12,8},{16,20},{20,16},{24,28},{28,24},{1,5},{5... | collective-permute-start | bytes 5505032 | tf_op jit(solution)/shard_map/ppermute | solution.py:80
  492.3 50.0 %collective-permute-start.42 = (bf16[2,128,1792]{2,1,0:T(8,128)(2,1)}, bf16[2,128,1792]{2,1,0:T(8,128)(2,1)S(1)}, u32[]{:S(2)}, u32[]{:S(2)}) collective-permute-start(bf16[2,128,1792]{2,1,0:T(8,128)(2,1)} %get-tuple-element.80), channel_id=1, source_target_pairs={{0,8},{4,12},{8,0},{12,4},{16,24},{20,28},{24,16},{28,20},{1,9},{5... | collective-permute-start | bytes 2752520 | tf_op jit(solution)/shard_map/ppermute | solution.py:80
  508.5 41.9 %collective-permute-start.43 = (bf16[2,128,1792]{2,1,0:T(8,128)(2,1)}, bf16[2,128,1792]{2,1,0:T(8,128)(2,1)S(1)}, u32[]{:S(2)}, u32[]{:S(2)}) collective-permute-start(bf16[2,128,1792]{2,1,0:T(8,128)(2,1)} %get-tuple-element.82), channel_id=1, source_target_pairs={{0,16},{4,20},{8,24},{12,28},{16,0},{20,4},{24,8},{28,12},{1,17},{... | collective-permute-start | bytes 2752520 | tf_op jit(solution)/shard_map/ppermute | solution.py:80
  522.6 41.7 %collective-permute-start.13 = (bf16[4,128,1792]{2,1,0:T(8,128)(2,1)}, bf16[4,128,1792]{2,1,0:T(8,128)(2,1)}, u32[]{:S(2)}, u32[]{:S(2)}) collective-permute-start(bf16[4,128,1792]{2,1,0:T(8,128)(2,1)} %get-tuple-element.44), channel_id=1, source_target_pairs={{0,4},{4,0},{8,12},{12,8},{16,20},{20,16},{24,28},{28,24},{1,5},{5... | collective-permute-start | bytes 5505032 | tf_op jit(solution)/shard_map/ppermute | solution.py:80
  525.7 46.8 %collective-permute-start.19 = (bf16[4,128,1792]{2,1,0:T(8,128)(2,1)}, bf16[4,128,1792]{2,1,0:T(8,128)(2,1)}, u32[]{:S(2)}, u32[]{:S(2)}) collective-permute-start(bf16[4,128,1792]{2,1,0:T(8,128)(2,1)} %get-tuple-element.49), channel_id=1, source_target_pairs={{0,4},{4,0},{8,12},{12,8},{16,20},{20,16},{24,28},{28,24},{1,5},{5... | collective-permute-start | bytes 5505032 | tf_op jit(solution)/shard_map/ppermute | solution.py:80
  554.2 100.2 %reduce-scatter.6.cloned.1.call-start = ((), (), s32[]{:S(2)}) async-start(), calls=%async_computation.5 | async-start | bytes 2293760 | tf_op jit(solution)/shard_map/reduce_scatter | solution.py:275
  571.0 41.1 %collective-permute-start.32 = (bf16[2,128,1792]{2,1,0:T(8,128)(2,1)S(1)}, bf16[2,128,1792]{2,1,0:T(8,128)(2,1)S(1)}, u32[]{:S(2)}, u32[]{:S(2)}) collective-permute-start(bf16[2,128,1792]{2,1,0:T(8,128)(2,1)S(1)} %get-tuple-element.72), channel_id=1, source_target_pairs={{0,8},{4,12},{8,0},{12,4},{16,24},{20,28},{24,16},{28,20},{1,9},{5... | collective-permute-start | bytes 2752520 | tf_op jit(solution)/shard_map/ppermute | solution.py:80
  (93 other events, 1398.3 us)
Sparse Core Ops, SparseCore 0:
  9.9 83.6 all-gather.5
  106.1 68.3 reduce-scatter.3
  179.7 41.7 all-gather.9
  222.9 40.2 all-gather.7
  554.3 37.4 reduce-scatter.7
  616.4 37.9 reduce-scatter.5

commit v3 on v2

--- a/solution.py
+++ b/solution.py
@@ -43,11 +43,28 @@
 
 
 def exchange_plan(
-    quantized, stream, expert_ids, route_weight, weights, inv_x, scale_h, inv_h, capacity, experts
+    attn_out,
+    out_weight,
+    residual,
+    norm_gain,
+    expert_ids,
+    route_weight,
+    w_gate,
+    w_up,
+    w_down,
+    top_x,
+    top_h,
+    capacity,
 ):
-    w_gate, w_up, w_down = (weight[0] for weight in weights)
-    local_rows, width = quantized.shape
+    experts = lax.axis_size("dp") * lax.axis_size("tensor")
+    inv_x, inv_h, scale_h = top_x / FP8_LIMIT, top_h / FP8_LIMIT, FP8_LIMIT / top_h
+    local_rows, width = residual.shape
     top_count = expert_ids.shape[1]
+    stream = residual.astype(jnp.float32) + project(attn_out, out_weight)
+    normed = (
+        stream * lax.rsqrt(jnp.mean(stream * stream, axis=-1, keepdims=True) + 1e-06) * norm_gain
+    )
+    quantized = jnp.clip(normed * (FP8_LIMIT / top_x), -FP8_LIMIT, FP8_LIMIT).astype(jnp.bfloat16)
     position = slots_of(expert_ids, experts, capacity)
     matches = (
         position.reshape(local_rows, top_count)[:, :, None]
@@ -60,11 +77,11 @@
     outgoing = outgoing.astype(jnp.bfloat16).reshape(experts, capacity, width)
     token_block = lax.all_to_all(outgoing, AXES, split_axis=0, concat_axis=0, tiled=True)
     flat_rows = token_block.reshape(-1, width)
-    gate = jnp.dot(flat_rows, w_gate, preferred_element_type=jnp.float32) * inv_x
-    upper = jnp.dot(flat_rows, w_up, preferred_element_type=jnp.float32) * inv_x
+    gate = jnp.dot(flat_rows, w_gate[0], preferred_element_type=jnp.float32) * inv_x
+    upper = jnp.dot(flat_rows, w_up[0], preferred_element_type=jnp.float32) * inv_x
     hidden = jax.nn.silu(gate) * upper
     hidden_q = jnp.clip(hidden * scale_h, -FP8_LIMIT, FP8_LIMIT).astype(jnp.bfloat16)
-    expert_out = (jnp.dot(hidden_q, w_down, preferred_element_type=jnp.float32) * inv_h).astype(
+    expert_out = (jnp.dot(hidden_q, w_down[0], preferred_element_type=jnp.float32) * inv_h).astype(
         jnp.bfloat16
     )
     returned = lax.all_to_all(
@@ -72,7 +89,8 @@
     )
     picked = returned.reshape(-1, width)[position].reshape(local_rows, top_count, width)
     mixture = jnp.sum(picked.astype(jnp.float32) * route_weight[:, :, None], axis=1)
-    return (stream + mixture).astype(jnp.bfloat16), jnp.max(jnp.abs(hidden))
+    peaks = jnp.max(jnp.abs(normed)), jnp.max(jnp.abs(hidden))
+    return (stream + mixture).astype(jnp.bfloat16), *peaks
 
 
 def swap(value, bits):
@@ -80,30 +98,83 @@
     return lax.ppermute(value, "dp", [(i, i ^ bits) for i in range(count)])
 
 
-def route_table(expert_ids, route_weight, experts):
-    rows = expert_ids.shape[0]
+def from_all(value):
+    count = lax.axis_size("tensor")
+    parts = [value]
+    for shift in range(1, count):
+        pairs = [(i, (i + shift) % count) for i in range(count)]
+        parts.append(lax.ppermute(value, "tensor", pairs))
+    order = (lax.axis_index("tensor") - jnp.arange(count)) % count
+    values = jnp.stack(parts)[order][None]
+    bit = 1
+    while bit < lax.axis_size("dp"):
+        values = jnp.concatenate([values, swap(values, bit)])
+        bit *= 2
+    return values
+
+
+def expert_weights(expert_ids, route_weight, experts):
     names = jnp.arange(experts, dtype=jnp.int32)[:, None, None]
     table = jnp.sum(jnp.where(expert_ids[None] == names, route_weight[None], 0.0), axis=2)
-    count = lax.axis_size("tensor")
-    here = lax.axis_index("tensor")
-    parts = [table]
-    for shift in range(1, count):
-        pairs = [(i, (i + shift) % count) for i in range(count)]
-        parts.append(lax.ppermute(table, "tensor", pairs))
-    order = (here - jnp.arange(count)) % count
-    table = jnp.stack(parts)[order]
-    bit = 1
-    while bit < lax.axis_size("dp"):
-        table = jnp.concatenate([table, swap(table, bit)])
-        bit *= 2
-    mine = lax.axis_index("dp") * count + here
-    table = lax.dynamic_index_in_dim(table, mine, axis=1, keepdims=False)
-    return table.reshape(-1, count, rows)
+    mine = lax.axis_index("dp") * lax.axis_size("tensor") + lax.axis_index("tensor")
+    return lax.dynamic_index_in_dim(from_all(table), mine, axis=2, keepdims=False)
+
+
+def chip_groups(value):
+    half = value.shape[0] // 2
+    along_x, along_y = swap(value, 2), swap(value, 4)
+    diagonal = [swap(along_x[:half], 4), swap(along_y[half:], 2)]
+    groups = [[value], [along_x], [along_y], diagonal]
+    return [(group, [swap(piece, 1) for piece in group]) for group in groups]
+
+
+def project_kernel(place_ref, attn_ref, *refs):
+    out_ref, joined, stage = refs[-3:]
+    pieces = refs[:-3]
+    columns = pieces[0].shape[0]
+    attn = attn_ref[...]
+    blocks = [pieces[0], pieces[1], pieces[2], pieces[3], pieces[4], pieces[5], None, None]
+    for k, block in enumerate(blocks):
+        if block is None:
+            low, high = pieces[2 * k - 6], pieces[2 * k - 5]
+            joined[: low.shape[0]] = low[...]
+            joined[low.shape[0] :] = high[...]
+            block = joined
+        terms = lax.dot_general(
+            attn, block[...], (((1,), (1,)), ((), ())), preferred_element_type=jnp.float32
+        )
+        stage[place_ref[0] ^ k, :, :columns] = terms
+    for j in range(stage.shape[0]):
+        out_ref[:, j * columns : (j + 1) * columns] = stage[j, :, :columns].astype(out_ref.dtype)
+
+
+def project_part(place, attn_out, groups):
+    rows, depth = attn_out.shape
+    pieces = [piece for pair in groups for group in pair for piece in group]
+    columns = pieces[0].shape[0]
+    return pl.pallas_call(
+        project_kernel,
+        in_specs=[pl.BlockSpec(memory_space=pltpu.SMEM)]
+        + [pl.BlockSpec(memory_space=pltpu.VMEM)] * (1 + len(pieces)),
+        out_specs=pl.BlockSpec(memory_space=pltpu.VMEM),
+        out_shape=jax.ShapeDtypeStruct((rows, 8 * columns), jnp.bfloat16),
+        scratch_shapes=[
+            pltpu.VMEM((columns, depth), jnp.bfloat16),
+            pltpu.VMEM((8, rows, -(-columns // 128) * 128), jnp.float32),
+        ],
+        compiler_params=pltpu.CompilerParams(vmem_limit_bytes=VMEM_LIMIT),
+        cost_estimate=pl.CostEstimate(
+            flops=16 * rows * depth * columns,
+            bytes_accessed=2 * depth * (rows + 8 * columns),
+            transcendentals=0,
+        ),
+        name="project",
+    )(place, attn_out, *pieces)
 
 
 def gate_up_kernel(counts, first, last, *refs):
     refs = list(refs)
-    scale_ref, chosen_ref = refs.pop(0), refs.pop(0)
+    scale_ref, gain_ref, chosen_ref, root_ref = (refs.pop(0) for _ in range(4))
     pieces = [refs.pop(0) for _ in counts]
     gate_w, up_w = refs.pop(0), refs.pop(0)
     before = [] if first else [refs.pop(0), refs.pop(0)]
@@ -115,12 +186,15 @@
         source = 0
         for piece, count in zip(pieces, counts):
             for i in range(count):
+                span = slice(source * capacity, (source + 1) * capacity)
                 picked = jnp.dot(chosen_ref[source], piece[i], preferred_element_type=jnp.float32)
-                rows[source * capacity : (source + 1) * capacity] = picked.astype(rows.dtype)
+                picked = picked * root_ref[span] * gain_ref[...]
+                rows[span] = jnp.clip(picked, -FP8_LIMIT, FP8_LIMIT).astype(rows.dtype)
                 source += 1
 
-    gate = jnp.dot(rows[...], gate_w[0], preferred_element_type=jnp.float32)
-    up = jnp.dot(rows[...], up_w[0], preferred_element_type=jnp.float32)
+    flat = lambda weight: weight[0].reshape(rows.shape[1], weight.shape[-1])
+    gate = jnp.dot(rows[...], flat(gate_w), preferred_element_type=jnp.float32)
+    up = jnp.dot(rows[...], flat(up_w), preferred_element_type=jnp.float32)
     if not first:
         gate += before[0][...]
         up += before[1][...]
@@ -136,15 +210,16 @@
     refs[1][...] = jnp.broadcast_to(peak, refs[1].shape)
 
 
-def gate_up(scales, chosen, pieces, w_gate, w_up, c, before, last):
+def gate_up(scales, gain, chosen, root, pieces, w_gate, w_up, c, before, last):
     sources, capacity, tokens = chosen.shape
     step = pieces[0].shape[-1]
-    hidden = w_gate.shape[2]
+    hidden = w_gate.shape[-1]
     tile = min(256, hidden)
     rows = sources * capacity
     whole = lambda shape: pl.BlockSpec(shape, lambda n: (0,) * len(shape))
     column = lambda height: pl.BlockSpec((height, tile), lambda n: (0, n))
-    weight = pl.BlockSpec((1, step, tile), lambda n: (0, c, n))
+    owners, columns = w_gate.shape[1], w_gate.shape[3]
+    weight = pl.BlockSpec((1, owners, None, columns, tile), lambda n: (0, 0, c, 0, n))
     if last:
         out_shape = [
             jax.ShapeDtypeStruct((rows, hidden), jnp.bfloat16),
@@ -157,7 +232,8 @@
     return pl.pallas_call(
         functools.partial(gate_up_kernel, [p.shape[0] for p in pieces], not before, last),
         grid=(hidden // tile,),
-        in_specs=[pl.BlockSpec(memory_space=pltpu.SMEM), whole(chosen.shape)]
+        in_specs=[pl.BlockSpec(memory_space=pltpu.SMEM)]
+        + [whole(gain.shape), whole(chosen.shape), whole(root.shape)]
         + [whole(p.shape) for p in pieces]
         + [weight] * 2
         + [column(rows)] * len(before),
@@ -171,7 +247,7 @@
             transcendentals=rows * hidden if last else 0,
         ),
         name="gate_up",
-    )(scales, chosen, *pieces, w_gate, w_up, *before)
+    )(scales, gain, chosen, root, *pieces, w_gate, w_up, *before)
 
 
 def down_kernel(hidden_ref, down_w, factor_ref, spread_ref, own_ref, other_ref):
@@ -223,46 +299,89 @@
 
 
 def gather_plan(
-    quantized, stream, expert_ids, route_weight, weights, inv_x, scale_h, inv_h, capacity, experts
+    attn_out,
+    out_weight,
+    residual,
+    norm_gain,
+    expert_ids,
+    route_weight,
+    w_gate,
+    w_up,
+    w_down,
+    top_x,
+    top_h,
+    capacity,
 ):
-    w_gate, w_up, w_down = weights
-    local_rows, width = quantized.shape
-    layers = lax.axis_size("tensor")
-    half = layers // 2
-    weight = route_table(expert_ids, route_weight, experts)
+    owners, layers = lax.axis_size("dp"), lax.axis_size("tensor")
+    experts = owners * layers
+    local_rows, width = residual.shape
+    half, step = layers // 2, width // CHUNKS
+    columns = step // owners
+
+    weight = expert_weights(expert_ids, route_weight, experts)
+    weight_rows = out_weight.T.reshape(CHUNKS, columns, -1)
+    blocks = [chip_groups(weight_rows[c]) for c in range(CHUNKS)]
+    attn_out, weight = lax.optimization_barrier((attn_out, weight))
+
     named = weight > 0.0
     earlier = jnp.triu(jnp.ones((local_rows, local_rows), jnp.bfloat16), 1)
     slot = lax.dot_general(
-        named.astype(jnp.bfloat16), earlier, (((2,), (0,)), ((), ())),
+        named.astype(jnp.bfloat16),
+        earlier,
+        (((2,), (0,)), ((), ())),
         preferred_element_type=jnp.float32,
     ).astype(jnp.int32)
     chosen = (
         slot[:, :, None, :] == jnp.arange(capacity, dtype=jnp.int32)[:, None]
     ) & named[:, :, None, :]
-    factor = jnp.sum(jnp.where(chosen, weight[:, :, None, :], 0.0), axis=3) * inv_h
-    chosen = chosen.astype(jnp.bfloat16).reshape(4, 2 * layers, capacity, local_rows)
-    factor = factor.reshape(4, 2 * layers * capacity, 1)
-    spread = chosen.transpose(0, 1, 3, 2)
-    scales = jnp.stack([inv_x, scale_h])
-    step = width // CHUNKS
-
+    by_slot = lambda values: jnp.sum(
+        jnp.where(chosen, values[:, :, None, :], 0.0), axis=3
+    ).reshape(4, 2 * layers * capacity, 1)
+    factor = by_slot(weight) * (top_h / FP8_LIMIT)
+    choice = chosen.astype(jnp.bfloat16).reshape(4, 2 * layers, capacity, local_rows)
+    spread = choice.transpose(0, 1, 3, 2)
+    scales = jnp.stack([top_x / FP8_LIMIT, FP8_LIMIT / top_h])
+
+    split = lambda value: value.reshape(-1, owners, CHUNKS, columns)
+    parts = lambda value, c: split(value)[:, :, c].reshape(-1, step)
+    place = lax.axis_index("dp")[None]
+    stream, tokens = [], []
+    for c in range(CHUNKS):
+        terms = project_part(place, attn_out, blocks[c])
+        total = lax.psum_scatter(terms, "tensor", scatter_dimension=0, tiled=True)
+        stream.append(parts(residual, c).astype(jnp.float32) + total.astype(jnp.float32))
+        own = lax.all_gather(stream[c].astype(jnp.bfloat16), "tensor", axis=0)
+        tokens.append(chip_groups(own))
+    squares = sum(jnp.sum(part * part, axis=1) for part in stream)
+    root = lax.rsqrt(squares / width + 1e-06)
+    gains = [parts(norm_gain, c) for c in range(CHUNKS)]
+    peak_x = jnp.max(
+        jnp.stack([jnp.max(jnp.abs(s * root[:, None] * g)) for s, g in zip(stream, gains)])
+    )
+    roots = by_slot(from_all(root))
+    gains = [g * (FP8_LIMIT / top_x) for g in gains]
+
+    gate_rows = w_gate.reshape(1, owners, CHUNKS, columns, -1)
+    up_rows = w_up.reshape(1, owners, CHUNKS, columns, -1)
     sums = [[] for _ in range(4)]
     for c in range(CHUNKS):
-        part = slice(c * step, (c + 1) * step)
-        own = lax.all_gather(quantized[:, part], "tensor", axis=0).reshape(layers, local_rows, step)
-        along_x, along_y = swap(own, 2), swap(own, 4)
-        diagonal = [swap(along_x[:half], 4), swap(along_y[half:], 2)]
-        groups = [[own], [along_x], [along_y], diagonal]
-        for r, group in enumerate(groups):
-            pieces = group + [swap(piece, 1) for piece in group]
+        for r, (near, far) in enumerate(tokens[c]):
             sums[r] = gate_up(
-                scales, chosen[r], pieces, w_gate, w_up, c, sums[r], c == CHUNKS - 1
+                scales,
+                gains[c],
+                choice[r],
+                roots[r],
+                near + far,
+                gate_rows,
+                up_rows,
+                c,
+                sums[r],
+                c == CHUNKS - 1,
             )
     peak_h = jnp.max(jnp.stack([jnp.max(s[1]) for s in sums]))
 
-    outputs = []
+    mixture = []
     for c in range(CHUNKS):
-        part = slice(c * step, (c + 1) * step)
         to = []
         for r in range(4):
             kept, given = down(sums[r][0], w_down, factor[r], spread[r], c, step)
@@ -272,9 +391,11 @@
         low = add(to[0][0], swap(to[1][0], 2), swap(add(to[2][0], over_x), 4))
         high = add(to[0][1], swap(add(to[1][1], over_y), 2), swap(to[2][1], 4))
         mixed = jnp.concatenate([low, high]).reshape(layers * local_rows, step)
-        mixed = lax.psum_scatter(mixed, "tensor", scatter_dimension=0, tiled=True)
-        outputs.append((stream[:, part] + mixed.astype(jnp.float32)).astype(jnp.bfloat16))
-    return jnp.concatenate(outputs, axis=1), peak_h
+        mixture.append(lax.psum_scatter(mixed, "tensor", scatter_dimension=0, tiled=True))
+    stream = jnp.stack([s.reshape(local_rows, owners, columns) for s in stream], axis=2)
+    stream = stream.reshape(local_rows, width)
+    layer_out = stream + jnp.concatenate(mixture, axis=1).astype(jnp.float32)
+    return layer_out.astype(jnp.bfloat16), peak_x, peak_h
 
 
 def body(
@@ -291,29 +412,24 @@
     history_h,
 ):
     experts = lax.axis_size("dp") * lax.axis_size("tensor")
-    local_rows = residual.shape[0]
-    top_count = expert_ids.shape[1]
+    local_rows, top_count = expert_ids.shape
     capacity = max(2, 3 * local_rows * top_count // (2 * experts))
-    stream = residual.astype(jnp.float32) + project(attn_out, out_weight)
-    normed = (
-        stream * lax.rsqrt(jnp.mean(stream * stream, axis=-1, keepdims=True) + 1e-06) * norm_gain
-    )
-    peak_x = jnp.max(jnp.abs(normed))
     top_x, top_h = jnp.max(history_x), jnp.max(history_h)
-    quantized = jnp.clip(normed * (FP8_LIMIT / top_x), -FP8_LIMIT, FP8_LIMIT).astype(jnp.bfloat16)
     gathers = lax.axis_size("dp") == 8 and local_rows < 4 * capacity
     plan = gather_plan if gathers else exchange_plan
-    layer_out, peak_h = plan(
-        quantized,
-        stream,
+    layer_out, peak_x, peak_h = plan(
+        attn_out,
+        out_weight,
+        residual,
+        norm_gain,
         expert_ids,
         route_weight,
-        (w_gate, w_up, w_down),
-        top_x / FP8_LIMIT,
-        FP8_LIMIT / top_h,
-        top_h / FP8_LIMIT,
+        w_gate,
+        w_up,
+        w_down,
+        top_x,
+        top_h,
         capacity,
-        experts,
     )
     peaks = peaks_over_all(jnp.stack([peak_x, peak_h]))
     new_history_x = jnp.concatenate([peaks[:1], history_x[:-1]])

time: 665 us -> 641 us (0.964); the launches traced: 664 us -> 630 us
  waiting for transfers between devices: 405 us -> 329 us
  starting transfers between devices: 29.8 us -> 53.6 us
  Pallas kernels: 114 us -> 129 us
  matrix products: 12.5 us -> 0.13 us
  local copies, waits for them, and re-layouts: 42.1 us -> 52.7 us
    all_gather x3 -> x2, waiting for transfers between devices: 166 us -> 78.7 us  [gather_plan(): own = lax.all_gather(stream[c].astype(jnp.bfloat16), 'tensor', axis=0)]
    ppermute x41 -> x62, waiting for transfers between devices: 132 us -> 194 us  [swap(): return lax.ppermute(value, 'dp', [(i, i ^ bits) for i in range(count)])]
    reduce_scatter x3 -> x2, waiting for transfers between devices: 72.5 us -> 32.5 us  [gather_plan(): total = lax.psum_scatter(terms, 'tensor', scatter_dimension=0, tiled=True)]
    pallas_call x0 -> x2, Pallas kernels: none -> 15.2 us  [project_part(): pl.pallas_call(project_kernel, in_specs=[pl.BlockSpec(memory_space=pltpu....]
    ppermute x41 -> x62, starting transfers between devices: 27.1 us -> 42.3 us  [swap(): return lax.ppermute(value, 'dp', [(i, i ^ bits) for i in range(count)])]
    dot_general x1 -> x0, matrix products: 12.3 us -> none  [project(): jnp.dot(attn_out, lax.all_gather(out_weight, 'dp', axis=1, tiled=True), p...]
    ppermute x3 -> x6, waiting for transfers between devices: 13.6 us -> 1.78 us  [from_all(): parts.append(lax.ppermute(value, 'tensor', pairs))]
    ppermute x3 -> x6, starting transfers between devices: 0.35 us -> 10.9 us  [from_all(): parts.append(lax.ppermute(value, 'tensor', pairs))]
  transfers between devices with their start and end apart: 55 -> 79, of which waited for: 25 -> 34; matrix products, arithmetic and copies ran while one was open for 7% -> 10% of each run, Pallas kernels for 17% -> 19%
where the time goes in v3:
time: 641 us; the launch traced here: 630 us
  waiting for transfers between devices  329 us (51%)
  Pallas kernels  129 us (20%)
  starting transfers between devices  53.6 us (8%)
  local copies, waits for them, and re-layouts  52.7 us (8%)
  other arithmetic  44 us (7%)
  between operations  22 us (3%)
    ppermute x62, waiting for transfers between devices, swap(): return lax.ppermute(value, 'dp', [(i, i ^ bits) for i in range(count)])  194 us
    all_gather x2, waiting for transfers between devices, gather_plan(): own = lax.all_gather(stream[c].astype(jnp.bfloat16), 'tensor', axis=0)  78.7 us
    pallas_call x8, Pallas kernels, gate_up(): pl.pallas_call(functools.partial(gate_up_kernel, [p.shape[0] for p in pie...  61.8 us
    pallas_call x8, Pallas kernels, down(): pl.pallas_call(down_kernel, grid=(tiles,), in_specs=[whole(hidden_q.shape...  51.5 us
    ppermute x62, starting transfers between devices, swap(): return lax.ppermute(value, 'dp', [(i, i ^ bits) for i in range(count)])  42.3 us
    unnamed x142, local copies, waits for them, and re-layouts  34.4 us
    reduce_scatter x2, waiting for transfers between devices, gather_plan(): total = lax.psum_scatter(terms, 'tensor', scatter_dimension=0, tiled=True)  32.5 us
    ppermute x5, waiting for transfers between devices, peaks_over_all(): peaks = jnp.maximum(peaks, lax.ppermute(peaks, axis, pairs))  22.2 us
  transfers between devices with their start and end apart: 79, of which 34 were waited for; matrix products, arithmetic and copies ran while one was open for 10% of the time, Pallas kernels for 19%

profile of v3, /device:TPU:0, one launch (start us, length us, event | category | flops | bytes accessed | tf_op | source)
XLA Modules:
  0.0 630.5 jit_solution(13533654912385151929)
XLA Ops:
  22.2 18.5 %collective-permute-done.4 = f32[2,4,32,128]{3,2,1,0:T(8,128)S(1)} collective-permute-done((f32[2,4,32,128]{3,2,1,0:T(8,128)S(1)}, f32[2,4,32,128]{3,2,1,0:T(8,128)S(1)}, u32[]{:S(2)}, u32[]{:S(2)}) %collective-permute-start.4) | collective-permute-done | bytes 131104 | tf_op jit(solution)/shard_map/ppermute | solution.py:98
  48.9 8.1 %collective-permute-done.11.refs_6_ = bf16[112,2048]{1,0:T(8,128)(2,1)S(1)} collective-permute-done((bf16[112,2048]{1,0:T(8,128)(2,1)S(1)}, bf16[112,2048]{1,0:T(8,128)(2,1)S(1)}, u32[]{:S(2)}, u32[]{:S(2)}) %collective-permute-start.11) | collective-permute-done | bytes 458784 | tf_op jit(solution)/shard_map/ppermute | solution.py:98
  61.4 8.8 %project.2 = bf16[512,1792]{1,0:T(8,128)(2,1)} custom-call(s32[1]{0:T(128)} %bitcast.2.place_ref, bf16[512,2048]{1,0:T(8,128)(2,1)S(1)} %copy-done.46, bf16[224,2048]{1,0:T(8,128)(2,1)S(1)} %get-tuple-element.108.refs_0_, bf16[224,2048]{1,0:T(8,128)(2,1)} %collective-permute-done.6.refs_1_, bf16[224,2048]{1,0:T(8,128)(2,1)S(1)} %collective-permute-done.7.refs_2_, ...), custom_call_target="tpu_custom_call" | custom-call | flops 3758096384 | bytes 9437184 | tf_op jit(solution)/shard_map/project/pallas_call | solution.py:155
  73.3 19.4 %collective-permute-done.16.refs_2_ = bf16[224,2048]{1,0:T(8,128)(2,1)S(1)} collective-permute-done((bf16[224,2048]{1,0:T(8,128)(2,1)S(1)}, bf16[224,2048]{1,0:T(8,128)(2,1)S(1)}, u32[]{:S(2)}, u32[]{:S(2)}) %collective-permute-start.16) | collective-permute-done | bytes 917536 | tf_op jit(solution)/shard_map/ppermute | solution.py:98
  96.4 8.2 %collective-permute-done.20.refs_6_ = bf16[112,2048]{1,0:T(8,128)(2,1)S(1)} collective-permute-done((bf16[112,2048]{1,0:T(8,128)(2,1)S(1)}, bf16[112,2048]{1,0:T(8,128)(2,1)S(1)}, u32[]{:S(2)}, u32[]{:S(2)}) %collective-permute-start.20) | collective-permute-done | bytes 458784 | tf_op jit(solution)/shard_map/ppermute | solution.py:98
  119.0 32.5 %reduce-scatter.11.cloned.1.call-done = bf16[128,1792]{1,0:T(8,128)(2,1)} async-done(((bf16[512,1792]{1,0:T(8,128)(2,1)}), bf16[128,1792]{1,0:T(8,128)(2,1)}) %reduce-scatter.11.cloned.1.call-update) | async-done | bytes 458768 | tf_op jit(solution)/shard_map/reduce_scatter | solution.py:351
  153.8 39.9 %all-gather.7.cloned.1.call-done = bf16[512,1792]{1,0:T(8,128)(2,1)} async-done(((bf16[128,1792]{1,0:T(8,128)(2,1)}), bf16[512,1792]{1,0:T(8,128)(2,1)}) %all-gather.7.cloned.1.call-update) | async-done | bytes 1835024 | tf_op jit(solution)/shard_map/all_gather | solution.py:353
  196.6 38.8 %all-gather.5.cloned.1.call-done = bf16[512,1792]{1,0:T(8,128)(2,1)} async-done(((bf16[128,1792]{1,0:T(8,128)(2,1)}), bf16[512,1792]{1,0:T(8,128)(2,1)}) %all-gather.5.cloned.1.call-update) | async-done | bytes 1835024 | tf_op jit(solution)/shard_map/all_gather | solution.py:353
  256.0 22.6 %collective-permute-done.33.refs_4_ = bf16[4,128,1792]{2,1,0:T(8,128)(2,1)} collective-permute-done((bf16[4,128,1792]{2,1,0:T(8,128)(2,1)}, bf16[4,128,1792]{2,1,0:T(8,128)(2,1)}, u32[]{:S(2)}, u32[]{:S(2)}) %collective-permute-start.33) | collective-permute-done | bytes 1835040 | tf_op jit(solution)/shard_map/ppermute | solution.py:98
  284.7 15.0 %collective-permute-done.48.refs_4_ = bf16[2,128,1792]{2,1,0:T(8,128)(2,1)} collective-permute-done((bf16[2,128,1792]{2,1,0:T(8,128)(2,1)S(1)}, bf16[2,128,1792]{2,1,0:T(8,128)(2,1)}, u32[]{:S(2)}, u32[]{:S(2)}) %collective-permute-start.48) | collective-permute-done | bytes 917536 | tf_op jit(solution)/shard_map/ppermute | solution.py:98
  302.5 15.5 %collective-permute-done.29 = f32[4,4,128]{2,1,0:T(4,128)S(1)} collective-permute-done((f32[4,4,128]{2,1,0:T(4,128)S(1)}, f32[4,4,128]{2,1,0:T(4,128)S(1)}, u32[]{:S(2)}, u32[]{:S(2)}) %collective-permute-start.29) | collective-permute-done | bytes 8224 | tf_op jit(solution)/shard_map/ppermute | solution.py:98
  327.9 7.2 %gate_up.14 = (f32[384,1024]{1,0:T(8,128)S(1)}, f32[384,1024]{1,0:T(8,128)S(1)}) custom-call(f32[2]{0:T(128)S(1)} %pad_maximum_fusion.10.refs_0_, f32[1,1792]{1,0:T(1,128)S(1)} %mul.79.refs_1_, bf16[8,48,128]{2,1,0:T(8,128)(2,1)S(1)} %bitcast.81, f32[384,1]{1,0:T(8,128)S(1)} %squeeze.93.refs_3_, bf16[2,128,1792]{2,1,0:T(8,128)(2,1)} %collective-permute-done.48.refs_4_, ...), custom_call_target="tpu_custom_call" | custom-call | flops 2994733056 | bytes 17301504 | tf_op jit(solution)/shard_map/gate_up/pallas_call | solution.py:232
  338.2 8.1 %gate_up.15 = (bf16[384,1024]{1,0:T(8,128)(2,1)S(1)}, f32[8,1024]{1,0:T(8,128)S(1)}) custom-call(f32[2]{0:T(128)S(1)} %pad_maximum_fusion.10.refs_0_, f32[1,1792]{1,0:T(1,128)S(1)} %mul.75.refs_1_, bf16[8,48,128]{2,1,0:T(8,128)(2,1)S(1)} %bitcast.82, f32[384,1]{1,0:T(8,128)S(1)} %squeeze.93.refs_3_, bf16[2,128,1792]{2,1,0:T(8,128)(2,1)} %collective-permute-done.44.refs_4_, ...), custom_call_target="tpu_custom_call" | custom-call | flops 2994733056 | bytes 17301504 | tf_op jit(solution)/shard_map/gate_up/pallas_call | solution.py:232
  361.0 7.5 %gate_up.8 = (f32[384,1024]{1,0:T(8,128)S(1)}, f32[384,1024]{1,0:T(8,128)S(1)}) custom-call(f32[2]{0:T(128)S(1)} %pad_maximum_fusion.10.refs_0_, f32[1,1792]{1,0:T(1,128)S(1)} %mul.79.refs_1_, bf16[8,48,128]{2,1,0:T(8,128)(2,1)S(1)} %bitcast.75, f32[384,1]{1,0:T(8,128)S(1)} %squeeze.87.refs_3_, bf16[4,128,1792]{2,1,0:T(8,128)(2,1)} %bitcast.27.refs_4_, ...), custom_call_target="tpu_custom_call" | custom-call | flops 2994733056 | bytes 17301504 | tf_op jit(solution)/shard_map/gate_up/pallas_call | solution.py:232
  371.3 7.5 %gate_up.10 = (f32[384,1024]{1,0:T(8,128)S(1)}, f32[384,1024]{1,0:T(8,128)S(1)}) custom-call(f32[2]{0:T(128)S(1)} %pad_maximum_fusion.10.refs_0_, f32[1,1792]{1,0:T(1,128)S(1)} %mul.79.refs_1_, bf16[8,48,128]{2,1,0:T(8,128)(2,1)S(1)} %bitcast.79, f32[384,1]{1,0:T(8,128)S(1)} %squeeze.89.refs_3_, bf16[4,128,1792]{2,1,0:T(8,128)(2,1)} %collective-permute-done.35.refs_4_, ...), custom_call_target="tpu_custom_call" | custom-call | flops 2994733056 | bytes 17301504 | tf_op jit(solution)/shard_map/gate_up/pallas_call | solution.py:232
  381.0 8.2 %gate_up.11 = (bf16[384,1024]{1,0:T(8,128)(2,1)S(1)}, f32[8,1024]{1,0:T(8,128)S(1)}) custom-call(f32[2]{0:T(128)S(1)} %pad_maximum_fusion.10.refs_0_, f32[1,1792]{1,0:T(1,128)S(1)} %mul.75.refs_1_, bf16[8,48,128]{2,1,0:T(8,128)(2,1)S(1)} %bitcast.80, f32[384,1]{1,0:T(8,128)S(1)} %copy-done.21, bf16[4,128,1792]{2,1,0:T(8,128)(2,1)} %collective-permute-done.33.refs_4_, ...), custom_call_target="tpu_custom_call" | custom-call | flops 2994733056 | bytes 17301504 | tf_op jit(solution)/shard_map/gate_up/pallas_call | solution.py:232
  401.0 7.1 %gate_up.12 = (f32[384,1024]{1,0:T(8,128)S(1)}, f32[384,1024]{1,0:T(8,128)S(1)}) custom-call(f32[2]{0:T(128)S(1)} %pad_maximum_fusion.10.refs_0_, f32[1,1792]{1,0:T(1,128)S(1)} %mul.79.refs_1_, bf16[8,48,128]{2,1,0:T(8,128)(2,1)S(1)} %bitcast.77, f32[384,1]{1,0:T(8,128)S(1)} %copy-done.19, bf16[4,128,1792]{2,1,0:T(8,128)(2,1)S(1)} %collective-permute-done.41.refs_4_, ...), custom_call_target="tpu_custom_call" | custom-call | flops 2994733056 | bytes 17301504 | tf_op jit(solution)/shard_map/gate_up/pallas_call | solution.py:232
  408.2 8.2 %gate_up.13 = (bf16[384,1024]{1,0:T(8,128)(2,1)S(1)}, f32[8,1024]{1,0:T(8,128)S(1)}) custom-call(f32[2]{0:T(128)S(1)} %pad_maximum_fusion.10.refs_0_, f32[1,1792]{1,0:T(1,128)S(1)} %mul.75.refs_1_, bf16[8,48,128]{2,1,0:T(8,128)(2,1)S(1)} %bitcast.78, f32[384,1]{1,0:T(8,128)S(1)} %copy-done.19, bf16[4,128,1792]{2,1,0:T(8,128)(2,1)} %collective-permute-done.39.refs_4_, ...), custom_call_target="tpu_custom_call" | custom-call | flops 2994733056 | bytes 17301504 | tf_op jit(solution)/shard_map/gate_up/pallas_call | solution.py:232
  428.4 8.1 %gate_up.9 = (bf16[384,1024]{1,0:T(8,128)(2,1)S(1)}, f32[8,1024]{1,0:T(8,128)S(1)}) custom-call(f32[2]{0:T(128)S(1)} %pad_maximum_fusion.10.refs_0_, f32[1,1792]{1,0:T(1,128)S(1)} %mul.75.refs_1_, bf16[8,48,128]{2,1,0:T(8,128)(2,1)S(1)} %bitcast.76, f32[384,1]{1,0:T(8,128)S(1)} %copy-done.18, bf16[4,128,1792]{2,1,0:T(8,128)(2,1)} %bitcast.24.refs_4_, ...), custom_call_target="tpu_custom_call" | custom-call | flops 2994733056 | bytes 17301504 | tf_op jit(solution)/shard_map/gate_up/pallas_call | solution.py:232
  455.2 11.1 %collective-permute-done.53 = bf16[2,128,1792]{2,1,0:T(8,128)(2,1)} collective-permute-done((bf16[2,128,1792]{2,1,0:T(8,128)(2,1)}, bf16[2,128,1792]{2,1,0:T(8,128)(2,1)}, u32[]{:S(2)}, u32[]{:S(2)}) %collective-permute-start.53) | collective-permute-done | bytes 917536 | tf_op jit(solution)/shard_map/ppermute | solution.py:98
  488.9 16.1 %collective-permute-done.56 = bf16[2,128,1792]{2,1,0:T(8,128)(2,1)S(1)} collective-permute-done((bf16[2,128,1792]{2,1,0:T(8,128)(2,1)}, bf16[2,128,1792]{2,1,0:T(8,128)(2,1)S(1)}, u32[]{:S(2)}, u32[]{:S(2)}) %collective-permute-start.56) | collective-permute-done | bytes 917536 | tf_op jit(solution)/shard_map/ppermute | solution.py:98
  505.5 7.6 %collective-permute-done.57 = bf16[2,128,1792]{2,1,0:T(8,128)(2,1)} collective-permute-done((bf16[2,128,1792]{2,1,0:T(8,128)(2,1)}, bf16[2,128,1792]{2,1,0:T(8,128)(2,1)}, u32[]{:S(2)}, u32[]{:S(2)}) %collective-permute-start.57) | collective-permute-done | bytes 917536 | tf_op jit(solution)/shard_map/ppermute | solution.py:98
  542.3 15.6 %collective-permute-done.60 = bf16[2,128,1792]{2,1,0:T(8,128)(2,1)S(1)} collective-permute-done((bf16[2,128,1792]{2,1,0:T(8,128)(2,1)S(1)}, bf16[2,128,1792]{2,1,0:T(8,128)(2,1)S(1)}, u32[]{:S(2)}, u32[]{:S(2)}) %collective-permute-start.60) | collective-permute-done | bytes 917536 | tf_op jit(solution)/shard_map/ppermute | solution.py:98
  557.8 17.7 %collective-permute-done.66 = bf16[2,128,1792]{2,1,0:T(8,128)(2,1)S(1)} collective-permute-done((bf16[2,128,1792]{2,1,0:T(8,128)(2,1)S(1)}, bf16[2,128,1792]{2,1,0:T(8,128)(2,1)S(1)}, u32[]{:S(2)}, u32[]{:S(2)}) %collective-permute-start.66) | collective-permute-done | bytes 917536 | tf_op jit(solution)/shard_map/ppermute | solution.py:98
  (391 shorter events, 251.3 us)
Async XLA Ops:
  7.2 109.4 %reduce-scatter.9.cloned.1.call-start = ((), (), s32[]{:S(2)}) async-start(), calls=%async_computation.4 | async-start | bytes 2293760 | tf_op jit(solution)/shard_map/reduce_scatter | solution.py:351
  70.2 81.2 %reduce-scatter.11.cloned.1.call-start = ((), (), s32[]{:S(2)}) async-start(), calls=%async_computation.5 | async-start | bytes 2293760 | tf_op jit(solution)/shard_map/reduce_scatter | solution.py:351
  114.3 79.3 %all-gather.7.cloned.1.call-start = ((), (), s32[]{:S(2)}) async-start(), calls=%async_computation.7 | async-start | bytes 2293760 | tf_op jit(solution)/shard_map/all_gather | solution.py:353
  118.5 116.9 %all-gather.5.cloned.1.call-start = ((), (), s32[]{:S(2)}) async-start(), calls=%async_computation.6 | async-start | bytes 2293760 | tf_op jit(solution)/shard_map/all_gather | solution.py:353
  153.7 463.7 %reduce-scatter.13.cloned.1.call-start = ((), (), s32[]{:S(2)}) async-start(), calls=%async_computation.8 | async-start | bytes 2293760
  193.6 51.7 %collective-permute-start.35 = (bf16[4,128,1792]{2,1,0:T(8,128)(2,1)}, bf16[4,128,1792]{2,1,0:T(8,128)(2,1)}, u32[]{:S(2)}, u32[]{:S(2)}) collective-permute-start(bf16[4,128,1792]{2,1,0:T(8,128)(2,1)} %bitcast.27.refs_4_), channel_id=1, source_target_pairs={{0,8},{4,12},{8,0},{12,4},{16,24},{20,28},{24,16},{28,20},{1,9},{5... | collective-permute-start | bytes 5505032 | tf_op jit(solution)/shard_map/ppermute | solution.py:98
  195.1 53.0 %collective-permute-start.41 = (bf16[4,128,1792]{2,1,0:T(8,128)(2,1)}, bf16[4,128,1792]{2,1,0:T(8,128)(2,1)S(1)}, u32[]{:S(2)}, u32[]{:S(2)}) collective-permute-start(bf16[4,128,1792]{2,1,0:T(8,128)(2,1)} %bitcast.27.refs_4_), channel_id=1, source_target_pairs={{0,16},{4,20},{8,24},{12,28},{16,0},{20,4},{24,8},{28,12},{1,17},{... | collective-permute-start | bytes 5505032 | tf_op jit(solution)/shard_map/ppermute | solution.py:98
  235.4 43.2 %collective-permute-start.33 = (bf16[4,128,1792]{2,1,0:T(8,128)(2,1)}, bf16[4,128,1792]{2,1,0:T(8,128)(2,1)}, u32[]{:S(2)}, u32[]{:S(2)}) collective-permute-start(bf16[4,128,1792]{2,1,0:T(8,128)(2,1)} %bitcast.24.refs_4_), channel_id=1, source_target_pairs={{0,8},{4,12},{8,0},{12,4},{16,24},{20,28},{24,16},{28,20},{1,9},{5... | collective-permute-start | bytes 5505032 | tf_op jit(solution)/shard_map/ppermute | solution.py:98
  236.8 46.0 %collective-permute-start.39 = (bf16[4,128,1792]{2,1,0:T(8,128)(2,1)}, bf16[4,128,1792]{2,1,0:T(8,128)(2,1)}, u32[]{:S(2)}, u32[]{:S(2)}) collective-permute-start(bf16[4,128,1792]{2,1,0:T(8,128)(2,1)} %bitcast.24.refs_4_), channel_id=1, source_target_pairs={{0,16},{4,20},{8,24},{12,28},{16,0},{20,4},{24,8},{28,12},{1,17},{... | collective-permute-start | bytes 5505032 | tf_op jit(solution)/shard_map/ppermute | solution.py:98
  248.1 51.6 %collective-permute-start.48 = (bf16[2,128,1792]{2,1,0:T(8,128)(2,1)S(1)}, bf16[2,128,1792]{2,1,0:T(8,128)(2,1)}, u32[]{:S(2)}, u32[]{:S(2)}) collective-permute-start(bf16[2,128,1792]{2,1,0:T(8,128)(2,1)S(1)} %slice.327), channel_id=1, source_target_pairs={{0,16},{4,20},{8,24},{12,28},{16,0},{20,4},{24,8},{28,12},{1,17},{... | collective-permute-start | bytes 2752520 | tf_op jit(solution)/shard_map/ppermute | solution.py:98
  252.2 49.9 %collective-permute-start.49 = (bf16[2,128,1792]{2,1,0:T(8,128)(2,1)}, bf16[2,128,1792]{2,1,0:T(8,128)(2,1)}, u32[]{:S(2)}, u32[]{:S(2)}) collective-permute-start(bf16[2,128,1792]{2,1,0:T(8,128)(2,1)} %slice.328), channel_id=1, source_target_pairs={{0,8},{4,12},{8,0},{12,4},{16,24},{20,28},{24,16},{28,20},{1,9},{5... | collective-permute-start | bytes 2752520 | tf_op jit(solution)/shard_map/ppermute | solution.py:98
  319.2 51.6 %collective-permute-start.36 = (bf16[4,128,1792]{2,1,0:T(8,128)(2,1)}, bf16[4,128,1792]{2,1,0:T(8,128)(2,1)}, u32[]{:S(2)}, u32[]{:S(2)}) collective-permute-start(bf16[4,128,1792]{2,1,0:T(8,128)(2,1)} %collective-permute-done.35.refs_4_), channel_id=1, source_target_pairs={{0,4},{4,0},{8,12},{12,8},{16,20},{20,16},{24,28},{28,24},{1,5},{5... | collective-permute-start | bytes 5505032 | tf_op jit(solution)/shard_map/ppermute | solution.py:98
  321.4 57.3 %collective-permute-start.34 = (bf16[4,128,1792]{2,1,0:T(8,128)(2,1)}, bf16[4,128,1792]{2,1,0:T(8,128)(2,1)}, u32[]{:S(2)}, u32[]{:S(2)}) collective-permute-start(bf16[4,128,1792]{2,1,0:T(8,128)(2,1)} %collective-permute-done.33.refs_4_), channel_id=1, source_target_pairs={{0,4},{4,0},{8,12},{12,8},{16,20},{20,16},{24,28},{28,24},{1,5},{5... | collective-permute-start | bytes 5505032 | tf_op jit(solution)/shard_map/ppermute | solution.py:98
  323.5 77.5 %collective-permute-start.42 = (bf16[4,128,1792]{2,1,0:T(8,128)(2,1)S(1)}, bf16[4,128,1792]{2,1,0:T(8,128)(2,1)}, u32[]{:S(2)}, u32[]{:S(2)}) collective-permute-start(bf16[4,128,1792]{2,1,0:T(8,128)(2,1)S(1)} %collective-permute-done.41.refs_4_), channel_id=1, source_target_pairs={{0,4},{4,0},{8,12},{12,8},{16,20},{20,16},{24,28},{28,24},{1,5},{5... | collective-permute-start | bytes 5505032 | tf_op jit(solution)/shard_map/ppermute | solution.py:98
  336.2 71.9 %collective-permute-start.40 = (bf16[4,128,1792]{2,1,0:T(8,128)(2,1)}, bf16[4,128,1792]{2,1,0:T(8,128)(2,1)}, u32[]{:S(2)}, u32[]{:S(2)}) collective-permute-start(bf16[4,128,1792]{2,1,0:T(8,128)(2,1)} %collective-permute-done.39.refs_4_), channel_id=1, source_target_pairs={{0,4},{4,0},{8,12},{12,8},{16,20},{20,16},{24,28},{28,24},{1,5},{5... | collective-permute-start | bytes 5505032 | tf_op jit(solution)/shard_map/ppermute | solution.py:98
  354.3 69.1 %collective-permute-start.52 = (bf16[4,128,1792]{2,1,0:T(8,128)(2,1)}, bf16[4,128,1792]{2,1,0:T(8,128)(2,1)}, u32[]{:S(2)}, u32[]{:S(2)}) collective-permute-start(bf16[4,128,1792]{2,1,0:T(8,128)(2,1)} %get-tuple-element.58), channel_id=1, source_target_pairs={{0,4},{4,0},{8,12},{12,8},{16,20},{20,16},{24,28},{28,24},{1,5},{5... | collective-permute-start | bytes 5505032 | tf_op jit(solution)/shard_map/ppermute | solution.py:98
  370.9 57.5 %collective-permute-start.30 = (bf16[4,128,1792]{2,1,0:T(8,128)(2,1)}, bf16[4,128,1792]{2,1,0:T(8,128)(2,1)}, u32[]{:S(2)}, u32[]{:S(2)}) collective-permute-start(bf16[4,128,1792]{2,1,0:T(8,128)(2,1)} %bitcast.24.refs_4_), channel_id=1, source_target_pairs={{0,4},{4,0},{8,12},{12,8},{16,20},{20,16},{24,28},{28,24},{1,5},{5... | collective-permute-start | bytes 5505032 | tf_op jit(solution)/shard_map/ppermute | solution.py:98
  400.8 48.6 %collective-permute-start.37 = (bf16[4,128,1792]{2,1,0:T(8,128)(2,1)}, bf16[4,128,1792]{2,1,0:T(8,128)(2,1)}, u32[]{:S(2)}, u32[]{:S(2)}) collective-permute-start(bf16[4,128,1792]{2,1,0:T(8,128)(2,1)} %get-tuple-element.48), channel_id=1, source_target_pairs={{0,4},{4,0},{8,12},{12,8},{16,20},{20,16},{24,28},{28,24},{1,5},{5... | collective-permute-start | bytes 5505032 | tf_op jit(solution)/shard_map/ppermute | solution.py:98
  454.4 50.6 %collective-permute-start.56 = (bf16[2,128,1792]{2,1,0:T(8,128)(2,1)}, bf16[2,128,1792]{2,1,0:T(8,128)(2,1)S(1)}, u32[]{:S(2)}, u32[]{:S(2)}) collective-permute-start(bf16[2,128,1792]{2,1,0:T(8,128)(2,1)} %get-tuple-element.95), channel_id=1, source_target_pairs={{0,8},{4,12},{8,0},{12,4},{16,24},{20,28},{24,16},{28,20},{1,9},{5... | collective-permute-start | bytes 2752520 | tf_op jit(solution)/shard_map/ppermute | solution.py:98
  470.5 42.7 %collective-permute-start.57 = (bf16[2,128,1792]{2,1,0:T(8,128)(2,1)}, bf16[2,128,1792]{2,1,0:T(8,128)(2,1)}, u32[]{:S(2)}, u32[]{:S(2)}) collective-permute-start(bf16[2,128,1792]{2,1,0:T(8,128)(2,1)} %get-tuple-element.97), channel_id=1, source_target_pairs={{0,16},{4,20},{8,24},{12,28},{16,0},{20,4},{24,8},{28,12},{1,17},{... | collective-permute-start | bytes 2752520 | tf_op jit(solution)/shard_map/ppermute | solution.py:98
  485.2 42.5 %collective-permute-start.59 = (bf16[4,128,1792]{2,1,0:T(8,128)(2,1)}, bf16[4,128,1792]{2,1,0:T(8,128)(2,1)}, u32[]{:S(2)}, u32[]{:S(2)}) collective-permute-start(bf16[4,128,1792]{2,1,0:T(8,128)(2,1)} %get-tuple-element.62), channel_id=1, source_target_pairs={{0,4},{4,0},{8,12},{12,8},{16,20},{20,16},{24,28},{28,24},{1,5},{5... | collective-permute-start | bytes 5505032 | tf_op jit(solution)/shard_map/ppermute | solution.py:98
  488.4 46.9 %collective-permute-start.61 = (bf16[4,128,1792]{2,1,0:T(8,128)(2,1)}, bf16[4,128,1792]{2,1,0:T(8,128)(2,1)}, u32[]{:S(2)}, u32[]{:S(2)}) collective-permute-start(bf16[4,128,1792]{2,1,0:T(8,128)(2,1)} %get-tuple-element.64), channel_id=1, source_target_pairs={{0,4},{4,0},{8,12},{12,8},{16,20},{20,16},{24,28},{28,24},{1,5},{5... | collective-permute-start | bytes 5505032 | tf_op jit(solution)/shard_map/ppermute | solution.py:98
  517.2 101.5 %reduce-scatter.15.cloned.1.call-start = ((), (), s32[]{:S(2)}) async-start(), calls=%async_computation.9 | async-start | bytes 2293760
  533.7 41.8 %collective-permute-start.66 = (bf16[2,128,1792]{2,1,0:T(8,128)(2,1)S(1)}, bf16[2,128,1792]{2,1,0:T(8,128)(2,1)S(1)}, u32[]{:S(2)}, u32[]{:S(2)}) collective-permute-start(bf16[2,128,1792]{2,1,0:T(8,128)(2,1)S(1)} %get-tuple-element.103), channel_id=1, source_target_pairs={{0,8},{4,12},{8,0},{12,4},{16,24},{20,28},{24,16},{28,20},{1,9},{5... | collective-permute-start | bytes 2752520 | tf_op jit(solution)/shard_map/ppermute | solution.py:98
  (124 other events, 2024.2 us)
Sparse Core Ops, SparseCore 0:
  70.3 37.7 reduce-scatter.8
  114.4 36.9 reduce-scatter.10
  153.0 40.5 all-gather.6
  195.1 40.2 all-gather.4
  517.3 36.8 reduce-scatter.12
  579.5 36.6 reduce-scatter.14

commit v4 on v3

--- a/solution.py
+++ b/solution.py
@@ -10,7 +10,7 @@
 FP8_LIMIT = 448.0
 AXES = ("dp", "tensor")
 CHUNKS = 2
-VMEM_LIMIT = 40 * 2**20
+VMEM_LIMIT = 48 * 2**20
 
 
 def project(attn_out, out_weight):
@@ -111,6 +111,16 @@
         values = jnp.concatenate([values, swap(values, bit)])
         bit *= 2
     return values
+
+
+def along_tensor(value):
+    count, here = lax.axis_size("tensor"), lax.axis_index("tensor")
+    blocks = jnp.zeros((count,) + value.shape, value.dtype)
+    for shift in range(count):
+        pairs = [(i, (i + shift) % count) for i in range(count)]
+        block = lax.ppermute(value, "tensor", pairs) if shift else value
+        blocks = lax.dynamic_update_index_in_dim(blocks, block, (here - shift) % count, 0)
+    return blocks
 
 
 def expert_weights(expert_ids, route_weight, experts):
@@ -172,82 +182,82 @@
     )(place, attn_out, *pieces)
 
 
-def gate_up_kernel(counts, first, last, *refs):
-    refs = list(refs)
-    scale_ref, gain_ref, chosen_ref, root_ref = (refs.pop(0) for _ in range(4))
-    pieces = [refs.pop(0) for _ in counts]
-    gate_w, up_w = refs.pop(0), refs.pop(0)
-    before = [] if first else [refs.pop(0), refs.pop(0)]
-    rows = refs.pop()
+def gate_up_kernel(parts, scale_ref, gain_ref, chosen_ref, *refs):
+    hidden_ref, peak_ref, rows = refs[-3:]
+    weights, pieces = refs[-3 - 2 * parts : -3], refs[: -3 - 2 * parts]
+    per_part = len(pieces) // parts
     capacity = chosen_ref.shape[1]
+    step = rows.shape[2]
 
     @pl.when(pl.program_id(0) == 0)
     def _():
         source = 0
-        for piece, count in zip(pieces, counts):
-            for i in range(count):
+        for p in range(per_part):
+            for i in range(pieces[p].shape[0]):
                 span = slice(source * capacity, (source + 1) * capacity)
-                picked = jnp.dot(chosen_ref[source], piece[i], preferred_element_type=jnp.float32)
-                picked = picked * root_ref[span] * gain_ref[...]
-                rows[span] = jnp.clip(picked, -FP8_LIMIT, FP8_LIMIT).astype(rows.dtype)
+                picked = [
+                    jnp.dot(
+                        chosen_ref[source],
+                        pieces[c * per_part + p][i],
+                        preferred_element_type=jnp.float32,
+                    )
+                    for c in range(parts)
+                ]
+                squares = sum(jnp.sum(x * x, axis=1, keepdims=True) for x in picked)
+                root = lax.rsqrt(squares / (parts * step) + 1e-06)
+                for c, x in enumerate(picked):
+                    x = jnp.clip(x * root * gain_ref[c], -FP8_LIMIT, FP8_LIMIT)
+                    rows[c, span] = x.astype(rows.dtype)
                 source += 1
 
-    flat = lambda weight: weight[0].reshape(rows.shape[1], weight.shape[-1])
-    gate = jnp.dot(rows[...], flat(gate_w), preferred_element_type=jnp.float32)
-    up = jnp.dot(rows[...], flat(up_w), preferred_element_type=jnp.float32)
-    if not first:
-        gate += before[0][...]
-        up += before[1][...]
-    if not last:
-        refs[0][...] = gate
-        refs[1][...] = up
-        return
-    inv_x, scale_h = scale_ref[0], scale_ref[1]
-    gate, up = gate * inv_x, up * inv_x
+    def product(side):
+        return sum(
+            jnp.dot(
+                rows[c],
+                weights[2 * c + side][0].reshape(step, -1),
+                preferred_element_type=jnp.float32,
+            )
+            for c in range(parts)
+        )
+
+    gate, up = product(0) * scale_ref[0], product(1) * scale_ref[0]
     hidden = gate / (1.0 + jnp.exp(-gate)) * up
-    refs[0][...] = jnp.clip(hidden * scale_h, -FP8_LIMIT, FP8_LIMIT).astype(jnp.bfloat16)
+    scaled = jnp.clip(hidden * scale_ref[1], -FP8_LIMIT, FP8_LIMIT)
+    hidden_ref[...] = scaled.astype(hidden_ref.dtype)
     peak = jnp.max(jnp.abs(hidden), axis=0, keepdims=True)
-    refs[1][...] = jnp.broadcast_to(peak, refs[1].shape)
-
-
-def gate_up(scales, gain, chosen, root, pieces, w_gate, w_up, c, before, last):
+    peak_ref[...] = jnp.broadcast_to(peak, peak_ref.shape)
+
+
+def gate_up(scales, gains, chosen, pieces, w_gate, w_up):
     sources, capacity, tokens = chosen.shape
-    step = pieces[0].shape[-1]
-    hidden = w_gate.shape[-1]
+    parts, _, step = gains.shape
+    owners, columns, hidden = w_gate.shape[1], w_gate.shape[3], w_gate.shape[-1]
     tile = min(256, hidden)
     rows = sources * capacity
-    whole = lambda shape: pl.BlockSpec(shape, lambda n: (0,) * len(shape))
+    once = pl.Buffered(buffer_count=1)
+    whole = lambda a: pl.BlockSpec(a.shape, lambda n: (0,) * a.ndim, pipeline_mode=once)
     column = lambda height: pl.BlockSpec((height, tile), lambda n: (0, n))
-    owners, columns = w_gate.shape[1], w_gate.shape[3]
-    weight = pl.BlockSpec((1, owners, None, columns, tile), lambda n: (0, 0, c, 0, n))
-    if last:
-        out_shape = [
+    weight = lambda c: pl.BlockSpec((1, owners, None, columns, tile), lambda n: (0, 0, c, 0, n))
+    return pl.pallas_call(
+        functools.partial(gate_up_kernel, parts),
+        grid=(hidden // tile,),
+        in_specs=[pl.BlockSpec(memory_space=pltpu.SMEM), whole(gains), whole(chosen)]
+        + [whole(p) for p in pieces]
+        + [weight(c) for c in range(parts) for _ in range(2)],
+        out_specs=[column(rows), column(8)],
+        out_shape=[
             jax.ShapeDtypeStruct((rows, hidden), jnp.bfloat16),
             jax.ShapeDtypeStruct((8, hidden), jnp.float32),
-        ]
-        out_specs = [column(rows), column(8)]
-    else:
-        out_shape = [jax.ShapeDtypeStruct((rows, hidden), jnp.float32)] * 2
-        out_specs = [column(rows)] * 2
-    return pl.pallas_call(
-        functools.partial(gate_up_kernel, [p.shape[0] for p in pieces], not before, last),
-        grid=(hidden // tile,),
-        in_specs=[pl.BlockSpec(memory_space=pltpu.SMEM)]
-        + [whole(gain.shape), whole(chosen.shape), whole(root.shape)]
-        + [whole(p.shape) for p in pieces]
-        + [weight] * 2
-        + [column(rows)] * len(before),
-        out_specs=out_specs,
-        out_shape=out_shape,
-        scratch_shapes=[pltpu.VMEM((rows, step), jnp.bfloat16)],
+        ],
+        scratch_shapes=[pltpu.VMEM((parts, rows, step), jnp.bfloat16)],
         compiler_params=pltpu.CompilerParams(vmem_limit_bytes=VMEM_LIMIT),
         cost_estimate=pl.CostEstimate(
-            flops=2 * rows * step * (2 * hidden + tokens),
-            bytes_accessed=2 * step * (2 * hidden + sources * tokens) + 16 * rows * hidden,
-            transcendentals=rows * hidden if last else 0,
+            flops=2 * rows * parts * step * (2 * hidden + tokens),
+            bytes_accessed=2 * parts * step * (2 * hidden + sources * tokens),
+            transcendentals=rows * hidden,
         ),
         name="gate_up",
-    )(scales, gain, chosen, root, *pieces, w_gate, w_up, *before)
+    )(scales, gains, chosen, *pieces, *([w_gate, w_up] * parts))
 
 
 def down_kernel(hidden_ref, down_w, factor_ref, spread_ref, own_ref, other_ref):
@@ -270,7 +280,7 @@
 def down(hidden_q, w_down, factor, spread, c, step):
     rows, hidden = hidden_q.shape
     sources, tokens, capacity = spread.shape
-    tile = 256 if step % 256 == 0 else 128
+    tile = step // 2 if step % 256 == 0 else step
     tiles = step // tile
     whole = lambda shape: pl.BlockSpec(shape, lambda j: (0,) * len(shape))
     return pl.pallas_call(
@@ -318,10 +328,13 @@
     half, step = layers // 2, width // CHUNKS
     columns = step // owners
 
-    weight = expert_weights(expert_ids, route_weight, experts)
     weight_rows = out_weight.T.reshape(CHUNKS, columns, -1)
     blocks = [chip_groups(weight_rows[c]) for c in range(CHUNKS)]
-    attn_out, weight = lax.optimization_barrier((attn_out, weight))
+    first = blocks[0][1][0][0]
+    first, expert_ids = lax.optimization_barrier((first, expert_ids))
+    blocks[0][1][0][0] = first
+    weight = expert_weights(expert_ids, route_weight, experts)
+    blocks[-1], weight = lax.optimization_barrier((blocks[-1], weight))
 
     named = weight > 0.0
     earlier = jnp.triu(jnp.ones((local_rows, local_rows), jnp.bfloat16), 1)
@@ -334,10 +347,8 @@
     chosen = (
         slot[:, :, None, :] == jnp.arange(capacity, dtype=jnp.int32)[:, None]
     ) & named[:, :, None, :]
-    by_slot = lambda values: jnp.sum(
-        jnp.where(chosen, values[:, :, None, :], 0.0), axis=3
-    ).reshape(4, 2 * layers * capacity, 1)
-    factor = by_slot(weight) * (top_h / FP8_LIMIT)
+    factor = jnp.sum(jnp.where(chosen, weight[:, :, None, :], 0.0), axis=3)
+    factor = factor.reshape(4, 2 * layers * capacity, 1) * (top_h / FP8_LIMIT)
     choice = chosen.astype(jnp.bfloat16).reshape(4, 2 * layers, capacity, local_rows)
     spread = choice.transpose(0, 1, 3, 2)
     scales = jnp.stack([top_x / FP8_LIMIT, FP8_LIMIT / top_h])
@@ -350,41 +361,28 @@
         terms = project_part(place, attn_out, blocks[c])
         total = lax.psum_scatter(terms, "tensor", scatter_dimension=0, tiled=True)
         stream.append(parts(residual, c).astype(jnp.float32) + total.astype(jnp.float32))
-        own = lax.all_gather(stream[c].astype(jnp.bfloat16), "tensor", axis=0)
-        tokens.append(chip_groups(own))
+        tokens.append(chip_groups(along_tensor(stream[c].astype(jnp.bfloat16))))
     squares = sum(jnp.sum(part * part, axis=1) for part in stream)
     root = lax.rsqrt(squares / width + 1e-06)
     gains = [parts(norm_gain, c) for c in range(CHUNKS)]
     peak_x = jnp.max(
         jnp.stack([jnp.max(jnp.abs(s * root[:, None] * g)) for s, g in zip(stream, gains)])
     )
-    roots = by_slot(from_all(root))
-    gains = [g * (FP8_LIMIT / top_x) for g in gains]
+    gains = jnp.stack(gains) * (FP8_LIMIT / top_x)
 
     gate_rows = w_gate.reshape(1, owners, CHUNKS, columns, -1)
     up_rows = w_up.reshape(1, owners, CHUNKS, columns, -1)
-    sums = [[] for _ in range(4)]
-    for c in range(CHUNKS):
-        for r, (near, far) in enumerate(tokens[c]):
-            sums[r] = gate_up(
-                scales,
-                gains[c],
-                choice[r],
-                roots[r],
-                near + far,
-                gate_rows,
-                up_rows,
-                c,
-                sums[r],
-                c == CHUNKS - 1,
-            )
-    peak_h = jnp.max(jnp.stack([jnp.max(s[1]) for s in sums]))
+    hidden = []
+    for r in range(4):
+        pieces = [piece for part in tokens for side in part[r] for piece in side]
+        hidden.append(gate_up(scales, gains, choice[r], pieces, gate_rows, up_rows))
+    peak_h = jnp.max(jnp.stack([jnp.max(peaks) for _, peaks in hidden]))
 
     mixture = []
     for c in range(CHUNKS):
         to = []
         for r in range(4):
-            kept, given = down(sums[r][0], w_down, factor[r], spread[r], c, step)
+            kept, given = down(hidden[r][0], w_down, factor[r], spread[r], c, step)
             taken = swap(given, 1)
             to.append([add(kept[:half], taken[:half]), add(kept[half:], taken[half:])])
         over_x, over_y = swap(to[3][0], 2), swap(to[3][1], 4)

time: 641 us -> 626 us (0.977)
  Pallas kernels: 129 us -> 114 us
  starting transfers between devices: 53.6 us -> 67.1 us
  local copies, waits for them, and re-layouts: 52.7 us -> 43.4 us
    all_gather x2 -> x0, waiting for transfers between devices: 78.7 us -> none  [gather_plan(): own = lax.all_gather(stream[c].astype(jnp.bfloat16), 'tensor', axis=0)]
    ppermute x62 -> x59, waiting for transfers between devices: 194 us -> 227 us  [swap(): return lax.ppermute(value, 'dp', [(i, i ^ bits) for i in range(count)])]
    reduce_scatter x2, waiting for transfers between devices: 32.5 us -> 56.6 us  [gather_plan(): total = lax.psum_scatter(terms, 'tensor', scatter_dimension=0, tiled=True)]
    ppermute x0 -> x6, waiting for transfers between devices: none -> 20.3 us  [along_tensor(): block = lax.ppermute(value, 'tensor', pairs) if shift else value]
    unnamed x142 -> x118, local copies, waits for them, and re-layouts: 34.4 us -> 14.8 us
    ppermute x0 -> x6, starting transfers between devices: none -> 17.2 us  [along_tensor(): block = lax.ppermute(value, 'tensor', pairs) if shift else value]
    pallas_call x8 -> x4, Pallas kernels: 61.8 us -> 52.6 us  [gate_up(): pl.pallas_call(functools.partial(gate_up_kernel, parts), grid=(hidden //...]
    pallas_call x8, Pallas kernels: 51.5 us -> 43.5 us  [down(): pl.pallas_call(down_kernel, grid=(tiles,), in_specs=[whole(hidden_q.shape...]
  transfers between devices with their start and end apart: 79 -> 77, of which waited for: 34 -> 34; matrix products, arithmetic and copies ran while one was open for 10% -> 11% of each run, Pallas kernels for 19% -> 17%
where the time goes in v4:
time: 626 us; the launch traced here: 617 us
  waiting for transfers between devices  328 us (52%)
  Pallas kernels  114 us (18%)
  starting transfers between devices  67.1 us (11%)
  local copies, waits for them, and re-layouts  43.4 us (7%)
  other arithmetic  42.1 us (7%)
  between operations  21.7 us (3%)
    ppermute x59, waiting for transfers between devices, swap(): return lax.ppermute(value, 'dp', [(i, i ^ bits) for i in range(count)])  227 us
    reduce_scatter x2, waiting for transfers between devices, gather_plan(): total = lax.psum_scatter(terms, 'tensor', scatter_dimension=0, tiled=True)  56.6 us
    pallas_call x4, Pallas kernels, gate_up(): pl.pallas_call(functools.partial(gate_up_kernel, parts), grid=(hidden //...  52.6 us
    pallas_call x8, Pallas kernels, down(): pl.pallas_call(down_kernel, grid=(tiles,), in_specs=[whole(hidden_q.shape...  43.5 us
    ppermute x59, starting transfers between devices, swap(): return lax.ppermute(value, 'dp', [(i, i ^ bits) for i in range(count)])  42.8 us
    convert_element_type x8, other arithmetic, add(): return sum((t.astype(jnp.float32) for t in terms)).astype(jnp.bfloat16)  21.5 us
    ppermute x5, waiting for transfers between devices, peaks_over_all(): peaks = jnp.maximum(peaks, lax.ppermute(peaks, axis, pairs))  21.1 us
    ppermute x6, waiting for transfers between devices, along_tensor(): block = lax.ppermute(value, 'tensor', pairs) if shift else value  20.3 us
  transfers between devices with their start and end apart: 77, of which 34 were waited for; matrix products, arithmetic and copies ran while one was open for 11% of the time, Pallas kernels for 17%

profile of v4, /device:TPU:0, one launch (start us, length us, event | category | flops | bytes accessed | tf_op | source)
XLA Modules:
  0.0 616.5 jit_solution(6697924698857783027)
XLA Ops:
  13.9 19.1 %collective-permute-done.1.refs_2_ = bf16[224,2048]{1,0:T(8,128)(2,1)S(1)} collective-permute-done((bf16[224,2048]{1,0:T(8,128)(2,1)S(1)}, bf16[224,2048]{1,0:T(8,128)(2,1)S(1)}, u32[]{:S(2)}, u32[]{:S(2)}) %collective-permute-start.1) | collective-permute-done | bytes 917536 | tf_op jit(solution)/shard_map/ppermute | solution.py:98
  42.2 9.7 %collective-permute-done.10.refs_2_ = bf16[224,2048]{1,0:T(8,128)(2,1)} collective-permute-done((bf16[224,2048]{1,0:T(8,128)(2,1)S(1)}, bf16[224,2048]{1,0:T(8,128)(2,1)}, u32[]{:S(2)}, u32[]{:S(2)}) %collective-permute-start.10) | collective-permute-done | bytes 917536 | tf_op jit(solution)/shard_map/ppermute | solution.py:98
  73.7 9.7 %project.3 = bf16[512,1792]{1,0:T(8,128)(2,1)} custom-call(s32[1]{0:T(128)} %bitcast.2.place_ref, bf16[512,2048]{1,0:T(8,128)(2,1)} %attn_ref.3, bf16[224,2048]{1,0:T(8,128)(2,1)S(1)} %get-tuple-element.42.refs_0_, bf16[224,2048]{1,0:T(8,128)(2,1)} %collective-permute-done.9.refs_1_, bf16[224,2048]{1,0:T(8,128)(2,1)} %collective-permute-done.10.refs_2_, ...), custom_call_target="tpu_custom_call" | custom-call | flops 3758096384 | bytes 9437184 | tf_op jit(solution)/shard_map/project/pallas_call | solution.py:165
  85.6 21.1 %collective-permute-done.3.refs_4_ = bf16[224,2048]{1,0:T(8,128)(2,1)S(1)} collective-permute-done((bf16[224,2048]{1,0:T(8,128)(2,1)S(1)}, bf16[224,2048]{1,0:T(8,128)(2,1)S(1)}, u32[]{:S(2)}, u32[]{:S(2)}) %collective-permute-start.3) | collective-permute-done | bytes 917536 | tf_op jit(solution)/shard_map/ppermute | solution.py:98
  108.4 7.3 %collective-permute-done.5.refs_6_ = bf16[112,2048]{1,0:T(8,128)(2,1)S(1)} collective-permute-done((bf16[112,2048]{1,0:T(8,128)(2,1)S(1)}, bf16[112,2048]{1,0:T(8,128)(2,1)S(1)}, u32[]{:S(2)}, u32[]{:S(2)}) %collective-permute-start.5) | collective-permute-done | bytes 458784 | tf_op jit(solution)/shard_map/ppermute | solution.py:98
  120.6 8.6 %project.2 = bf16[512,1792]{1,0:T(8,128)(2,1)} custom-call(s32[1]{0:T(128)} %bitcast.2.place_ref, bf16[512,2048]{1,0:T(8,128)(2,1)} %attn_ref.3, bf16[224,2048]{1,0:T(8,128)(2,1)S(1)} %get-tuple-element.114.refs_0_, bf16[224,2048]{1,0:T(8,128)(2,1)S(1)} %collective-permute-done.refs_1_, bf16[224,2048]{1,0:T(8,128)(2,1)S(1)} %collective-permute-done.1.refs_2_, ...), custom_call_target="tpu_custom_call" | custom-call | flops 3758096384 | bytes 9437184 | tf_op jit(solution)/shard_map/project/pallas_call | solution.py:165
  141.7 56.6 %reduce-scatter.9.cloned.1.call-done = bf16[128,1792]{1,0:T(8,128)(2,1)} async-done(((bf16[512,1792]{1,0:T(8,128)(2,1)}), bf16[128,1792]{1,0:T(8,128)(2,1)}) %reduce-scatter.9.cloned.1.call-update) | async-done | bytes 458768 | tf_op jit(solution)/shard_map/reduce_scatter | solution.py:362
  200.9 6.9 %collective-permute-start.24 = (bf16[128,1792]{1,0:T(8,128)(2,1)S(1)}, bf16[128,1792]{1,0:T(8,128)(2,1)S(1)}, u32[]{:S(2)}, u32[]{:S(2)}) collective-permute-start(bf16[128,1792]{1,0:T(8,128)(2,1)S(1)} %get-tuple-element.97), channel_id=1, source_target_pairs={{0,1},{1,2},{2,3},{3,0},{4,5},{5,6},{6,7},{7,4},{8,9},{9,10},{10,1... | collective-permute-start | bytes 1376264 | tf_op jit(solution)/shard_map/ppermute | solution.py:121
  219.9 18.7 %collective-permute-done.25 = bf16[128,1792]{1,0:T(8,128)(2,1)S(1)} collective-permute-done((bf16[128,1792]{1,0:T(8,128)(2,1)S(1)}, bf16[128,1792]{1,0:T(8,128)(2,1)S(1)}, u32[]{:S(2)}, u32[]{:S(2)}) %collective-permute-start.25) | collective-permute-done | bytes 458784 | tf_op jit(solution)/shard_map/ppermute | solution.py:121
  242.0 16.5 %collective-permute-done.35.refs_2_ = bf16[4,128,1792]{2,1,0:T(8,128)(2,1)} collective-permute-done((bf16[4,128,1792]{2,1,0:T(8,128)(2,1)}, bf16[4,128,1792]{2,1,0:T(8,128)(2,1)}, u32[]{:S(2)}, u32[]{:S(2)}) %collective-permute-start.35) | collective-permute-done | bytes 1835040 | tf_op jit(solution)/shard_map/ppermute | solution.py:98
  271.0 26.8 %collective-permute-done.33.refs_0_ = bf16[4,128,1792]{2,1,0:T(8,128)(2,1)} collective-permute-done((bf16[4,128,1792]{2,1,0:T(8,128)(2,1)S(1)}, bf16[4,128,1792]{2,1,0:T(8,128)(2,1)}, u32[]{:S(2)}, u32[]{:S(2)}) %collective-permute-start.33) | collective-permute-done | bytes 1835040 | tf_op jit(solution)/shard_map/ppermute | solution.py:98
  305.3 13.7 %collective-permute-done.48.refs_4_ = bf16[2,128,1792]{2,1,0:T(8,128)(2,1)S(1)} collective-permute-done((bf16[2,128,1792]{2,1,0:T(8,128)(2,1)}, bf16[2,128,1792]{2,1,0:T(8,128)(2,1)S(1)}, u32[]{:S(2)}, u32[]{:S(2)}) %collective-permute-start.48) | collective-permute-done | bytes 917536 | tf_op jit(solution)/shard_map/ppermute | solution.py:98
  321.4 15.1 %collective-permute-done.44.refs_0_ = bf16[2,128,1792]{2,1,0:T(8,128)(2,1)} collective-permute-done((bf16[2,128,1792]{2,1,0:T(8,128)(2,1)}, bf16[2,128,1792]{2,1,0:T(8,128)(2,1)}, u32[]{:S(2)}, u32[]{:S(2)}) %collective-permute-start.44) | collective-permute-done | bytes 917536 | tf_op jit(solution)/shard_map/ppermute | solution.py:98
  341.9 12.8 %gate_up.7 = (bf16[384,1024]{1,0:T(8,128)(2,1)S(1)}, f32[8,1024]{1,0:T(8,128)S(1)}) custom-call(f32[2]{0:T(128)S(1)} %copy-done.32, f32[2,1,1792]{2,1,0:T(1,128)S(1)} %maximum_multiply_fusion.gain_ref, bf16[8,48,128]{2,1,0:T(8,128)(2,1)S(1)} %bitcast.73, bf16[2,128,1792]{2,1,0:T(8,128)(2,1)} %collective-permute-done.44.refs_0_, ...), custom_call_target="tpu_custom_call" | custom-call | flops 5989466112 | bytes 22020096 | tf_op jit(solution)/shard_map/gate_up/pallas_call | solution.py:241
  367.6 13.6 %gate_up.5 = (bf16[384,1024]{1,0:T(8,128)(2,1)S(1)}, f32[8,1024]{1,0:T(8,128)S(1)}) custom-call(f32[2]{0:T(128)S(1)} %copy-done.33, f32[2,1,1792]{2,1,0:T(1,128)S(1)} %maximum_multiply_fusion.gain_ref, bf16[8,48,128]{2,1,0:T(8,128)(2,1)S(1)} %bitcast.72, bf16[4,128,1792]{2,1,0:T(8,128)(2,1)} %collective-permute-done.33.refs_0_, ...), custom_call_target="tpu_custom_call" | custom-call | flops 5989466112 | bytes 22020096 | tf_op jit(solution)/shard_map/gate_up/pallas_call | solution.py:241
  387.2 13.6 %gate_up.6 = (bf16[384,1024]{1,0:T(8,128)(2,1)S(1)}, f32[8,1024]{1,0:T(8,128)S(1)}) custom-call(f32[2]{0:T(128)S(1)} %copy-done.33, f32[2,1,1792]{2,1,0:T(1,128)S(1)} %maximum_multiply_fusion.gain_ref, bf16[8,48,128]{2,1,0:T(8,128)(2,1)S(1)} %bitcast.71, bf16[4,128,1792]{2,1,0:T(8,128)(2,1)} %collective-permute-done.39.refs_0_, ...), custom_call_target="tpu_custom_call" | custom-call | flops 5989466112 | bytes 22020096 | tf_op jit(solution)/shard_map/gate_up/pallas_call | solution.py:241
  400.8 5.8 down.10
  411.2 12.6 %gate_up.4 = (bf16[384,1024]{1,0:T(8,128)(2,1)S(1)}, f32[8,1024]{1,0:T(8,128)S(1)}) custom-call(f32[2]{0:T(128)S(1)} %copy-done.33, f32[2,1,1792]{2,1,0:T(1,128)S(1)} %maximum_multiply_fusion.gain_ref, bf16[8,48,128]{2,1,0:T(8,128)(2,1)S(1)} %bitcast.70, bf16[4,128,1792]{2,1,0:T(8,128)(2,1)S(1)} %bitcast_dynamic-update-slice_fusion.4.refs_0_, ...), custom_call_target="tpu_custom_call" | custom-call | flops 5989466112 | bytes 22020096 | tf_op jit(solution)/shard_map/gate_up/pallas_call | solution.py:241
  441.2 11.7 %collective-permute-done.53 = bf16[2,128,1792]{2,1,0:T(8,128)(2,1)} collective-permute-done((bf16[2,128,1792]{2,1,0:T(8,128)(2,1)}, bf16[2,128,1792]{2,1,0:T(8,128)(2,1)}, u32[]{:S(2)}, u32[]{:S(2)}) %collective-permute-start.53) | collective-permute-done | bytes 917536 | tf_op jit(solution)/shard_map/ppermute | solution.py:98
  474.8 16.9 %collective-permute-done.56 = bf16[2,128,1792]{2,1,0:T(8,128)(2,1)S(1)} collective-permute-done((bf16[2,128,1792]{2,1,0:T(8,128)(2,1)}, bf16[2,128,1792]{2,1,0:T(8,128)(2,1)S(1)}, u32[]{:S(2)}, u32[]{:S(2)}) %collective-permute-start.56) | collective-permute-done | bytes 917536 | tf_op jit(solution)/shard_map/ppermute | solution.py:98
  492.3 7.3 %collective-permute-done.57 = bf16[2,128,1792]{2,1,0:T(8,128)(2,1)S(1)} collective-permute-done((bf16[2,128,1792]{2,1,0:T(8,128)(2,1)}, bf16[2,128,1792]{2,1,0:T(8,128)(2,1)S(1)}, u32[]{:S(2)}, u32[]{:S(2)}) %collective-permute-start.57) | collective-permute-done | bytes 917536 | tf_op jit(solution)/shard_map/ppermute | solution.py:98
  510.2 7.3 %collective-permute-done.65 = bf16[2,128,1792]{2,1,0:T(8,128)(2,1)} collective-permute-done((bf16[2,128,1792]{2,1,0:T(8,128)(2,1)}, bf16[2,128,1792]{2,1,0:T(8,128)(2,1)}, u32[]{:S(2)}, u32[]{:S(2)}) %collective-permute-start.65) | collective-permute-done | bytes 917536 | tf_op jit(solution)/shard_map/ppermute | solution.py:98
  529.6 15.5 %collective-permute-done.60 = bf16[2,128,1792]{2,1,0:T(8,128)(2,1)S(1)} collective-permute-done((bf16[2,128,1792]{2,1,0:T(8,128)(2,1)S(1)}, bf16[2,128,1792]{2,1,0:T(8,128)(2,1)S(1)}, u32[]{:S(2)}, u32[]{:S(2)}) %collective-permute-start.60) | collective-permute-done | bytes 917536 | tf_op jit(solution)/shard_map/ppermute | solution.py:98
  545.1 17.4 %collective-permute-done.66 = bf16[2,128,1792]{2,1,0:T(8,128)(2,1)S(1)} collective-permute-done((bf16[2,128,1792]{2,1,0:T(8,128)(2,1)S(1)}, bf16[2,128,1792]{2,1,0:T(8,128)(2,1)S(1)}, u32[]{:S(2)}, u32[]{:S(2)}) %collective-permute-start.66) | collective-permute-done | bytes 917536 | tf_op jit(solution)/shard_map/ppermute | solution.py:98
  (353 shorter events, 230.6 us)
Async XLA Ops:
  7.2 124.7 %reduce-scatter.11.cloned.1.call-start = ((), (), s32[]{:S(2)}) async-start(), calls=%async_computation.5 | async-start | bytes 2293760 | tf_op jit(solution)/shard_map/reduce_scatter | solution.py:362
  11.9 44.5 %collective-permute-start.12 = (bf16[224,2048]{1,0:T(8,128)(2,1)S(1)}, bf16[224,2048]{1,0:T(8,128)(2,1)}, u32[]{:S(2)}, u32[]{:S(2)}) collective-permute-start(bf16[224,2048]{1,0:T(8,128)(2,1)S(1)} %get-tuple-element.42.refs_0_), channel_id=1, source_target_pairs={{0,16},{4,20},{8,24},{12,28},{16,0},{20,4},{24,8},{28,12},{1,17},{... | collective-permute-start | bytes 2752520 | tf_op jit(solution)/shard_map/ppermute | solution.py:98
  83.4 114.9 %reduce-scatter.9.cloned.1.call-start = ((), (), s32[]{:S(2)}) async-start(), calls=%async_computation.4 | async-start | bytes 2293760 | tf_op jit(solution)/shard_map/reduce_scatter | solution.py:362
  129.2 474.6 %reduce-scatter.13.cloned.1.call-start = ((), (), s32[]{:S(2)}) async-start(), calls=%async_computation.6 | async-start | bytes 2293760
  136.2 73.6 %collective-permute-start.28 = (bf16[128,1792]{1,0:T(8,128)(2,1)}, bf16[128,1792]{1,0:T(8,128)(2,1)S(1)}, u32[]{:S(2)}, u32[]{:S(2)}) collective-permute-start(bf16[128,1792]{1,0:T(8,128)(2,1)} %get-tuple-element.95), channel_id=1, source_target_pairs={{0,1},{1,2},{2,3},{3,0},{4,5},{5,6},{6,7},{7,4},{8,9},{9,10},{10,1... | collective-permute-start | bytes 1376264 | tf_op jit(solution)/shard_map/ppermute | solution.py:121
  137.3 76.2 %collective-permute-start.29 = (bf16[128,1792]{1,0:T(8,128)(2,1)}, bf16[128,1792]{1,0:T(8,128)(2,1)S(1)}, u32[]{:S(2)}, u32[]{:S(2)}) collective-permute-start(bf16[128,1792]{1,0:T(8,128)(2,1)} %get-tuple-element.95), channel_id=1, source_target_pairs={{0,2},{1,3},{2,0},{3,1},{4,6},{5,7},{6,4},{7,5},{8,10},{9,11},{10,... | collective-permute-start | bytes 1376264 | tf_op jit(solution)/shard_map/ppermute | solution.py:121
  140.0 74.4 %collective-permute-start.30 = (bf16[128,1792]{1,0:T(8,128)(2,1)}, bf16[128,1792]{1,0:T(8,128)(2,1)S(1)}, u32[]{:S(2)}, u32[]{:S(2)}) collective-permute-start(bf16[128,1792]{1,0:T(8,128)(2,1)} %get-tuple-element.95), channel_id=1, source_target_pairs={{0,3},{1,0},{2,1},{3,2},{4,7},{5,4},{6,5},{7,6},{8,11},{9,8},{10,9... | collective-permute-start | bytes 1376264 | tf_op jit(solution)/shard_map/ppermute | solution.py:121
  215.1 43.3 %collective-permute-start.35 = (bf16[4,128,1792]{2,1,0:T(8,128)(2,1)}, bf16[4,128,1792]{2,1,0:T(8,128)(2,1)}, u32[]{:S(2)}, u32[]{:S(2)}) collective-permute-start(bf16[4,128,1792]{2,1,0:T(8,128)(2,1)} %bitcast_dynamic-update-slice_fusion.refs_2_), channel_id=1, source_target_pairs={{0,8},{4,12},{8,0},{12,4},{16,24},{20,28},{24,16},{28,20},{1,9},{5... | collective-permute-start | bytes 5505032 | tf_op jit(solution)/shard_map/ppermute | solution.py:98
  216.8 50.5 %collective-permute-start.41 = (bf16[4,128,1792]{2,1,0:T(8,128)(2,1)}, bf16[4,128,1792]{2,1,0:T(8,128)(2,1)}, u32[]{:S(2)}, u32[]{:S(2)}) collective-permute-start(bf16[4,128,1792]{2,1,0:T(8,128)(2,1)} %bitcast_dynamic-update-slice_fusion.refs_2_), channel_id=1, source_target_pairs={{0,16},{4,20},{8,24},{12,28},{16,0},{20,4},{24,8},{28,12},{1,17},{... | collective-permute-start | bytes 5505032 | tf_op jit(solution)/shard_map/ppermute | solution.py:98
  238.8 59.0 %collective-permute-start.33 = (bf16[4,128,1792]{2,1,0:T(8,128)(2,1)S(1)}, bf16[4,128,1792]{2,1,0:T(8,128)(2,1)}, u32[]{:S(2)}, u32[]{:S(2)}) collective-permute-start(bf16[4,128,1792]{2,1,0:T(8,128)(2,1)S(1)} %bitcast_dynamic-update-slice_fusion.4.refs_0_), channel_id=1, source_target_pairs={{0,8},{4,12},{8,0},{12,4},{16,24},{20,28},{24,16},{28,20},{1,9},{5... | collective-permute-start | bytes 5505032 | tf_op jit(solution)/shard_map/ppermute | solution.py:98
  240.5 61.2 %collective-permute-start.39 = (bf16[4,128,1792]{2,1,0:T(8,128)(2,1)S(1)}, bf16[4,128,1792]{2,1,0:T(8,128)(2,1)}, u32[]{:S(2)}, u32[]{:S(2)}) collective-permute-start(bf16[4,128,1792]{2,1,0:T(8,128)(2,1)S(1)} %bitcast_dynamic-update-slice_fusion.4.refs_0_), channel_id=1, source_target_pairs={{0,16},{4,20},{8,24},{12,28},{16,0},{20,4},{24,8},{28,12},{1,17},{... | collective-permute-start | bytes 5505032 | tf_op jit(solution)/shard_map/ppermute | solution.py:98
  260.6 58.4 %collective-permute-start.48 = (bf16[2,128,1792]{2,1,0:T(8,128)(2,1)}, bf16[2,128,1792]{2,1,0:T(8,128)(2,1)S(1)}, u32[]{:S(2)}, u32[]{:S(2)}) collective-permute-start(bf16[2,128,1792]{2,1,0:T(8,128)(2,1)} %slice.293), channel_id=1, source_target_pairs={{0,16},{4,20},{8,24},{12,28},{16,0},{20,4},{24,8},{28,12},{1,17},{... | collective-permute-start | bytes 2752520 | tf_op jit(solution)/shard_map/ppermute | solution.py:98
  269.5 51.3 %collective-permute-start.49 = (bf16[2,128,1792]{2,1,0:T(8,128)(2,1)}, bf16[2,128,1792]{2,1,0:T(8,128)(2,1)}, u32[]{:S(2)}, u32[]{:S(2)}) collective-permute-start(bf16[2,128,1792]{2,1,0:T(8,128)(2,1)} %slice.294), channel_id=1, source_target_pairs={{0,8},{4,12},{8,0},{12,4},{16,24},{20,28},{24,16},{28,20},{1,9},{5... | collective-permute-start | bytes 2752520 | tf_op jit(solution)/shard_map/ppermute | solution.py:98
  340.8 46.0 %collective-permute-start.42 = (bf16[4,128,1792]{2,1,0:T(8,128)(2,1)}, bf16[4,128,1792]{2,1,0:T(8,128)(2,1)}, u32[]{:S(2)}, u32[]{:S(2)}) collective-permute-start(bf16[4,128,1792]{2,1,0:T(8,128)(2,1)} %collective-permute-done.41.refs_2_), channel_id=1, source_target_pairs={{0,4},{4,0},{8,12},{12,8},{16,20},{20,16},{24,28},{28,24},{1,5},{5... | collective-permute-start | bytes 5505032 | tf_op jit(solution)/shard_map/ppermute | solution.py:98
  340.9 46.3 %collective-permute-start.40 = (bf16[4,128,1792]{2,1,0:T(8,128)(2,1)}, bf16[4,128,1792]{2,1,0:T(8,128)(2,1)}, u32[]{:S(2)}, u32[]{:S(2)}) collective-permute-start(bf16[4,128,1792]{2,1,0:T(8,128)(2,1)} %collective-permute-done.39.refs_0_), channel_id=1, source_target_pairs={{0,4},{4,0},{8,12},{12,8},{16,20},{20,16},{24,28},{28,24},{1,5},{5... | collective-permute-start | bytes 5505032 | tf_op jit(solution)/shard_map/ppermute | solution.py:98
  361.5 45.2 %collective-permute-start.52 = (bf16[4,128,1792]{2,1,0:T(8,128)(2,1)}, bf16[4,128,1792]{2,1,0:T(8,128)(2,1)}, u32[]{:S(2)}, u32[]{:S(2)}) collective-permute-start(bf16[4,128,1792]{2,1,0:T(8,128)(2,1)} %get-tuple-element.64), channel_id=1, source_target_pairs={{0,4},{4,0},{8,12},{12,8},{16,20},{20,16},{24,28},{28,24},{1,5},{5... | collective-permute-start | bytes 5505032 | tf_op jit(solution)/shard_map/ppermute | solution.py:98
  365.4 45.8 %collective-permute-start.31 = (bf16[4,128,1792]{2,1,0:T(8,128)(2,1)}, bf16[4,128,1792]{2,1,0:T(8,128)(2,1)}, u32[]{:S(2)}, u32[]{:S(2)}) collective-permute-start(bf16[4,128,1792]{2,1,0:T(8,128)(2,1)} %bitcast_dynamic-update-slice_fusion.refs_2_), channel_id=1, source_target_pairs={{0,4},{4,0},{8,12},{12,8},{16,20},{20,16},{24,28},{28,24},{1,5},{5... | collective-permute-start | bytes 5505032 | tf_op jit(solution)/shard_map/ppermute | solution.py:98
  365.9 45.3 %collective-permute-start.27 = (bf16[4,128,1792]{2,1,0:T(8,128)(2,1)S(1)}, bf16[4,128,1792]{2,1,0:T(8,128)(2,1)S(1)}, u32[]{:S(2)}, u32[]{:S(2)}) collective-permute-start(bf16[4,128,1792]{2,1,0:T(8,128)(2,1)S(1)} %bitcast_dynamic-update-slice_fusion.4.refs_0_), channel_id=1, source_target_pairs={{0,4},{4,0},{8,12},{12,8},{16,20},{20,16},{24,28},{28,24},{1,5},{5... | collective-permute-start | bytes 5505032 | tf_op jit(solution)/shard_map/ppermute | solution.py:98
  386.8 48.7 %collective-permute-start.37 = (bf16[4,128,1792]{2,1,0:T(8,128)(2,1)}, bf16[4,128,1792]{2,1,0:T(8,128)(2,1)}, u32[]{:S(2)}, u32[]{:S(2)}) collective-permute-start(bf16[4,128,1792]{2,1,0:T(8,128)(2,1)} %get-tuple-element.58), channel_id=1, source_target_pairs={{0,4},{4,0},{8,12},{12,8},{16,20},{20,16},{24,28},{28,24},{1,5},{5... | collective-permute-start | bytes 5505032 | tf_op jit(solution)/shard_map/ppermute | solution.py:98
  440.6 51.0 %collective-permute-start.56 = (bf16[2,128,1792]{2,1,0:T(8,128)(2,1)}, bf16[2,128,1792]{2,1,0:T(8,128)(2,1)S(1)}, u32[]{:S(2)}, u32[]{:S(2)}) collective-permute-start(bf16[2,128,1792]{2,1,0:T(8,128)(2,1)} %get-tuple-element.101), channel_id=1, source_target_pairs={{0,8},{4,12},{8,0},{12,4},{16,24},{20,28},{24,16},{28,20},{1,9},{5... | collective-permute-start | bytes 2752520 | tf_op jit(solution)/shard_map/ppermute | solution.py:98
  457.1 42.5 %collective-permute-start.57 = (bf16[2,128,1792]{2,1,0:T(8,128)(2,1)}, bf16[2,128,1792]{2,1,0:T(8,128)(2,1)S(1)}, u32[]{:S(2)}, u32[]{:S(2)}) collective-permute-start(bf16[2,128,1792]{2,1,0:T(8,128)(2,1)} %get-tuple-element.103), channel_id=1, source_target_pairs={{0,16},{4,20},{8,24},{12,28},{16,0},{20,4},{24,8},{28,12},{1,17},{... | collective-permute-start | bytes 2752520 | tf_op jit(solution)/shard_map/ppermute | solution.py:98
  474.7 47.3 %collective-permute-start.61 = (bf16[4,128,1792]{2,1,0:T(8,128)(2,1)}, bf16[4,128,1792]{2,1,0:T(8,128)(2,1)}, u32[]{:S(2)}, u32[]{:S(2)}) collective-permute-start(bf16[4,128,1792]{2,1,0:T(8,128)(2,1)} %get-tuple-element.70), channel_id=1, source_target_pairs={{0,4},{4,0},{8,12},{12,8},{16,20},{20,16},{24,28},{28,24},{1,5},{5... | collective-permute-start | bytes 5505032 | tf_op jit(solution)/shard_map/ppermute | solution.py:98
  503.4 101.7 %reduce-scatter.15.cloned.1.call-start = ((), (), s32[]{:S(2)}) async-start(), calls=%async_computation.7 | async-start | bytes 2293760
  520.6 41.9 %collective-permute-start.66 = (bf16[2,128,1792]{2,1,0:T(8,128)(2,1)S(1)}, bf16[2,128,1792]{2,1,0:T(8,128)(2,1)S(1)}, u32[]{:S(2)}, u32[]{:S(2)}) collective-permute-start(bf16[2,128,1792]{2,1,0:T(8,128)(2,1)S(1)} %get-tuple-element.109), channel_id=1, source_target_pairs={{0,8},{4,12},{8,0},{12,4},{16,24},{20,28},{24,16},{28,20},{1,9},{5... | collective-permute-start | bytes 2752520 | tf_op jit(solution)/shard_map/ppermute | solution.py:98
  (110 other events, 1702.9 us)
Sparse Core Ops, SparseCore 0:
  83.5 40.2 reduce-scatter.10
  129.3 68.8 reduce-scatter.8
  503.5 35.8 reduce-scatter.12
  566.3 35.9 reduce-scatter.14

commit v5 on v4

--- a/solution.py
+++ b/solution.py
@@ -116,10 +116,15 @@
 def along_tensor(value):
     count, here = lax.axis_size("tensor"), lax.axis_index("tensor")
     blocks = jnp.zeros((count,) + value.shape, value.dtype)
-    for shift in range(count):
-        pairs = [(i, (i + shift) % count) for i in range(count)]
-        block = lax.ppermute(value, "tensor", pairs) if shift else value
-        blocks = lax.dynamic_update_index_in_dim(blocks, block, (here - shift) % count, 0)
+    blocks = lax.dynamic_update_index_in_dim(blocks, value, here, 0)
+    below, above = [value], [value]
+    for hop in range(1, count):
+        up = [(i, i + 1) for i in range(hop - 1, count - 1)]
+        below.append(lax.ppermute(below[-1], "tensor", up))
+        above.append(lax.ppermute(above[-1], "tensor", [(count - 1 - i, count - 1 - j) for i, j in up]))
+    for hop in range(1, count):
+        block = jnp.where(here >= hop, below[hop], above[count - hop])
+        blocks = lax.dynamic_update_index_in_dim(blocks, block, (here - hop) % count, 0)
     return blocks
 
 
@@ -130,12 +135,21 @@
     return lax.dynamic_index_in_dim(from_all(table), mine, axis=2, keepdims=False)
 
 
-def chip_groups(value):
-    half = value.shape[0] // 2
-    along_x, along_y = swap(value, 2), swap(value, 4)
-    diagonal = [swap(along_x[:half], 4), swap(along_y[half:], 2)]
-    groups = [[value], [along_x], [along_y], diagonal]
-    return [(group, [swap(piece, 1) for piece in group]) for group in groups]
+def neighbours(value):
+    return swap(value, 2), swap(value, 4)
+
+
+def diagonal(along_x, along_y):
+    half = along_x.shape[0] // 2
+    return [swap(along_x[:half], 4), swap(along_y[half:], 2)]
+
+
+def both_cores(group):
+    return group + [swap(piece, 1) for piece in group]
+
+
+def tie(*values):
+    return lax.optimization_barrier(values)
 
 
 def project_kernel(place_ref, attn_ref, *refs):
@@ -160,7 +174,7 @@
 
 def project_part(place, attn_out, groups):
     rows, depth = attn_out.shape
-    pieces = [piece for pair in groups for group in pair for piece in group]
+    pieces = [piece for group in groups for piece in group]
     columns = pieces[0].shape[0]
     return pl.pallas_call(
         project_kernel,
@@ -224,8 +238,9 @@
     hidden = gate / (1.0 + jnp.exp(-gate)) * up
     scaled = jnp.clip(hidden * scale_ref[1], -FP8_LIMIT, FP8_LIMIT)
     hidden_ref[...] = scaled.astype(hidden_ref.dtype)
-    peak = jnp.max(jnp.abs(hidden), axis=0, keepdims=True)
-    peak_ref[...] = jnp.broadcast_to(peak, peak_ref.shape)
+    peak = jnp.broadcast_to(jnp.max(jnp.abs(hidden)), peak_ref.shape)
+    first = pl.program_id(0) == 0
+    peak_ref[...] = jnp.where(first, peak, jnp.maximum(peak_ref[...], peak))
 
 
 def gate_up(scales, gains, chosen, pieces, w_gate, w_up):
@@ -244,10 +259,10 @@
         in_specs=[pl.BlockSpec(memory_space=pltpu.SMEM), whole(gains), whole(chosen)]
         + [whole(p) for p in pieces]
         + [weight(c) for c in range(parts) for _ in range(2)],
-        out_specs=[column(rows), column(8)],
+        out_specs=[column(rows), pl.BlockSpec((8, 128), lambda n: (0, 0))],
         out_shape=[
             jax.ShapeDtypeStruct((rows, hidden), jnp.bfloat16),
-            jax.ShapeDtypeStruct((8, hidden), jnp.float32),
+            jax.ShapeDtypeStruct((8, 128), jnp.float32),
         ],
         scratch_shapes=[pltpu.VMEM((parts, rows, step), jnp.bfloat16)],
         compiler_params=pltpu.CompilerParams(vmem_limit_bytes=VMEM_LIMIT),
@@ -304,6 +319,24 @@
     )(hidden_q, w_down, factor, spread)
 
 
+def natural_kernel(columns, *refs):
+    *parts, out_ref = refs
+    for j in range(parts[0].shape[1] // columns):
+        for c, part in enumerate(parts):
+            place = (j * len(parts) + c) * columns
+            out_ref[:, place : place + columns] = part[:, j * columns : (j + 1) * columns]
+
+
+def natural(parts, columns):
+    rows, step = parts[0].shape
+    return pl.pallas_call(
+        functools.partial(natural_kernel, columns),
+        out_shape=jax.ShapeDtypeStruct((rows, step * len(parts)), parts[0].dtype),
+        compiler_params=pltpu.CompilerParams(vmem_limit_bytes=VMEM_LIMIT),
+        name="natural",
+    )(*parts)
+
+
 def add(*terms):
     return sum(t.astype(jnp.float32) for t in terms).astype(jnp.bfloat16)
 
@@ -328,13 +361,26 @@
     half, step = layers // 2, width // CHUNKS
     columns = step // owners
 
-    weight_rows = out_weight.T.reshape(CHUNKS, columns, -1)
-    blocks = [chip_groups(weight_rows[c]) for c in range(CHUNKS)]
-    first = blocks[0][1][0][0]
-    first, expert_ids = lax.optimization_barrier((first, expert_ids))
-    blocks[0][1][0][0] = first
-    weight = expert_weights(expert_ids, route_weight, experts)
-    blocks[-1], weight = lax.optimization_barrier((blocks[-1], weight))
+    split = lambda value: value.reshape(-1, owners, CHUNKS, columns)
+    parts = lambda value, c: split(value)[:, :, c].reshape(-1, step)
+    place = lax.axis_index("dp")[None]
+
+    weight_rows = list(out_weight.T.reshape(CHUNKS, columns, -1))
+    stream, sent = [], []
+    for c in range(CHUNKS):
+        along_x, along_y = neighbours(weight_rows[c])
+        if c + 1 < CHUNKS:
+            along_x, along_y, weight_rows[c + 1] = tie(along_x, along_y, weight_rows[c + 1])
+        groups = [[weight_rows[c]], [along_x], [along_y], diagonal(along_x, along_y)]
+        terms = project_part(place, attn_out, [both_cores(group) for group in groups])
+        if c == 0:
+            terms, expert_ids = tie(terms, expert_ids)
+            weight = expert_weights(expert_ids, route_weight, experts)
+        else:
+            terms, sent[-1], weight = tie(terms, sent[-1], weight)
+        total = lax.psum_scatter(terms, "tensor", scatter_dimension=0, tiled=True)
+        stream.append(parts(residual, c).astype(jnp.float32) + total.astype(jnp.float32))
+        sent.append(stream[c].astype(jnp.bfloat16))
 
     named = weight > 0.0
     earlier = jnp.triu(jnp.ones((local_rows, local_rows), jnp.bfloat16), 1)
@@ -353,15 +399,6 @@
     spread = choice.transpose(0, 1, 3, 2)
     scales = jnp.stack([top_x / FP8_LIMIT, FP8_LIMIT / top_h])
 
-    split = lambda value: value.reshape(-1, owners, CHUNKS, columns)
-    parts = lambda value, c: split(value)[:, :, c].reshape(-1, step)
-    place = lax.axis_index("dp")[None]
-    stream, tokens = [], []
-    for c in range(CHUNKS):
-        terms = project_part(place, attn_out, blocks[c])
-        total = lax.psum_scatter(terms, "tensor", scatter_dimension=0, tiled=True)
-        stream.append(parts(residual, c).astype(jnp.float32) + total.astype(jnp.float32))
-        tokens.append(chip_groups(along_tensor(stream[c].astype(jnp.bfloat16))))
     squares = sum(jnp.sum(part * part, axis=1) for part in stream)
     root = lax.rsqrt(squares / width + 1e-06)
     gains = [parts(norm_gain, c) for c in range(CHUNKS)]
@@ -372,26 +409,51 @@
 
     gate_rows = w_gate.reshape(1, owners, CHUNKS, columns, -1)
     up_rows = w_up.reshape(1, owners, CHUNKS, columns, -1)
-    hidden = []
-    for r in range(4):
-        pieces = [piece for part in tokens for side in part[r] for piece in side]
-        hidden.append(gate_up(scales, gains, choice[r], pieces, gate_rows, up_rows))
-    peak_h = jnp.max(jnp.stack([jnp.max(peaks) for _, peaks in hidden]))
-
+
+    def hidden_of(r, tokens):
+        pieces = [piece for part in tokens for piece in part]
+        return gate_up(scales, gains, choice[r], pieces, gate_rows, up_rows)
+
+    groups = [[] for _ in range(4)]
+    own = along_tensor(sent[0])
+    for c in range(CHUNKS):
+        along_x, along_y = neighbours(own)
+        groups[0].append(both_cores([own]))
+        if c + 1 < CHUNKS:
+            own = along_tensor(sent[c + 1])
+            along_x, along_y, own = tie(along_x, along_y, own)
+        else:
+            hidden = [hidden_of(0, groups[0])]
+            stream = natural(stream, columns)
+            along_x, along_y, hidden[0], stream = tie(along_x, along_y, hidden[0], stream)
+        groups[1].append(both_cores([along_x]))
+        groups[2].append(both_cores([along_y]))
+        across = diagonal(along_x, along_y)
+        if c + 1 == CHUNKS:
+            hidden += [hidden_of(1, groups[1]), hidden_of(2, groups[2])]
+            across, hidden = tie(across, hidden)
+        groups[3].append(both_cores(across))
+
+    def outputs(r, c):
+        kept, given = down(hidden[r][0], w_down, factor[r], spread[r], c, step)
+        taken = swap(given, 1)
+        return [(kept[:half], taken[:half]), (kept[half:], taken[half:])]
+
+    summed = lambda r, c: [add(*terms) for terms in outputs(r, c)]
+    to_x, to_y = summed(1, 0), summed(2, 0)
+    groups[3], to_x, to_y = tie(groups[3], to_x, to_y)
+    hidden.append(hidden_of(3, groups[3]))
+    peak_h = jnp.max(jnp.stack([peaks for _, peaks in hidden]))
     mixture = []
     for c in range(CHUNKS):
-        to = []
-        for r in range(4):
-            kept, given = down(hidden[r][0], w_down, factor[r], spread[r], c, step)
-            taken = swap(given, 1)
-            to.append([add(kept[:half], taken[:half]), add(kept[half:], taken[half:])])
-        over_x, over_y = swap(to[3][0], 2), swap(to[3][1], 4)
-        low = add(to[0][0], swap(to[1][0], 2), swap(add(to[2][0], over_x), 4))
-        high = add(to[0][1], swap(add(to[1][1], over_y), 2), swap(to[2][1], 4))
+        if c > 0:
+            to_x, to_y = summed(1, c), summed(2, c)
+        beyond, to_own = summed(3, c), outputs(0, c)
+        over_x, over_y = swap(beyond[0], 2), swap(beyond[1], 4)
+        low = add(*to_own[0], swap(to_x[0], 2), swap(add(to_y[0], over_x), 4))
+        high = add(*to_own[1], swap(add(to_x[1], over_y), 2), swap(to_y[1], 4))
         mixed = jnp.concatenate([low, high]).reshape(layers * local_rows, step)
         mixture.append(lax.psum_scatter(mixed, "tensor", scatter_dimension=0, tiled=True))
-    stream = jnp.stack([s.reshape(local_rows, owners, columns) for s in stream], axis=2)
-    stream = stream.reshape(local_rows, width)
     layer_out = stream + jnp.concatenate(mixture, axis=1).astype(jnp.float32)
     return layer_out.astype(jnp.bfloat16), peak_x, peak_h
 

time: 626 us -> 625 us (level)
  other arithmetic: 42.1 us -> 56.3 us
  waiting for transfers between devices: 328 us -> 317 us
    reduce_scatter x2, waiting for transfers between devices: 56.6 us -> 0.02 us  [gather_plan(): total = lax.psum_scatter(terms, 'tensor', scatter_dimension=0, tiled=True)]
    ppermute x6 -> x12, waiting for transfers between devices: 20.3 us -> 71.7 us  [the longest x6 71.7 us: along_tensor(): lax.ppermute(above[-1], 'tensor', [(count - 1 - i, count - 1 - j) for i,...]
    ppermute x59, starting transfers between devices: 42.8 us -> 34.4 us  [swap(): return lax.ppermute(value, 'dp', [(i, i ^ bits) for i in range(count)])]
    dynamic_update_slice x2 -> x7, other arithmetic: 1.06 us -> 9.26 us  [the longest x6 8.43 us: along_tensor(): lax.dynamic_update_index_in_dim(blocks, block, (here - hop) % count, 0)]
    ppermute x59, waiting for transfers between devices: 227 us -> 220 us  [swap(): return lax.ppermute(value, 'dp', [(i, i ^ bits) for i in range(count)])]
    convert_element_type x8 -> x10, other arithmetic: 21.5 us -> 26.2 us  [add(): return sum((t.astype(jnp.float32) for t in terms)).astype(jnp.bfloat16)]
    slice x11 -> x10, local copies, waits for them, and re-layouts: 13.8 us -> 11.2 us  [the longest x8 9.86 us: diagonal(): return [swap(along_x[:half], 4), swap(along_y[half:], 2)]]
    unnamed x118 -> x115, local copies, waits for them, and re-layouts: 14.8 us -> 13.6 us
  transfers between devices with their start and end apart: 77 -> 83, of which waited for: 34 -> 36; matrix products, arithmetic and copies ran while one was open for 11% -> 12% of each run, Pallas kernels for 17% -> 13%
where the time goes in v5:
time: 625 us; the launch traced here: 615 us
  waiting for transfers between devices  317 us (51%)
  Pallas kernels  117 us (19%)
  starting transfers between devices  63.1 us (10%)
  other arithmetic  56.3 us (9%)
  local copies, waits for them, and re-layouts  40.5 us (6%)
  between operations  21.4 us (3%)
    ppermute x59, waiting for transfers between devices, swap(): return lax.ppermute(value, 'dp', [(i, i ^ bits) for i in range(count)])  220 us
    ppermute x6, waiting for transfers between devices, along_tensor(): lax.ppermute(above[-1], 'tensor', [(count - 1 - i, count - 1 - j) for i,...  71.7 us
    pallas_call x4, Pallas kernels, gate_up(): pl.pallas_call(functools.partial(gate_up_kernel, parts), grid=(hidden //...  54.8 us
    pallas_call x8, Pallas kernels, down(): pl.pallas_call(down_kernel, grid=(tiles,), in_specs=[whole(hidden_q.shape...  43.5 us
    ppermute x59, starting transfers between devices, swap(): return lax.ppermute(value, 'dp', [(i, i ^ bits) for i in range(count)])  34.4 us
    convert_element_type x10, other arithmetic, add(): return sum((t.astype(jnp.float32) for t in terms)).astype(jnp.bfloat16)  26.2 us
    pallas_call x2, Pallas kernels, project_part(): pl.pallas_call(project_kernel, in_specs=[pl.BlockSpec(memory_space=pltpu....  18.6 us
    ppermute x5, waiting for transfers between devices, peaks_over_all(): peaks = jnp.maximum(peaks, lax.ppermute(peaks, axis, pairs))  18.4 us
  transfers between devices with their start and end apart: 83, of which 36 were waited for; matrix products, arithmetic and copies ran while one was open for 12% of the time, Pallas kernels for 13%

profile of v5, /device:TPU:0, one launch (start us, length us, event | category | flops | bytes accessed | tf_op | source)
XLA Modules:
  0.0 615.4 jit_solution(6707871048942744189)
XLA Ops:
  13.4 18.8 %collective-permute-done.refs_2_ = bf16[224,2048]{1,0:T(8,128)(2,1)S(1)} collective-permute-done((bf16[224,2048]{1,0:T(8,128)(2,1)S(1)}, bf16[224,2048]{1,0:T(8,128)(2,1)S(1)}, u32[]{:S(2)}, u32[]{:S(2)}) %collective-permute-start) | collective-permute-done | bytes 917536 | tf_op jit(solution)/shard_map/ppermute | solution.py:98
  37.6 7.4 %collective-permute-done.14.refs_6_ = bf16[112,2048]{1,0:T(8,128)(2,1)S(1)} collective-permute-done((bf16[112,2048]{1,0:T(8,128)(2,1)S(1)}, bf16[112,2048]{1,0:T(8,128)(2,1)S(1)}, u32[]{:S(2)}, u32[]{:S(2)}) %collective-permute-start.14) | collective-permute-done | bytes 458784 | tf_op jit(solution)/shard_map/ppermute | solution.py:98
  49.6 9.4 %project.3 = bf16[512,1792]{1,0:T(8,128)(2,1)} custom-call(s32[1]{0:T(128)} %bitcast.place_ref, bf16[512,2048]{1,0:T(8,128)(2,1)} %attn_ref.3, bf16[224,2048]{1,0:T(8,128)(2,1)S(1)} %get-tuple-element.150.refs_0_, bf16[224,2048]{1,0:T(8,128)(2,1)} %collective-permute-done.11.refs_1_, bf16[224,2048]{1,0:T(8,128)(2,1)S(1)} %collective-permute-done.refs_2_, ...), custom_call_target="tpu_custom_call" | custom-call | flops 3758096384 | bytes 9437184 | tf_op jit(solution)/shard_map/project/pallas_call | solution.py:179
  65.9 15.6 %collective-permute-done.5.refs_4_ = bf16[224,2048]{1,0:T(8,128)(2,1)S(1)} collective-permute-done((bf16[224,2048]{1,0:T(8,128)(2,1)S(1)}, bf16[224,2048]{1,0:T(8,128)(2,1)S(1)}, u32[]{:S(2)}, u32[]{:S(2)}) %collective-permute-start.5) | collective-permute-done | bytes 917536 | tf_op jit(solution)/shard_map/ppermute | solution.py:98
  88.3 9.0 %collective-permute-done.22 = f32[2,4,32,128]{3,2,1,0:T(8,128)S(1)} collective-permute-done((f32[2,4,32,128]{3,2,1,0:T(8,128)S(1)}, f32[2,4,32,128]{3,2,1,0:T(8,128)S(1)}, u32[]{:S(2)}, u32[]{:S(2)}) %collective-permute-start.22) | collective-permute-done | bytes 131104 | tf_op jit(solution)/shard_map/ppermute | solution.py:98
  111.5 9.2 %project.2 = bf16[512,1792]{1,0:T(8,128)(2,1)} custom-call(s32[1]{0:T(128)} %bitcast.place_ref, bf16[512,2048]{1,0:T(8,128)(2,1)} %attn_ref.3, bf16[224,2048]{1,0:T(8,128)(2,1)S(1)} %get-tuple-element.63.refs_0_, bf16[224,2048]{1,0:T(8,128)(2,1)S(1)} %collective-permute-done.2.refs_1_, bf16[224,2048]{1,0:T(8,128)(2,1)S(1)} %collective-permute-done.3.refs_2_, ...), custom_call_target="tpu_custom_call" | custom-call | flops 3758096384 | bytes 9437184 | tf_op jit(solution)/shard_map/project/pallas_call | solution.py:179
  129.9 21.5 %collective-permute-done.25 = bf16[128,1792]{1,0:T(8,128)(2,1)} collective-permute-done((bf16[128,1792]{1,0:T(8,128)(2,1)S(1)}, bf16[128,1792]{1,0:T(8,128)(2,1)}, u32[]{:S(2)}, u32[]{:S(2)}) %collective-permute-start.25) | collective-permute-done | bytes 458784 | tf_op jit(solution)/shard_map/ppermute | solution.py:124
  156.3 20.8 %collective-permute-done.26 = bf16[128,1792]{1,0:T(8,128)(2,1)} collective-permute-done((bf16[128,1792]{1,0:T(8,128)(2,1)}, bf16[128,1792]{1,0:T(8,128)(2,1)}, u32[]{:S(2)}, u32[]{:S(2)}) %collective-permute-start.26) | collective-permute-done | bytes 458784 | tf_op jit(solution)/shard_map/ppermute | solution.py:124
  184.7 8.1 %collective-permute-done.27 = bf16[128,1792]{1,0:T(8,128)(2,1)} collective-permute-done((bf16[128,1792]{1,0:T(8,128)(2,1)}, bf16[128,1792]{1,0:T(8,128)(2,1)}, u32[]{:S(2)}, u32[]{:S(2)}) %collective-permute-start.27) | collective-permute-done | bytes 458784 | tf_op jit(solution)/shard_map/ppermute | solution.py:124
  205.0 9.2 %collective-permute-done.34 = bf16[128,1792]{1,0:T(8,128)(2,1)S(1)} collective-permute-done((bf16[128,1792]{1,0:T(8,128)(2,1)S(1)}, bf16[128,1792]{1,0:T(8,128)(2,1)S(1)}, u32[]{:S(2)}, u32[]{:S(2)}) %collective-permute-start.34) | collective-permute-done | bytes 458784 | tf_op jit(solution)/shard_map/ppermute | solution.py:124
  219.2 7.2 %collective-permute-done.35 = bf16[128,1792]{1,0:T(8,128)(2,1)S(1)} collective-permute-done((bf16[128,1792]{1,0:T(8,128)(2,1)S(1)}, bf16[128,1792]{1,0:T(8,128)(2,1)S(1)}, u32[]{:S(2)}, u32[]{:S(2)}) %collective-permute-start.35) | collective-permute-done | bytes 458784 | tf_op jit(solution)/shard_map/ppermute | solution.py:124
  229.0 28.5 %collective-permute-done.30.refs_0_ = bf16[4,128,1792]{2,1,0:T(8,128)(2,1)} collective-permute-done((bf16[4,128,1792]{2,1,0:T(8,128)(2,1)}, bf16[4,128,1792]{2,1,0:T(8,128)(2,1)}, u32[]{:S(2)}, u32[]{:S(2)}) %collective-permute-start.30) | collective-permute-done | bytes 1835040 | tf_op jit(solution)/shard_map/ppermute | solution.py:98
  266.5 13.9 %gate_up.4 = (bf16[384,1024]{1,0:T(8,128)(2,1)S(1)}, f32[8,128]{1,0:T(8,128)S(1)}) custom-call(f32[2]{0:T(128)S(1)} %pad_maximum_fusion.5.scale_ref, f32[2,1,1792]{2,1,0:T(1,128)S(1)} %maximum_multiply_fusion.gain_ref, bf16[8,48,128]{2,1,0:T(8,128)(2,1)S(1)} %bitcast.65, bf16[4,128,1792]{2,1,0:T(8,128)(2,1)} %bitcast_dynamic-update-slice_fusion.4.refs_0_, ...), custom_call_target="tpu_custom_call" | custom-call | flops 5989466112 | bytes 22020096 | tf_op jit(solution)/shard_map/gate_up/pallas_call | solution.py:256
  280.4 20.4 %collective-permute-done.38.refs_2_ = bf16[4,128,1792]{2,1,0:T(8,128)(2,1)} collective-permute-done((bf16[4,128,1792]{2,1,0:T(8,128)(2,1)}, bf16[4,128,1792]{2,1,0:T(8,128)(2,1)}, u32[]{:S(2)}, u32[]{:S(2)}) %collective-permute-start.38) | collective-permute-done | bytes 1835040 | tf_op jit(solution)/shard_map/ppermute | solution.py:98
  310.8 13.9 %gate_up.6 = (bf16[384,1024]{1,0:T(8,128)(2,1)S(1)}, f32[8,128]{1,0:T(8,128)S(1)}) custom-call(f32[2]{0:T(128)S(1)} %pad_maximum_fusion.5.scale_ref, f32[2,1,1792]{2,1,0:T(1,128)S(1)} %maximum_multiply_fusion.gain_ref, bf16[8,48,128]{2,1,0:T(8,128)(2,1)S(1)} %bitcast.64, bf16[4,128,1792]{2,1,0:T(8,128)(2,1)} %collective-permute-done.31.refs_0_, ...), custom_call_target="tpu_custom_call" | custom-call | flops 5989466112 | bytes 22020096 | tf_op jit(solution)/shard_map/gate_up/pallas_call | solution.py:256
  324.7 13.9 %gate_up.5 = (bf16[384,1024]{1,0:T(8,128)(2,1)S(1)}, f32[8,128]{1,0:T(8,128)S(1)}) custom-call(f32[2]{0:T(128)S(1)} %pad_maximum_fusion.5.scale_ref, f32[2,1,1792]{2,1,0:T(1,128)S(1)} %maximum_multiply_fusion.gain_ref, bf16[8,48,128]{2,1,0:T(8,128)(2,1)S(1)} %bitcast.63, bf16[4,128,1792]{2,1,0:T(8,128)(2,1)} %collective-permute-done.30.refs_0_, ...), custom_call_target="tpu_custom_call" | custom-call | flops 5989466112 | bytes 22020096 | tf_op jit(solution)/shard_map/gate_up/pallas_call | solution.py:256
  364.7 17.1 %collective-permute-done.49.refs_0_ = bf16[2,128,1792]{2,1,0:T(8,128)(2,1)} collective-permute-done((bf16[2,128,1792]{2,1,0:T(8,128)(2,1)}, bf16[2,128,1792]{2,1,0:T(8,128)(2,1)}, u32[]{:S(2)}, u32[]{:S(2)}) %collective-permute-start.49) | collective-permute-done | bytes 917536 | tf_op jit(solution)/shard_map/ppermute | solution.py:98
  394.3 13.1 %gate_up.7 = (bf16[384,1024]{1,0:T(8,128)(2,1)S(1)}, f32[8,128]{1,0:T(8,128)S(1)}) custom-call(f32[2]{0:T(128)S(1)} %pad_maximum_fusion.5.scale_ref, f32[2,1,1792]{2,1,0:T(1,128)S(1)} %maximum_multiply_fusion.gain_ref, bf16[8,48,128]{2,1,0:T(8,128)(2,1)S(1)} %bitcast.62, bf16[2,128,1792]{2,1,0:T(8,128)(2,1)} %collective-permute-done.49.refs_0_, ...), custom_call_target="tpu_custom_call" | custom-call | flops 5989466112 | bytes 22020096 | tf_op jit(solution)/shard_map/gate_up/pallas_call | solution.py:256
  435.1 10.3 %collective-permute-done.61 = bf16[2,128,1792]{2,1,0:T(8,128)(2,1)} collective-permute-done((bf16[2,128,1792]{2,1,0:T(8,128)(2,1)}, bf16[2,128,1792]{2,1,0:T(8,128)(2,1)}, u32[]{:S(2)}, u32[]{:S(2)}) %collective-permute-start.61) | collective-permute-done | bytes 917536 | tf_op jit(solution)/shard_map/ppermute | solution.py:98
  448.1 8.4 %collective-permute-done.59 = bf16[2,128,1792]{2,1,0:T(8,128)(2,1)S(1)} collective-permute-done((bf16[2,128,1792]{2,1,0:T(8,128)(2,1)}, bf16[2,128,1792]{2,1,0:T(8,128)(2,1)S(1)}, u32[]{:S(2)}, u32[]{:S(2)}) %collective-permute-start.59) | collective-permute-done | bytes 917536 | tf_op jit(solution)/shard_map/ppermute | solution.py:98
  479.2 15.9 %collective-permute-done.62 = bf16[2,128,1792]{2,1,0:T(8,128)(2,1)S(1)} collective-permute-done((bf16[2,128,1792]{2,1,0:T(8,128)(2,1)}, bf16[2,128,1792]{2,1,0:T(8,128)(2,1)S(1)}, u32[]{:S(2)}, u32[]{:S(2)}) %collective-permute-start.62) | collective-permute-done | bytes 917536 | tf_op jit(solution)/shard_map/ppermute | solution.py:98
  511.4 11.4 %collective-permute-done.69 = bf16[2,128,1792]{2,1,0:T(8,128)(2,1)S(1)} collective-permute-done((bf16[2,128,1792]{2,1,0:T(8,128)(2,1)}, bf16[2,128,1792]{2,1,0:T(8,128)(2,1)S(1)}, u32[]{:S(2)}, u32[]{:S(2)}) %collective-permute-start.69) | collective-permute-done | bytes 917536 | tf_op jit(solution)/shard_map/ppermute | solution.py:98
  526.9 15.5 %collective-permute-done.66 = bf16[2,128,1792]{2,1,0:T(8,128)(2,1)S(1)} collective-permute-done((bf16[2,128,1792]{2,1,0:T(8,128)(2,1)S(1)}, bf16[2,128,1792]{2,1,0:T(8,128)(2,1)S(1)}, u32[]{:S(2)}, u32[]{:S(2)}) %collective-permute-start.66) | collective-permute-done | bytes 917536 | tf_op jit(solution)/shard_map/ppermute | solution.py:98
  542.4 18.1 %collective-permute-done.72 = bf16[2,128,1792]{2,1,0:T(8,128)(2,1)S(1)} collective-permute-done((bf16[2,128,1792]{2,1,0:T(8,128)(2,1)S(1)}, bf16[2,128,1792]{2,1,0:T(8,128)(2,1)S(1)}, u32[]{:S(2)}, u32[]{:S(2)}) %collective-permute-start.72) | collective-permute-done | bytes 917536 | tf_op jit(solution)/shard_map/ppermute | solution.py:98
  (362 shorter events, 257.6 us)
Async XLA Ops:
  7.2 113.5 %reduce-scatter.5.cloned.1.call-start = ((), (), s32[]{:S(2)}) async-start(), calls=%async_computation.4 | async-start | bytes 2293760 | tf_op jit(solution)/shard_map/reduce_scatter | solution.py:381
  13.4 34.0 %collective-permute-start.11 = (bf16[224,2048]{1,0:T(8,128)(2,1)S(1)}, bf16[224,2048]{1,0:T(8,128)(2,1)}, u32[]{:S(2)}, u32[]{:S(2)}) collective-permute-start(bf16[224,2048]{1,0:T(8,128)(2,1)S(1)} %get-tuple-element.150.refs_0_), channel_id=1, source_target_pairs={{0,4},{4,0},{8,12},{12,8},{16,20},{20,16},{24,28},{28,24},{1,5},{5... | collective-permute-start | bytes 2752520 | tf_op jit(solution)/shard_map/ppermute | solution.py:98
  59.0 120.4 %reduce-scatter.7.cloned.1.call-start = ((), (), s32[]{:S(2)}) async-start(), calls=%async_computation.5 | async-start | bytes 2293760 | tf_op jit(solution)/shard_map/reduce_scatter | solution.py:381
  122.7 477.3 %reduce-scatter.9.cloned.1.call-start = ((), (), s32[]{:S(2)}) async-start(), calls=%async_computation.6 | async-start | bytes 2293760 | tf_op jit(solution)/shard_map/reduce_scatter | solution.py:456
  178.4 37.1 %collective-permute-start.29 = (bf16[128,1792]{1,0:T(8,128)(2,1)}, bf16[128,1792]{1,0:T(8,128)(2,1)S(1)}, u32[]{:S(2)}, u32[]{:S(2)}) collective-permute-start(bf16[128,1792]{1,0:T(8,128)(2,1)} %collective-permute-done.28), channel_id=1, source_target_pairs={{2,3},{6,7},{10,11},{14,15},{18,19},{22,23},{26,27},{30,31}} | collective-permute-start | bytes 1376264 | tf_op jit(solution)/shard_map/ppermute | solution.py:123
  217.4 40.1 %collective-permute-start.30 = (bf16[4,128,1792]{2,1,0:T(8,128)(2,1)}, bf16[4,128,1792]{2,1,0:T(8,128)(2,1)}, u32[]{:S(2)}, u32[]{:S(2)}) collective-permute-start(bf16[4,128,1792]{2,1,0:T(8,128)(2,1)} %bitcast_dynamic-update-slice_fusion.4.refs_0_), channel_id=1, source_target_pairs={{0,8},{4,12},{8,0},{12,4},{16,24},{20,28},{24,16},{28,20},{1,9},{5... | collective-permute-start | bytes 5505032 | tf_op jit(solution)/shard_map/ppermute | solution.py:98
  218.0 39.8 %collective-permute-start.31 = (bf16[4,128,1792]{2,1,0:T(8,128)(2,1)}, bf16[4,128,1792]{2,1,0:T(8,128)(2,1)}, u32[]{:S(2)}, u32[]{:S(2)}) collective-permute-start(bf16[4,128,1792]{2,1,0:T(8,128)(2,1)} %bitcast_dynamic-update-slice_fusion.4.refs_0_), channel_id=1, source_target_pairs={{0,16},{4,20},{8,24},{12,28},{16,0},{20,4},{24,8},{28,12},{1,17},{... | collective-permute-start | bytes 5505032 | tf_op jit(solution)/shard_map/ppermute | solution.py:98
  218.5 48.0 %collective-permute-start.40 = (bf16[4,128,1792]{2,1,0:T(8,128)(2,1)}, bf16[4,128,1792]{2,1,0:T(8,128)(2,1)}, u32[]{:S(2)}, u32[]{:S(2)}) collective-permute-start(bf16[4,128,1792]{2,1,0:T(8,128)(2,1)} %bitcast_dynamic-update-slice_fusion.4.refs_0_), channel_id=1, source_target_pairs={{0,4},{4,0},{8,12},{12,8},{16,20},{20,16},{24,28},{28,24},{1,5},{5... | collective-permute-start | bytes 5505032 | tf_op jit(solution)/shard_map/ppermute | solution.py:98
  258.0 42.8 %collective-permute-start.38 = (bf16[4,128,1792]{2,1,0:T(8,128)(2,1)}, bf16[4,128,1792]{2,1,0:T(8,128)(2,1)}, u32[]{:S(2)}, u32[]{:S(2)}) collective-permute-start(bf16[4,128,1792]{2,1,0:T(8,128)(2,1)} %bitcast_dynamic-update-slice_fusion.refs_2_), channel_id=1, source_target_pairs={{0,8},{4,12},{8,0},{12,4},{16,24},{20,28},{24,16},{28,20},{1,9},{5... | collective-permute-start | bytes 5505032 | tf_op jit(solution)/shard_map/ppermute | solution.py:98
  259.4 42.5 %collective-permute-start.39 = (bf16[4,128,1792]{2,1,0:T(8,128)(2,1)}, bf16[4,128,1792]{2,1,0:T(8,128)(2,1)}, u32[]{:S(2)}, u32[]{:S(2)}) collective-permute-start(bf16[4,128,1792]{2,1,0:T(8,128)(2,1)} %bitcast_dynamic-update-slice_fusion.refs_2_), channel_id=1, source_target_pairs={{0,16},{4,20},{8,24},{12,28},{16,0},{20,4},{24,8},{28,12},{1,17},{... | collective-permute-start | bytes 5505032 | tf_op jit(solution)/shard_map/ppermute | solution.py:98
  266.5 43.8 %collective-permute-start.46 = (bf16[4,128,1792]{2,1,0:T(8,128)(2,1)}, bf16[4,128,1792]{2,1,0:T(8,128)(2,1)}, u32[]{:S(2)}, u32[]{:S(2)}) collective-permute-start(bf16[4,128,1792]{2,1,0:T(8,128)(2,1)} %collective-permute-done.31.refs_0_), channel_id=1, source_target_pairs={{0,4},{4,0},{8,12},{12,8},{16,20},{20,16},{24,28},{28,24},{1,5},{5... | collective-permute-start | bytes 5505032 | tf_op jit(solution)/shard_map/ppermute | solution.py:98
  346.3 39.5 %collective-permute-start.56 = (bf16[4,128,1792]{2,1,0:T(8,128)(2,1)}, bf16[4,128,1792]{2,1,0:T(8,128)(2,1)}, u32[]{:S(2)}, u32[]{:S(2)}) collective-permute-start(bf16[4,128,1792]{2,1,0:T(8,128)(2,1)} %get-tuple-element.95), channel_id=1, source_target_pairs={{0,4},{4,0},{8,12},{12,8},{16,20},{20,16},{24,28},{28,24},{1,5},{5... | collective-permute-start | bytes 5505032 | tf_op jit(solution)/shard_map/ppermute | solution.py:98
  355.8 33.9 %collective-permute-start.55 = (bf16[4,128,1792]{2,1,0:T(8,128)(2,1)}, bf16[4,128,1792]{2,1,0:T(8,128)(2,1)}, u32[]{:S(2)}, u32[]{:S(2)}) collective-permute-start(bf16[4,128,1792]{2,1,0:T(8,128)(2,1)} %get-tuple-element.92), channel_id=1, source_target_pairs={{0,4},{4,0},{8,12},{12,8},{16,20},{20,16},{24,28},{28,24},{1,5},{5... | collective-permute-start | bytes 5505032 | tf_op jit(solution)/shard_map/ppermute | solution.py:98
  432.7 42.0 %collective-permute-start.68 = (bf16[4,128,1792]{2,1,0:T(8,128)(2,1)S(1)}, bf16[4,128,1792]{2,1,0:T(8,128)(2,1)}, u32[]{:S(2)}, u32[]{:S(2)}) collective-permute-start(bf16[4,128,1792]{2,1,0:T(8,128)(2,1)S(1)} %get-tuple-element.118), channel_id=1, source_target_pairs={{0,4},{4,0},{8,12},{12,8},{16,20},{20,16},{24,28},{28,24},{1,5},{5... | collective-permute-start | bytes 5505032 | tf_op jit(solution)/shard_map/ppermute | solution.py:98
  434.7 43.9 %collective-permute-start.57 = (bf16[2,128,1792]{2,1,0:T(8,128)(2,1)}, bf16[2,128,1792]{2,1,0:T(8,128)(2,1)}, u32[]{:S(2)}, u32[]{:S(2)}) collective-permute-start(bf16[2,128,1792]{2,1,0:T(8,128)(2,1)} %get-tuple-element.96), channel_id=1, source_target_pairs={{0,8},{4,12},{8,0},{12,4},{16,24},{20,28},{24,16},{28,20},{1,9},{5... | collective-permute-start | bytes 2752520 | tf_op jit(solution)/shard_map/ppermute | solution.py:98
  445.4 33.1 %collective-permute-start.63 = (bf16[2,128,1792]{2,1,0:T(8,128)(2,1)}, bf16[2,128,1792]{2,1,0:T(8,128)(2,1)}, u32[]{:S(2)}, u32[]{:S(2)}) collective-permute-start(bf16[2,128,1792]{2,1,0:T(8,128)(2,1)} %get-tuple-element.110), channel_id=1, source_target_pairs={{0,16},{4,20},{8,24},{12,28},{16,0},{20,4},{24,8},{28,12},{1,17},{... | collective-permute-start | bytes 2752520 | tf_op jit(solution)/shard_map/ppermute | solution.py:98
  456.5 38.5 %collective-permute-start.62 = (bf16[2,128,1792]{2,1,0:T(8,128)(2,1)}, bf16[2,128,1792]{2,1,0:T(8,128)(2,1)S(1)}, u32[]{:S(2)}, u32[]{:S(2)}) collective-permute-start(bf16[2,128,1792]{2,1,0:T(8,128)(2,1)} %add_convert_fusion.12), channel_id=1, source_target_pairs={{0,8},{4,12},{8,0},{12,4},{16,24},{20,28},{24,16},{28,20},{1,9},{5... | collective-permute-start | bytes 2752520 | tf_op jit(solution)/shard_map/ppermute | solution.py:98
  460.6 34.5 %collective-permute-start.60 = (bf16[2,128,1792]{2,1,0:T(8,128)(2,1)}, bf16[2,128,1792]{2,1,0:T(8,128)(2,1)}, u32[]{:S(2)}, u32[]{:S(2)}) collective-permute-start(bf16[2,128,1792]{2,1,0:T(8,128)(2,1)} %add_convert_fusion.15), channel_id=1, source_target_pairs={{0,16},{4,20},{8,24},{12,28},{16,0},{20,4},{24,8},{28,12},{1,17},{... | collective-permute-start | bytes 2752520 | tf_op jit(solution)/shard_map/ppermute | solution.py:98
  478.5 32.9 %collective-permute-start.67 = (bf16[4,128,1792]{2,1,0:T(8,128)(2,1)}, bf16[4,128,1792]{2,1,0:T(8,128)(2,1)}, u32[]{:S(2)}, u32[]{:S(2)}) collective-permute-start(bf16[4,128,1792]{2,1,0:T(8,128)(2,1)} %get-tuple-element.116), channel_id=1, source_target_pairs={{0,4},{4,0},{8,12},{12,8},{16,20},{20,16},{24,28},{28,24},{1,5},{5... | collective-permute-start | bytes 5505032 | tf_op jit(solution)/shard_map/ppermute | solution.py:98
  499.2 106.7 %reduce-scatter.11.cloned.1.call-start = ((), (), s32[]{:S(2)}) async-start(), calls=%async_computation.7 | async-start | bytes 2293760 | tf_op jit(solution)/shard_map/reduce_scatter | solution.py:456
  509.3 33.1 %collective-permute-start.66 = (bf16[2,128,1792]{2,1,0:T(8,128)(2,1)S(1)}, bf16[2,128,1792]{2,1,0:T(8,128)(2,1)S(1)}, u32[]{:S(2)}, u32[]{:S(2)}) collective-permute-start(bf16[2,128,1792]{2,1,0:T(8,128)(2,1)S(1)} %get-tuple-element.139), channel_id=1, source_target_pairs={{0,8},{4,12},{8,0},{12,4},{16,24},{20,28},{24,16},{28,20},{1,9},{5... | collective-permute-start | bytes 2752520 | tf_op jit(solution)/shard_map/ppermute | solution.py:98
  510.8 49.7 %collective-permute-start.72 = (bf16[2,128,1792]{2,1,0:T(8,128)(2,1)S(1)}, bf16[2,128,1792]{2,1,0:T(8,128)(2,1)S(1)}, u32[]{:S(2)}, u32[]{:S(2)}) collective-permute-start(bf16[2,128,1792]{2,1,0:T(8,128)(2,1)S(1)} %get-tuple-element.140), channel_id=1, source_target_pairs={{0,8},{4,12},{8,0},{12,4},{16,24},{20,28},{24,16},{28,20},{1,9},{5... | collective-permute-start | bytes 2752520 | tf_op jit(solution)/shard_map/ppermute | solution.py:98
  524.8 35.7 %collective-permute-start.70 = (bf16[2,128,1792]{2,1,0:T(8,128)(2,1)S(1)}, bf16[2,128,1792]{2,1,0:T(8,128)(2,1)S(1)}, u32[]{:S(2)}, u32[]{:S(2)}) collective-permute-start(bf16[2,128,1792]{2,1,0:T(8,128)(2,1)S(1)} %get-tuple-element.141), channel_id=1, source_target_pairs={{0,16},{4,20},{8,24},{12,28},{16,0},{20,4},{24,8},{28,12},{1,17},{... | collective-permute-start | bytes 2752520 | tf_op jit(solution)/shard_map/ppermute | solution.py:98
  526.6 37.3 %collective-permute-start.73 = (bf16[2,128,1792]{2,1,0:T(8,128)(2,1)S(1)}, bf16[2,128,1792]{2,1,0:T(8,128)(2,1)S(1)}, u32[]{:S(2)}, u32[]{:S(2)}) collective-permute-start(bf16[2,128,1792]{2,1,0:T(8,128)(2,1)S(1)} %get-tuple-element.142), channel_id=1, source_target_pairs={{0,16},{4,20},{8,24},{12,28},{16,0},{20,4},{24,8},{28,12},{1,17},{... | collective-permute-start | bytes 2752520 | tf_op jit(solution)/shard_map/ppermute | solution.py:98
  (116 other events, 1473.6 us)
Sparse Core Ops, SparseCore 0:
  59.2 38.8 reduce-scatter.4
  122.9 49.8 reduce-scatter.6
  499.3 39.4 reduce-scatter.8
  566.3 39.5 reduce-scatter.10

commit v6 on v5

--- a/solution.py
+++ b/solution.py
@@ -11,6 +11,7 @@
 AXES = ("dp", "tensor")
 CHUNKS = 2
 VMEM_LIMIT = 48 * 2**20
+COST_SHARE = 16
 
 
 def project(attn_out, out_weight):
@@ -93,24 +94,15 @@
     return (stream + mixture).astype(jnp.bfloat16), *peaks
 
 
+def cost(flops, bytes_accessed):
+    return pl.CostEstimate(
+        flops=flops // COST_SHARE, bytes_accessed=bytes_accessed // COST_SHARE, transcendentals=0
+    )
+
+
 def swap(value, bits):
     count = lax.axis_size("dp")
     return lax.ppermute(value, "dp", [(i, i ^ bits) for i in range(count)])
-
-
-def from_all(value):
-    count = lax.axis_size("tensor")
-    parts = [value]
-    for shift in range(1, count):
-        pairs = [(i, (i + shift) % count) for i in range(count)]
-        parts.append(lax.ppermute(value, "tensor", pairs))
-    order = (lax.axis_index("tensor") - jnp.arange(count)) % count
-    values = jnp.stack(parts)[order][None]
-    bit = 1
-    while bit < lax.axis_size("dp"):
-        values = jnp.concatenate([values, swap(values, bit)])
-        bit *= 2
-    return values
 
 
 def along_tensor(value):
@@ -128,11 +120,24 @@
     return blocks
 
 
-def expert_weights(expert_ids, route_weight, experts):
+def chip_table(expert_ids, route_weight, experts):
     names = jnp.arange(experts, dtype=jnp.int32)[:, None, None]
     table = jnp.sum(jnp.where(expert_ids[None] == names, route_weight[None], 0.0), axis=2)
+    count = lax.axis_size("tensor")
+    parts = [table]
+    for shift in range(1, count):
+        pairs = [(i, (i + shift) % count) for i in range(count)]
+        parts.append(lax.ppermute(table, "tensor", pairs))
+    order = (lax.axis_index("tensor") - jnp.arange(count)) % count
+    table = jnp.stack(parts)[order][None]
+    return jnp.concatenate([table, swap(table, 1)])
+
+
+def expert_weights(table):
+    for bit in (2, 4):
+        table = jnp.concatenate([table, swap(table, bit)])
     mine = lax.axis_index("dp") * lax.axis_size("tensor") + lax.axis_index("tensor")
-    return lax.dynamic_index_in_dim(from_all(table), mine, axis=2, keepdims=False)
+    return lax.dynamic_index_in_dim(table, mine, axis=2, keepdims=False)
 
 
 def neighbours(value):
@@ -187,11 +192,7 @@
             pltpu.VMEM((8, rows, -(-columns // 128) * 128), jnp.float32),
         ],
         compiler_params=pltpu.CompilerParams(vmem_limit_bytes=VMEM_LIMIT),
-        cost_estimate=pl.CostEstimate(
-            flops=16 * rows * depth * columns,
-            bytes_accessed=2 * depth * (rows + 8 * columns),
-            transcendentals=0,
-        ),
+        cost_estimate=cost(16 * rows * depth * columns, 2 * depth * (rows + 8 * columns)),
         name="project",
     )(place, attn_out, *pieces)
 
@@ -266,10 +267,9 @@
         ],
         scratch_shapes=[pltpu.VMEM((parts, rows, step), jnp.bfloat16)],
         compiler_params=pltpu.CompilerParams(vmem_limit_bytes=VMEM_LIMIT),
-        cost_estimate=pl.CostEstimate(
-            flops=2 * rows * parts * step * (2 * hidden + tokens),
-            bytes_accessed=2 * parts * step * (2 * hidden + sources * tokens),
-            transcendentals=rows * hidden,
+        cost_estimate=cost(
+            2 * rows * parts * step * (2 * hidden + tokens),
+            2 * parts * step * (2 * hidden + sources * tokens),
         ),
         name="gate_up",
     )(scales, gains, chosen, *pieces, *([w_gate, w_up] * parts))
@@ -310,10 +310,8 @@
         out_specs=[pl.BlockSpec((sources // 2, tokens, tile), lambda j: (0, 0, j))] * 2,
         out_shape=[jax.ShapeDtypeStruct((sources // 2, tokens, step), jnp.bfloat16)] * 2,
         compiler_params=pltpu.CompilerParams(vmem_limit_bytes=VMEM_LIMIT),
-        cost_estimate=pl.CostEstimate(
-            flops=2 * rows * step * (hidden + tokens),
-            bytes_accessed=2 * step * (hidden + sources * tokens),
-            transcendentals=0,
+        cost_estimate=cost(
+            2 * rows * step * (hidden + tokens), 2 * step * (hidden + sources * tokens)
         ),
         name="down",
     )(hidden_q, w_down, factor, spread)
@@ -366,18 +364,25 @@
     place = lax.axis_index("dp")[None]
 
     weight_rows = list(out_weight.T.reshape(CHUNKS, columns, -1))
+    table = chip_table(expert_ids, route_weight, experts)
+    near = neighbours(weight_rows[0])
     stream, sent = [], []
     for c in range(CHUNKS):
-        along_x, along_y = neighbours(weight_rows[c])
         if c + 1 < CHUNKS:
-            along_x, along_y, weight_rows[c + 1] = tie(along_x, along_y, weight_rows[c + 1])
-        groups = [[weight_rows[c]], [along_x], [along_y], diagonal(along_x, along_y)]
-        terms = project_part(place, attn_out, [both_cores(group) for group in groups])
+            near, table, weight_rows[c + 1] = tie(near, table, weight_rows[c + 1])
+        groups = [[weight_rows[c]], [near[0]], [near[1]], diagonal(*near)]
+        if c + 1 < CHUNKS:
+            near = neighbours(weight_rows[c + 1])
+            groups[3], near = tie(groups[3], near)
+        groups = [both_cores(group) for group in groups]
+        if c > 0:
+            groups, weight = tie(groups, weight)
+        terms = project_part(place, attn_out, groups)
         if c == 0:
-            terms, expert_ids = tie(terms, expert_ids)
-            weight = expert_weights(expert_ids, route_weight, experts)
+            terms, table = tie(terms, table)
+            weight = expert_weights(table)
         else:
-            terms, sent[-1], weight = tie(terms, sent[-1], weight)
+            terms, sent[-1] = tie(terms, sent[-1])
         total = lax.psum_scatter(terms, "tensor", scatter_dimension=0, tiled=True)
         stream.append(parts(residual, c).astype(jnp.float32) + total.astype(jnp.float32))
         sent.append(stream[c].astype(jnp.bfloat16))
@@ -425,7 +430,9 @@
         else:
             hidden = [hidden_of(0, groups[0])]
             stream = natural(stream, columns)
-            along_x, along_y, hidden[0], stream = tie(along_x, along_y, hidden[0], stream)
+            along_x, along_y, hidden[0], stream, groups[3] = tie(
+                along_x, along_y, hidden[0], stream, groups[3]
+            )
         groups[1].append(both_cores([along_x]))
         groups[2].append(both_cores([along_y]))
         across = diagonal(along_x, along_y)
@@ -435,25 +442,37 @@
         groups[3].append(both_cores(across))
 
     def outputs(r, c):
-        kept, given = down(hidden[r][0], w_down, factor[r], spread[r], c, step)
+        return down(hidden[r][0], w_down, factor[r], spread[r], c, step)
+
+    def halves(kept, given):
         taken = swap(given, 1)
         return [(kept[:half], taken[:half]), (kept[half:], taken[half:])]
 
-    summed = lambda r, c: [add(*terms) for terms in outputs(r, c)]
+    summed = lambda r, c: [add(*terms) for terms in halves(*outputs(r, c))]
     to_x, to_y = summed(1, 0), summed(2, 0)
     groups[3], to_x, to_y = tie(groups[3], to_x, to_y)
     hidden.append(hidden_of(3, groups[3]))
     peak_h = jnp.max(jnp.stack([peaks for _, peaks in hidden]))
     mixture = []
     for c in range(CHUNKS):
+        early_x, early_y = swap(to_x[0], 2), swap(to_y[1], 4)
+        kept, given = outputs(3, c)
+        given, early_x, early_y = tie(given, early_x, early_y)
+        beyond = [add(*terms) for terms in halves(kept, given)]
         if c > 0:
-            to_x, to_y = summed(1, c), summed(2, c)
-        beyond, to_own = summed(3, c), outputs(0, c)
+            beyond, mixed = tie(beyond, mixed)
+            mixture.append(lax.psum_scatter(mixed, "tensor", scatter_dimension=0, tiled=True))
         over_x, over_y = swap(beyond[0], 2), swap(beyond[1], 4)
-        low = add(*to_own[0], swap(to_x[0], 2), swap(add(to_y[0], over_x), 4))
-        high = add(*to_own[1], swap(add(to_x[1], over_y), 2), swap(to_y[1], 4))
+        late_x, late_y = to_x[1], to_y[0]
+        if c + 1 < CHUNKS:
+            to_x, to_y = summed(1, c + 1), summed(2, c + 1)
+            over_x, over_y, to_x, to_y = tie(over_x, over_y, to_x, to_y)
+        to_own = halves(*outputs(0, c))
+        low = add(*to_own[0], early_x, swap(add(late_y, over_x), 4))
+        high = add(*to_own[1], swap(add(late_x, over_y), 2), early_y)
         mixed = jnp.concatenate([low, high]).reshape(layers * local_rows, step)
-        mixture.append(lax.psum_scatter(mixed, "tensor", scatter_dimension=0, tiled=True))
+    mixed, mixture = tie(mixed, mixture)
+    mixture.append(lax.psum_scatter(mixed, "tensor", scatter_dimension=0, tiled=True))
     layer_out = stream + jnp.concatenate(mixture, axis=1).astype(jnp.float32)
     return layer_out.astype(jnp.bfloat16), peak_x, peak_h
 

time: 625 us -> 609 us (0.974)
  waiting for transfers between devices: 317 us -> 291 us
  local copies, waits for them, and re-layouts: 40.5 us -> 49.9 us
    ppermute x59, waiting for transfers between devices: 220 us -> 193 us  [swap(): return lax.ppermute(value, 'dp', [(i, i ^ bits) for i in range(count)])]
    unnamed x115 -> x151, local copies, waits for them, and re-layouts: 13.6 us -> 21.3 us
    convert_element_type x10 -> x12, other arithmetic: 26.2 us -> 23.3 us  [add(): return sum((t.astype(jnp.float32) for t in terms)).astype(jnp.bfloat16)]
  transfers between devices with their start and end apart: 83 -> 83, of which waited for: 36 -> 43; matrix products, arithmetic and copies ran while one was open for 12% -> 13% of each run, Pallas kernels for 13% -> 17%
where the time goes in v6:
time: 609 us; the launch traced here: 599 us
  waiting for transfers between devices  291 us (48%)
  Pallas kernels  115 us (19%)
  starting transfers between devices  66.1 us (11%)
  other arithmetic  54.4 us (9%)
  local copies, waits for them, and re-layouts  49.9 us (8%)
  between operations  21.4 us (4%)
    ppermute x59, waiting for transfers between devices, swap(): return lax.ppermute(value, 'dp', [(i, i ^ bits) for i in range(count)])  193 us
    ppermute x6, waiting for transfers between devices, along_tensor(): lax.ppermute(above[-1], 'tensor', [(count - 1 - i, count - 1 - j) for i,...  67.6 us
    pallas_call x4, Pallas kernels, gate_up(): pl.pallas_call(functools.partial(gate_up_kernel, parts), grid=(hidden //...  54 us
    pallas_call x8, Pallas kernels, down(): pl.pallas_call(down_kernel, grid=(tiles,), in_specs=[whole(hidden_q.shape...  42 us
    ppermute x59, starting transfers between devices, swap(): return lax.ppermute(value, 'dp', [(i, i ^ bits) for i in range(count)])  37.8 us
    convert_element_type x12, other arithmetic, add(): return sum((t.astype(jnp.float32) for t in terms)).astype(jnp.bfloat16)  23.3 us
    unnamed x151, local copies, waits for them, and re-layouts  21.3 us
    pallas_call x2, Pallas kernels, project_part(): pl.pallas_call(project_kernel, in_specs=[pl.BlockSpec(memory_space=pltpu....  18.8 us
  transfers between devices with their start and end apart: 83, of which 43 were waited for; matrix products, arithmetic and copies ran while one was open for 13% of the time, Pallas kernels for 17%

profile of v6, /device:TPU:0, one launch (start us, length us, event | category | flops | bytes accessed | tf_op | source)
XLA Modules:
  0.0 598.9 jit_solution(8131297653390904190)
XLA Ops:
  23.3 9.0 %collective-permute-done.refs_2_ = bf16[224,2048]{1,0:T(8,128)(2,1)} collective-permute-done((bf16[224,2048]{1,0:T(8,128)(2,1)S(1)}, bf16[224,2048]{1,0:T(8,128)(2,1)}, u32[]{:S(2)}, u32[]{:S(2)}) %collective-permute-start) | collective-permute-done | bytes 917536 | tf_op jit(solution)/shard_map/ppermute | solution.py:105
  40.0 24.4 %collective-permute-done.7.refs_6_ = bf16[112,2048]{1,0:T(8,128)(2,1)S(1)} collective-permute-done((bf16[112,2048]{1,0:T(8,128)(2,1)S(1)}, bf16[112,2048]{1,0:T(8,128)(2,1)S(1)}, u32[]{:S(2)}, u32[]{:S(2)}) %collective-permute-start.7) | collective-permute-done | bytes 458784 | tf_op jit(solution)/shard_map/ppermute | solution.py:105
  69.9 9.6 %project.2 = bf16[512,1792]{1,0:T(8,128)(2,1)} custom-call(s32[1]{0:T(128)} %bitcast.place_ref, bf16[512,2048]{1,0:T(8,128)(2,1)} %attn_ref.3, bf16[224,2048]{1,0:T(8,128)(2,1)S(1)} %get-tuple-element.222.refs_0_, bf16[224,2048]{1,0:T(8,128)(2,1)} %collective-permute-done.17.refs_1_, bf16[224,2048]{1,0:T(8,128)(2,1)} %collective-permute-done.refs_2_, ...), custom_call_target="tpu_custom_call" | custom-call | flops 234881024 | bytes 589824 | tf_op jit(solution)/shard_map/project/pallas_call | solution.py:184
  105.3 9.2 %project.3 = bf16[512,1792]{1,0:T(8,128)(2,1)} custom-call(s32[1]{0:T(128)} %bitcast.place_ref, bf16[512,2048]{1,0:T(8,128)(2,1)} %attn_ref.3, bf16[224,2048]{1,0:T(8,128)(2,1)S(1)} %get-tuple-element.108.refs_0_, bf16[224,2048]{1,0:T(8,128)(2,1)S(1)} %collective-permute-done.6.refs_1_, bf16[224,2048]{1,0:T(8,128)(2,1)S(1)} %collective-permute-done.9.refs_2_, ...), custom_call_target="tpu_custom_call" | custom-call | flops 234881024 | bytes 589824 | tf_op jit(solution)/shard_map/project/pallas_call | solution.py:184
  128.7 22.8 %collective-permute-done.25 = bf16[128,1792]{1,0:T(8,128)(2,1)} collective-permute-done((bf16[128,1792]{1,0:T(8,128)(2,1)S(1)}, bf16[128,1792]{1,0:T(8,128)(2,1)}, u32[]{:S(2)}, u32[]{:S(2)}) %collective-permute-start.25) | collective-permute-done | bytes 458784 | tf_op jit(solution)/shard_map/ppermute | solution.py:116
  156.5 18.6 %collective-permute-done.26 = bf16[128,1792]{1,0:T(8,128)(2,1)} collective-permute-done((bf16[128,1792]{1,0:T(8,128)(2,1)}, bf16[128,1792]{1,0:T(8,128)(2,1)}, u32[]{:S(2)}, u32[]{:S(2)}) %collective-permute-start.26) | collective-permute-done | bytes 458784 | tf_op jit(solution)/shard_map/ppermute | solution.py:116
  182.7 7.9 %collective-permute-done.27 = bf16[128,1792]{1,0:T(8,128)(2,1)} collective-permute-done((bf16[128,1792]{1,0:T(8,128)(2,1)}, bf16[128,1792]{1,0:T(8,128)(2,1)}, u32[]{:S(2)}, u32[]{:S(2)}) %collective-permute-start.27) | collective-permute-done | bytes 458784 | tf_op jit(solution)/shard_map/ppermute | solution.py:116
  202.0 8.9 %collective-permute-done.34 = bf16[128,1792]{1,0:T(8,128)(2,1)S(1)} collective-permute-done((bf16[128,1792]{1,0:T(8,128)(2,1)S(1)}, bf16[128,1792]{1,0:T(8,128)(2,1)S(1)}, u32[]{:S(2)}, u32[]{:S(2)}) %collective-permute-start.34) | collective-permute-done | bytes 458784 | tf_op jit(solution)/shard_map/ppermute | solution.py:116
  225.5 28.5 %collective-permute-done.30.refs_0_ = bf16[4,128,1792]{2,1,0:T(8,128)(2,1)} collective-permute-done((bf16[4,128,1792]{2,1,0:T(8,128)(2,1)}, bf16[4,128,1792]{2,1,0:T(8,128)(2,1)}, u32[]{:S(2)}, u32[]{:S(2)}) %collective-permute-start.30) | collective-permute-done | bytes 1835040 | tf_op jit(solution)/shard_map/ppermute | solution.py:105
  267.4 13.6 %collective-permute-done.42.refs_0_ = bf16[2,128,1792]{2,1,0:T(8,128)(2,1)S(1)} collective-permute-done((bf16[2,128,1792]{2,1,0:T(8,128)(2,1)}, bf16[2,128,1792]{2,1,0:T(8,128)(2,1)S(1)}, u32[]{:S(2)}, u32[]{:S(2)}) %collective-permute-start.42) | collective-permute-done | bytes 917536 | tf_op jit(solution)/shard_map/ppermute | solution.py:105
  287.1 13.3 %gate_up.4 = (bf16[384,1024]{1,0:T(8,128)(2,1)S(1)}, f32[8,128]{1,0:T(8,128)S(1)}) custom-call(f32[2]{0:T(128)S(1)} %pad_maximum_fusion.5.scale_ref, f32[2,1,1792]{2,1,0:T(1,128)S(1)} %maximum_multiply_fusion.gain_ref, bf16[8,48,128]{2,1,0:T(8,128)(2,1)S(1)} %bitcast.65, bf16[4,128,1792]{2,1,0:T(8,128)(2,1)} %bitcast_dynamic-update-slice_fusion.4.refs_0_, ...), custom_call_target="tpu_custom_call" | custom-call | flops 374341632 | bytes 1376256 | tf_op jit(solution)/shard_map/gate_up/pallas_call | solution.py:257
  303.0 18.5 %collective-permute-done.38.refs_2_ = bf16[4,128,1792]{2,1,0:T(8,128)(2,1)} collective-permute-done((bf16[4,128,1792]{2,1,0:T(8,128)(2,1)}, bf16[4,128,1792]{2,1,0:T(8,128)(2,1)}, u32[]{:S(2)}, u32[]{:S(2)}) %collective-permute-start.38) | collective-permute-done | bytes 1835040 | tf_op jit(solution)/shard_map/ppermute | solution.py:105
  332.6 13.4 %gate_up.6 = (bf16[384,1024]{1,0:T(8,128)(2,1)S(1)}, f32[8,128]{1,0:T(8,128)S(1)}) custom-call(f32[2]{0:T(128)S(1)} %copy-done.43, f32[2,1,1792]{2,1,0:T(1,128)S(1)} %maximum_multiply_fusion.gain_ref, bf16[8,48,128]{2,1,0:T(8,128)(2,1)S(1)} %bitcast.64, bf16[4,128,1792]{2,1,0:T(8,128)(2,1)S(1)} %copy-done.2, ...), custom_call_target="tpu_custom_call" | custom-call | flops 374341632 | bytes 1376256 | tf_op jit(solution)/shard_map/gate_up/pallas_call | solution.py:257
  346.1 14.2 %gate_up.5 = (bf16[384,1024]{1,0:T(8,128)(2,1)S(1)}, f32[8,128]{1,0:T(8,128)S(1)}) custom-call(f32[2]{0:T(128)S(1)} %copy-done.43, f32[2,1,1792]{2,1,0:T(1,128)S(1)} %maximum_multiply_fusion.gain_ref, bf16[8,48,128]{2,1,0:T(8,128)(2,1)S(1)} %bitcast.63, bf16[4,128,1792]{2,1,0:T(8,128)(2,1)} %collective-permute-done.30.refs_0_, ...), custom_call_target="tpu_custom_call" | custom-call | flops 374341632 | bytes 1376256 | tf_op jit(solution)/shard_map/gate_up/pallas_call | solution.py:257
  360.3 5.7 down.10
  389.5 13.1 %gate_up.7 = (bf16[384,1024]{1,0:T(8,128)(2,1)S(1)}, f32[8,128]{1,0:T(8,128)S(1)}) custom-call(f32[2]{0:T(128)S(1)} %copy-done.43, f32[2,1,1792]{2,1,0:T(1,128)S(1)} %maximum_multiply_fusion.gain_ref, bf16[8,48,128]{2,1,0:T(8,128)(2,1)S(1)} %bitcast.62, bf16[2,128,1792]{2,1,0:T(8,128)(2,1)S(1)} %copy-done.34, ...), custom_call_target="tpu_custom_call" | custom-call | flops 374341632 | bytes 1376256 | tf_op jit(solution)/shard_map/gate_up/pallas_call | solution.py:257
  402.6 5.6 down.12
  409.7 5.6 down.14
  442.1 14.4 %collective-permute-done.60 = bf16[2,128,1792]{2,1,0:T(8,128)(2,1)S(1)} collective-permute-done((bf16[2,128,1792]{2,1,0:T(8,128)(2,1)S(1)}, bf16[2,128,1792]{2,1,0:T(8,128)(2,1)S(1)}, u32[]{:S(2)}, u32[]{:S(2)}) %collective-permute-start.60) | collective-permute-done | bytes 917536 | tf_op jit(solution)/shard_map/ppermute | solution.py:105
  468.0 12.4 %collective-permute-done.64 = bf16[2,128,1792]{2,1,0:T(8,128)(2,1)S(1)} collective-permute-done((bf16[2,128,1792]{2,1,0:T(8,128)(2,1)}, bf16[2,128,1792]{2,1,0:T(8,128)(2,1)S(1)}, u32[]{:S(2)}, u32[]{:S(2)}) %collective-permute-start.64) | collective-permute-done | bytes 917536 | tf_op jit(solution)/shard_map/ppermute | solution.py:105
  481.8 16.3 %collective-permute-done.69 = bf16[2,128,1792]{2,1,0:T(8,128)(2,1)} collective-permute-done((bf16[2,128,1792]{2,1,0:T(8,128)(2,1)}, bf16[2,128,1792]{2,1,0:T(8,128)(2,1)}, u32[]{:S(2)}, u32[]{:S(2)}) %collective-permute-start.69) | collective-permute-done | bytes 917536 | tf_op jit(solution)/shard_map/ppermute | solution.py:105
  513.0 14.0 %collective-permute-done.72 = bf16[2,128,1792]{2,1,0:T(8,128)(2,1)} collective-permute-done((bf16[2,128,1792]{2,1,0:T(8,128)(2,1)}, bf16[2,128,1792]{2,1,0:T(8,128)(2,1)}, u32[]{:S(2)}, u32[]{:S(2)}) %collective-permute-start.72) | collective-permute-done | bytes 917536 | tf_op jit(solution)/shard_map/ppermute | solution.py:105
  530.3 17.4 %collective-permute-done.73 = bf16[2,128,1792]{2,1,0:T(8,128)(2,1)S(1)} collective-permute-done((bf16[2,128,1792]{2,1,0:T(8,128)(2,1)S(1)}, bf16[2,128,1792]{2,1,0:T(8,128)(2,1)S(1)}, u32[]{:S(2)}, u32[]{:S(2)}) %collective-permute-start.73) | collective-permute-done | bytes 917536 | tf_op jit(solution)/shard_map/ppermute | solution.py:105
  583.5 5.9 reduce-scatter.11.cloned.1.call-done
  (400 shorter events, 255.0 us)
Async XLA Ops:
  7.2 112.3 %reduce-scatter.5.cloned.1.call-start = ((), (), s32[]{:S(2)}) async-start(), calls=%async_computation.4 | async-start | bytes 2293760 | tf_op jit(solution)/shard_map/reduce_scatter | solution.py:386
  33.7 32.1 %collective-permute-start.10 = (bf16[224,2048]{1,0:T(8,128)(2,1)S(1)}, bf16[224,2048]{1,0:T(8,128)(2,1)}, u32[]{:S(2)}, u32[]{:S(2)}) collective-permute-start(bf16[224,2048]{1,0:T(8,128)(2,1)S(1)} %get-tuple-element.108.refs_0_), channel_id=1, source_target_pairs={{0,16},{4,20},{8,24},{12,28},{16,0},{20,4},{24,8},{28,12},{1,17},{... | collective-permute-start | bytes 2752520 | tf_op jit(solution)/shard_map/ppermute | solution.py:105
  35.3 30.5 %collective-permute-start.9 = (bf16[224,2048]{1,0:T(8,128)(2,1)S(1)}, bf16[224,2048]{1,0:T(8,128)(2,1)S(1)}, u32[]{:S(2)}, u32[]{:S(2)}) collective-permute-start(bf16[224,2048]{1,0:T(8,128)(2,1)S(1)} %get-tuple-element.108.refs_0_), channel_id=1, source_target_pairs={{0,8},{4,12},{8,0},{12,4},{16,24},{20,28},{24,16},{28,20},{1,9},{5... | collective-permute-start | bytes 2752520 | tf_op jit(solution)/shard_map/ppermute | solution.py:105
  36.8 27.6 %collective-permute-start.7 = (bf16[112,2048]{1,0:T(8,128)(2,1)S(1)}, bf16[112,2048]{1,0:T(8,128)(2,1)S(1)}, u32[]{:S(2)}, u32[]{:S(2)}) collective-permute-start(bf16[112,2048]{1,0:T(8,128)(2,1)S(1)} %slice.198), channel_id=1, source_target_pairs={{0,16},{4,20},{8,24},{12,28},{16,0},{20,4},{24,8},{28,12},{1,17},{... | collective-permute-start | bytes 1376264 | tf_op jit(solution)/shard_map/ppermute | solution.py:105
  38.3 27.5 %collective-permute-start.8 = (bf16[112,2048]{1,0:T(8,128)(2,1)S(1)}, bf16[112,2048]{1,0:T(8,128)(2,1)}, u32[]{:S(2)}, u32[]{:S(2)}) collective-permute-start(bf16[112,2048]{1,0:T(8,128)(2,1)S(1)} %slice.199), channel_id=1, source_target_pairs={{0,8},{4,12},{8,0},{12,4},{16,24},{20,28},{24,16},{28,20},{1,9},{5... | collective-permute-start | bytes 1376264 | tf_op jit(solution)/shard_map/ppermute | solution.py:105
  79.6 97.9 %reduce-scatter.7.cloned.1.call-start = ((), (), s32[]{:S(2)}) async-start(), calls=%async_computation.5 | async-start | bytes 2293760 | tf_op jit(solution)/shard_map/reduce_scatter | solution.py:386
  121.6 429.2 %reduce-scatter.9.cloned.1.call-start = ((), (), s32[]{:S(2)}) async-start(), calls=%async_computation.6 | async-start | bytes 2293760 | tf_op jit(solution)/shard_map/reduce_scatter | solution.py:464
  121.7 29.8 %collective-permute-start.25 = (bf16[128,1792]{1,0:T(8,128)(2,1)S(1)}, bf16[128,1792]{1,0:T(8,128)(2,1)}, u32[]{:S(2)}, u32[]{:S(2)}) collective-permute-start(bf16[128,1792]{1,0:T(8,128)(2,1)S(1)} %convert_element_type.248), channel_id=1, source_target_pairs={{3,2},{2,1},{1,0},{7,6},{6,5},{5,4},{11,10},{10,9},{9,8},{15,14},{... | collective-permute-start | bytes 1376264 | tf_op jit(solution)/shard_map/ppermute | solution.py:116
  123.0 29.8 %collective-permute-start.24 = (bf16[128,1792]{1,0:T(8,128)(2,1)S(1)}, bf16[128,1792]{1,0:T(8,128)(2,1)}, u32[]{:S(2)}, u32[]{:S(2)}) collective-permute-start(bf16[128,1792]{1,0:T(8,128)(2,1)S(1)} %convert_element_type.248), channel_id=1, source_target_pairs={{0,1},{1,2},{2,3},{4,5},{5,6},{6,7},{8,9},{9,10},{10,11},{12,13},{... | collective-permute-start | bytes 1376264 | tf_op jit(solution)/shard_map/ppermute | solution.py:115
  176.4 35.8 %collective-permute-start.29 = (bf16[128,1792]{1,0:T(8,128)(2,1)}, bf16[128,1792]{1,0:T(8,128)(2,1)S(1)}, u32[]{:S(2)}, u32[]{:S(2)}) collective-permute-start(bf16[128,1792]{1,0:T(8,128)(2,1)} %collective-permute-done.28), channel_id=1, source_target_pairs={{2,3},{6,7},{10,11},{14,15},{18,19},{22,23},{26,27},{30,31}} | collective-permute-start | bytes 1376264 | tf_op jit(solution)/shard_map/ppermute | solution.py:115
  214.1 39.9 %collective-permute-start.30 = (bf16[4,128,1792]{2,1,0:T(8,128)(2,1)}, bf16[4,128,1792]{2,1,0:T(8,128)(2,1)}, u32[]{:S(2)}, u32[]{:S(2)}) collective-permute-start(bf16[4,128,1792]{2,1,0:T(8,128)(2,1)} %bitcast_dynamic-update-slice_fusion.4.refs_0_), channel_id=1, source_target_pairs={{0,8},{4,12},{8,0},{12,4},{16,24},{20,28},{24,16},{28,20},{1,9},{5... | collective-permute-start | bytes 5505032 | tf_op jit(solution)/shard_map/ppermute | solution.py:105
  215.4 39.3 %collective-permute-start.31 = (bf16[4,128,1792]{2,1,0:T(8,128)(2,1)}, bf16[4,128,1792]{2,1,0:T(8,128)(2,1)S(1)}, u32[]{:S(2)}, u32[]{:S(2)}) collective-permute-start(bf16[4,128,1792]{2,1,0:T(8,128)(2,1)} %bitcast_dynamic-update-slice_fusion.4.refs_0_), channel_id=1, source_target_pairs={{0,16},{4,20},{8,24},{12,28},{16,0},{20,4},{24,8},{28,12},{1,17},{... | collective-permute-start | bytes 5505032 | tf_op jit(solution)/shard_map/ppermute | solution.py:105
  216.9 45.2 %collective-permute-start.40 = (bf16[4,128,1792]{2,1,0:T(8,128)(2,1)}, bf16[4,128,1792]{2,1,0:T(8,128)(2,1)S(1)}, u32[]{:S(2)}, u32[]{:S(2)}) collective-permute-start(bf16[4,128,1792]{2,1,0:T(8,128)(2,1)} %bitcast_dynamic-update-slice_fusion.4.refs_0_), channel_id=1, source_target_pairs={{0,4},{4,0},{8,12},{12,8},{16,20},{20,16},{24,28},{28,24},{1,5},{5... | collective-permute-start | bytes 5505032 | tf_op jit(solution)/shard_map/ppermute | solution.py:105
  254.8 28.9 %collective-permute-start.41 = (bf16[4,128,1792]{2,1,0:T(8,128)(2,1)}, bf16[4,128,1792]{2,1,0:T(8,128)(2,1)}, u32[]{:S(2)}, u32[]{:S(2)}) collective-permute-start(bf16[4,128,1792]{2,1,0:T(8,128)(2,1)} %bitcast_dynamic-update-slice_fusion.refs_2_), channel_id=1, source_target_pairs={{0,4},{4,0},{8,12},{12,8},{16,20},{20,16},{24,28},{28,24},{1,5},{5... | collective-permute-start | bytes 5505032 | tf_op jit(solution)/shard_map/ppermute | solution.py:105
  260.6 60.9 %collective-permute-start.38 = (bf16[4,128,1792]{2,1,0:T(8,128)(2,1)}, bf16[4,128,1792]{2,1,0:T(8,128)(2,1)}, u32[]{:S(2)}, u32[]{:S(2)}) collective-permute-start(bf16[4,128,1792]{2,1,0:T(8,128)(2,1)} %bitcast_dynamic-update-slice_fusion.refs_2_), channel_id=1, source_target_pairs={{0,8},{4,12},{8,0},{12,4},{16,24},{20,28},{24,16},{28,20},{1,9},{5... | collective-permute-start | bytes 5505032 | tf_op jit(solution)/shard_map/ppermute | solution.py:105
  263.3 58.2 %collective-permute-start.39 = (bf16[4,128,1792]{2,1,0:T(8,128)(2,1)}, bf16[4,128,1792]{2,1,0:T(8,128)(2,1)}, u32[]{:S(2)}, u32[]{:S(2)}) collective-permute-start(bf16[4,128,1792]{2,1,0:T(8,128)(2,1)} %bitcast_dynamic-update-slice_fusion.refs_2_), channel_id=1, source_target_pairs={{0,16},{4,20},{8,24},{12,28},{16,0},{20,4},{24,8},{28,12},{1,17},{... | collective-permute-start | bytes 5505032 | tf_op jit(solution)/shard_map/ppermute | solution.py:105
  281.1 47.5 %collective-permute-start.50 = (bf16[4,128,1792]{2,1,0:T(8,128)(2,1)}, bf16[4,128,1792]{2,1,0:T(8,128)(2,1)}, u32[]{:S(2)}, u32[]{:S(2)}) collective-permute-start(bf16[4,128,1792]{2,1,0:T(8,128)(2,1)} %copy-done.1), channel_id=1, source_target_pairs={{0,4},{4,0},{8,12},{12,8},{16,20},{20,16},{24,28},{28,24},{1,5},{5... | collective-permute-start | bytes 5505032 | tf_op jit(solution)/shard_map/ppermute | solution.py:105
  328.0 32.3 %collective-permute-start.46 = (bf16[2,128,1792]{2,1,0:T(8,128)(2,1)}, bf16[2,128,1792]{2,1,0:T(8,128)(2,1)}, u32[]{:S(2)}, u32[]{:S(2)}) collective-permute-start(bf16[2,128,1792]{2,1,0:T(8,128)(2,1)} %slice.209), channel_id=1, source_target_pairs={{0,16},{4,20},{8,24},{12,28},{16,0},{20,4},{24,8},{28,12},{1,17},{... | collective-permute-start | bytes 2752520 | tf_op jit(solution)/shard_map/ppermute | solution.py:105
  328.6 31.7 %collective-permute-start.47 = (bf16[2,128,1792]{2,1,0:T(8,128)(2,1)}, bf16[2,128,1792]{2,1,0:T(8,128)(2,1)}, u32[]{:S(2)}, u32[]{:S(2)}) collective-permute-start(bf16[2,128,1792]{2,1,0:T(8,128)(2,1)} %slice.210), channel_id=1, source_target_pairs={{0,8},{4,12},{8,0},{12,4},{16,24},{20,28},{24,16},{28,20},{1,9},{5... | collective-permute-start | bytes 2752520 | tf_op jit(solution)/shard_map/ppermute | solution.py:105
  382.5 27.0 %collective-permute-start.57 = (bf16[2,128,1792]{2,1,0:T(8,128)(2,1)}, bf16[2,128,1792]{2,1,0:T(8,128)(2,1)}, u32[]{:S(2)}, u32[]{:S(2)}) collective-permute-start(bf16[2,128,1792]{2,1,0:T(8,128)(2,1)} %get-tuple-element.163), channel_id=1, source_target_pairs={{0,8},{4,12},{8,0},{12,4},{16,24},{20,28},{24,16},{28,20},{1,9},{5... | collective-permute-start | bytes 2752520 | tf_op jit(solution)/shard_map/ppermute | solution.py:105
  431.6 50.2 %collective-permute-start.67 = (bf16[4,128,1792]{2,1,0:T(8,128)(2,1)S(1)}, bf16[4,128,1792]{2,1,0:T(8,128)(2,1)}, u32[]{:S(2)}, u32[]{:S(2)}) collective-permute-start(bf16[4,128,1792]{2,1,0:T(8,128)(2,1)S(1)} %get-tuple-element.177), channel_id=1, source_target_pairs={{0,4},{4,0},{8,12},{12,8},{16,20},{20,16},{24,28},{28,24},{1,5},{5... | collective-permute-start | bytes 5505032 | tf_op jit(solution)/shard_map/ppermute | solution.py:105
  460.1 38.0 %collective-permute-start.69 = (bf16[2,128,1792]{2,1,0:T(8,128)(2,1)}, bf16[2,128,1792]{2,1,0:T(8,128)(2,1)}, u32[]{:S(2)}, u32[]{:S(2)}) collective-permute-start(bf16[2,128,1792]{2,1,0:T(8,128)(2,1)} %add_convert_fusion.6), channel_id=1, source_target_pairs={{0,8},{4,12},{8,0},{12,4},{16,24},{20,28},{24,16},{28,20},{1,9},{5... | collective-permute-start | bytes 2752520 | tf_op jit(solution)/shard_map/ppermute | solution.py:105
  462.1 37.0 %collective-permute-start.68 = (bf16[2,128,1792]{2,1,0:T(8,128)(2,1)}, bf16[2,128,1792]{2,1,0:T(8,128)(2,1)S(1)}, u32[]{:S(2)}, u32[]{:S(2)}) collective-permute-start(bf16[2,128,1792]{2,1,0:T(8,128)(2,1)} %add_convert_fusion.8), channel_id=1, source_target_pairs={{0,16},{4,20},{8,24},{12,28},{16,0},{20,4},{24,8},{28,12},{1,17},{... | collective-permute-start | bytes 2752520 | tf_op jit(solution)/shard_map/ppermute | solution.py:105
  507.3 82.2 %reduce-scatter.11.cloned.1.call-start = ((), (), s32[]{:S(2)}) async-start(), calls=%async_computation.7 | async-start | bytes 2293760 | tf_op jit(solution)/shard_map/reduce_scatter | solution.py:475
  (134 other events, 1560.9 us)
Sparse Core Ops, SparseCore 0:
  79.7 39.7 reduce-scatter.4
  121.8 50.6 reduce-scatter.6
  507.4 38.4 reduce-scatter.8
  550.9 38.4 reduce-scatter.10

commit v7 on v6

--- a/solution.py
+++ b/solution.py
@@ -105,17 +105,19 @@
     return lax.ppermute(value, "dp", [(i, i ^ bits) for i in range(count)])
 
 
-def along_tensor(value):
+def along_tensor(value, at_hop=None):
     count, here = lax.axis_size("tensor"), lax.axis_index("tensor")
+    passed = [(value, value)]
+    for hop in range(1, count):
+        up = [(i, i + 1) for i in range(hop - 1, count - 1)]
+        back = [(count - 1 - i, count - 1 - j) for i, j in up]
+        below, above = passed[-1]
+        arrived = lax.ppermute(below, "tensor", up), lax.ppermute(above, "tensor", back)
+        passed.append(at_hop(hop, arrived) if at_hop else arrived)
     blocks = jnp.zeros((count,) + value.shape, value.dtype)
     blocks = lax.dynamic_update_index_in_dim(blocks, value, here, 0)
-    below, above = [value], [value]
     for hop in range(1, count):
-        up = [(i, i + 1) for i in range(hop - 1, count - 1)]
-        below.append(lax.ppermute(below[-1], "tensor", up))
-        above.append(lax.ppermute(above[-1], "tensor", [(count - 1 - i, count - 1 - j) for i, j in up]))
-    for hop in range(1, count):
-        block = jnp.where(here >= hop, below[hop], above[count - hop])
+        block = jnp.where(here >= hop, passed[hop][0], passed[count - hop][1])
         blocks = lax.dynamic_update_index_in_dim(blocks, block, (here - hop) % count, 0)
     return blocks
 
@@ -363,29 +365,39 @@
     parts = lambda value, c: split(value)[:, :, c].reshape(-1, step)
     place = lax.axis_index("dp")[None]
 
+    def summed_over_tensor(terms, c):
+        total = lax.psum_scatter(terms, "tensor", scatter_dimension=0, tiled=True)
+        part = parts(residual, c).astype(jnp.float32) + total.astype(jnp.float32)
+        return part, part.astype(jnp.bfloat16)
+
     weight_rows = list(out_weight.T.reshape(CHUNKS, columns, -1))
+    near = neighbours(weight_rows[0])
     table = chip_table(expert_ids, route_weight, experts)
-    near = neighbours(weight_rows[0])
-    stream, sent = [], []
-    for c in range(CHUNKS):
-        if c + 1 < CHUNKS:
-            near, table, weight_rows[c + 1] = tie(near, table, weight_rows[c + 1])
-        groups = [[weight_rows[c]], [near[0]], [near[1]], diagonal(*near)]
-        if c + 1 < CHUNKS:
-            near = neighbours(weight_rows[c + 1])
-            groups[3], near = tie(groups[3], near)
-        groups = [both_cores(group) for group in groups]
-        if c > 0:
-            groups, weight = tie(groups, weight)
-        terms = project_part(place, attn_out, groups)
-        if c == 0:
-            terms, table = tie(terms, table)
-            weight = expert_weights(table)
-        else:
-            terms, sent[-1] = tie(terms, sent[-1])
-        total = lax.psum_scatter(terms, "tensor", scatter_dimension=0, tiled=True)
-        stream.append(parts(residual, c).astype(jnp.float32) + total.astype(jnp.float32))
-        sent.append(stream[c].astype(jnp.bfloat16))
+    near, table = tie(near, table)
+    groups = [[weight_rows[0]], [near[0]], [near[1]], diagonal(*near)]
+    terms = project_part(place, attn_out, [both_cores(group) for group in groups])
+    terms, table, weight_rows[1] = tie(terms, table, weight_rows[1])
+    weight = expert_weights(table)
+    near = neighbours(weight_rows[1])
+    groups = [[weight_rows[1]], [near[0]], [near[1]], diagonal(*near)]
+    groups = [both_cores(group) for group in groups]
+    first, sent = summed_over_tensor(terms, 0)
+    sent, weight = tie(sent, weight)
+
+    second = []
+
+    def at_hop(hop, arrived):
+        if hop == 1:
+            arrived, tied = tie(arrived, groups)
+            second.append(project_part(place, attn_out, tied))
+        if hop == 2:
+            arrived, terms = tie(arrived, second.pop())
+            second.append(summed_over_tensor(terms, 1))
+        return arrived
+
+    own = along_tensor(sent, at_hop)
+    stream = [first, second[0][0]]
+    sent = second[0][1]
 
     named = weight > 0.0
     earlier = jnp.triu(jnp.ones((local_rows, local_rows), jnp.bfloat16), 1)
@@ -415,29 +427,36 @@
     gate_rows = w_gate.reshape(1, owners, CHUNKS, columns, -1)
     up_rows = w_up.reshape(1, owners, CHUNKS, columns, -1)
 
-    def hidden_of(r, tokens):
+    def hidden_of(r, tokens, choice):
         pieces = [piece for part in tokens for piece in part]
         return gate_up(scales, gains, choice[r], pieces, gate_rows, up_rows)
 
     groups = [[] for _ in range(4)]
-    own = along_tensor(sent[0])
     for c in range(CHUNKS):
         along_x, along_y = neighbours(own)
         groups[0].append(both_cores([own]))
         if c + 1 < CHUNKS:
-            own = along_tensor(sent[c + 1])
-            along_x, along_y, own = tie(along_x, along_y, own)
+            along_x, along_y, sent = tie(along_x, along_y, sent)
+            across = diagonal(along_x, along_y)
+
+            def at_hop(hop, arrived):
+                nonlocal across
+                if hop == 2:
+                    arrived, across = tie(arrived, across)
+                return arrived
+
+            own = along_tensor(sent, at_hop)
         else:
-            hidden = [hidden_of(0, groups[0])]
+            hidden = [hidden_of(0, groups[0], choice)]
             stream = natural(stream, columns)
-            along_x, along_y, hidden[0], stream, groups[3] = tie(
-                along_x, along_y, hidden[0], stream, groups[3]
+            along_x, along_y, hidden[0], stream, groups[3], choice, spread, factor = tie(
+                along_x, along_y, hidden[0], stream, groups[3], choice, spread, factor
             )
         groups[1].append(both_cores([along_x]))
         groups[2].append(both_cores([along_y]))
-        across = diagonal(along_x, along_y)
         if c + 1 == CHUNKS:
-            hidden += [hidden_of(1, groups[1]), hidden_of(2, groups[2])]
+            across = diagonal(along_x, along_y)
+            hidden += [hidden_of(1, groups[1], choice), hidden_of(2, groups[2], choice)]
             across, hidden = tie(across, hidden)
         groups[3].append(both_cores(across))
 
@@ -451,13 +470,14 @@
     summed = lambda r, c: [add(*terms) for terms in halves(*outputs(r, c))]
     to_x, to_y = summed(1, 0), summed(2, 0)
     groups[3], to_x, to_y = tie(groups[3], to_x, to_y)
-    hidden.append(hidden_of(3, groups[3]))
+    hidden.append(hidden_of(3, groups[3], choice))
     peak_h = jnp.max(jnp.stack([peaks for _, peaks in hidden]))
     mixture = []
     for c in range(CHUNKS):
         early_x, early_y = swap(to_x[0], 2), swap(to_y[1], 4)
         kept, given = outputs(3, c)
-        given, early_x, early_y = tie(given, early_x, early_y)
+        if c == 0:
+            given, early_x, early_y = tie(given, early_x, early_y)
         beyond = [add(*terms) for terms in halves(kept, given)]
         if c > 0:
             beyond, mixed = tie(beyond, mixed)
@@ -465,8 +485,8 @@
         over_x, over_y = swap(beyond[0], 2), swap(beyond[1], 4)
         late_x, late_y = to_x[1], to_y[0]
         if c + 1 < CHUNKS:
+            over_x, over_y, hidden = tie(over_x, over_y, hidden)
             to_x, to_y = summed(1, c + 1), summed(2, c + 1)
-            over_x, over_y, to_x, to_y = tie(over_x, over_y, to_x, to_y)
         to_own = halves(*outputs(0, c))
         low = add(*to_own[0], early_x, swap(add(late_y, over_x), 4))
         high = add(*to_own[1], swap(add(late_x, over_y), 2), early_y)

time: 609 us -> 599 us (0.984)
  waiting for transfers between devices: 291 us -> 309 us
  local copies, waits for them, and re-layouts: 49.9 us -> 32.2 us
  starting transfers between devices: 66.1 us -> 56.6 us
  Pallas kernels: 115 us -> 124 us
    unnamed x151 -> x73, local copies, waits for them, and re-layouts: 21.3 us -> 8.88 us
    ppermute x12, waiting for transfers between devices: 67.6 us -> 77.9 us  [the longest x6 69.6 us: along_tensor(): lax.ppermute(above, 'tensor', back)]
    pallas_call x8, Pallas kernels: 42 us -> 49.2 us  [down(): pl.pallas_call(down_kernel, grid=(tiles,), in_specs=[whole(hidden_q.shape...]
    convert_element_type x12 -> x10, other arithmetic: 23.3 us -> 23.1 us  [add(): return sum((t.astype(jnp.float32) for t in terms)).astype(jnp.bfloat16)]
  transfers between devices with their start and end apart: 83 -> 83, of which waited for: 43 -> 44; matrix products, arithmetic and copies ran while one was open for 13% -> 12% of each run, Pallas kernels for 17% -> 18%
where the time goes in v7:
time: 599 us; the launch traced here: 594 us
  waiting for transfers between devices  309 us (52%)
  Pallas kernels  124 us (21%)
  starting transfers between devices  56.6 us (9%)
  other arithmetic  50.8 us (8%)
  local copies, waits for them, and re-layouts  32.2 us (5%)
  between operations  21.3 us (4%)
    ppermute x59, waiting for transfers between devices, swap(): return lax.ppermute(value, 'dp', [(i, i ^ bits) for i in range(count)])  197 us
    ppermute x6, waiting for transfers between devices, along_tensor(): lax.ppermute(above, 'tensor', back)  69.6 us
    pallas_call x4, Pallas kernels, gate_up(): pl.pallas_call(functools.partial(gate_up_kernel, parts), grid=(hidden //...  55.4 us
    pallas_call x8, Pallas kernels, down(): pl.pallas_call(down_kernel, grid=(tiles,), in_specs=[whole(hidden_q.shape...  49.2 us
    ppermute x59, starting transfers between devices, swap(): return lax.ppermute(value, 'dp', [(i, i ^ bits) for i in range(count)])  33.8 us
    convert_element_type x10, other arithmetic, add(): return sum((t.astype(jnp.float32) for t in terms)).astype(jnp.bfloat16)  23.1 us
    ppermute x5, waiting for transfers between devices, peaks_over_all(): peaks = jnp.maximum(peaks, lax.ppermute(peaks, axis, pairs))  21.7 us
    pallas_call x2, Pallas kernels, project_part(): pl.pallas_call(project_kernel, in_specs=[pl.BlockSpec(memory_space=pltpu....  18.8 us
  transfers between devices with their start and end apart: 83, of which 44 were waited for; matrix products, arithmetic and copies ran while one was open for 12% of the time, Pallas kernels for 18%

profile of v7, /device:TPU:0, one launch (start us, length us, event | category | flops | bytes accessed | tf_op | source)
XLA Modules:
  0.0 594.1 jit_solution(8961670051314121929)
XLA Ops:
  24.5 7.7 %collective-permute-done.1.refs_2_ = bf16[224,2048]{1,0:T(8,128)(2,1)S(1)} collective-permute-done((bf16[224,2048]{1,0:T(8,128)(2,1)S(1)}, bf16[224,2048]{1,0:T(8,128)(2,1)S(1)}, u32[]{:S(2)}, u32[]{:S(2)}) %collective-permute-start.1) | collective-permute-done | bytes 917536 | tf_op jit(solution)/shard_map/ppermute | solution.py:105
  37.5 9.3 %collective-permute-done.9.refs_6_ = bf16[112,2048]{1,0:T(8,128)(2,1)S(1)} collective-permute-done((bf16[112,2048]{1,0:T(8,128)(2,1)S(1)}, bf16[112,2048]{1,0:T(8,128)(2,1)S(1)}, u32[]{:S(2)}, u32[]{:S(2)}) %collective-permute-start.9) | collective-permute-done | bytes 458784 | tf_op jit(solution)/shard_map/ppermute | solution.py:105
  51.5 9.4 %project.2 = bf16[512,1792]{1,0:T(8,128)(2,1)} custom-call(s32[1]{0:T(128)} %bitcast.2.place_ref, bf16[512,2048]{1,0:T(8,128)(2,1)} %attn_ref.3, bf16[224,2048]{1,0:T(8,128)(2,1)S(1)} %get-tuple-element.228.refs_0_, bf16[224,2048]{1,0:T(8,128)(2,1)} %collective-permute-done.refs_1_, bf16[224,2048]{1,0:T(8,128)(2,1)S(1)} %collective-permute-done.1.refs_2_, ...), custom_call_target="tpu_custom_call" | custom-call | flops 234881024 | bytes 589824 | tf_op jit(solution)/shard_map/project/pallas_call | solution.py:186
  63.5 22.7 %collective-permute-done.13 = f32[2,4,32,128]{3,2,1,0:T(8,128)S(1)} collective-permute-done((f32[2,4,32,128]{3,2,1,0:T(8,128)S(1)}, f32[2,4,32,128]{3,2,1,0:T(8,128)S(1)}, u32[]{:S(2)}, u32[]{:S(2)}) %collective-permute-start.13) | collective-permute-done | bytes 131104 | tf_op jit(solution)/shard_map/ppermute | solution.py:105
  97.6 7.0 %collective-permute-done.22.refs_6_ = bf16[112,2048]{1,0:T(8,128)(2,1)S(1)} collective-permute-done((bf16[112,2048]{1,0:T(8,128)(2,1)}, bf16[112,2048]{1,0:T(8,128)(2,1)S(1)}, u32[]{:S(2)}, u32[]{:S(2)}) %collective-permute-start.22) | collective-permute-done | bytes 458784 | tf_op jit(solution)/shard_map/ppermute | solution.py:105
  114.4 8.3 %collective-permute-done.15 = bf16[128,1792]{1,0:T(8,128)(2,1)} collective-permute-done((bf16[128,1792]{1,0:T(8,128)(2,1)S(1)}, bf16[128,1792]{1,0:T(8,128)(2,1)}, u32[]{:S(2)}, u32[]{:S(2)}) %collective-permute-start.15) | collective-permute-done | bytes 458784 | tf_op jit(solution)/shard_map/ppermute | solution.py:115
  130.5 9.4 %project.3 = bf16[512,1792]{1,0:T(8,128)(2,1)} custom-call(s32[1]{0:T(128)} %bitcast.2.place_ref, bf16[512,2048]{1,0:T(8,128)(2,1)} %attn_ref.3, bf16[224,2048]{1,0:T(8,128)(2,1)S(1)} %get-tuple-element.112.refs_0_, bf16[224,2048]{1,0:T(8,128)(2,1)} %collective-permute-done.17.refs_1_, bf16[224,2048]{1,0:T(8,128)(2,1)S(1)} %collective-permute-done.18.refs_2_, ...), custom_call_target="tpu_custom_call" | custom-call | flops 234881024 | bytes 589824 | tf_op jit(solution)/shard_map/project/pallas_call | solution.py:186
  149.5 30.3 %collective-permute-done.28 = bf16[128,1792]{1,0:T(8,128)(2,1)S(1)} collective-permute-done((bf16[128,1792]{1,0:T(8,128)(2,1)}, bf16[128,1792]{1,0:T(8,128)(2,1)S(1)}, u32[]{:S(2)}, u32[]{:S(2)}) %collective-permute-start.28) | collective-permute-done | bytes 458784 | tf_op jit(solution)/shard_map/ppermute | solution.py:115
  191.2 29.5 %collective-permute-done.30.refs_0_ = bf16[4,128,1792]{2,1,0:T(8,128)(2,1)} collective-permute-done((bf16[4,128,1792]{2,1,0:T(8,128)(2,1)}, bf16[4,128,1792]{2,1,0:T(8,128)(2,1)}, u32[]{:S(2)}, u32[]{:S(2)}) %collective-permute-start.30) | collective-permute-done | bytes 1835040 | tf_op jit(solution)/shard_map/ppermute | solution.py:105
  230.3 9.6 %collective-permute-done.34 = bf16[128,1792]{1,0:T(8,128)(2,1)S(1)} collective-permute-done((bf16[128,1792]{1,0:T(8,128)(2,1)S(1)}, bf16[128,1792]{1,0:T(8,128)(2,1)S(1)}, u32[]{:S(2)}, u32[]{:S(2)}) %collective-permute-start.34) | collective-permute-done | bytes 458784 | tf_op jit(solution)/shard_map/ppermute | solution.py:115
  241.4 13.6 %collective-permute-done.35 = bf16[128,1792]{1,0:T(8,128)(2,1)S(1)} collective-permute-done((bf16[128,1792]{1,0:T(8,128)(2,1)S(1)}, bf16[128,1792]{1,0:T(8,128)(2,1)S(1)}, u32[]{:S(2)}, u32[]{:S(2)}) %collective-permute-start.35) | collective-permute-done | bytes 458784 | tf_op jit(solution)/shard_map/ppermute | solution.py:115
  259.2 6.1 %collective-permute-done.38 = bf16[128,1792]{1,0:T(8,128)(2,1)S(1)} collective-permute-done((bf16[128,1792]{1,0:T(8,128)(2,1)S(1)}, bf16[128,1792]{1,0:T(8,128)(2,1)S(1)}, u32[]{:S(2)}, u32[]{:S(2)}) %collective-permute-start.38) | collective-permute-done | bytes 458784 | tf_op jit(solution)/shard_map/ppermute | solution.py:115
  280.5 13.8 %gate_up.4 = (bf16[384,1024]{1,0:T(8,128)(2,1)S(1)}, f32[8,128]{1,0:T(8,128)S(1)}) custom-call(f32[2]{0:T(128)S(1)} %pad_maximum_fusion.5.scale_ref, f32[2,1,1792]{2,1,0:T(1,128)S(1)} %maximum_multiply_fusion.gain_ref, bf16[8,48,128]{2,1,0:T(8,128)(2,1)S(1)} %bitcast.73, bf16[4,128,1792]{2,1,0:T(8,128)(2,1)} %bitcast_dynamic-update-slice_fusion.4.refs_0_, ...), custom_call_target="tpu_custom_call" | custom-call | flops 374341632 | bytes 1376256 | tf_op jit(solution)/shard_map/gate_up/pallas_call | solution.py:259
  294.4 19.7 %collective-permute-done.40.refs_2_ = bf16[4,128,1792]{2,1,0:T(8,128)(2,1)} collective-permute-done((bf16[4,128,1792]{2,1,0:T(8,128)(2,1)}, bf16[4,128,1792]{2,1,0:T(8,128)(2,1)}, u32[]{:S(2)}, u32[]{:S(2)}) %collective-permute-start.40) | collective-permute-done | bytes 1835040 | tf_op jit(solution)/shard_map/ppermute | solution.py:105
  323.3 14.0 %gate_up.5 = (bf16[384,1024]{1,0:T(8,128)(2,1)S(1)}, f32[8,128]{1,0:T(8,128)S(1)}) custom-call(f32[2]{0:T(128)S(1)} %pad_maximum_fusion.5.scale_ref, f32[2,1,1792]{2,1,0:T(1,128)S(1)} %maximum_multiply_fusion.gain_ref, bf16[8,48,128]{2,1,0:T(8,128)(2,1)S(1)} %get-tuple-element.237.chosen_ref, bf16[4,128,1792]{2,1,0:T(8,128)(2,1)} %collective-permute-done.30.refs_0_, ...), custom_call_target="tpu_custom_call" | custom-call | flops 374341632 | bytes 1376256 | tf_op jit(solution)/shard_map/gate_up/pallas_call | solution.py:259
  337.3 13.9 %gate_up.6 = (bf16[384,1024]{1,0:T(8,128)(2,1)S(1)}, f32[8,128]{1,0:T(8,128)S(1)}) custom-call(f32[2]{0:T(128)S(1)} %pad_maximum_fusion.5.scale_ref, f32[2,1,1792]{2,1,0:T(1,128)S(1)} %maximum_multiply_fusion.gain_ref, bf16[8,48,128]{2,1,0:T(8,128)(2,1)S(1)} %get-tuple-element.236.chosen_ref, bf16[4,128,1792]{2,1,0:T(8,128)(2,1)} %collective-permute-done.31.refs_0_, ...), custom_call_target="tpu_custom_call" | custom-call | flops 374341632 | bytes 1376256 | tf_op jit(solution)/shard_map/gate_up/pallas_call | solution.py:259
  358.3 13.4 %down.9 = (bf16[4,128,1792]{2,1,0:T(8,128)(2,1)S(1)}, bf16[4,128,1792]{2,1,0:T(8,128)(2,1)S(1)}) custom-call(bf16[384,1024]{1,0:T(8,128)(2,1)S(1)} %get-tuple-element.184.hidden_ref, bf16[1,1024,3584]{2,1,0:T(8,128)(2,1)} %down_w.15, f32[384,1]{1,0:T(8,128)S(1)} %copy.44.factor_ref, bf16[8,128,48]{2,1,0:T(8,128)(2,1)S(1)} %get-tuple-element.231.spread_ref), custom_call_target="tpu_custom_call" | custom-call | flops 99090432 | bytes 458752 | tf_op jit(solution)/shard_map/down/pallas_call | solution.py:303
  382.2 13.7 %gate_up.7 = (bf16[384,1024]{1,0:T(8,128)(2,1)S(1)}, f32[8,128]{1,0:T(8,128)S(1)}) custom-call(f32[2]{0:T(128)S(1)} %pad_maximum_fusion.5.scale_ref, f32[2,1,1792]{2,1,0:T(1,128)S(1)} %maximum_multiply_fusion.gain_ref, bf16[8,48,128]{2,1,0:T(8,128)(2,1)S(1)} %get-tuple-element.238.chosen_ref, bf16[2,128,1792]{2,1,0:T(8,128)(2,1)S(1)} %copy-done.23, ...), custom_call_target="tpu_custom_call" | custom-call | flops 374341632 | bytes 1376256 | tf_op jit(solution)/shard_map/gate_up/pallas_call | solution.py:259
  410.8 19.7 %collective-permute-done.59 = bf16[2,128,1792]{2,1,0:T(8,128)(2,1)} collective-permute-done((bf16[2,128,1792]{2,1,0:T(8,128)(2,1)}, bf16[2,128,1792]{2,1,0:T(8,128)(2,1)}, u32[]{:S(2)}, u32[]{:S(2)}) %collective-permute-start.59) | collective-permute-done | bytes 917536 | tf_op jit(solution)/shard_map/ppermute | solution.py:105
  456.4 5.7 down.12
  462.1 6.8 %collective-permute-done.67 = bf16[2,128,1792]{2,1,0:T(8,128)(2,1)} collective-permute-done((bf16[2,128,1792]{2,1,0:T(8,128)(2,1)}, bf16[2,128,1792]{2,1,0:T(8,128)(2,1)}, u32[]{:S(2)}, u32[]{:S(2)}) %collective-permute-start.67) | collective-permute-done | bytes 917536 | tf_op jit(solution)/shard_map/ppermute | solution.py:105
  486.3 14.7 %collective-permute-done.69 = bf16[2,128,1792]{2,1,0:T(8,128)(2,1)} collective-permute-done((bf16[2,128,1792]{2,1,0:T(8,128)(2,1)}, bf16[2,128,1792]{2,1,0:T(8,128)(2,1)}, u32[]{:S(2)}, u32[]{:S(2)}) %collective-permute-start.69) | collective-permute-done | bytes 917536 | tf_op jit(solution)/shard_map/ppermute | solution.py:105
  509.7 17.1 %collective-permute-done.70 = bf16[2,128,1792]{2,1,0:T(8,128)(2,1)S(1)} collective-permute-done((bf16[2,128,1792]{2,1,0:T(8,128)(2,1)S(1)}, bf16[2,128,1792]{2,1,0:T(8,128)(2,1)S(1)}, u32[]{:S(2)}, u32[]{:S(2)}) %collective-permute-start.70) | collective-permute-done | bytes 917536 | tf_op jit(solution)/shard_map/ppermute | solution.py:105
  530.4 13.0 %collective-permute-done.73 = bf16[2,128,1792]{2,1,0:T(8,128)(2,1)S(1)} collective-permute-done((bf16[2,128,1792]{2,1,0:T(8,128)(2,1)S(1)}, bf16[2,128,1792]{2,1,0:T(8,128)(2,1)S(1)}, u32[]{:S(2)}, u32[]{:S(2)}) %collective-permute-start.73) | collective-permute-done | bytes 917536 | tf_op jit(solution)/shard_map/ppermute | solution.py:105
  (323 shorter events, 244.4 us)
Async XLA Ops:
  7.2 100.0 %reduce-scatter.5.cloned.1.call-start = ((), (), s32[]{:S(2)}) async-start(), calls=%async_computation.4 | async-start | bytes 2293760 | tf_op jit(solution)/shard_map/reduce_scatter | solution.py:369
  23.2 26.1 %collective-permute-start = (bf16[224,2048]{1,0:T(8,128)(2,1)S(1)}, bf16[224,2048]{1,0:T(8,128)(2,1)}, u32[]{:S(2)}, u32[]{:S(2)}) collective-permute-start(bf16[224,2048]{1,0:T(8,128)(2,1)S(1)} %get-tuple-element.228.refs_0_), channel_id=1, source_target_pairs={{0,4},{4,0},{8,12},{12,8},{16,20},{20,16},{24,28},{28,24},{1,5},{5... | collective-permute-start | bytes 2752520 | tf_op jit(solution)/shard_map/ppermute | solution.py:105
  60.9 128.2 %reduce-scatter.7.cloned.1.call-start = ((), (), s32[]{:S(2)}) async-start(), calls=%async_computation.5 | async-start | bytes 2293760 | tf_op jit(solution)/shard_map/reduce_scatter | solution.py:369
  60.9 28.1 %collective-permute-start.18 = (bf16[224,2048]{1,0:T(8,128)(2,1)S(1)}, bf16[224,2048]{1,0:T(8,128)(2,1)S(1)}, u32[]{:S(2)}, u32[]{:S(2)}) collective-permute-start(bf16[224,2048]{1,0:T(8,128)(2,1)S(1)} %get-tuple-element.112.refs_0_), channel_id=1, source_target_pairs={{0,8},{4,12},{8,0},{12,4},{16,24},{20,28},{24,16},{28,20},{1,9},{5... | collective-permute-start | bytes 2752520 | tf_op jit(solution)/shard_map/ppermute | solution.py:105
  61.5 31.3 %collective-permute-start.20 = (bf16[224,2048]{1,0:T(8,128)(2,1)S(1)}, bf16[224,2048]{1,0:T(8,128)(2,1)}, u32[]{:S(2)}, u32[]{:S(2)}) collective-permute-start(bf16[224,2048]{1,0:T(8,128)(2,1)S(1)} %get-tuple-element.112.refs_0_), channel_id=1, source_target_pairs={{0,16},{4,20},{8,24},{12,28},{16,0},{20,4},{24,8},{28,12},{1,17},{... | collective-permute-start | bytes 2752520 | tf_op jit(solution)/shard_map/ppermute | solution.py:105
  144.9 404.3 %reduce-scatter.9.cloned.1.call-start = ((), (), s32[]{:S(2)}) async-start(), calls=%async_computation.6 | async-start | bytes 2293760 | tf_op jit(solution)/shard_map/reduce_scatter | solution.py:484
  145.0 34.9 %collective-permute-start.28 = (bf16[128,1792]{1,0:T(8,128)(2,1)}, bf16[128,1792]{1,0:T(8,128)(2,1)S(1)}, u32[]{:S(2)}, u32[]{:S(2)}) collective-permute-start(bf16[128,1792]{1,0:T(8,128)(2,1)} %collective-permute-done.27), channel_id=1, source_target_pairs={{1,0},{5,4},{9,8},{13,12},{17,16},{21,20},{25,24},{29,28}} | collective-permute-start | bytes 1376264 | tf_op jit(solution)/shard_map/ppermute | solution.py:115
  148.4 34.2 %collective-permute-start.29 = (bf16[128,1792]{1,0:T(8,128)(2,1)}, bf16[128,1792]{1,0:T(8,128)(2,1)S(1)}, u32[]{:S(2)}, u32[]{:S(2)}) collective-permute-start(bf16[128,1792]{1,0:T(8,128)(2,1)} %collective-permute-done.26), channel_id=1, source_target_pairs={{2,3},{6,7},{10,11},{14,15},{18,19},{22,23},{26,27},{30,31}} | collective-permute-start | bytes 1376264 | tf_op jit(solution)/shard_map/ppermute | solution.py:115
  184.5 36.1 %collective-permute-start.30 = (bf16[4,128,1792]{2,1,0:T(8,128)(2,1)}, bf16[4,128,1792]{2,1,0:T(8,128)(2,1)}, u32[]{:S(2)}, u32[]{:S(2)}) collective-permute-start(bf16[4,128,1792]{2,1,0:T(8,128)(2,1)} %bitcast_dynamic-update-slice_fusion.4.refs_0_), channel_id=1, source_target_pairs={{0,8},{4,12},{8,0},{12,4},{16,24},{20,28},{24,16},{28,20},{1,9},{5... | collective-permute-start | bytes 5505032 | tf_op jit(solution)/shard_map/ppermute | solution.py:105
  184.5 37.8 %collective-permute-start.31 = (bf16[4,128,1792]{2,1,0:T(8,128)(2,1)}, bf16[4,128,1792]{2,1,0:T(8,128)(2,1)}, u32[]{:S(2)}, u32[]{:S(2)}) collective-permute-start(bf16[4,128,1792]{2,1,0:T(8,128)(2,1)} %bitcast_dynamic-update-slice_fusion.4.refs_0_), channel_id=1, source_target_pairs={{0,16},{4,20},{8,24},{12,28},{16,0},{20,4},{24,8},{28,12},{1,17},{... | collective-permute-start | bytes 5505032 | tf_op jit(solution)/shard_map/ppermute | solution.py:105
  241.2 33.4 %collective-permute-start.42 = (bf16[4,128,1792]{2,1,0:T(8,128)(2,1)}, bf16[4,128,1792]{2,1,0:T(8,128)(2,1)}, u32[]{:S(2)}, u32[]{:S(2)}) collective-permute-start(bf16[4,128,1792]{2,1,0:T(8,128)(2,1)} %bitcast_dynamic-update-slice_fusion.4.refs_0_), channel_id=1, source_target_pairs={{0,4},{4,0},{8,12},{12,8},{16,20},{20,16},{24,28},{28,24},{1,5},{5... | collective-permute-start | bytes 5505032 | tf_op jit(solution)/shard_map/ppermute | solution.py:105
  271.3 42.8 %collective-permute-start.40 = (bf16[4,128,1792]{2,1,0:T(8,128)(2,1)}, bf16[4,128,1792]{2,1,0:T(8,128)(2,1)}, u32[]{:S(2)}, u32[]{:S(2)}) collective-permute-start(bf16[4,128,1792]{2,1,0:T(8,128)(2,1)} %bitcast_dynamic-update-slice_fusion.refs_2_), channel_id=1, source_target_pairs={{0,8},{4,12},{8,0},{12,4},{16,24},{20,28},{24,16},{28,20},{1,9},{5... | collective-permute-start | bytes 5505032 | tf_op jit(solution)/shard_map/ppermute | solution.py:105
  271.4 42.8 %collective-permute-start.41 = (bf16[4,128,1792]{2,1,0:T(8,128)(2,1)}, bf16[4,128,1792]{2,1,0:T(8,128)(2,1)}, u32[]{:S(2)}, u32[]{:S(2)}) collective-permute-start(bf16[4,128,1792]{2,1,0:T(8,128)(2,1)} %bitcast_dynamic-update-slice_fusion.refs_2_), channel_id=1, source_target_pairs={{0,16},{4,20},{8,24},{12,28},{16,0},{20,4},{24,8},{28,12},{1,17},{... | collective-permute-start | bytes 5505032 | tf_op jit(solution)/shard_map/ppermute | solution.py:105
  274.3 46.3 %collective-permute-start.48 = (bf16[4,128,1792]{2,1,0:T(8,128)(2,1)}, bf16[4,128,1792]{2,1,0:T(8,128)(2,1)}, u32[]{:S(2)}, u32[]{:S(2)}) collective-permute-start(bf16[4,128,1792]{2,1,0:T(8,128)(2,1)} %collective-permute-done.30.refs_0_), channel_id=1, source_target_pairs={{0,4},{4,0},{8,12},{12,8},{16,20},{20,16},{24,28},{28,24},{1,5},{5... | collective-permute-start | bytes 5505032 | tf_op jit(solution)/shard_map/ppermute | solution.py:105
  319.1 32.1 %collective-permute-start.46 = (bf16[2,128,1792]{2,1,0:T(8,128)(2,1)}, bf16[2,128,1792]{2,1,0:T(8,128)(2,1)}, u32[]{:S(2)}, u32[]{:S(2)}) collective-permute-start(bf16[2,128,1792]{2,1,0:T(8,128)(2,1)} %slice.204), channel_id=1, source_target_pairs={{0,16},{4,20},{8,24},{12,28},{16,0},{20,4},{24,8},{28,12},{1,17},{... | collective-permute-start | bytes 2752520 | tf_op jit(solution)/shard_map/ppermute | solution.py:105
  320.6 30.7 %collective-permute-start.47 = (bf16[2,128,1792]{2,1,0:T(8,128)(2,1)}, bf16[2,128,1792]{2,1,0:T(8,128)(2,1)}, u32[]{:S(2)}, u32[]{:S(2)}) collective-permute-start(bf16[2,128,1792]{2,1,0:T(8,128)(2,1)} %slice.205), channel_id=1, source_target_pairs={{0,8},{4,12},{8,0},{12,4},{16,24},{20,28},{24,16},{28,20},{1,9},{5... | collective-permute-start | bytes 2752520 | tf_op jit(solution)/shard_map/ppermute | solution.py:105
  438.5 36.5 %collective-permute-start.65 = (bf16[4,128,1792]{2,1,0:T(8,128)(2,1)S(1)}, bf16[4,128,1792]{2,1,0:T(8,128)(2,1)}, u32[]{:S(2)}, u32[]{:S(2)}) collective-permute-start(bf16[4,128,1792]{2,1,0:T(8,128)(2,1)S(1)} %get-tuple-element.189), channel_id=1, source_target_pairs={{0,4},{4,0},{8,12},{12,8},{16,20},{20,16},{24,28},{28,24},{1,5},{5... | collective-permute-start | bytes 5505032 | tf_op jit(solution)/shard_map/ppermute | solution.py:105
  443.4 28.1 %collective-permute-start.66 = (bf16[4,128,1792]{2,1,0:T(8,128)(2,1)S(1)}, bf16[4,128,1792]{2,1,0:T(8,128)(2,1)}, u32[]{:S(2)}, u32[]{:S(2)}) collective-permute-start(bf16[4,128,1792]{2,1,0:T(8,128)(2,1)S(1)} %get-tuple-element.191), channel_id=1, source_target_pairs={{0,4},{4,0},{8,12},{12,8},{16,20},{20,16},{24,28},{28,24},{1,5},{5... | collective-permute-start | bytes 5505032 | tf_op jit(solution)/shard_map/ppermute | solution.py:105
  456.4 29.9 %collective-permute-start.64 = (bf16[4,128,1792]{2,1,0:T(8,128)(2,1)}, bf16[4,128,1792]{2,1,0:T(8,128)(2,1)}, u32[]{:S(2)}, u32[]{:S(2)}) collective-permute-start(bf16[4,128,1792]{2,1,0:T(8,128)(2,1)} %get-tuple-element.186), channel_id=1, source_target_pairs={{0,4},{4,0},{8,12},{12,8},{16,20},{20,16},{24,28},{28,24},{1,5},{5... | collective-permute-start | bytes 5505032 | tf_op jit(solution)/shard_map/ppermute | solution.py:105
  468.9 36.1 %collective-permute-start.62 = (bf16[4,128,1792]{2,1,0:T(8,128)(2,1)}, bf16[4,128,1792]{2,1,0:T(8,128)(2,1)}, u32[]{:S(2)}, u32[]{:S(2)}) collective-permute-start(bf16[4,128,1792]{2,1,0:T(8,128)(2,1)} %get-tuple-element.183), channel_id=1, source_target_pairs={{0,4},{4,0},{8,12},{12,8},{16,20},{20,16},{24,28},{28,24},{1,5},{5... | collective-permute-start | bytes 5505032 | tf_op jit(solution)/shard_map/ppermute | solution.py:105
  479.9 105.2 %reduce-scatter.11.cloned.1.call-start = ((), (), s32[]{:S(2)}) async-start(), calls=%async_computation.7 | async-start | bytes 2293760 | tf_op jit(solution)/shard_map/reduce_scatter | solution.py:495
  480.0 25.0 %collective-permute-start.71 = (bf16[2,128,1792]{2,1,0:T(8,128)(2,1)}, bf16[2,128,1792]{2,1,0:T(8,128)(2,1)S(1)}, u32[]{:S(2)}, u32[]{:S(2)}) collective-permute-start(bf16[2,128,1792]{2,1,0:T(8,128)(2,1)} %get-tuple-element.199), channel_id=1, source_target_pairs={{0,16},{4,20},{8,24},{12,28},{16,0},{20,4},{24,8},{28,12},{1,17},{... | collective-permute-start | bytes 2752520 | tf_op jit(solution)/shard_map/ppermute | solution.py:105
  507.5 36.0 %collective-permute-start.73 = (bf16[2,128,1792]{2,1,0:T(8,128)(2,1)S(1)}, bf16[2,128,1792]{2,1,0:T(8,128)(2,1)S(1)}, u32[]{:S(2)}, u32[]{:S(2)}) collective-permute-start(bf16[2,128,1792]{2,1,0:T(8,128)(2,1)S(1)} %get-tuple-element.216), channel_id=1, source_target_pairs={{0,16},{4,20},{8,24},{12,28},{16,0},{20,4},{24,8},{28,12},{1,17},{... | collective-permute-start | bytes 2752520 | tf_op jit(solution)/shard_map/ppermute | solution.py:105
  508.1 38.7 %collective-permute-start.72 = (bf16[2,128,1792]{2,1,0:T(8,128)(2,1)S(1)}, bf16[2,128,1792]{2,1,0:T(8,128)(2,1)S(1)}, u32[]{:S(2)}, u32[]{:S(2)}) collective-permute-start(bf16[2,128,1792]{2,1,0:T(8,128)(2,1)S(1)} %get-tuple-element.214), channel_id=1, source_target_pairs={{0,8},{4,12},{8,0},{12,4},{16,24},{20,28},{24,16},{28,20},{1,9},{5... | collective-permute-start | bytes 2752520 | tf_op jit(solution)/shard_map/ppermute | solution.py:105
  (95 other events, 1199.5 us)
Sparse Core Ops, SparseCore 0:
  61.0 38.7 reduce-scatter.4
  145.0 44.0 reduce-scatter.6
  480.0 37.7 reduce-scatter.8
  549.3 35.7 reduce-scatter.10

commit v8 on v7

--- a/solution.py
+++ b/solution.py
@@ -199,33 +199,53 @@
     )(place, attn_out, *pieces)
 
 
-def gate_up_kernel(parts, scale_ref, gain_ref, chosen_ref, *refs):
+def pick(chosen_ref, pieces):
+    source = 0
+    for piece in pieces:
+        for i in range(piece.shape[0]):
+            yield jnp.dot(chosen_ref[source], piece[i], preferred_element_type=jnp.float32)
+            source += 1
+
+
+def rows_kernel(chosen_ref, *refs):
+    *pieces, rows_ref, squares_ref = refs
+    capacity = chosen_ref.shape[1]
+    for source, picked in enumerate(pick(chosen_ref, pieces)):
+        span = slice(source * capacity, (source + 1) * capacity)
+        rows_ref[span] = picked.astype(rows_ref.dtype)
+        squares_ref[span] = jnp.sum(picked * picked, axis=1, keepdims=True)
+
+
+def rows_of(chosen, pieces):
+    sources, capacity, tokens = chosen.shape
+    rows, step = sources * capacity, pieces[0].shape[-1]
+    return pl.pallas_call(
+        rows_kernel,
+        out_shape=[
+            jax.ShapeDtypeStruct((rows, step), jnp.bfloat16),
+            jax.ShapeDtypeStruct((rows, 1), jnp.float32),
+        ],
+        compiler_params=pltpu.CompilerParams(vmem_limit_bytes=VMEM_LIMIT),
+        cost_estimate=cost(2 * rows * step * tokens, 2 * step * sources * tokens),
+        name="rows",
+    )(chosen, *pieces)
+
+
+def gate_up_kernel(scale_ref, gain_ref, chosen_ref, first_ref, squares_ref, *refs):
     hidden_ref, peak_ref, rows = refs[-3:]
-    weights, pieces = refs[-3 - 2 * parts : -3], refs[: -3 - 2 * parts]
-    per_part = len(pieces) // parts
+    weights, pieces = refs[-7:-3], refs[:-7]
     capacity = chosen_ref.shape[1]
     step = rows.shape[2]
 
     @pl.when(pl.program_id(0) == 0)
     def _():
-        source = 0
-        for p in range(per_part):
-            for i in range(pieces[p].shape[0]):
-                span = slice(source * capacity, (source + 1) * capacity)
-                picked = [
-                    jnp.dot(
-                        chosen_ref[source],
-                        pieces[c * per_part + p][i],
-                        preferred_element_type=jnp.float32,
-                    )
-                    for c in range(parts)
-                ]
-                squares = sum(jnp.sum(x * x, axis=1, keepdims=True) for x in picked)
-                root = lax.rsqrt(squares / (parts * step) + 1e-06)
-                for c, x in enumerate(picked):
-                    x = jnp.clip(x * root * gain_ref[c], -FP8_LIMIT, FP8_LIMIT)
-                    rows[c, span] = x.astype(rows.dtype)
-                source += 1
+        for source, picked in enumerate(pick(chosen_ref, pieces)):
+            span = slice(source * capacity, (source + 1) * capacity)
+            squares = squares_ref[span] + jnp.sum(picked * picked, axis=1, keepdims=True)
+            root = lax.rsqrt(squares / (2 * step) + 1e-06)
+            for c, x in enumerate((first_ref[span].astype(jnp.float32), picked)):
+                x = jnp.clip(x * root * gain_ref[c], -FP8_LIMIT, FP8_LIMIT)
+                rows[c, span] = x.astype(rows.dtype)
 
     def product(side):
         return sum(
@@ -234,7 +254,7 @@
                 weights[2 * c + side][0].reshape(step, -1),
                 preferred_element_type=jnp.float32,
             )
-            for c in range(parts)
+            for c in range(2)
         )
 
     gate, up = product(0) * scale_ref[0], product(1) * scale_ref[0]
@@ -246,7 +266,7 @@
     peak_ref[...] = jnp.where(first, peak, jnp.maximum(peak_ref[...], peak))
 
 
-def gate_up(scales, gains, chosen, pieces, w_gate, w_up):
+def gate_up(scales, gains, chosen, first, pieces, w_gate, w_up):
     sources, capacity, tokens = chosen.shape
     parts, _, step = gains.shape
     owners, columns, hidden = w_gate.shape[1], w_gate.shape[3], w_gate.shape[-1]
@@ -254,15 +274,18 @@
     rows = sources * capacity
     once = pl.Buffered(buffer_count=1)
     whole = lambda a: pl.BlockSpec(a.shape, lambda n: (0,) * a.ndim, pipeline_mode=once)
-    column = lambda height: pl.BlockSpec((height, tile), lambda n: (0, n))
     weight = lambda c: pl.BlockSpec((1, owners, None, columns, tile), lambda n: (0, 0, c, 0, n))
     return pl.pallas_call(
-        functools.partial(gate_up_kernel, parts),
+        gate_up_kernel,
         grid=(hidden // tile,),
         in_specs=[pl.BlockSpec(memory_space=pltpu.SMEM), whole(gains), whole(chosen)]
+        + [whole(a) for a in first]
         + [whole(p) for p in pieces]
         + [weight(c) for c in range(parts) for _ in range(2)],
-        out_specs=[column(rows), pl.BlockSpec((8, 128), lambda n: (0, 0))],
+        out_specs=[
+            pl.BlockSpec((rows, tile), lambda n: (0, n)),
+            pl.BlockSpec((8, 128), lambda n: (0, 0)),
+        ],
         out_shape=[
             jax.ShapeDtypeStruct((rows, hidden), jnp.bfloat16),
             jax.ShapeDtypeStruct((8, 128), jnp.float32),
@@ -274,7 +297,7 @@
             2 * parts * step * (2 * hidden + sources * tokens),
         ),
         name="gate_up",
-    )(scales, gains, chosen, *pieces, *([w_gate, w_up] * parts))
+    )(scales, gains, chosen, *first, *pieces, *([w_gate, w_up] * parts))
 
 
 def down_kernel(hidden_ref, down_w, factor_ref, spread_ref, own_ref, other_ref):
@@ -376,28 +399,28 @@
     near, table = tie(near, table)
     groups = [[weight_rows[0]], [near[0]], [near[1]], diagonal(*near)]
     terms = project_part(place, attn_out, [both_cores(group) for group in groups])
-    terms, table, weight_rows[1] = tie(terms, table, weight_rows[1])
-    weight = expert_weights(table)
+    terms, weight_rows[1] = tie(terms, weight_rows[1])
     near = neighbours(weight_rows[1])
     groups = [[weight_rows[1]], [near[0]], [near[1]], diagonal(*near)]
     groups = [both_cores(group) for group in groups]
     first, sent = summed_over_tensor(terms, 0)
-    sent, weight = tie(sent, weight)
-
-    second = []
+
+    beside = {}
 
     def at_hop(hop, arrived):
         if hop == 1:
-            arrived, tied = tie(arrived, groups)
-            second.append(project_part(place, attn_out, tied))
-        if hop == 2:
-            arrived, terms = tie(arrived, second.pop())
-            second.append(summed_over_tensor(terms, 1))
+            arrived, tied, routes = tie(arrived, groups, table)
+            beside["terms"] = project_part(place, attn_out, tied)
+            beside["weight"] = expert_weights(routes)
+        if hop == layers - 1:
+            arrived, terms, weight = tie(arrived, beside["terms"], beside["weight"])
+            beside["sum"], beside["weight"] = summed_over_tensor(terms, 1), weight
         return arrived
 
     own = along_tensor(sent, at_hop)
-    stream = [first, second[0][0]]
-    sent = second[0][1]
+    weight = beside["weight"]
+    stream = [first, beside["sum"][0]]
+    sent = beside["sum"][1]
 
     named = weight > 0.0
     earlier = jnp.triu(jnp.ones((local_rows, local_rows), jnp.bfloat16), 1)
@@ -427,38 +450,35 @@
     gate_rows = w_gate.reshape(1, owners, CHUNKS, columns, -1)
     up_rows = w_up.reshape(1, owners, CHUNKS, columns, -1)
 
-    def hidden_of(r, tokens, choice):
-        pieces = [piece for part in tokens for piece in part]
-        return gate_up(scales, gains, choice[r], pieces, gate_rows, up_rows)
-
-    groups = [[] for _ in range(4)]
-    for c in range(CHUNKS):
-        along_x, along_y = neighbours(own)
-        groups[0].append(both_cores([own]))
-        if c + 1 < CHUNKS:
-            along_x, along_y, sent = tie(along_x, along_y, sent)
-            across = diagonal(along_x, along_y)
-
-            def at_hop(hop, arrived):
-                nonlocal across
-                if hop == 2:
-                    arrived, across = tie(arrived, across)
-                return arrived
-
-            own = along_tensor(sent, at_hop)
-        else:
-            hidden = [hidden_of(0, groups[0], choice)]
-            stream = natural(stream, columns)
-            along_x, along_y, hidden[0], stream, groups[3], choice, spread, factor = tie(
-                along_x, along_y, hidden[0], stream, groups[3], choice, spread, factor
-            )
-        groups[1].append(both_cores([along_x]))
-        groups[2].append(both_cores([along_y]))
-        if c + 1 == CHUNKS:
-            across = diagonal(along_x, along_y)
-            hidden += [hidden_of(1, groups[1], choice), hidden_of(2, groups[2], choice)]
-            across, hidden = tie(across, hidden)
-        groups[3].append(both_cores(across))
+    def hidden_of(r, choice):
+        rows, pieces = groups[r]
+        return gate_up(scales, gains, choice[r], rows, pieces, gate_rows, up_rows)
+
+    along_x, along_y = neighbours(own)
+    first = [[own], [along_x], [along_y]]
+    along_x, along_y, sent = tie(along_x, along_y, sent)
+    across = diagonal(along_x, along_y)
+
+    def at_middle_hop(hop, arrived):
+        nonlocal across
+        if hop == 2:
+            arrived, across = tie(arrived, across)
+        return arrived
+
+    own = along_tensor(sent, at_middle_hop)
+    first = [rows_of(choice[r], both_cores(p)) for r, p in enumerate(first + [across])]
+    along_x, along_y = neighbours(own)
+    groups = [(first[0], both_cores([own]))]
+    hidden = [hidden_of(0, choice)]
+    stream = natural(stream, columns)
+    along_x, along_y, hidden[0], stream, first, choice, spread, factor = tie(
+        along_x, along_y, hidden[0], stream, first, choice, spread, factor
+    )
+    across = diagonal(along_x, along_y)
+    groups += [(first[1], both_cores([along_x])), (first[2], both_cores([along_y]))]
+    hidden += [hidden_of(1, choice), hidden_of(2, choice)]
+    across, hidden = tie(across, hidden)
+    groups.append((first[3], both_cores(across)))
 
     def outputs(r, c):
         return down(hidden[r][0], w_down, factor[r], spread[r], c, step)
@@ -470,7 +490,7 @@
     summed = lambda r, c: [add(*terms) for terms in halves(*outputs(r, c))]
     to_x, to_y = summed(1, 0), summed(2, 0)
     groups[3], to_x, to_y = tie(groups[3], to_x, to_y)
-    hidden.append(hidden_of(3, groups[3], choice))
+    hidden.append(hidden_of(3, choice))
     peak_h = jnp.max(jnp.stack([peaks for _, peaks in hidden]))
     mixture = []
     for c in range(CHUNKS):
@@ -480,16 +500,20 @@
             given, early_x, early_y = tie(given, early_x, early_y)
         beyond = [add(*terms) for terms in halves(kept, given)]
         if c > 0:
-            beyond, mixed = tie(beyond, mixed)
+            beyond, early_x, early_y, mixed = tie(beyond, early_x, early_y, mixed)
             mixture.append(lax.psum_scatter(mixed, "tensor", scatter_dimension=0, tiled=True))
         over_x, over_y = swap(beyond[0], 2), swap(beyond[1], 4)
-        late_x, late_y = to_x[1], to_y[0]
+        to_own = outputs(0, c)
         if c + 1 < CHUNKS:
-            over_x, over_y, hidden = tie(over_x, over_y, hidden)
-            to_x, to_y = summed(1, c + 1), summed(2, c + 1)
-        to_own = halves(*outputs(0, c))
-        low = add(*to_own[0], early_x, swap(add(late_y, over_x), 4))
-        high = add(*to_own[1], swap(add(late_x, over_y), 2), early_y)
+            coming = outputs(1, c + 1), outputs(2, c + 1)
+            over_x, over_y, to_own, coming = tie(over_x, over_y, to_own, coming)
+        late_x, late_y = add(to_x[1], over_y), add(to_y[0], over_x)
+        if c + 1 < CHUNKS:
+            late_x, late_y, hidden = tie(late_x, late_y, hidden)
+            to_x, to_y = ([add(*terms) for terms in halves(*pair)] for pair in coming)
+        to_own = halves(*to_own)
+        low = add(*to_own[0], early_x, swap(late_y, 4))
+        high = add(*to_own[1], swap(late_x, 2), early_y)
         mixed = jnp.concatenate([low, high]).reshape(layers * local_rows, step)
     mixed, mixture = tie(mixed, mixture)
     mixture.append(lax.psum_scatter(mixed, "tensor", scatter_dimension=0, tiled=True))

time: 599 us -> 556 us (0.928)
  waiting for transfers between devices: 309 us -> 238 us
  starting transfers between devices: 56.6 us -> 74 us
  local copies, waits for them, and re-layouts: 32.2 us -> 45.6 us
    ppermute x59, waiting for transfers between devices: 197 us -> 145 us  [swap(): return lax.ppermute(value, 'dp', [(i, i ^ bits) for i in range(count)])]
    ppermute x6, waiting for transfers between devices: 69.6 us -> 31.6 us  [along_tensor(): lax.ppermute(above, 'tensor', back)]
    reduce_scatter x2, waiting for transfers between devices: 3.55 us -> 22.3 us  [summed_over_tensor(): total = lax.psum_scatter(terms, 'tensor', scatter_dimension=0, tiled=True)]
    reduce_scatter x2, starting transfers between devices: 0.08 us -> 11.3 us  [gather_plan(): lax.psum_scatter(mixed, 'tensor', scatter_dimension=0, tiled=True)]
    unnamed x73 -> x105, local copies, waits for them, and re-layouts: 8.88 us -> 20 us
    pallas_call x8, Pallas kernels: 49.2 us -> 42.4 us  [down(): pl.pallas_call(down_kernel, grid=(tiles,), in_specs=[whole(hidden_q.shape...]
    pallas_call x4 -> x8, Pallas kernels: 55.4 us -> 58 us  [the longest x4 48.4 us: gate_up(): pl.pallas_call(gate_up_kernel, grid=(hidden // tile,), in_specs=[pl.Block...]
    convert_element_type x10 -> x11, other arithmetic: 23.1 us -> 22.7 us  [add(): return sum((t.astype(jnp.float32) for t in terms)).astype(jnp.bfloat16)]
  transfers between devices with their start and end apart: 83 -> 83, of which waited for: 44 -> 42; matrix products, arithmetic and copies ran while one was open for 12% -> 14% of each run, Pallas kernels for 18% -> 19%
where the time goes in v8:
time: 556 us; the launch traced here: 552 us
  waiting for transfers between devices  238 us (43%)
  Pallas kernels  120 us (22%)
  starting transfers between devices  74 us (13%)
  other arithmetic  53.2 us (10%)
  local copies, waits for them, and re-layouts  45.6 us (8%)
  between operations  21.3 us (4%)
    ppermute x59, waiting for transfers between devices, swap(): return lax.ppermute(value, 'dp', [(i, i ^ bits) for i in range(count)])  145 us
    pallas_call x4, Pallas kernels, gate_up(): pl.pallas_call(gate_up_kernel, grid=(hidden // tile,), in_specs=[pl.Block...  48.4 us
    pallas_call x8, Pallas kernels, down(): pl.pallas_call(down_kernel, grid=(tiles,), in_specs=[whole(hidden_q.shape...  42.4 us
    ppermute x59, starting transfers between devices, swap(): return lax.ppermute(value, 'dp', [(i, i ^ bits) for i in range(count)])  35.3 us
    ppermute x6, waiting for transfers between devices, along_tensor(): lax.ppermute(above, 'tensor', back)  31.6 us
    convert_element_type x11, other arithmetic, add(): return sum((t.astype(jnp.float32) for t in terms)).astype(jnp.bfloat16)  22.7 us
    reduce_scatter x2, waiting for transfers between devices, summed_over_tensor(): total = lax.psum_scatter(terms, 'tensor', scatter_dimension=0, tiled=True)  22.3 us
    ppermute x5, waiting for transfers between devices, peaks_over_all(): peaks = jnp.maximum(peaks, lax.ppermute(peaks, axis, pairs))  20.1 us
  transfers between devices with their start and end apart: 83, of which 42 were waited for; matrix products, arithmetic and copies ran while one was open for 14% of the time, Pallas kernels for 19%

profile of v8, /device:TPU:0, one launch (start us, length us, event | category | flops | bytes accessed | tf_op | source)
XLA Modules:
  0.0 552.1 jit_solution(3239771990076928800)
XLA Ops:
  24.5 7.7 %collective-permute-done.1.refs_2_ = bf16[224,2048]{1,0:T(8,128)(2,1)S(1)} collective-permute-done((bf16[224,2048]{1,0:T(8,128)(2,1)S(1)}, bf16[224,2048]{1,0:T(8,128)(2,1)S(1)}, u32[]{:S(2)}, u32[]{:S(2)}) %collective-permute-start.1) | collective-permute-done | bytes 917536 | tf_op jit(solution)/shard_map/ppermute | solution.py:105
  37.5 9.3 %collective-permute-done.9.refs_6_ = bf16[112,2048]{1,0:T(8,128)(2,1)S(1)} collective-permute-done((bf16[112,2048]{1,0:T(8,128)(2,1)S(1)}, bf16[112,2048]{1,0:T(8,128)(2,1)S(1)}, u32[]{:S(2)}, u32[]{:S(2)}) %collective-permute-start.9) | collective-permute-done | bytes 458784 | tf_op jit(solution)/shard_map/ppermute | solution.py:105
  51.5 9.4 %project.2 = bf16[512,1792]{1,0:T(8,128)(2,1)} custom-call(s32[1]{0:T(128)} %bitcast.2.place_ref, bf16[512,2048]{1,0:T(8,128)(2,1)} %attn_ref.3, bf16[224,2048]{1,0:T(8,128)(2,1)S(1)} %get-tuple-element.256.refs_0_, bf16[224,2048]{1,0:T(8,128)(2,1)} %collective-permute-done.refs_1_, bf16[224,2048]{1,0:T(8,128)(2,1)S(1)} %collective-permute-done.1.refs_2_, ...), custom_call_target="tpu_custom_call" | custom-call | flops 234881024 | bytes 589824 | tf_op jit(solution)/shard_map/project/pallas_call | solution.py:186
  64.3 19.1 %collective-permute-done.16.refs_2_ = bf16[224,2048]{1,0:T(8,128)(2,1)S(1)} collective-permute-done((bf16[224,2048]{1,0:T(8,128)(2,1)S(1)}, bf16[224,2048]{1,0:T(8,128)(2,1)S(1)}, u32[]{:S(2)}, u32[]{:S(2)}) %collective-permute-start.16) | collective-permute-done | bytes 917536 | tf_op jit(solution)/shard_map/ppermute | solution.py:105
  89.0 7.3 %collective-permute-done.20.refs_6_ = bf16[112,2048]{1,0:T(8,128)(2,1)S(1)} collective-permute-done((bf16[112,2048]{1,0:T(8,128)(2,1)}, bf16[112,2048]{1,0:T(8,128)(2,1)S(1)}, u32[]{:S(2)}, u32[]{:S(2)}) %collective-permute-start.20) | collective-permute-done | bytes 458784 | tf_op jit(solution)/shard_map/ppermute | solution.py:105
  107.5 8.7 %collective-permute-done.13 = bf16[128,1792]{1,0:T(8,128)(2,1)S(1)} collective-permute-done((bf16[128,1792]{1,0:T(8,128)(2,1)S(1)}, bf16[128,1792]{1,0:T(8,128)(2,1)S(1)}, u32[]{:S(2)}, u32[]{:S(2)}) %collective-permute-start.13) | collective-permute-done | bytes 458784 | tf_op jit(solution)/shard_map/ppermute | solution.py:115
  125.6 12.4 %collective-permute-done.26 = bf16[128,1792]{1,0:T(8,128)(2,1)} collective-permute-done((bf16[128,1792]{1,0:T(8,128)(2,1)S(1)}, bf16[128,1792]{1,0:T(8,128)(2,1)}, u32[]{:S(2)}, u32[]{:S(2)}) %collective-permute-start.26) | collective-permute-done | bytes 458784 | tf_op jit(solution)/shard_map/ppermute | solution.py:115
  141.5 9.5 %project.3 = bf16[512,1792]{1,0:T(8,128)(2,1)} custom-call(s32[1]{0:T(128)} %bitcast.2.place_ref, bf16[512,2048]{1,0:T(8,128)(2,1)} %attn_ref.3, bf16[224,2048]{1,0:T(8,128)(2,1)S(1)} %get-tuple-element.125.refs_0_, bf16[224,2048]{1,0:T(8,128)(2,1)} %collective-permute-done.15.refs_1_, bf16[224,2048]{1,0:T(8,128)(2,1)S(1)} %collective-permute-done.16.refs_2_, ...), custom_call_target="tpu_custom_call" | custom-call | flops 234881024 | bytes 589824 | tf_op jit(solution)/shard_map/project/pallas_call | solution.py:186
  152.0 11.3 %reduce-scatter.9.cloned.1.call-start = ((), (), s32[]{:S(2)}) async-start(), calls=%async_computation.6 | async-start | bytes 2293760 | tf_op jit(solution)/shard_map/reduce_scatter | solution.py:504
  169.7 21.0 %reduce-scatter.7.cloned.1.call-done = bf16[128,1792]{1,0:T(8,128)(2,1)} async-done(((bf16[512,1792]{1,0:T(8,128)(2,1)}), bf16[128,1792]{1,0:T(8,128)(2,1)}) %reduce-scatter.7.cloned.1.call-update) | async-done | bytes 458768 | tf_op jit(solution)/shard_map/reduce_scatter | solution.py:392
  192.8 15.8 %collective-permute-done.30.refs_0_ = bf16[4,128,1792]{2,1,0:T(8,128)(2,1)} collective-permute-done((bf16[4,128,1792]{2,1,0:T(8,128)(2,1)}, bf16[4,128,1792]{2,1,0:T(8,128)(2,1)}, u32[]{:S(2)}, u32[]{:S(2)}) %collective-permute-start.30) | collective-permute-done | bytes 1835040 | tf_op jit(solution)/shard_map/ppermute | solution.py:105
  242.6 7.6 %collective-permute-done.38 = bf16[128,1792]{1,0:T(8,128)(2,1)S(1)} collective-permute-done((bf16[128,1792]{1,0:T(8,128)(2,1)}, bf16[128,1792]{1,0:T(8,128)(2,1)S(1)}, u32[]{:S(2)}, u32[]{:S(2)}) %collective-permute-start.38) | collective-permute-done | bytes 458784 | tf_op jit(solution)/shard_map/ppermute | solution.py:115
  279.9 12.2 %gate_up.4 = (bf16[384,1024]{1,0:T(8,128)(2,1)S(1)}, f32[8,128]{1,0:T(8,128)S(1)}) custom-call(f32[2]{0:T(128)S(1)} %pad_maximum_fusion.5.scale_ref, f32[2,1,1792]{2,1,0:T(1,128)S(1)} %maximum_multiply_fusion.gain_ref, bf16[8,48,128]{2,1,0:T(8,128)(2,1)S(1)} %bitcast.77, bf16[384,1792]{1,0:T(8,128)(2,1)S(1)} %get-tuple-element.145.first_ref, ...), custom_call_target="tpu_custom_call" | custom-call | flops 374341632 | bytes 1376256 | tf_op jit(solution)/shard_map/gate_up/pallas_call | solution.py:278
  304.3 12.3 %gate_up.5 = (bf16[384,1024]{1,0:T(8,128)(2,1)S(1)}, f32[8,128]{1,0:T(8,128)S(1)}) custom-call(f32[2]{0:T(128)S(1)} %pad_maximum_fusion.5.scale_ref, f32[2,1,1792]{2,1,0:T(1,128)S(1)} %maximum_multiply_fusion.gain_ref, bf16[8,48,128]{2,1,0:T(8,128)(2,1)S(1)} %get-tuple-element.266.chosen_ref, bf16[384,1792]{1,0:T(8,128)(2,1)S(1)} %copy-done.29, ...), custom_call_target="tpu_custom_call" | custom-call | flops 374341632 | bytes 1376256 | tf_op jit(solution)/shard_map/gate_up/pallas_call | solution.py:278
  316.6 12.2 %gate_up.6 = (bf16[384,1024]{1,0:T(8,128)(2,1)S(1)}, f32[8,128]{1,0:T(8,128)S(1)}) custom-call(f32[2]{0:T(128)S(1)} %pad_maximum_fusion.5.scale_ref, f32[2,1,1792]{2,1,0:T(1,128)S(1)} %maximum_multiply_fusion.gain_ref, bf16[8,48,128]{2,1,0:T(8,128)(2,1)S(1)} %get-tuple-element.264.chosen_ref, bf16[384,1792]{1,0:T(8,128)(2,1)S(1)} %copy-done.27, ...), custom_call_target="tpu_custom_call" | custom-call | flops 374341632 | bytes 1376256 | tf_op jit(solution)/shard_map/gate_up/pallas_call | solution.py:278
  328.9 5.9 %down.8 = (bf16[4,128,1792]{2,1,0:T(8,128)(2,1)S(1)}, bf16[4,128,1792]{2,1,0:T(8,128)(2,1)}) custom-call(bf16[384,1024]{1,0:T(8,128)(2,1)S(1)} %get-tuple-element.175.hidden_ref, bf16[1,1024,3584]{2,1,0:T(8,128)(2,1)} %down_w.15, f32[384,1]{1,0:T(8,128)S(1)} %copy.43.factor_ref, bf16[8,128,48]{2,1,0:T(8,128)(2,1)S(1)} %get-tuple-element.260.spread_ref), custom_call_target="tpu_custom_call" | custom-call | flops 99090432 | bytes 458752 | tf_op jit(solution)/shard_map/down/pallas_call | solution.py:326
  359.1 11.6 %gate_up.7 = (bf16[384,1024]{1,0:T(8,128)(2,1)S(1)}, f32[8,128]{1,0:T(8,128)S(1)}) custom-call(f32[2]{0:T(128)S(1)} %pad_maximum_fusion.5.scale_ref, f32[2,1,1792]{2,1,0:T(1,128)S(1)} %maximum_multiply_fusion.gain_ref, bf16[8,48,128]{2,1,0:T(8,128)(2,1)S(1)} %get-tuple-element.265.chosen_ref, bf16[384,1792]{1,0:T(8,128)(2,1)S(1)} %copy-done.25, ...), custom_call_target="tpu_custom_call" | custom-call | flops 374341632 | bytes 1376256 | tf_op jit(solution)/shard_map/gate_up/pallas_call | solution.py:278
  385.0 5.6 %down.12 = (bf16[4,128,1792]{2,1,0:T(8,128)(2,1)S(1)}, bf16[4,128,1792]{2,1,0:T(8,128)(2,1)}) custom-call(bf16[384,1024]{1,0:T(8,128)(2,1)S(1)} %get-tuple-element.175.hidden_ref, bf16[1,1024,3584]{2,1,0:T(8,128)(2,1)} %down_w.15, f32[384,1]{1,0:T(8,128)S(1)} %copy-done.17, bf16[8,128,48]{2,1,0:T(8,128)(2,1)S(1)} %copy-done.7), custom_call_target="tpu_custom_call" | custom-call | flops 99090432 | bytes 458752 | tf_op jit(solution)/shard_map/down/pallas_call | solution.py:326
  390.7 6.2 %down.13 = (bf16[4,128,1792]{2,1,0:T(8,128)(2,1)S(1)}, bf16[4,128,1792]{2,1,0:T(8,128)(2,1)}) custom-call(bf16[384,1024]{1,0:T(8,128)(2,1)S(1)} %get-tuple-element.180.hidden_ref, bf16[1,1024,3584]{2,1,0:T(8,128)(2,1)} %down_w.15, f32[384,1]{1,0:T(8,128)S(1)} %copy-done.21, bf16[8,128,48]{2,1,0:T(8,128)(2,1)S(1)} %copy-done.5), custom_call_target="tpu_custom_call" | custom-call | flops 99090432 | bytes 458752 | tf_op jit(solution)/shard_map/down/pallas_call | solution.py:326
  418.7 16.9 %collective-permute-done.68 = bf16[2,128,1792]{2,1,0:T(8,128)(2,1)S(1)} collective-permute-done((bf16[2,128,1792]{2,1,0:T(8,128)(2,1)}, bf16[2,128,1792]{2,1,0:T(8,128)(2,1)S(1)}, u32[]{:S(2)}, u32[]{:S(2)}) %collective-permute-start.68) | collective-permute-done | bytes 917536 | tf_op jit(solution)/shard_map/ppermute | solution.py:105
  443.2 12.4 %collective-permute-done.64 = bf16[2,128,1792]{2,1,0:T(8,128)(2,1)} collective-permute-done((bf16[2,128,1792]{2,1,0:T(8,128)(2,1)S(1)}, bf16[2,128,1792]{2,1,0:T(8,128)(2,1)}, u32[]{:S(2)}, u32[]{:S(2)}) %collective-permute-start.64) | collective-permute-done | bytes 917536 | tf_op jit(solution)/shard_map/ppermute | solution.py:105
  464.4 13.8 %collective-permute-done.70 = bf16[2,128,1792]{2,1,0:T(8,128)(2,1)} collective-permute-done((bf16[2,128,1792]{2,1,0:T(8,128)(2,1)}, bf16[2,128,1792]{2,1,0:T(8,128)(2,1)}, u32[]{:S(2)}, u32[]{:S(2)}) %collective-permute-start.70) | collective-permute-done | bytes 917536 | tf_op jit(solution)/shard_map/ppermute | solution.py:105
  483.7 15.9 %collective-permute-done.71 = bf16[2,128,1792]{2,1,0:T(8,128)(2,1)S(1)} collective-permute-done((bf16[2,128,1792]{2,1,0:T(8,128)(2,1)S(1)}, bf16[2,128,1792]{2,1,0:T(8,128)(2,1)S(1)}, u32[]{:S(2)}, u32[]{:S(2)}) %collective-permute-start.71) | collective-permute-done | bytes 917536 | tf_op jit(solution)/shard_map/ppermute | solution.py:105
  537.1 6.1 %reduce-scatter.11.cloned.1.call-done = bf16[128,1792]{1,0:T(8,128)(2,1)} async-done(((bf16[512,1792]{1,0:T(8,128)(2,1)}), bf16[128,1792]{1,0:T(8,128)(2,1)}) %reduce-scatter.11.cloned.1.call-update) | async-done | bytes 458768 | tf_op jit(solution)/shard_map/reduce_scatter | solution.py:519
  (359 shorter events, 260.5 us)
Async XLA Ops:
  7.2 92.7 %reduce-scatter.5.cloned.1.call-start = ((), (), s32[]{:S(2)}) async-start(), calls=%async_computation.4 | async-start | bytes 2293760 | tf_op jit(solution)/shard_map/reduce_scatter | solution.py:392
  8.8 23.4 %collective-permute-start.1 = (bf16[224,2048]{1,0:T(8,128)(2,1)S(1)}, bf16[224,2048]{1,0:T(8,128)(2,1)S(1)}, u32[]{:S(2)}, u32[]{:S(2)}) collective-permute-start(bf16[224,2048]{1,0:T(8,128)(2,1)S(1)} %get-tuple-element.256.refs_0_), channel_id=1, source_target_pairs={{0,8},{4,12},{8,0},{12,4},{16,24},{20,28},{24,16},{28,20},{1,9},{5... | collective-permute-start | bytes 2752520 | tf_op jit(solution)/shard_map/ppermute | solution.py:105
  23.2 26.1 %collective-permute-start = (bf16[224,2048]{1,0:T(8,128)(2,1)S(1)}, bf16[224,2048]{1,0:T(8,128)(2,1)}, u32[]{:S(2)}, u32[]{:S(2)}) collective-permute-start(bf16[224,2048]{1,0:T(8,128)(2,1)S(1)} %get-tuple-element.256.refs_0_), channel_id=1, source_target_pairs={{0,4},{4,0},{8,12},{12,8},{16,20},{20,16},{24,28},{28,24},{1,5},{5... | collective-permute-start | bytes 2752520 | tf_op jit(solution)/shard_map/ppermute | solution.py:105
  60.9 129.8 %reduce-scatter.7.cloned.1.call-start = ((), (), s32[]{:S(2)}) async-start(), calls=%async_computation.5 | async-start | bytes 2293760 | tf_op jit(solution)/shard_map/reduce_scatter | solution.py:392
  61.6 23.2 %collective-permute-start.18 = (bf16[224,2048]{1,0:T(8,128)(2,1)S(1)}, bf16[224,2048]{1,0:T(8,128)(2,1)}, u32[]{:S(2)}, u32[]{:S(2)}) collective-permute-start(bf16[224,2048]{1,0:T(8,128)(2,1)S(1)} %get-tuple-element.125.refs_0_), channel_id=1, source_target_pairs={{0,16},{4,20},{8,24},{12,28},{16,0},{20,4},{24,8},{28,12},{1,17},{... | collective-permute-start | bytes 2752520 | tf_op jit(solution)/shard_map/ppermute | solution.py:105
  64.3 39.3 %collective-permute-start.15 = (bf16[224,2048]{1,0:T(8,128)(2,1)S(1)}, bf16[224,2048]{1,0:T(8,128)(2,1)}, u32[]{:S(2)}, u32[]{:S(2)}) collective-permute-start(bf16[224,2048]{1,0:T(8,128)(2,1)S(1)} %get-tuple-element.125.refs_0_), channel_id=1, source_target_pairs={{0,4},{4,0},{8,12},{12,8},{16,20},{20,16},{24,28},{28,24},{1,5},{5... | collective-permute-start | bytes 2752520 | tf_op jit(solution)/shard_map/ppermute | solution.py:105
  124.1 27.8 %collective-permute-start.25 = (bf16[128,1792]{1,0:T(8,128)(2,1)}, bf16[128,1792]{1,0:T(8,128)(2,1)}, u32[]{:S(2)}, u32[]{:S(2)}) collective-permute-start(bf16[128,1792]{1,0:T(8,128)(2,1)} %collective-permute-done.24), channel_id=1, source_target_pairs={{2,3},{6,7},{10,11},{14,15},{18,19},{22,23},{26,27},{30,31}} | collective-permute-start | bytes 1376264 | tf_op jit(solution)/shard_map/ppermute | solution.py:115
  152.0 353.5 %reduce-scatter.9.cloned.1.call-start = ((), (), s32[]{:S(2)}) async-start(), calls=%async_computation.6 | async-start | bytes 2293760 | tf_op jit(solution)/shard_map/reduce_scatter | solution.py:504
  168.2 40.4 %collective-permute-start.30 = (bf16[4,128,1792]{2,1,0:T(8,128)(2,1)}, bf16[4,128,1792]{2,1,0:T(8,128)(2,1)}, u32[]{:S(2)}, u32[]{:S(2)}) collective-permute-start(bf16[4,128,1792]{2,1,0:T(8,128)(2,1)} %bitcast_dynamic-update-slice_fusion.4.refs_0_), channel_id=1, source_target_pairs={{0,8},{4,12},{8,0},{12,4},{16,24},{20,28},{24,16},{28,20},{1,9},{5... | collective-permute-start | bytes 5505032 | tf_op jit(solution)/shard_map/ppermute | solution.py:105
  168.5 40.1 %collective-permute-start.31 = (bf16[4,128,1792]{2,1,0:T(8,128)(2,1)}, bf16[4,128,1792]{2,1,0:T(8,128)(2,1)}, u32[]{:S(2)}, u32[]{:S(2)}) collective-permute-start(bf16[4,128,1792]{2,1,0:T(8,128)(2,1)} %bitcast_dynamic-update-slice_fusion.4.refs_0_), channel_id=1, source_target_pairs={{0,16},{4,20},{8,24},{12,28},{16,0},{20,4},{24,8},{28,12},{1,17},{... | collective-permute-start | bytes 5505032 | tf_op jit(solution)/shard_map/ppermute | solution.py:105
  229.0 27.9 %collective-permute-start.42 = (bf16[4,128,1792]{2,1,0:T(8,128)(2,1)}, bf16[4,128,1792]{2,1,0:T(8,128)(2,1)S(1)}, u32[]{:S(2)}, u32[]{:S(2)}) collective-permute-start(bf16[4,128,1792]{2,1,0:T(8,128)(2,1)} %bitcast_dynamic-update-slice_fusion.4.refs_0_), channel_id=1, source_target_pairs={{0,4},{4,0},{8,12},{12,8},{16,20},{20,16},{24,28},{28,24},{1,5},{5... | collective-permute-start | bytes 5505032 | tf_op jit(solution)/shard_map/ppermute | solution.py:105
  229.1 30.4 %collective-permute-start.44 = (bf16[4,128,1792]{2,1,0:T(8,128)(2,1)}, bf16[4,128,1792]{2,1,0:T(8,128)(2,1)}, u32[]{:S(2)}, u32[]{:S(2)}) collective-permute-start(bf16[4,128,1792]{2,1,0:T(8,128)(2,1)} %collective-permute-done.30.refs_0_), channel_id=1, source_target_pairs={{0,4},{4,0},{8,12},{12,8},{16,20},{20,16},{24,28},{28,24},{1,5},{5... | collective-permute-start | bytes 5505032 | tf_op jit(solution)/shard_map/ppermute | solution.py:105
  235.2 24.9 %collective-permute-start.45 = (bf16[4,128,1792]{2,1,0:T(8,128)(2,1)}, bf16[4,128,1792]{2,1,0:T(8,128)(2,1)}, u32[]{:S(2)}, u32[]{:S(2)}) collective-permute-start(bf16[4,128,1792]{2,1,0:T(8,128)(2,1)} %collective-permute-done.31.refs_0_), channel_id=1, source_target_pairs={{0,4},{4,0},{8,12},{12,8},{16,20},{20,16},{24,28},{28,24},{1,5},{5... | collective-permute-start | bytes 5505032 | tf_op jit(solution)/shard_map/ppermute | solution.py:105
  255.0 38.5 %collective-permute-start.40 = (bf16[4,128,1792]{2,1,0:T(8,128)(2,1)}, bf16[4,128,1792]{2,1,0:T(8,128)(2,1)}, u32[]{:S(2)}, u32[]{:S(2)}) collective-permute-start(bf16[4,128,1792]{2,1,0:T(8,128)(2,1)} %bitcast_dynamic-update-slice_fusion.refs_0_), channel_id=1, source_target_pairs={{0,8},{4,12},{8,0},{12,4},{16,24},{20,28},{24,16},{28,20},{1,9},{5... | collective-permute-start | bytes 5505032 | tf_op jit(solution)/shard_map/ppermute | solution.py:105
  256.4 38.2 %collective-permute-start.41 = (bf16[4,128,1792]{2,1,0:T(8,128)(2,1)}, bf16[4,128,1792]{2,1,0:T(8,128)(2,1)}, u32[]{:S(2)}, u32[]{:S(2)}) collective-permute-start(bf16[4,128,1792]{2,1,0:T(8,128)(2,1)} %bitcast_dynamic-update-slice_fusion.refs_0_), channel_id=1, source_target_pairs={{0,16},{4,20},{8,24},{12,28},{16,0},{20,4},{24,8},{28,12},{1,17},{... | collective-permute-start | bytes 5505032 | tf_op jit(solution)/shard_map/ppermute | solution.py:105
  299.6 29.3 %collective-permute-start.48 = (bf16[2,128,1792]{2,1,0:T(8,128)(2,1)}, bf16[2,128,1792]{2,1,0:T(8,128)(2,1)}, u32[]{:S(2)}, u32[]{:S(2)}) collective-permute-start(bf16[2,128,1792]{2,1,0:T(8,128)(2,1)} %slice.218), channel_id=1, source_target_pairs={{0,16},{4,20},{8,24},{12,28},{16,0},{20,4},{24,8},{28,12},{1,17},{... | collective-permute-start | bytes 2752520 | tf_op jit(solution)/shard_map/ppermute | solution.py:105
  299.9 29.0 %collective-permute-start.49 = (bf16[2,128,1792]{2,1,0:T(8,128)(2,1)}, bf16[2,128,1792]{2,1,0:T(8,128)(2,1)}, u32[]{:S(2)}, u32[]{:S(2)}) collective-permute-start(bf16[2,128,1792]{2,1,0:T(8,128)(2,1)} %slice.219), channel_id=1, source_target_pairs={{0,8},{4,12},{8,0},{12,4},{16,24},{20,28},{24,16},{28,20},{1,9},{5... | collective-permute-start | bytes 2752520 | tf_op jit(solution)/shard_map/ppermute | solution.py:105
  350.6 25.0 %collective-permute-start.56 = (bf16[2,128,1792]{2,1,0:T(8,128)(2,1)}, bf16[2,128,1792]{2,1,0:T(8,128)(2,1)}, u32[]{:S(2)}, u32[]{:S(2)}) collective-permute-start(bf16[2,128,1792]{2,1,0:T(8,128)(2,1)} %get-tuple-element.193), channel_id=1, source_target_pairs={{0,8},{4,12},{8,0},{12,4},{16,24},{20,28},{24,16},{28,20},{1,9},{5... | collective-permute-start | bytes 2752520 | tf_op jit(solution)/shard_map/ppermute | solution.py:105
  352.0 23.6 %collective-permute-start.57 = (bf16[2,128,1792]{2,1,0:T(8,128)(2,1)}, bf16[2,128,1792]{2,1,0:T(8,128)(2,1)}, u32[]{:S(2)}, u32[]{:S(2)}) collective-permute-start(bf16[2,128,1792]{2,1,0:T(8,128)(2,1)} %get-tuple-element.194), channel_id=1, source_target_pairs={{0,16},{4,20},{8,24},{12,28},{16,0},{20,4},{24,8},{28,12},{1,17},{... | collective-permute-start | bytes 2752520 | tf_op jit(solution)/shard_map/ppermute | solution.py:105
  404.6 32.5 %collective-permute-start.67 = (bf16[4,128,1792]{2,1,0:T(8,128)(2,1)S(1)}, bf16[4,128,1792]{2,1,0:T(8,128)(2,1)}, u32[]{:S(2)}, u32[]{:S(2)}) collective-permute-start(bf16[4,128,1792]{2,1,0:T(8,128)(2,1)S(1)} %get-tuple-element.221), channel_id=1, source_target_pairs={{0,4},{4,0},{8,12},{12,8},{16,20},{20,16},{24,28},{28,24},{1,5},{5... | collective-permute-start | bytes 5505032 | tf_op jit(solution)/shard_map/ppermute | solution.py:105
  412.6 28.9 %collective-permute-start.62 = (bf16[4,128,1792]{2,1,0:T(8,128)(2,1)S(1)}, bf16[4,128,1792]{2,1,0:T(8,128)(2,1)S(1)}, u32[]{:S(2)}, u32[]{:S(2)}) collective-permute-start(bf16[4,128,1792]{2,1,0:T(8,128)(2,1)S(1)} %get-tuple-element.215), channel_id=1, source_target_pairs={{0,4},{4,0},{8,12},{12,8},{16,20},{20,16},{24,28},{28,24},{1,5},{5... | collective-permute-start | bytes 5505032 | tf_op jit(solution)/shard_map/ppermute | solution.py:105
  413.8 23.2 %collective-permute-start.69 = (bf16[2,128,1792]{2,1,0:T(8,128)(2,1)S(1)}, bf16[2,128,1792]{2,1,0:T(8,128)(2,1)S(1)}, u32[]{:S(2)}, u32[]{:S(2)}) collective-permute-start(bf16[2,128,1792]{2,1,0:T(8,128)(2,1)S(1)} %copy-done.42), channel_id=1, source_target_pairs={{0,8},{4,12},{8,0},{12,4},{16,24},{20,28},{24,16},{28,20},{1,9},{5... | collective-permute-start | bytes 2752520 | tf_op jit(solution)/shard_map/ppermute | solution.py:105
  416.7 39.0 %collective-permute-start.64 = (bf16[2,128,1792]{2,1,0:T(8,128)(2,1)S(1)}, bf16[2,128,1792]{2,1,0:T(8,128)(2,1)}, u32[]{:S(2)}, u32[]{:S(2)}) collective-permute-start(bf16[2,128,1792]{2,1,0:T(8,128)(2,1)S(1)} %add_convert_fusion.10), channel_id=1, source_target_pairs={{0,8},{4,12},{8,0},{12,4},{16,24},{20,28},{24,16},{28,20},{1,9},{5... | collective-permute-start | bytes 2752520 | tf_op jit(solution)/shard_map/ppermute | solution.py:105
  458.7 84.4 %reduce-scatter.11.cloned.1.call-start = ((), (), s32[]{:S(2)}) async-start(), calls=%async_computation.7 | async-start | bytes 2293760 | tf_op jit(solution)/shard_map/reduce_scatter | solution.py:519
  (111 other events, 1225.4 us)
Sparse Core Ops, SparseCore 0:
  61.0 38.7 reduce-scatter.4
  152.1 38.5 reduce-scatter.6
  458.8 35.9 reduce-scatter.8
  505.6 37.4 reduce-scatter.10

commit v9 on v8

--- a/solution.py
+++ b/solution.py
@@ -10,7 +10,7 @@
 FP8_LIMIT = 448.0
 AXES = ("dp", "tensor")
 CHUNKS = 2
-VMEM_LIMIT = 48 * 2**20
+VMEM_LIMIT = 58 * 2**20
 COST_SHARE = 16
 
 
@@ -317,26 +317,25 @@
             other_ref[source - half] = spread
 
 
-def down(hidden_q, w_down, factor, spread, c, step):
+def down(hidden_q, w_down, factor, spread, start, width):
     rows, hidden = hidden_q.shape
     sources, tokens, capacity = spread.shape
-    tile = step // 2 if step % 256 == 0 else step
-    tiles = step // tile
+    tile = next(t for t in (1024, 512, 256, 128) if start % t == 0 and width % t == 0)
     whole = lambda shape: pl.BlockSpec(shape, lambda j: (0,) * len(shape))
     return pl.pallas_call(
         down_kernel,
-        grid=(tiles,),
+        grid=(width // tile,),
         in_specs=[
             whole(hidden_q.shape),
-            pl.BlockSpec((1, hidden, tile), lambda j: (0, 0, c * tiles + j)),
+            pl.BlockSpec((1, hidden, tile), lambda j: (0, 0, start // tile + j)),
             whole(factor.shape),
             whole(spread.shape),
         ],
         out_specs=[pl.BlockSpec((sources // 2, tokens, tile), lambda j: (0, 0, j))] * 2,
-        out_shape=[jax.ShapeDtypeStruct((sources // 2, tokens, step), jnp.bfloat16)] * 2,
+        out_shape=[jax.ShapeDtypeStruct((sources // 2, tokens, width), jnp.bfloat16)] * 2,
         compiler_params=pltpu.CompilerParams(vmem_limit_bytes=VMEM_LIMIT),
         cost_estimate=cost(
-            2 * rows * step * (hidden + tokens), 2 * step * (hidden + sources * tokens)
+            2 * rows * width * (hidden + tokens), 2 * width * (hidden + sources * tokens)
         ),
         name="down",
     )(hidden_q, w_down, factor, spread)
@@ -418,9 +417,11 @@
         return arrived
 
     own = along_tensor(sent, at_hop)
+    along_x, along_y = neighbours(own)
+    own = both_cores([own])
     weight = beside["weight"]
-    stream = [first, beside["sum"][0]]
-    sent = beside["sum"][1]
+    second, sent = beside["sum"]
+    stream = [first, second]
 
     named = weight > 0.0
     earlier = jnp.triu(jnp.ones((local_rows, local_rows), jnp.bfloat16), 1)
@@ -434,9 +435,10 @@
         slot[:, :, None, :] == jnp.arange(capacity, dtype=jnp.int32)[:, None]
     ) & named[:, :, None, :]
     factor = jnp.sum(jnp.where(chosen, weight[:, :, None, :], 0.0), axis=3)
-    factor = factor.reshape(4, 2 * layers * capacity, 1) * (top_h / FP8_LIMIT)
+    factor = list(factor.reshape(4, 2 * layers * capacity, 1) * (top_h / FP8_LIMIT))
     choice = chosen.astype(jnp.bfloat16).reshape(4, 2 * layers, capacity, local_rows)
-    spread = choice.transpose(0, 1, 3, 2)
+    spread = list(choice.transpose(0, 1, 3, 2))
+    choice = list(choice)
     scales = jnp.stack([top_x / FP8_LIMIT, FP8_LIMIT / top_h])
 
     squares = sum(jnp.sum(part * part, axis=1) for part in stream)
@@ -454,19 +456,22 @@
         rows, pieces = groups[r]
         return gate_up(scales, gains, choice[r], rows, pieces, gate_rows, up_rows)
 
-    along_x, along_y = neighbours(own)
-    first = [[own], [along_x], [along_y]]
-    along_x, along_y, sent = tie(along_x, along_y, sent)
-    across = diagonal(along_x, along_y)
+    own, sent = tie(own, sent)
 
     def at_middle_hop(hop, arrived):
-        nonlocal across
-        if hop == 2:
+        nonlocal along_x, along_y, across
+        if hop == 1:
+            arrived, along_x, along_y = tie(arrived, along_x, along_y)
+            across = diagonal(along_x, along_y)
+        if hop == layers - 1:
             arrived, across = tie(arrived, across)
         return arrived
 
-    own = along_tensor(sent, at_middle_hop)
-    first = [rows_of(choice[r], both_cores(p)) for r, p in enumerate(first + [across])]
+    across = []
+    later = along_tensor(sent, at_middle_hop)
+    first = [own, both_cores([along_x]), both_cores([along_y])]
+    own = later
+    first = [rows_of(choice[r], p) for r, p in enumerate(first + [both_cores(across)])]
     along_x, along_y = neighbours(own)
     groups = [(first[0], both_cores([own]))]
     hidden = [hidden_of(0, choice)]
@@ -480,8 +485,12 @@
     across, hidden = tie(across, hidden)
     groups.append((first[3], both_cores(across)))
 
+    unit = 512 if width % 512 == 0 else 128
+    cut = (width // unit + 1) // 2 * unit
+    spans = [(0, cut), (cut, width - cut)]
+
     def outputs(r, c):
-        return down(hidden[r][0], w_down, factor[r], spread[r], c, step)
+        return down(hidden[r][0], w_down, factor[r], spread[r], *spans[c])
 
     def halves(kept, given):
         taken = swap(given, 1)
@@ -514,7 +523,7 @@
         to_own = halves(*to_own)
         low = add(*to_own[0], early_x, swap(late_y, 4))
         high = add(*to_own[1], swap(late_x, 2), early_y)
-        mixed = jnp.concatenate([low, high]).reshape(layers * local_rows, step)
+        mixed = jnp.concatenate([low, high]).reshape(layers * local_rows, -1)
     mixed, mixture = tie(mixed, mixture)
     mixture.append(lax.psum_scatter(mixed, "tensor", scatter_dimension=0, tiled=True))
     layer_out = stream + jnp.concatenate(mixture, axis=1).astype(jnp.float32)

time: 556 us -> 555 us (level)
  Pallas kernels: 120 us -> 140 us
  local copies, waits for them, and re-layouts: 45.6 us -> 29.4 us
  other arithmetic: 53.2 us -> 44 us
    ppermute x6, waiting for transfers between devices: 31.6 us -> 17.7 us  [along_tensor(): lax.ppermute(above, 'tensor', back)]
    unnamed x105 -> x89, local copies, waits for them, and re-layouts: 20 us -> 6.91 us
    ppermute x59, waiting for transfers between devices: 145 us -> 155 us  [swap(): return lax.ppermute(value, 'dp', [(i, i ^ bits) for i in range(count)])]
    pallas_call x8, Pallas kernels: 42.4 us -> 48.5 us  [down(): pl.pallas_call(down_kernel, grid=(width // tile,), in_specs=[whole(hidden...]
    pallas_call x4, Pallas kernels: 9.6 us -> 15.6 us  [rows_of(): pl.pallas_call(rows_kernel, out_shape=[jax.ShapeDtypeStruct((rows, step),...]
  transfers between devices with their start and end apart: 83 -> 83, of which waited for: 42 -> 44; matrix products, arithmetic and copies ran while one was open for 14% -> 11% of each run, Pallas kernels for 19% -> 23%
where the time goes in v9:
time: 555 us; the launch traced here: 547 us
  waiting for transfers between devices  239 us (43%)
  Pallas kernels  140 us (25%)
  starting transfers between devices  72.4 us (13%)
  other arithmetic  44 us (8%)
  local copies, waits for them, and re-layouts  29.4 us (5%)
  between operations  21.5 us (4%)
    ppermute x59, waiting for transfers between devices, swap(): return lax.ppermute(value, 'dp', [(i, i ^ bits) for i in range(count)])  155 us
    pallas_call x4, Pallas kernels, gate_up(): pl.pallas_call(gate_up_kernel, grid=(hidden // tile,), in_specs=[pl.Block...  52.9 us
    pallas_call x8, Pallas kernels, down(): pl.pallas_call(down_kernel, grid=(width // tile,), in_specs=[whole(hidden...  48.5 us
    ppermute x59, starting transfers between devices, swap(): return lax.ppermute(value, 'dp', [(i, i ^ bits) for i in range(count)])  37.2 us
    reduce_scatter x2, waiting for transfers between devices, summed_over_tensor(): total = lax.psum_scatter(terms, 'tensor', scatter_dimension=0, tiled=True)  22 us
    ppermute x5, waiting for transfers between devices, peaks_over_all(): peaks = jnp.maximum(peaks, lax.ppermute(peaks, axis, pairs))  20.7 us
    pallas_call x2, Pallas kernels, project_part(): pl.pallas_call(project_kernel, in_specs=[pl.BlockSpec(memory_space=pltpu....  20.2 us
    convert_element_type x11, other arithmetic, add(): return sum((t.astype(jnp.float32) for t in terms)).astype(jnp.bfloat16)  19.1 us
  transfers between devices with their start and end apart: 83, of which 44 were waited for; matrix products, arithmetic and copies ran while one was open for 11% of the time, Pallas kernels for 23%

profile of v9, /device:TPU:0, one launch (start us, length us, event | category | flops | bytes accessed | tf_op | source)
XLA Modules:
  0.0 546.9 jit_solution(8728978669972078723)
XLA Ops:
  24.5 7.7 %collective-permute-done.1.refs_2_ = bf16[224,2048]{1,0:T(8,128)(2,1)S(1)} collective-permute-done((bf16[224,2048]{1,0:T(8,128)(2,1)S(1)}, bf16[224,2048]{1,0:T(8,128)(2,1)S(1)}, u32[]{:S(2)}, u32[]{:S(2)}) %collective-permute-start.1) | collective-permute-done | bytes 917536 | tf_op jit(solution)/shard_map/ppermute | solution.py:105
  37.5 9.4 %collective-permute-done.9.refs_6_ = bf16[112,2048]{1,0:T(8,128)(2,1)} collective-permute-done((bf16[112,2048]{1,0:T(8,128)(2,1)S(1)}, bf16[112,2048]{1,0:T(8,128)(2,1)}, u32[]{:S(2)}, u32[]{:S(2)}) %collective-permute-start.9) | collective-permute-done | bytes 458784 | tf_op jit(solution)/shard_map/ppermute | solution.py:105
  51.5 10.1 %project.2 = bf16[512,1792]{1,0:T(8,128)(2,1)} custom-call(s32[1]{0:T(128)} %bitcast.2.place_ref, bf16[512,2048]{1,0:T(8,128)(2,1)} %attn_ref.3, bf16[224,2048]{1,0:T(8,128)(2,1)} %copy-done.5, bf16[224,2048]{1,0:T(8,128)(2,1)} %collective-permute-done.refs_1_, bf16[224,2048]{1,0:T(8,128)(2,1)} %copy-done.10, ...), custom_call_target="tpu_custom_call" | custom-call | flops 234881024 | bytes 589824 | tf_op jit(solution)/shard_map/project/pallas_call | solution.py:186
  64.3 19.9 %collective-permute-done.16.refs_2_ = bf16[224,2048]{1,0:T(8,128)(2,1)} collective-permute-done((bf16[224,2048]{1,0:T(8,128)(2,1)S(1)}, bf16[224,2048]{1,0:T(8,128)(2,1)}, u32[]{:S(2)}, u32[]{:S(2)}) %collective-permute-start.16) | collective-permute-done | bytes 917536 | tf_op jit(solution)/shard_map/ppermute | solution.py:105
  88.8 9.3 %collective-permute-done.20.refs_6_ = bf16[112,2048]{1,0:T(8,128)(2,1)} collective-permute-done((bf16[112,2048]{1,0:T(8,128)(2,1)}, bf16[112,2048]{1,0:T(8,128)(2,1)}, u32[]{:S(2)}, u32[]{:S(2)}) %collective-permute-start.20) | collective-permute-done | bytes 458784 | tf_op jit(solution)/shard_map/ppermute | solution.py:105
  108.0 8.7 %collective-permute-done.13 = bf16[128,1792]{1,0:T(8,128)(2,1)S(1)} collective-permute-done((bf16[128,1792]{1,0:T(8,128)(2,1)S(1)}, bf16[128,1792]{1,0:T(8,128)(2,1)S(1)}, u32[]{:S(2)}, u32[]{:S(2)}) %collective-permute-start.13) | collective-permute-done | bytes 458784 | tf_op jit(solution)/shard_map/ppermute | solution.py:115
  125.4 12.3 %collective-permute-done.26 = bf16[128,1792]{1,0:T(8,128)(2,1)} collective-permute-done((bf16[128,1792]{1,0:T(8,128)(2,1)S(1)}, bf16[128,1792]{1,0:T(8,128)(2,1)}, u32[]{:S(2)}, u32[]{:S(2)}) %collective-permute-start.26) | collective-permute-done | bytes 458784 | tf_op jit(solution)/shard_map/ppermute | solution.py:115
  141.2 10.1 %project.3 = bf16[512,1792]{1,0:T(8,128)(2,1)} custom-call(s32[1]{0:T(128)} %bitcast.2.place_ref, bf16[512,2048]{1,0:T(8,128)(2,1)} %attn_ref.3, bf16[224,2048]{1,0:T(8,128)(2,1)} %copy-done.4, bf16[224,2048]{1,0:T(8,128)(2,1)} %collective-permute-done.15.refs_1_, bf16[224,2048]{1,0:T(8,128)(2,1)} %collective-permute-done.16.refs_2_, ...), custom_call_target="tpu_custom_call" | custom-call | flops 234881024 | bytes 589824 | tf_op jit(solution)/shard_map/project/pallas_call | solution.py:186
  151.3 11.2 %reduce-scatter.9.cloned.1.call-start = ((), (), s32[]{:S(2)}) async-start(), calls=%async_computation.6 | async-start | bytes 2621440 | tf_op jit(solution)/shard_map/reduce_scatter | solution.py:513
  169.5 20.6 %reduce-scatter.7.cloned.1.call-done = bf16[128,1792]{1,0:T(8,128)(2,1)} async-done(((bf16[512,1792]{1,0:T(8,128)(2,1)}), bf16[128,1792]{1,0:T(8,128)(2,1)}) %reduce-scatter.7.cloned.1.call-update) | async-done | bytes 458768 | tf_op jit(solution)/shard_map/reduce_scatter | solution.py:391
  196.2 13.9 %collective-permute-done.33.refs_0_ = bf16[4,128,1792]{2,1,0:T(8,128)(2,1)} collective-permute-done((bf16[4,128,1792]{2,1,0:T(8,128)(2,1)}, bf16[4,128,1792]{2,1,0:T(8,128)(2,1)}, u32[]{:S(2)}, u32[]{:S(2)}) %collective-permute-start.33) | collective-permute-done | bytes 1835040 | tf_op jit(solution)/shard_map/ppermute | solution.py:105
  228.6 8.7 %collective-permute-done.39.refs_0_ = bf16[2,128,1792]{2,1,0:T(8,128)(2,1)S(1)} collective-permute-done((bf16[2,128,1792]{2,1,0:T(8,128)(2,1)}, bf16[2,128,1792]{2,1,0:T(8,128)(2,1)S(1)}, u32[]{:S(2)}, u32[]{:S(2)}) %collective-permute-start.39) | collective-permute-done | bytes 917536 | tf_op jit(solution)/shard_map/ppermute | solution.py:105
  269.2 13.2 %gate_up.4 = (bf16[384,1024]{1,0:T(8,128)(2,1)}, f32[8,128]{1,0:T(8,128)}) custom-call(f32[2]{0:T(128)} %pad_maximum_fusion.5.scale_ref, f32[2,1,1792]{2,1,0:T(1,128)} %maximum_multiply_fusion.gain_ref, bf16[8,48,128]{2,1,0:T(8,128)(2,1)} %bitcast.89, bf16[384,1792]{1,0:T(8,128)(2,1)} %get-tuple-element.161.first_ref, ...), custom_call_target="tpu_custom_call" | custom-call | flops 374341632 | bytes 1376256 | tf_op jit(solution)/shard_map/gate_up/pallas_call | solution.py:278
  290.1 13.2 %gate_up.5 = (bf16[384,1024]{1,0:T(8,128)(2,1)}, f32[8,128]{1,0:T(8,128)}) custom-call(f32[2]{0:T(128)} %pad_maximum_fusion.5.scale_ref, f32[2,1,1792]{2,1,0:T(1,128)} %maximum_multiply_fusion.gain_ref, bf16[8,48,128]{2,1,0:T(8,128)(2,1)} %bitcast.87, bf16[384,1792]{1,0:T(8,128)(2,1)} %get-tuple-element.181.first_ref, ...), custom_call_target="tpu_custom_call" | custom-call | flops 374341632 | bytes 1376256 | tf_op jit(solution)/shard_map/gate_up/pallas_call | solution.py:278
  304.6 13.2 %gate_up.6 = (bf16[384,1024]{1,0:T(8,128)(2,1)}, f32[8,128]{1,0:T(8,128)}) custom-call(f32[2]{0:T(128)} %pad_maximum_fusion.5.scale_ref, f32[2,1,1792]{2,1,0:T(1,128)} %maximum_multiply_fusion.gain_ref, bf16[8,48,128]{2,1,0:T(8,128)(2,1)} %bitcast.85, bf16[384,1792]{1,0:T(8,128)(2,1)} %get-tuple-element.186.first_ref, ...), custom_call_target="tpu_custom_call" | custom-call | flops 374341632 | bytes 1376256 | tf_op jit(solution)/shard_map/gate_up/pallas_call | solution.py:278
  317.8 6.5 %down.8 = (bf16[4,128,2048]{2,1,0:T(8,128)(2,1)}, bf16[4,128,2048]{2,1,0:T(8,128)(2,1)}) custom-call(bf16[384,1024]{1,0:T(8,128)(2,1)} %get-tuple-element.192.hidden_ref, bf16[1,1024,3584]{2,1,0:T(8,128)(2,1)} %down_w.15, f32[384,1]{1,0:T(8,128)} %copy.43.factor_ref, bf16[8,128,48]{2,1,0:T(8,128)(2,1)} %get-tuple-element.194.spread_ref), custom_call_target="tpu_custom_call" | custom-call | flops 113246208 | bytes 524288 | tf_op jit(solution)/shard_map/down/pallas_call | solution.py:325
  325.2 6.3 %down.9 = (bf16[4,128,2048]{2,1,0:T(8,128)(2,1)}, bf16[4,128,2048]{2,1,0:T(8,128)(2,1)}) custom-call(bf16[384,1024]{1,0:T(8,128)(2,1)} %get-tuple-element.197.hidden_ref, bf16[1,1024,3584]{2,1,0:T(8,128)(2,1)} %down_w.15, f32[384,1]{1,0:T(8,128)} %copy.44.factor_ref, bf16[8,128,48]{2,1,0:T(8,128)(2,1)} %get-tuple-element.199.spread_ref), custom_call_target="tpu_custom_call" | custom-call | flops 113246208 | bytes 524288 | tf_op jit(solution)/shard_map/down/pallas_call | solution.py:325
  342.3 13.2 %gate_up.7 = (bf16[384,1024]{1,0:T(8,128)(2,1)}, f32[8,128]{1,0:T(8,128)}) custom-call(f32[2]{0:T(128)} %pad_maximum_fusion.5.scale_ref, f32[2,1,1792]{2,1,0:T(1,128)} %maximum_multiply_fusion.gain_ref, bf16[8,48,128]{2,1,0:T(8,128)(2,1)} %bitcast.83, bf16[384,1792]{1,0:T(8,128)(2,1)} %get-tuple-element.204.first_ref, ...), custom_call_target="tpu_custom_call" | custom-call | flops 374341632 | bytes 1376256 | tf_op jit(solution)/shard_map/gate_up/pallas_call | solution.py:278
  355.5 6.1 %down.10 = (bf16[4,128,2048]{2,1,0:T(8,128)(2,1)}, bf16[4,128,2048]{2,1,0:T(8,128)(2,1)}) custom-call(bf16[384,1024]{1,0:T(8,128)(2,1)} %get-tuple-element.237.hidden_ref, bf16[1,1024,3584]{2,1,0:T(8,128)(2,1)} %down_w.15, f32[384,1]{1,0:T(8,128)} %copy.45.factor_ref, bf16[8,128,48]{2,1,0:T(8,128)(2,1)} %get-tuple-element.212.spread_ref), custom_call_target="tpu_custom_call" | custom-call | flops 113246208 | bytes 524288 | tf_op jit(solution)/shard_map/down/pallas_call | solution.py:325
  388.2 6.3 %down.11 = (bf16[4,128,2048]{2,1,0:T(8,128)(2,1)}, bf16[4,128,2048]{2,1,0:T(8,128)(2,1)}) custom-call(bf16[384,1024]{1,0:T(8,128)(2,1)} %get-tuple-element.234.hidden_ref, bf16[1,1024,3584]{2,1,0:T(8,128)(2,1)} %down_w.15, f32[384,1]{1,0:T(8,128)} %copy.46.factor_ref, bf16[8,128,48]{2,1,0:T(8,128)(2,1)} %get-tuple-element.220.spread_ref), custom_call_target="tpu_custom_call" | custom-call | flops 113246208 | bytes 524288 | tf_op jit(solution)/shard_map/down/pallas_call | solution.py:325
  417.9 19.0 %collective-permute-done.68 = bf16[2,128,2048]{2,1,0:T(8,128)(2,1)S(1)} collective-permute-done((bf16[2,128,2048]{2,1,0:T(8,128)(2,1)}, bf16[2,128,2048]{2,1,0:T(8,128)(2,1)S(1)}, u32[]{:S(2)}, u32[]{:S(2)}) %collective-permute-start.68) | collective-permute-done | bytes 1048608 | tf_op jit(solution)/shard_map/ppermute | solution.py:105
  442.1 11.1 %collective-permute-done.64 = bf16[2,128,1536]{2,1,0:T(8,128)(2,1)S(1)} collective-permute-done((bf16[2,128,1536]{2,1,0:T(8,128)(2,1)S(1)}, bf16[2,128,1536]{2,1,0:T(8,128)(2,1)S(1)}, u32[]{:S(2)}, u32[]{:S(2)}) %collective-permute-start.64) | collective-permute-done | bytes 786464 | tf_op jit(solution)/shard_map/ppermute | solution.py:105
  463.2 10.6 %collective-permute-done.70 = bf16[2,128,1536]{2,1,0:T(8,128)(2,1)S(1)} collective-permute-done((bf16[2,128,1536]{2,1,0:T(8,128)(2,1)}, bf16[2,128,1536]{2,1,0:T(8,128)(2,1)S(1)}, u32[]{:S(2)}, u32[]{:S(2)}) %collective-permute-start.70) | collective-permute-done | bytes 786464 | tf_op jit(solution)/shard_map/ppermute | solution.py:105
  477.8 15.0 %collective-permute-done.71 = bf16[2,128,1536]{2,1,0:T(8,128)(2,1)S(1)} collective-permute-done((bf16[2,128,1536]{2,1,0:T(8,128)(2,1)S(1)}, bf16[2,128,1536]{2,1,0:T(8,128)(2,1)S(1)}, u32[]{:S(2)}, u32[]{:S(2)}) %collective-permute-start.71) | collective-permute-done | bytes 786464 | tf_op jit(solution)/shard_map/ppermute | solution.py:105
  (344 shorter events, 249.7 us)
Async XLA Ops:
  7.2 93.4 %reduce-scatter.5.cloned.1.call-start = ((), (), s32[]{:S(2)}) async-start(), calls=%async_computation.4 | async-start | bytes 2293760 | tf_op jit(solution)/shard_map/reduce_scatter | solution.py:391
  23.3 26.1 %collective-permute-start = (bf16[224,2048]{1,0:T(8,128)(2,1)S(1)}, bf16[224,2048]{1,0:T(8,128)(2,1)}, u32[]{:S(2)}, u32[]{:S(2)}) collective-permute-start(bf16[224,2048]{1,0:T(8,128)(2,1)S(1)} %get-tuple-element.280.refs_0_), channel_id=1, source_target_pairs={{0,4},{4,0},{8,12},{12,8},{16,20},{20,16},{24,28},{28,24},{1,5},{5... | collective-permute-start | bytes 2752520 | tf_op jit(solution)/shard_map/ppermute | solution.py:105
  61.6 128.5 %reduce-scatter.7.cloned.1.call-start = ((), (), s32[]{:S(2)}) async-start(), calls=%async_computation.5 | async-start | bytes 2293760 | tf_op jit(solution)/shard_map/reduce_scatter | solution.py:391
  64.3 39.9 %collective-permute-start.15 = (bf16[224,2048]{1,0:T(8,128)(2,1)S(1)}, bf16[224,2048]{1,0:T(8,128)(2,1)}, u32[]{:S(2)}, u32[]{:S(2)}) collective-permute-start(bf16[224,2048]{1,0:T(8,128)(2,1)S(1)} %get-tuple-element.137.refs_0_), channel_id=1, source_target_pairs={{0,4},{4,0},{8,12},{12,8},{16,20},{20,16},{24,28},{28,24},{1,5},{5... | collective-permute-start | bytes 2752520 | tf_op jit(solution)/shard_map/ppermute | solution.py:105
  123.9 27.4 %collective-permute-start.25 = (bf16[128,1792]{1,0:T(8,128)(2,1)S(1)}, bf16[128,1792]{1,0:T(8,128)(2,1)}, u32[]{:S(2)}, u32[]{:S(2)}) collective-permute-start(bf16[128,1792]{1,0:T(8,128)(2,1)S(1)} %collective-permute-done.24), channel_id=1, source_target_pairs={{2,3},{6,7},{10,11},{14,15},{18,19},{22,23},{26,27},{30,31}} | collective-permute-start | bytes 1376264 | tf_op jit(solution)/shard_map/ppermute | solution.py:115
  151.3 349.9 %reduce-scatter.9.cloned.1.call-start = ((), (), s32[]{:S(2)}) async-start(), calls=%async_computation.6 | async-start | bytes 2621440 | tf_op jit(solution)/shard_map/reduce_scatter | solution.py:513
  167.4 24.9 %collective-permute-start.30 = (bf16[4,128,1792]{2,1,0:T(8,128)(2,1)}, bf16[4,128,1792]{2,1,0:T(8,128)(2,1)}, u32[]{:S(2)}, u32[]{:S(2)}) collective-permute-start(bf16[4,128,1792]{2,1,0:T(8,128)(2,1)} %bitcast_dynamic-update-slice_fusion.4.refs_0_), channel_id=1, source_target_pairs={{0,4},{4,0},{8,12},{12,8},{16,20},{20,16},{24,28},{28,24},{1,5},{5... | collective-permute-start | bytes 5505032 | tf_op jit(solution)/shard_map/ppermute | solution.py:105
  167.4 42.7 %collective-permute-start.33 = (bf16[4,128,1792]{2,1,0:T(8,128)(2,1)}, bf16[4,128,1792]{2,1,0:T(8,128)(2,1)}, u32[]{:S(2)}, u32[]{:S(2)}) collective-permute-start(bf16[4,128,1792]{2,1,0:T(8,128)(2,1)} %bitcast_dynamic-update-slice_fusion.4.refs_0_), channel_id=1, source_target_pairs={{0,8},{4,12},{8,0},{12,4},{16,24},{20,28},{24,16},{28,20},{1,9},{5... | collective-permute-start | bytes 5505032 | tf_op jit(solution)/shard_map/ppermute | solution.py:105
  167.8 42.5 %collective-permute-start.34 = (bf16[4,128,1792]{2,1,0:T(8,128)(2,1)}, bf16[4,128,1792]{2,1,0:T(8,128)(2,1)}, u32[]{:S(2)}, u32[]{:S(2)}) collective-permute-start(bf16[4,128,1792]{2,1,0:T(8,128)(2,1)} %bitcast_dynamic-update-slice_fusion.4.refs_0_), channel_id=1, source_target_pairs={{0,16},{4,20},{8,24},{12,28},{16,0},{20,4},{24,8},{28,12},{1,17},{... | collective-permute-start | bytes 5505032 | tf_op jit(solution)/shard_map/ppermute | solution.py:105
  241.9 40.6 %collective-permute-start.41 = (bf16[4,128,1792]{2,1,0:T(8,128)(2,1)S(1)}, bf16[4,128,1792]{2,1,0:T(8,128)(2,1)}, u32[]{:S(2)}, u32[]{:S(2)}) collective-permute-start(bf16[4,128,1792]{2,1,0:T(8,128)(2,1)S(1)} %bitcast_dynamic-update-slice_fusion.refs_0_), channel_id=1, source_target_pairs={{0,8},{4,12},{8,0},{12,4},{16,24},{20,28},{24,16},{28,20},{1,9},{5... | collective-permute-start | bytes 5505032 | tf_op jit(solution)/shard_map/ppermute | solution.py:105
  243.2 39.8 %collective-permute-start.42 = (bf16[4,128,1792]{2,1,0:T(8,128)(2,1)S(1)}, bf16[4,128,1792]{2,1,0:T(8,128)(2,1)}, u32[]{:S(2)}, u32[]{:S(2)}) collective-permute-start(bf16[4,128,1792]{2,1,0:T(8,128)(2,1)S(1)} %bitcast_dynamic-update-slice_fusion.refs_0_), channel_id=1, source_target_pairs={{0,16},{4,20},{8,24},{12,28},{16,0},{20,4},{24,8},{28,12},{1,17},{... | collective-permute-start | bytes 5505032 | tf_op jit(solution)/shard_map/ppermute | solution.py:105
  244.2 25.1 %collective-permute-start.43 = (bf16[4,128,1792]{2,1,0:T(8,128)(2,1)S(1)}, bf16[4,128,1792]{2,1,0:T(8,128)(2,1)}, u32[]{:S(2)}, u32[]{:S(2)}) collective-permute-start(bf16[4,128,1792]{2,1,0:T(8,128)(2,1)S(1)} %bitcast_dynamic-update-slice_fusion.refs_0_), channel_id=1, source_target_pairs={{0,4},{4,0},{8,12},{12,8},{16,20},{20,16},{24,28},{28,24},{1,5},{5... | collective-permute-start | bytes 5505032 | tf_op jit(solution)/shard_map/ppermute | solution.py:105
  287.0 30.9 %collective-permute-start.48 = (bf16[2,128,1792]{2,1,0:T(8,128)(2,1)}, bf16[2,128,1792]{2,1,0:T(8,128)(2,1)}, u32[]{:S(2)}, u32[]{:S(2)}) collective-permute-start(bf16[2,128,1792]{2,1,0:T(8,128)(2,1)} %slice.164), channel_id=1, source_target_pairs={{0,16},{4,20},{8,24},{12,28},{16,0},{20,4},{24,8},{28,12},{1,17},{... | collective-permute-start | bytes 2752520 | tf_op jit(solution)/shard_map/ppermute | solution.py:105
  288.1 29.8 %collective-permute-start.49 = (bf16[2,128,1792]{2,1,0:T(8,128)(2,1)S(1)}, bf16[2,128,1792]{2,1,0:T(8,128)(2,1)}, u32[]{:S(2)}, u32[]{:S(2)}) collective-permute-start(bf16[2,128,1792]{2,1,0:T(8,128)(2,1)S(1)} %slice.165), channel_id=1, source_target_pairs={{0,8},{4,12},{8,0},{12,4},{16,24},{20,28},{24,16},{28,20},{1,9},{5... | collective-permute-start | bytes 2752520 | tf_op jit(solution)/shard_map/ppermute | solution.py:105
  339.6 25.6 %collective-permute-start.56 = (bf16[2,128,2048]{2,1,0:T(8,128)(2,1)}, bf16[2,128,2048]{2,1,0:T(8,128)(2,1)S(1)}, u32[]{:S(2)}, u32[]{:S(2)}) collective-permute-start(bf16[2,128,2048]{2,1,0:T(8,128)(2,1)} %get-tuple-element.215), channel_id=1, source_target_pairs={{0,8},{4,12},{8,0},{12,4},{16,24},{20,28},{24,16},{28,20},{1,9},{5... | collective-permute-start | bytes 3145736 | tf_op jit(solution)/shard_map/ppermute | solution.py:105
  340.4 25.5 %collective-permute-start.57 = (bf16[2,128,2048]{2,1,0:T(8,128)(2,1)}, bf16[2,128,2048]{2,1,0:T(8,128)(2,1)}, u32[]{:S(2)}, u32[]{:S(2)}) collective-permute-start(bf16[2,128,2048]{2,1,0:T(8,128)(2,1)} %get-tuple-element.216), channel_id=1, source_target_pairs={{0,16},{4,20},{8,24},{12,28},{16,0},{20,4},{24,8},{28,12},{1,17},{... | collective-permute-start | bytes 3145736 | tf_op jit(solution)/shard_map/ppermute | solution.py:105
  373.9 25.4 %collective-permute-start.59 = (bf16[2,128,2048]{2,1,0:T(8,128)(2,1)}, bf16[2,128,2048]{2,1,0:T(8,128)(2,1)S(1)}, u32[]{:S(2)}, u32[]{:S(2)}) collective-permute-start(bf16[2,128,2048]{2,1,0:T(8,128)(2,1)} %get-tuple-element.270), channel_id=1, source_target_pairs={{0,8},{4,12},{8,0},{12,4},{16,24},{20,28},{24,16},{28,20},{1,9},{5... | collective-permute-start | bytes 3145736 | tf_op jit(solution)/shard_map/ppermute | solution.py:105
  375.1 25.2 %collective-permute-start.60 = (bf16[2,128,2048]{2,1,0:T(8,128)(2,1)}, bf16[2,128,2048]{2,1,0:T(8,128)(2,1)}, u32[]{:S(2)}, u32[]{:S(2)}) collective-permute-start(bf16[2,128,2048]{2,1,0:T(8,128)(2,1)} %get-tuple-element.269), channel_id=1, source_target_pairs={{0,16},{4,20},{8,24},{12,28},{16,0},{20,4},{24,8},{28,12},{1,17},{... | collective-permute-start | bytes 3145736 | tf_op jit(solution)/shard_map/ppermute | solution.py:105
  410.1 27.5 %collective-permute-start.67 = (bf16[4,128,2048]{2,1,0:T(8,128)(2,1)}, bf16[4,128,2048]{2,1,0:T(8,128)(2,1)S(1)}, u32[]{:S(2)}, u32[]{:S(2)}) collective-permute-start(bf16[4,128,2048]{2,1,0:T(8,128)(2,1)} %get-tuple-element.245), channel_id=1, source_target_pairs={{0,4},{4,0},{8,12},{12,8},{16,20},{20,16},{24,28},{28,24},{1,5},{5... | collective-permute-start | bytes 6291464 | tf_op jit(solution)/shard_map/ppermute | solution.py:105
  410.6 26.2 %collective-permute-start.68 = (bf16[2,128,2048]{2,1,0:T(8,128)(2,1)}, bf16[2,128,2048]{2,1,0:T(8,128)(2,1)S(1)}, u32[]{:S(2)}, u32[]{:S(2)}) collective-permute-start(bf16[2,128,2048]{2,1,0:T(8,128)(2,1)} %get-tuple-element.247), channel_id=1, source_target_pairs={{0,16},{4,20},{8,24},{12,28},{16,0},{20,4},{24,8},{28,12},{1,17},{... | collective-permute-start | bytes 3145736 | tf_op jit(solution)/shard_map/ppermute | solution.py:105
  411.3 26.3 %collective-permute-start.69 = (bf16[2,128,2048]{2,1,0:T(8,128)(2,1)}, bf16[2,128,2048]{2,1,0:T(8,128)(2,1)S(1)}, u32[]{:S(2)}, u32[]{:S(2)}) collective-permute-start(bf16[2,128,2048]{2,1,0:T(8,128)(2,1)} %get-tuple-element.248), channel_id=1, source_target_pairs={{0,8},{4,12},{8,0},{12,4},{16,24},{20,28},{24,16},{28,20},{1,9},{5... | collective-permute-start | bytes 3145736 | tf_op jit(solution)/shard_map/ppermute | solution.py:105
  412.7 40.5 %collective-permute-start.64 = (bf16[2,128,1536]{2,1,0:T(8,128)(2,1)S(1)}, bf16[2,128,1536]{2,1,0:T(8,128)(2,1)S(1)}, u32[]{:S(2)}, u32[]{:S(2)}) collective-permute-start(bf16[2,128,1536]{2,1,0:T(8,128)(2,1)S(1)} %add_convert_fusion.18), channel_id=1, source_target_pairs={{0,8},{4,12},{8,0},{12,4},{16,24},{20,28},{24,16},{28,20},{1,9},{5... | collective-permute-start | bytes 2359304 | tf_op jit(solution)/shard_map/ppermute | solution.py:105
  415.0 38.3 %collective-permute-start.66 = (bf16[2,128,1536]{2,1,0:T(8,128)(2,1)S(1)}, bf16[2,128,1536]{2,1,0:T(8,128)(2,1)S(1)}, u32[]{:S(2)}, u32[]{:S(2)}) collective-permute-start(bf16[2,128,1536]{2,1,0:T(8,128)(2,1)S(1)} %add_convert_fusion.17), channel_id=1, source_target_pairs={{0,16},{4,20},{8,24},{12,28},{16,0},{20,4},{24,8},{28,12},{1,17},{... | collective-permute-start | bytes 2359304 | tf_op jit(solution)/shard_map/ppermute | solution.py:105
  455.1 83.1 %reduce-scatter.11.cloned.1.call-start = ((), (), s32[]{:S(2)}) async-start(), calls=%async_computation.7 | async-start | bytes 1966080 | tf_op jit(solution)/shard_map/reduce_scatter | solution.py:528
  (103 other events, 1374.9 us)
Sparse Core Ops, SparseCore 0:
  61.8 38.7 reduce-scatter.4
  151.5 38.5 reduce-scatter.6
  455.2 45.9 reduce-scatter.8
  503.5 34.5 reduce-scatter.10

commit v10 on v9

--- a/solution.py
+++ b/solution.py
@@ -10,7 +10,7 @@
 FP8_LIMIT = 448.0
 AXES = ("dp", "tensor")
 CHUNKS = 2
-VMEM_LIMIT = 58 * 2**20
+VMEM_LIMIT = 48 * 2**20
 COST_SHARE = 16
 
 
@@ -320,7 +320,7 @@
 def down(hidden_q, w_down, factor, spread, start, width):
     rows, hidden = hidden_q.shape
     sources, tokens, capacity = spread.shape
-    tile = next(t for t in (1024, 512, 256, 128) if start % t == 0 and width % t == 0)
+    tile = width // 2 if width % 256 == 0 else width
     whole = lambda shape: pl.BlockSpec(shape, lambda j: (0,) * len(shape))
     return pl.pallas_call(
         down_kernel,
@@ -485,9 +485,7 @@
     across, hidden = tie(across, hidden)
     groups.append((first[3], both_cores(across)))
 
-    unit = 512 if width % 512 == 0 else 128
-    cut = (width // unit + 1) // 2 * unit
-    spans = [(0, cut), (cut, width - cut)]
+    spans = [(c * step, step) for c in range(CHUNKS)]
 
     def outputs(r, c):
         return down(hidden[r][0], w_down, factor[r], spread[r], *spans[c])
@@ -504,7 +502,7 @@
     mixture = []
     for c in range(CHUNKS):
         early_x, early_y = swap(to_x[0], 2), swap(to_y[1], 4)
-        kept, given = outputs(3, c)
+        kept, given = outputs(3, c) if c == 0 else coming[2]
         if c == 0:
             given, early_x, early_y = tie(given, early_x, early_y)
         beyond = [add(*terms) for terms in halves(kept, given)]
@@ -514,12 +512,12 @@
         over_x, over_y = swap(beyond[0], 2), swap(beyond[1], 4)
         to_own = outputs(0, c)
         if c + 1 < CHUNKS:
-            coming = outputs(1, c + 1), outputs(2, c + 1)
+            coming = [outputs(r, c + 1) for r in (1, 2, 3)]
             over_x, over_y, to_own, coming = tie(over_x, over_y, to_own, coming)
         late_x, late_y = add(to_x[1], over_y), add(to_y[0], over_x)
         if c + 1 < CHUNKS:
             late_x, late_y, hidden = tie(late_x, late_y, hidden)
-            to_x, to_y = ([add(*terms) for terms in halves(*pair)] for pair in coming)
+            to_x, to_y = ([add(*terms) for terms in halves(*pair)] for pair in coming[:2])
         to_own = halves(*to_own)
         low = add(*to_own[0], early_x, swap(late_y, 4))
         high = add(*to_own[1], swap(late_x, 2), early_y)

time: 555 us -> 553 us (level)
  Pallas kernels: 140 us -> 119 us
  local copies, waits for them, and re-layouts: 29.4 us -> 45.7 us
  starting transfers between devices: 72.4 us -> 80.1 us
  waiting for transfers between devices: 239 us -> 232 us
    unnamed x89 -> x117, local copies, waits for them, and re-layouts: 6.91 us -> 22 us
    pallas_call x8, Pallas kernels: 48.5 us -> 40.7 us  [down(): pl.pallas_call(down_kernel, grid=(width // tile,), in_specs=[whole(hidden...]
    ppermute x5, starting transfers between devices: 2.04 us -> 8.72 us  [peaks_over_all(): peaks = jnp.maximum(peaks, lax.ppermute(peaks, axis, pairs))]
    ppermute x5, waiting for transfers between devices: 20.7 us -> 14.3 us  [peaks_over_all(): peaks = jnp.maximum(peaks, lax.ppermute(peaks, axis, pairs))]
  transfers between devices with their start and end apart: 83 -> 83, of which waited for: 44 -> 41; matrix products, arithmetic and copies ran while one was open for 11% -> 12% of each run, Pallas kernels for 23% -> 19%
where the time goes in v10:
time: 553 us; the launch traced here: 544 us
  waiting for transfers between devices  232 us (42%)
  Pallas kernels  119 us (22%)
  starting transfers between devices  80.1 us (14%)
  other arithmetic  46 us (8%)
  local copies, waits for them, and re-layouts  45.7 us (8%)
  between operations  21.5 us (4%)
    ppermute x59, waiting for transfers between devices, swap(): return lax.ppermute(value, 'dp', [(i, i ^ bits) for i in range(count)])  150 us
    pallas_call x4, Pallas kernels, gate_up(): pl.pallas_call(gate_up_kernel, grid=(hidden // tile,), in_specs=[pl.Block...  48.3 us
    pallas_call x8, Pallas kernels, down(): pl.pallas_call(down_kernel, grid=(width // tile,), in_specs=[whole(hidden...  40.7 us
    ppermute x59, starting transfers between devices, swap(): return lax.ppermute(value, 'dp', [(i, i ^ bits) for i in range(count)])  36.7 us
    reduce_scatter x2, waiting for transfers between devices, summed_over_tensor(): total = lax.psum_scatter(terms, 'tensor', scatter_dimension=0, tiled=True)  22.2 us
    unnamed x117, local copies, waits for them, and re-layouts  22 us
    ppermute x6, waiting for transfers between devices, along_tensor(): lax.ppermute(above, 'tensor', back)  21.8 us
    pallas_call x2, Pallas kernels, project_part(): pl.pallas_call(project_kernel, in_specs=[pl.BlockSpec(memory_space=pltpu....  18.9 us
  transfers between devices with their start and end apart: 83, of which 41 were waited for; matrix products, arithmetic and copies ran while one was open for 12% of the time, Pallas kernels for 19%

profile of v10, /device:TPU:0, one launch (start us, length us, event | category | flops | bytes accessed | tf_op | source)
XLA Modules:
  0.0 544.4 jit_solution(3793557053118451374)
XLA Ops:
  24.5 7.7 %collective-permute-done.1.refs_2_ = bf16[224,2048]{1,0:T(8,128)(2,1)S(1)} collective-permute-done((bf16[224,2048]{1,0:T(8,128)(2,1)S(1)}, bf16[224,2048]{1,0:T(8,128)(2,1)S(1)}, u32[]{:S(2)}, u32[]{:S(2)}) %collective-permute-start.1) | collective-permute-done | bytes 917536 | tf_op jit(solution)/shard_map/ppermute | solution.py:105
  37.5 9.3 %collective-permute-done.9.refs_6_ = bf16[112,2048]{1,0:T(8,128)(2,1)S(1)} collective-permute-done((bf16[112,2048]{1,0:T(8,128)(2,1)S(1)}, bf16[112,2048]{1,0:T(8,128)(2,1)S(1)}, u32[]{:S(2)}, u32[]{:S(2)}) %collective-permute-start.9) | collective-permute-done | bytes 458784 | tf_op jit(solution)/shard_map/ppermute | solution.py:105
  51.5 9.4 %project.2 = bf16[512,1792]{1,0:T(8,128)(2,1)} custom-call(s32[1]{0:T(128)} %bitcast.2.place_ref, bf16[512,2048]{1,0:T(8,128)(2,1)} %attn_ref.3, bf16[224,2048]{1,0:T(8,128)(2,1)S(1)} %get-tuple-element.282.refs_0_, bf16[224,2048]{1,0:T(8,128)(2,1)} %collective-permute-done.refs_1_, bf16[224,2048]{1,0:T(8,128)(2,1)S(1)} %collective-permute-done.1.refs_2_, ...), custom_call_target="tpu_custom_call" | custom-call | flops 234881024 | bytes 589824 | tf_op jit(solution)/shard_map/project/pallas_call | solution.py:186
  64.3 19.1 %collective-permute-done.16.refs_2_ = bf16[224,2048]{1,0:T(8,128)(2,1)S(1)} collective-permute-done((bf16[224,2048]{1,0:T(8,128)(2,1)S(1)}, bf16[224,2048]{1,0:T(8,128)(2,1)S(1)}, u32[]{:S(2)}, u32[]{:S(2)}) %collective-permute-start.16) | collective-permute-done | bytes 917536 | tf_op jit(solution)/shard_map/ppermute | solution.py:105
  89.0 7.3 %collective-permute-done.20.refs_6_ = bf16[112,2048]{1,0:T(8,128)(2,1)S(1)} collective-permute-done((bf16[112,2048]{1,0:T(8,128)(2,1)}, bf16[112,2048]{1,0:T(8,128)(2,1)S(1)}, u32[]{:S(2)}, u32[]{:S(2)}) %collective-permute-start.20) | collective-permute-done | bytes 458784 | tf_op jit(solution)/shard_map/ppermute | solution.py:105
  107.4 8.7 %collective-permute-done.13 = bf16[128,1792]{1,0:T(8,128)(2,1)S(1)} collective-permute-done((bf16[128,1792]{1,0:T(8,128)(2,1)S(1)}, bf16[128,1792]{1,0:T(8,128)(2,1)S(1)}, u32[]{:S(2)}, u32[]{:S(2)}) %collective-permute-start.13) | collective-permute-done | bytes 458784 | tf_op jit(solution)/shard_map/ppermute | solution.py:115
  125.6 12.4 %collective-permute-done.26 = bf16[128,1792]{1,0:T(8,128)(2,1)} collective-permute-done((bf16[128,1792]{1,0:T(8,128)(2,1)S(1)}, bf16[128,1792]{1,0:T(8,128)(2,1)}, u32[]{:S(2)}, u32[]{:S(2)}) %collective-permute-start.26) | collective-permute-done | bytes 458784 | tf_op jit(solution)/shard_map/ppermute | solution.py:115
  141.5 9.5 %project.3 = bf16[512,1792]{1,0:T(8,128)(2,1)} custom-call(s32[1]{0:T(128)} %bitcast.2.place_ref, bf16[512,2048]{1,0:T(8,128)(2,1)} %attn_ref.3, bf16[224,2048]{1,0:T(8,128)(2,1)S(1)} %get-tuple-element.138.refs_0_, bf16[224,2048]{1,0:T(8,128)(2,1)} %collective-permute-done.15.refs_1_, bf16[224,2048]{1,0:T(8,128)(2,1)S(1)} %collective-permute-done.16.refs_2_, ...), custom_call_target="tpu_custom_call" | custom-call | flops 234881024 | bytes 589824 | tf_op jit(solution)/shard_map/project/pallas_call | solution.py:186
  151.9 11.2 %reduce-scatter.9.cloned.1.call-start = ((), (), s32[]{:S(2)}) async-start(), calls=%async_computation.6 | async-start | bytes 2293760 | tf_op jit(solution)/shard_map/reduce_scatter | solution.py:511
  169.8 20.9 %reduce-scatter.7.cloned.1.call-done = bf16[128,1792]{1,0:T(8,128)(2,1)} async-done(((bf16[512,1792]{1,0:T(8,128)(2,1)}), bf16[128,1792]{1,0:T(8,128)(2,1)}) %reduce-scatter.7.cloned.1.call-update) | async-done | bytes 458768 | tf_op jit(solution)/shard_map/reduce_scatter | solution.py:391
  197.4 13.3 %collective-permute-done.33.refs_0_ = bf16[4,128,1792]{2,1,0:T(8,128)(2,1)} collective-permute-done((bf16[4,128,1792]{2,1,0:T(8,128)(2,1)}, bf16[4,128,1792]{2,1,0:T(8,128)(2,1)}, u32[]{:S(2)}, u32[]{:S(2)}) %collective-permute-start.33) | collective-permute-done | bytes 1835040 | tf_op jit(solution)/shard_map/ppermute | solution.py:105
  231.2 6.7 %collective-permute-done.39.refs_0_ = bf16[2,128,1792]{2,1,0:T(8,128)(2,1)} collective-permute-done((bf16[2,128,1792]{2,1,0:T(8,128)(2,1)}, bf16[2,128,1792]{2,1,0:T(8,128)(2,1)}, u32[]{:S(2)}, u32[]{:S(2)}) %collective-permute-start.39) | collective-permute-done | bytes 917536 | tf_op jit(solution)/shard_map/ppermute | solution.py:105
  269.4 12.2 %gate_up.4 = (bf16[384,1024]{1,0:T(8,128)(2,1)S(1)}, f32[8,128]{1,0:T(8,128)S(1)}) custom-call(f32[2]{0:T(128)S(1)} %pad_maximum_fusion.5.scale_ref, f32[2,1,1792]{2,1,0:T(1,128)S(1)} %maximum_multiply_fusion.gain_ref, bf16[8,48,128]{2,1,0:T(8,128)(2,1)S(1)} %bitcast.69, bf16[384,1792]{1,0:T(8,128)(2,1)S(1)} %get-tuple-element.162.first_ref, ...), custom_call_target="tpu_custom_call" | custom-call | flops 374341632 | bytes 1376256 | tf_op jit(solution)/shard_map/gate_up/pallas_call | solution.py:278
  295.3 12.2 %gate_up.5 = (bf16[384,1024]{1,0:T(8,128)(2,1)S(1)}, f32[8,128]{1,0:T(8,128)S(1)}) custom-call(f32[2]{0:T(128)S(1)} %pad_maximum_fusion.5.scale_ref, f32[2,1,1792]{2,1,0:T(1,128)S(1)} %maximum_multiply_fusion.gain_ref, bf16[8,48,128]{2,1,0:T(8,128)(2,1)S(1)} %bitcast.67, bf16[384,1792]{1,0:T(8,128)(2,1)S(1)} %copy-done.27, f32[384,1]{1,0:T(8,128)S(1)} %copy-done.39, ...), custom_call_target="tpu_custom_call" | custom-call | flops 374341632 | bytes 1376256 | tf_op jit(solution)/shard_map/gate_up/pallas_call | solution.py:278
  307.6 12.2 %gate_up.6 = (bf16[384,1024]{1,0:T(8,128)(2,1)S(1)}, f32[8,128]{1,0:T(8,128)S(1)}) custom-call(f32[2]{0:T(128)S(1)} %pad_maximum_fusion.5.scale_ref, f32[2,1,1792]{2,1,0:T(1,128)S(1)} %maximum_multiply_fusion.gain_ref, bf16[8,48,128]{2,1,0:T(8,128)(2,1)S(1)} %bitcast.65, bf16[384,1792]{1,0:T(8,128)(2,1)S(1)} %copy-done.25, f32[384,1]{1,0:T(8,128)S(1)} %copy-done.37, ...), custom_call_target="tpu_custom_call" | custom-call | flops 374341632 | bytes 1376256 | tf_op jit(solution)/shard_map/gate_up/pallas_call | solution.py:278
  319.8 5.9 %down.8 = (bf16[4,128,1792]{2,1,0:T(8,128)(2,1)S(1)}, bf16[4,128,1792]{2,1,0:T(8,128)(2,1)}) custom-call(bf16[384,1024]{1,0:T(8,128)(2,1)S(1)} %get-tuple-element.193.hidden_ref, bf16[1,1024,3584]{2,1,0:T(8,128)(2,1)} %down_w.15, f32[384,1]{1,0:T(8,128)S(1)} %copy.43.factor_ref, bf16[8,128,48]{2,1,0:T(8,128)(2,1)S(1)} %get-tuple-element.195.spread_ref), custom_call_target="tpu_custom_call" | custom-call | flops 99090432 | bytes 458752 | tf_op jit(solution)/shard_map/down/pallas_call | solution.py:325
  349.3 11.6 %gate_up.7 = (bf16[384,1024]{1,0:T(8,128)(2,1)S(1)}, f32[8,128]{1,0:T(8,128)S(1)}) custom-call(f32[2]{0:T(128)S(1)} %pad_maximum_fusion.5.scale_ref, f32[2,1,1792]{2,1,0:T(1,128)S(1)} %maximum_multiply_fusion.gain_ref, bf16[8,48,128]{2,1,0:T(8,128)(2,1)S(1)} %bitcast.63, bf16[384,1792]{1,0:T(8,128)(2,1)S(1)} %copy-done.23, f32[384,1]{1,0:T(8,128)S(1)} %copy-done.35, ...), custom_call_target="tpu_custom_call" | custom-call | flops 374341632 | bytes 1376256 | tf_op jit(solution)/shard_map/gate_up/pallas_call | solution.py:278
  381.8 5.4 down.13
  388.4 5.5 %down.11 = (bf16[4,128,1792]{2,1,0:T(8,128)(2,1)S(1)}, bf16[4,128,1792]{2,1,0:T(8,128)(2,1)S(1)}) custom-call(bf16[384,1024]{1,0:T(8,128)(2,1)S(1)} %get-tuple-element.237.hidden_ref, bf16[1,1024,3584]{2,1,0:T(8,128)(2,1)} %down_w.15, f32[384,1]{1,0:T(8,128)S(1)} %copy-done.14, bf16[8,128,48]{2,1,0:T(8,128)(2,1)S(1)} %get-tuple-element.221.spread_ref), custom_call_target="tpu_custom_call" | custom-call | flops 99090432 | bytes 458752 | tf_op jit(solution)/shard_map/down/pallas_call | solution.py:325
  409.4 15.1 %collective-permute-done.68 = bf16[2,128,1792]{2,1,0:T(8,128)(2,1)S(1)} collective-permute-done((bf16[2,128,1792]{2,1,0:T(8,128)(2,1)S(1)}, bf16[2,128,1792]{2,1,0:T(8,128)(2,1)S(1)}, u32[]{:S(2)}, u32[]{:S(2)}) %collective-permute-start.68) | collective-permute-done | bytes 917536 | tf_op jit(solution)/shard_map/ppermute | solution.py:105
  432.1 13.1 %collective-permute-done.64 = bf16[2,128,1792]{2,1,0:T(8,128)(2,1)} collective-permute-done((bf16[2,128,1792]{2,1,0:T(8,128)(2,1)S(1)}, bf16[2,128,1792]{2,1,0:T(8,128)(2,1)}, u32[]{:S(2)}, u32[]{:S(2)}) %collective-permute-start.64) | collective-permute-done | bytes 917536 | tf_op jit(solution)/shard_map/ppermute | solution.py:105
  453.4 13.6 %collective-permute-done.70 = bf16[2,128,1792]{2,1,0:T(8,128)(2,1)} collective-permute-done((bf16[2,128,1792]{2,1,0:T(8,128)(2,1)}, bf16[2,128,1792]{2,1,0:T(8,128)(2,1)}, u32[]{:S(2)}, u32[]{:S(2)}) %collective-permute-start.70) | collective-permute-done | bytes 917536 | tf_op jit(solution)/shard_map/ppermute | solution.py:105
  471.3 16.9 %collective-permute-done.71 = bf16[2,128,1792]{2,1,0:T(8,128)(2,1)S(1)} collective-permute-done((bf16[2,128,1792]{2,1,0:T(8,128)(2,1)S(1)}, bf16[2,128,1792]{2,1,0:T(8,128)(2,1)S(1)}, u32[]{:S(2)}, u32[]{:S(2)}) %collective-permute-start.71) | collective-permute-done | bytes 917536 | tf_op jit(solution)/shard_map/ppermute | solution.py:105
  525.4 10.0 %reduce-scatter.11.cloned.1.call-done = bf16[128,1792]{1,0:T(8,128)(2,1)} async-done(((bf16[512,1792]{1,0:T(8,128)(2,1)}), bf16[128,1792]{1,0:T(8,128)(2,1)}) %reduce-scatter.11.cloned.1.call-update) | async-done | bytes 458768 | tf_op jit(solution)/shard_map/reduce_scatter | solution.py:526
  (372 shorter events, 253.6 us)
Async XLA Ops:
  7.2 92.7 %reduce-scatter.5.cloned.1.call-start = ((), (), s32[]{:S(2)}) async-start(), calls=%async_computation.4 | async-start | bytes 2293760 | tf_op jit(solution)/shard_map/reduce_scatter | solution.py:391
  8.8 23.4 %collective-permute-start.1 = (bf16[224,2048]{1,0:T(8,128)(2,1)S(1)}, bf16[224,2048]{1,0:T(8,128)(2,1)S(1)}, u32[]{:S(2)}, u32[]{:S(2)}) collective-permute-start(bf16[224,2048]{1,0:T(8,128)(2,1)S(1)} %get-tuple-element.282.refs_0_), channel_id=1, source_target_pairs={{0,8},{4,12},{8,0},{12,4},{16,24},{20,28},{24,16},{28,20},{1,9},{5... | collective-permute-start | bytes 2752520 | tf_op jit(solution)/shard_map/ppermute | solution.py:105
  23.2 26.1 %collective-permute-start = (bf16[224,2048]{1,0:T(8,128)(2,1)S(1)}, bf16[224,2048]{1,0:T(8,128)(2,1)}, u32[]{:S(2)}, u32[]{:S(2)}) collective-permute-start(bf16[224,2048]{1,0:T(8,128)(2,1)S(1)} %get-tuple-element.282.refs_0_), channel_id=1, source_target_pairs={{0,4},{4,0},{8,12},{12,8},{16,20},{20,16},{24,28},{28,24},{1,5},{5... | collective-permute-start | bytes 2752520 | tf_op jit(solution)/shard_map/ppermute | solution.py:105
  60.9 129.7 %reduce-scatter.7.cloned.1.call-start = ((), (), s32[]{:S(2)}) async-start(), calls=%async_computation.5 | async-start | bytes 2293760 | tf_op jit(solution)/shard_map/reduce_scatter | solution.py:391
  61.5 23.2 %collective-permute-start.18 = (bf16[224,2048]{1,0:T(8,128)(2,1)S(1)}, bf16[224,2048]{1,0:T(8,128)(2,1)}, u32[]{:S(2)}, u32[]{:S(2)}) collective-permute-start(bf16[224,2048]{1,0:T(8,128)(2,1)S(1)} %get-tuple-element.138.refs_0_), channel_id=1, source_target_pairs={{0,16},{4,20},{8,24},{12,28},{16,0},{20,4},{24,8},{28,12},{1,17},{... | collective-permute-start | bytes 2752520 | tf_op jit(solution)/shard_map/ppermute | solution.py:105
  64.3 39.3 %collective-permute-start.15 = (bf16[224,2048]{1,0:T(8,128)(2,1)S(1)}, bf16[224,2048]{1,0:T(8,128)(2,1)}, u32[]{:S(2)}, u32[]{:S(2)}) collective-permute-start(bf16[224,2048]{1,0:T(8,128)(2,1)S(1)} %get-tuple-element.138.refs_0_), channel_id=1, source_target_pairs={{0,4},{4,0},{8,12},{12,8},{16,20},{20,16},{24,28},{28,24},{1,5},{5... | collective-permute-start | bytes 2752520 | tf_op jit(solution)/shard_map/ppermute | solution.py:105
  124.1 27.8 %collective-permute-start.25 = (bf16[128,1792]{1,0:T(8,128)(2,1)}, bf16[128,1792]{1,0:T(8,128)(2,1)}, u32[]{:S(2)}, u32[]{:S(2)}) collective-permute-start(bf16[128,1792]{1,0:T(8,128)(2,1)} %collective-permute-done.24), channel_id=1, source_target_pairs={{2,3},{6,7},{10,11},{14,15},{18,19},{22,23},{26,27},{30,31}} | collective-permute-start | bytes 1376264 | tf_op jit(solution)/shard_map/ppermute | solution.py:115
  151.9 341.4 %reduce-scatter.9.cloned.1.call-start = ((), (), s32[]{:S(2)}) async-start(), calls=%async_computation.6 | async-start | bytes 2293760 | tf_op jit(solution)/shard_map/reduce_scatter | solution.py:511
  168.0 24.7 %collective-permute-start.30 = (bf16[4,128,1792]{2,1,0:T(8,128)(2,1)}, bf16[4,128,1792]{2,1,0:T(8,128)(2,1)}, u32[]{:S(2)}, u32[]{:S(2)}) collective-permute-start(bf16[4,128,1792]{2,1,0:T(8,128)(2,1)} %bitcast_dynamic-update-slice_fusion.4.refs_0_), channel_id=1, source_target_pairs={{0,4},{4,0},{8,12},{12,8},{16,20},{20,16},{24,28},{28,24},{1,5},{5... | collective-permute-start | bytes 5505032 | tf_op jit(solution)/shard_map/ppermute | solution.py:105
  168.0 42.7 %collective-permute-start.33 = (bf16[4,128,1792]{2,1,0:T(8,128)(2,1)}, bf16[4,128,1792]{2,1,0:T(8,128)(2,1)}, u32[]{:S(2)}, u32[]{:S(2)}) collective-permute-start(bf16[4,128,1792]{2,1,0:T(8,128)(2,1)} %bitcast_dynamic-update-slice_fusion.4.refs_0_), channel_id=1, source_target_pairs={{0,8},{4,12},{8,0},{12,4},{16,24},{20,28},{24,16},{28,20},{1,9},{5... | collective-permute-start | bytes 5505032 | tf_op jit(solution)/shard_map/ppermute | solution.py:105
  168.5 42.5 %collective-permute-start.34 = (bf16[4,128,1792]{2,1,0:T(8,128)(2,1)}, bf16[4,128,1792]{2,1,0:T(8,128)(2,1)}, u32[]{:S(2)}, u32[]{:S(2)}) collective-permute-start(bf16[4,128,1792]{2,1,0:T(8,128)(2,1)} %bitcast_dynamic-update-slice_fusion.4.refs_0_), channel_id=1, source_target_pairs={{0,16},{4,20},{8,24},{12,28},{16,0},{20,4},{24,8},{28,12},{1,17},{... | collective-permute-start | bytes 5505032 | tf_op jit(solution)/shard_map/ppermute | solution.py:105
  245.9 40.3 %collective-permute-start.41 = (bf16[4,128,1792]{2,1,0:T(8,128)(2,1)}, bf16[4,128,1792]{2,1,0:T(8,128)(2,1)}, u32[]{:S(2)}, u32[]{:S(2)}) collective-permute-start(bf16[4,128,1792]{2,1,0:T(8,128)(2,1)} %bitcast_dynamic-update-slice_fusion.refs_0_), channel_id=1, source_target_pairs={{0,8},{4,12},{8,0},{12,4},{16,24},{20,28},{24,16},{28,20},{1,9},{5... | collective-permute-start | bytes 5505032 | tf_op jit(solution)/shard_map/ppermute | solution.py:105
  247.2 39.9 %collective-permute-start.42 = (bf16[4,128,1792]{2,1,0:T(8,128)(2,1)}, bf16[4,128,1792]{2,1,0:T(8,128)(2,1)}, u32[]{:S(2)}, u32[]{:S(2)}) collective-permute-start(bf16[4,128,1792]{2,1,0:T(8,128)(2,1)} %bitcast_dynamic-update-slice_fusion.refs_0_), channel_id=1, source_target_pairs={{0,16},{4,20},{8,24},{12,28},{16,0},{20,4},{24,8},{28,12},{1,17},{... | collective-permute-start | bytes 5505032 | tf_op jit(solution)/shard_map/ppermute | solution.py:105
  292.0 27.9 %collective-permute-start.48 = (bf16[2,128,1792]{2,1,0:T(8,128)(2,1)}, bf16[2,128,1792]{2,1,0:T(8,128)(2,1)}, u32[]{:S(2)}, u32[]{:S(2)}) collective-permute-start(bf16[2,128,1792]{2,1,0:T(8,128)(2,1)} %slice.164), channel_id=1, source_target_pairs={{0,16},{4,20},{8,24},{12,28},{16,0},{20,4},{24,8},{28,12},{1,17},{... | collective-permute-start | bytes 2752520 | tf_op jit(solution)/shard_map/ppermute | solution.py:105
  292.5 27.4 %collective-permute-start.49 = (bf16[2,128,1792]{2,1,0:T(8,128)(2,1)}, bf16[2,128,1792]{2,1,0:T(8,128)(2,1)}, u32[]{:S(2)}, u32[]{:S(2)}) collective-permute-start(bf16[2,128,1792]{2,1,0:T(8,128)(2,1)} %slice.165), channel_id=1, source_target_pairs={{0,8},{4,12},{8,0},{12,4},{16,24},{20,28},{24,16},{28,20},{1,9},{5... | collective-permute-start | bytes 2752520 | tf_op jit(solution)/shard_map/ppermute | solution.py:105
  341.5 24.2 %collective-permute-start.56 = (bf16[2,128,1792]{2,1,0:T(8,128)(2,1)}, bf16[2,128,1792]{2,1,0:T(8,128)(2,1)}, u32[]{:S(2)}, u32[]{:S(2)}) collective-permute-start(bf16[2,128,1792]{2,1,0:T(8,128)(2,1)} %get-tuple-element.216), channel_id=1, source_target_pairs={{0,8},{4,12},{8,0},{12,4},{16,24},{20,28},{24,16},{28,20},{1,9},{5... | collective-permute-start | bytes 2752520 | tf_op jit(solution)/shard_map/ppermute | solution.py:105
  342.3 23.4 %collective-permute-start.57 = (bf16[2,128,1792]{2,1,0:T(8,128)(2,1)}, bf16[2,128,1792]{2,1,0:T(8,128)(2,1)}, u32[]{:S(2)}, u32[]{:S(2)}) collective-permute-start(bf16[2,128,1792]{2,1,0:T(8,128)(2,1)} %get-tuple-element.217), channel_id=1, source_target_pairs={{0,16},{4,20},{8,24},{12,28},{16,0},{20,4},{24,8},{28,12},{1,17},{... | collective-permute-start | bytes 2752520 | tf_op jit(solution)/shard_map/ppermute | solution.py:105
  371.2 27.6 %collective-permute-start.59 = (bf16[2,128,1792]{2,1,0:T(8,128)(2,1)}, bf16[2,128,1792]{2,1,0:T(8,128)(2,1)}, u32[]{:S(2)}, u32[]{:S(2)}) collective-permute-start(bf16[2,128,1792]{2,1,0:T(8,128)(2,1)} %get-tuple-element.276), channel_id=1, source_target_pairs={{0,8},{4,12},{8,0},{12,4},{16,24},{20,28},{24,16},{28,20},{1,9},{5... | collective-permute-start | bytes 2752520 | tf_op jit(solution)/shard_map/ppermute | solution.py:105
  372.1 26.7 %collective-permute-start.60 = (bf16[2,128,1792]{2,1,0:T(8,128)(2,1)}, bf16[2,128,1792]{2,1,0:T(8,128)(2,1)}, u32[]{:S(2)}, u32[]{:S(2)}) collective-permute-start(bf16[2,128,1792]{2,1,0:T(8,128)(2,1)} %get-tuple-element.275), channel_id=1, source_target_pairs={{0,16},{4,20},{8,24},{12,28},{16,0},{20,4},{24,8},{28,12},{1,17},{... | collective-permute-start | bytes 2752520 | tf_op jit(solution)/shard_map/ppermute | solution.py:105
  399.4 27.2 %collective-permute-start.67 = (bf16[4,128,1792]{2,1,0:T(8,128)(2,1)S(1)}, bf16[4,128,1792]{2,1,0:T(8,128)(2,1)S(1)}, u32[]{:S(2)}, u32[]{:S(2)}) collective-permute-start(bf16[4,128,1792]{2,1,0:T(8,128)(2,1)S(1)} %get-tuple-element.247), channel_id=1, source_target_pairs={{0,4},{4,0},{8,12},{12,8},{16,20},{20,16},{24,28},{28,24},{1,5},{5... | collective-permute-start | bytes 5505032 | tf_op jit(solution)/shard_map/ppermute | solution.py:105
  399.5 30.9 %collective-permute-start.62 = (bf16[4,128,1792]{2,1,0:T(8,128)(2,1)S(1)}, bf16[4,128,1792]{2,1,0:T(8,128)(2,1)S(1)}, u32[]{:S(2)}, u32[]{:S(2)}) collective-permute-start(bf16[4,128,1792]{2,1,0:T(8,128)(2,1)S(1)} %get-tuple-element.241), channel_id=1, source_target_pairs={{0,4},{4,0},{8,12},{12,8},{16,20},{20,16},{24,28},{28,24},{1,5},{5... | collective-permute-start | bytes 5505032 | tf_op jit(solution)/shard_map/ppermute | solution.py:105
  403.4 23.2 %collective-permute-start.69 = (bf16[2,128,1792]{2,1,0:T(8,128)(2,1)S(1)}, bf16[2,128,1792]{2,1,0:T(8,128)(2,1)S(1)}, u32[]{:S(2)}, u32[]{:S(2)}) collective-permute-start(bf16[2,128,1792]{2,1,0:T(8,128)(2,1)S(1)} %get-tuple-element.250), channel_id=1, source_target_pairs={{0,8},{4,12},{8,0},{12,4},{16,24},{20,28},{24,16},{28,20},{1,9},{5... | collective-permute-start | bytes 2752520 | tf_op jit(solution)/shard_map/ppermute | solution.py:105
  408.2 37.0 %collective-permute-start.64 = (bf16[2,128,1792]{2,1,0:T(8,128)(2,1)S(1)}, bf16[2,128,1792]{2,1,0:T(8,128)(2,1)}, u32[]{:S(2)}, u32[]{:S(2)}) collective-permute-start(bf16[2,128,1792]{2,1,0:T(8,128)(2,1)S(1)} %add_convert_fusion.10), channel_id=1, source_target_pairs={{0,8},{4,12},{8,0},{12,4},{16,24},{20,28},{24,16},{28,20},{1,9},{5... | collective-permute-start | bytes 2752520 | tf_op jit(solution)/shard_map/ppermute | solution.py:105
  447.1 88.3 %reduce-scatter.11.cloned.1.call-start = ((), (), s32[]{:S(2)}) async-start(), calls=%async_computation.7 | async-start | bytes 2293760 | tf_op jit(solution)/shard_map/reduce_scatter | solution.py:526
  (117 other events, 1435.8 us)
Sparse Core Ops, SparseCore 0:
  61.0 38.7 reduce-scatter.4
  152.1 38.5 reduce-scatter.6
  447.2 41.9 reduce-scatter.8
  493.5 41.8 reduce-scatter.10

commit v11 on v10

--- a/solution.py
+++ b/solution.py
@@ -320,7 +320,7 @@
 def down(hidden_q, w_down, factor, spread, start, width):
     rows, hidden = hidden_q.shape
     sources, tokens, capacity = spread.shape
-    tile = width // 2 if width % 256 == 0 else width
+    tile = next(t for t in (1024, 512, 256, 128) if start % t == 0 and width % t == 0)
     whole = lambda shape: pl.BlockSpec(shape, lambda j: (0,) * len(shape))
     return pl.pallas_call(
         down_kernel,
@@ -485,7 +485,9 @@
     across, hidden = tie(across, hidden)
     groups.append((first[3], both_cores(across)))
 
-    spans = [(c * step, step) for c in range(CHUNKS)]
+    unit = 512 if width % 512 == 0 else 128
+    cut = (width // unit + 1) // 2 * unit
+    spans = [(0, cut), (cut, width - cut)]
 
     def outputs(r, c):
         return down(hidden[r][0], w_down, factor[r], spread[r], *spans[c])

time: 553 us -> 553 us (level)
    ppermute x5, starting transfers between devices: 8.72 us -> 2.05 us  [peaks_over_all(): peaks = jnp.maximum(peaks, lax.ppermute(peaks, axis, pairs))]
    ppermute x5, waiting for transfers between devices: 14.3 us -> 20.7 us  [peaks_over_all(): peaks = jnp.maximum(peaks, lax.ppermute(peaks, axis, pairs))]
    unnamed x117 -> x127, local copies, waits for them, and re-layouts: 22 us -> 23.6 us
  transfers between devices with their start and end apart: 83 -> 83, of which waited for: 41 -> 45; matrix products, arithmetic and copies ran while one was open for 12% -> 12% of each run, Pallas kernels for 19% -> 19%
where the time goes in v11:
time: 553 us; the launch traced here: 543 us
  waiting for transfers between devices  235 us (42%)
  Pallas kernels  118 us (21%)
  starting transfers between devices  74.8 us (14%)
  local copies, waits for them, and re-layouts  47.3 us (9%)
  other arithmetic  45.8 us (8%)
  between operations  21.6 us (4%)
    ppermute x59, waiting for transfers between devices, swap(): return lax.ppermute(value, 'dp', [(i, i ^ bits) for i in range(count)])  148 us
    pallas_call x4, Pallas kernels, gate_up(): pl.pallas_call(gate_up_kernel, grid=(hidden // tile,), in_specs=[pl.Block...  48.3 us
    pallas_call x8, Pallas kernels, down(): pl.pallas_call(down_kernel, grid=(width // tile,), in_specs=[whole(hidden...  40.3 us
    ppermute x59, starting transfers between devices, swap(): return lax.ppermute(value, 'dp', [(i, i ^ bits) for i in range(count)])  36.1 us
    unnamed x127, local copies, waits for them, and re-layouts  23.6 us
    reduce_scatter x2, waiting for transfers between devices, summed_over_tensor(): total = lax.psum_scatter(terms, 'tensor', scatter_dimension=0, tiled=True)  22.2 us
    ppermute x6, waiting for transfers between devices, along_tensor(): lax.ppermute(above, 'tensor', back)  21.1 us
    ppermute x5, waiting for transfers between devices, peaks_over_all(): peaks = jnp.maximum(peaks, lax.ppermute(peaks, axis, pairs))  20.7 us
  transfers between devices with their start and end apart: 83, of which 45 were waited for; matrix products, arithmetic and copies ran while one was open for 12% of the time, Pallas kernels for 19%

profile of v11, /device:TPU:0, one launch (start us, length us, event | category | flops | bytes accessed | tf_op | source)
XLA Modules:
  0.0 543.5 jit_solution(17144158049797277925)
XLA Ops:
  24.5 7.8 %collective-permute-done.2.refs_4_ = bf16[224,2048]{1,0:T(8,128)(2,1)} collective-permute-done((bf16[224,2048]{1,0:T(8,128)(2,1)S(1)}, bf16[224,2048]{1,0:T(8,128)(2,1)}, u32[]{:S(2)}, u32[]{:S(2)}) %collective-permute-start.2) | collective-permute-done | bytes 917536 | tf_op jit(solution)/shard_map/ppermute | solution.py:105
  37.4 8.6 %collective-permute-done.10.refs_7_ = bf16[112,2048]{1,0:T(8,128)(2,1)S(1)} collective-permute-done((bf16[112,2048]{1,0:T(8,128)(2,1)S(1)}, bf16[112,2048]{1,0:T(8,128)(2,1)S(1)}, u32[]{:S(2)}, u32[]{:S(2)}) %collective-permute-start.10) | collective-permute-done | bytes 458784 | tf_op jit(solution)/shard_map/ppermute | solution.py:105
  49.5 9.5 %project.2 = bf16[512,1792]{1,0:T(8,128)(2,1)} custom-call(s32[1]{0:T(128)} %bitcast.2.place_ref, bf16[512,2048]{1,0:T(8,128)(2,1)} %attn_ref.3, bf16[224,2048]{1,0:T(8,128)(2,1)S(1)} %get-tuple-element.282.refs_0_, bf16[224,2048]{1,0:T(8,128)(2,1)} %collective-permute-done.refs_1_, bf16[224,2048]{1,0:T(8,128)(2,1)S(1)} %collective-permute-done.1.refs_2_, ...), custom_call_target="tpu_custom_call" | custom-call | flops 234881024 | bytes 589824 | tf_op jit(solution)/shard_map/project/pallas_call | solution.py:186
  62.9 18.7 %collective-permute-done.18.refs_4_ = bf16[224,2048]{1,0:T(8,128)(2,1)} collective-permute-done((bf16[224,2048]{1,0:T(8,128)(2,1)S(1)}, bf16[224,2048]{1,0:T(8,128)(2,1)}, u32[]{:S(2)}, u32[]{:S(2)}) %collective-permute-start.18) | collective-permute-done | bytes 917536 | tf_op jit(solution)/shard_map/ppermute | solution.py:105
  87.4 8.0 %collective-permute-done.21.refs_7_ = bf16[112,2048]{1,0:T(8,128)(2,1)S(1)} collective-permute-done((bf16[112,2048]{1,0:T(8,128)(2,1)}, bf16[112,2048]{1,0:T(8,128)(2,1)S(1)}, u32[]{:S(2)}, u32[]{:S(2)}) %collective-permute-start.21) | collective-permute-done | bytes 458784 | tf_op jit(solution)/shard_map/ppermute | solution.py:105
  105.8 8.6 %collective-permute-done.13 = bf16[128,1792]{1,0:T(8,128)(2,1)S(1)} collective-permute-done((bf16[128,1792]{1,0:T(8,128)(2,1)S(1)}, bf16[128,1792]{1,0:T(8,128)(2,1)S(1)}, u32[]{:S(2)}, u32[]{:S(2)}) %collective-permute-start.13) | collective-permute-done | bytes 458784 | tf_op jit(solution)/shard_map/ppermute | solution.py:115
  124.1 12.1 %collective-permute-done.26 = bf16[128,1792]{1,0:T(8,128)(2,1)} collective-permute-done((bf16[128,1792]{1,0:T(8,128)(2,1)S(1)}, bf16[128,1792]{1,0:T(8,128)(2,1)}, u32[]{:S(2)}, u32[]{:S(2)}) %collective-permute-start.26) | collective-permute-done | bytes 458784 | tf_op jit(solution)/shard_map/ppermute | solution.py:115
  138.6 9.4 %project.3 = bf16[512,1792]{1,0:T(8,128)(2,1)} custom-call(s32[1]{0:T(128)} %bitcast.2.place_ref, bf16[512,2048]{1,0:T(8,128)(2,1)} %attn_ref.3, bf16[224,2048]{1,0:T(8,128)(2,1)S(1)} %get-tuple-element.138.refs_0_, bf16[224,2048]{1,0:T(8,128)(2,1)} %collective-permute-done.15.refs_1_, bf16[224,2048]{1,0:T(8,128)(2,1)S(1)} %collective-permute-done.16.refs_2_, ...), custom_call_target="tpu_custom_call" | custom-call | flops 234881024 | bytes 589824 | tf_op jit(solution)/shard_map/project/pallas_call | solution.py:186
  149.3 11.2 %reduce-scatter.9.cloned.1.call-start = ((), (), s32[]{:S(2)}) async-start(), calls=%async_computation.6 | async-start | bytes 2621440 | tf_op jit(solution)/shard_map/reduce_scatter | solution.py:513
  168.8 20.8 %reduce-scatter.7.cloned.1.call-done = bf16[128,1792]{1,0:T(8,128)(2,1)} async-done(((bf16[512,1792]{1,0:T(8,128)(2,1)}), bf16[128,1792]{1,0:T(8,128)(2,1)}) %reduce-scatter.7.cloned.1.call-update) | async-done | bytes 458768 | tf_op jit(solution)/shard_map/reduce_scatter | solution.py:391
  198.4 9.8 %collective-permute-done.34.refs_0_ = bf16[4,128,1792]{2,1,0:T(8,128)(2,1)} collective-permute-done((bf16[4,128,1792]{2,1,0:T(8,128)(2,1)}, bf16[4,128,1792]{2,1,0:T(8,128)(2,1)}, u32[]{:S(2)}, u32[]{:S(2)}) %collective-permute-start.34) | collective-permute-done | bytes 1835040 | tf_op jit(solution)/shard_map/ppermute | solution.py:105
  229.5 6.7 %collective-permute-done.40.refs_1_ = bf16[2,128,1792]{2,1,0:T(8,128)(2,1)} collective-permute-done((bf16[2,128,1792]{2,1,0:T(8,128)(2,1)}, bf16[2,128,1792]{2,1,0:T(8,128)(2,1)}, u32[]{:S(2)}, u32[]{:S(2)}) %collective-permute-start.40) | collective-permute-done | bytes 917536 | tf_op jit(solution)/shard_map/ppermute | solution.py:105
  267.4 12.2 %gate_up.4 = (bf16[384,1024]{1,0:T(8,128)(2,1)S(1)}, f32[8,128]{1,0:T(8,128)S(1)}) custom-call(f32[2]{0:T(128)S(1)} %pad_maximum_fusion.5.scale_ref, f32[2,1,1792]{2,1,0:T(1,128)S(1)} %maximum_multiply_fusion.gain_ref, bf16[8,48,128]{2,1,0:T(8,128)(2,1)S(1)} %bitcast.69, bf16[384,1792]{1,0:T(8,128)(2,1)S(1)} %get-tuple-element.162.first_ref, ...), custom_call_target="tpu_custom_call" | custom-call | flops 374341632 | bytes 1376256 | tf_op jit(solution)/shard_map/gate_up/pallas_call | solution.py:278
  279.6 7.2 %collective-permute-done.42.refs_0_ = bf16[4,128,1792]{2,1,0:T(8,128)(2,1)} collective-permute-done((bf16[4,128,1792]{2,1,0:T(8,128)(2,1)}, bf16[4,128,1792]{2,1,0:T(8,128)(2,1)}, u32[]{:S(2)}, u32[]{:S(2)}) %collective-permute-start.42) | collective-permute-done | bytes 1835040 | tf_op jit(solution)/shard_map/ppermute | solution.py:105
  296.4 12.2 %gate_up.5 = (bf16[384,1024]{1,0:T(8,128)(2,1)S(1)}, f32[8,128]{1,0:T(8,128)S(1)}) custom-call(f32[2]{0:T(128)S(1)} %pad_maximum_fusion.5.scale_ref, f32[2,1,1792]{2,1,0:T(1,128)S(1)} %maximum_multiply_fusion.gain_ref, bf16[8,48,128]{2,1,0:T(8,128)(2,1)S(1)} %bitcast.67, bf16[384,1792]{1,0:T(8,128)(2,1)S(1)} %copy-done.26, f32[384,1]{1,0:T(8,128)S(1)} %copy-done.38, ...), custom_call_target="tpu_custom_call" | custom-call | flops 374341632 | bytes 1376256 | tf_op jit(solution)/shard_map/gate_up/pallas_call | solution.py:278
  308.7 12.2 %gate_up.6 = (bf16[384,1024]{1,0:T(8,128)(2,1)S(1)}, f32[8,128]{1,0:T(8,128)S(1)}) custom-call(f32[2]{0:T(128)S(1)} %pad_maximum_fusion.5.scale_ref, f32[2,1,1792]{2,1,0:T(1,128)S(1)} %maximum_multiply_fusion.gain_ref, bf16[8,48,128]{2,1,0:T(8,128)(2,1)S(1)} %bitcast.65, bf16[384,1792]{1,0:T(8,128)(2,1)S(1)} %copy-done.24, f32[384,1]{1,0:T(8,128)S(1)} %copy-done.36, ...), custom_call_target="tpu_custom_call" | custom-call | flops 374341632 | bytes 1376256 | tf_op jit(solution)/shard_map/gate_up/pallas_call | solution.py:278
  321.0 6.3 %down.9 = (bf16[4,128,2048]{2,1,0:T(8,128)(2,1)S(1)}, bf16[4,128,2048]{2,1,0:T(8,128)(2,1)}) custom-call(bf16[384,1024]{1,0:T(8,128)(2,1)S(1)} %get-tuple-element.198.hidden_ref, bf16[1,1024,3584]{2,1,0:T(8,128)(2,1)} %down_w.15, f32[384,1]{1,0:T(8,128)S(1)} %copy.44.factor_ref, bf16[8,128,48]{2,1,0:T(8,128)(2,1)S(1)} %get-tuple-element.200.spread_ref), custom_call_target="tpu_custom_call" | custom-call | flops 113246208 | bytes 524288 | tf_op jit(solution)/shard_map/down/pallas_call | solution.py:325
  351.3 11.7 %gate_up.7 = (bf16[384,1024]{1,0:T(8,128)(2,1)S(1)}, f32[8,128]{1,0:T(8,128)S(1)}) custom-call(f32[2]{0:T(128)S(1)} %pad_maximum_fusion.5.scale_ref, f32[2,1,1792]{2,1,0:T(1,128)S(1)} %maximum_multiply_fusion.gain_ref, bf16[8,48,128]{2,1,0:T(8,128)(2,1)S(1)} %bitcast.63, bf16[384,1792]{1,0:T(8,128)(2,1)S(1)} %copy-done.22, f32[384,1]{1,0:T(8,128)S(1)} %copy-done.34, ...), custom_call_target="tpu_custom_call" | custom-call | flops 374341632 | bytes 1376256 | tf_op jit(solution)/shard_map/gate_up/pallas_call | solution.py:278
  393.4 5.7 %down.11 = (bf16[4,128,2048]{2,1,0:T(8,128)(2,1)S(1)}, bf16[4,128,2048]{2,1,0:T(8,128)(2,1)S(1)}) custom-call(bf16[384,1024]{1,0:T(8,128)(2,1)S(1)} %get-tuple-element.237.hidden_ref, bf16[1,1024,3584]{2,1,0:T(8,128)(2,1)} %down_w.15, f32[384,1]{1,0:T(8,128)S(1)} %copy-done.12, bf16[8,128,48]{2,1,0:T(8,128)(2,1)S(1)} %get-tuple-element.221.spread_ref), custom_call_target="tpu_custom_call" | custom-call | flops 113246208 | bytes 524288 | tf_op jit(solution)/shard_map/down/pallas_call | solution.py:325
  416.0 17.1 %collective-permute-done.68 = bf16[2,128,2048]{2,1,0:T(8,128)(2,1)S(1)} collective-permute-done((bf16[2,128,2048]{2,1,0:T(8,128)(2,1)S(1)}, bf16[2,128,2048]{2,1,0:T(8,128)(2,1)S(1)}, u32[]{:S(2)}, u32[]{:S(2)}) %collective-permute-start.68) | collective-permute-done | bytes 1048608 | tf_op jit(solution)/shard_map/ppermute | solution.py:105
  439.6 10.8 %collective-permute-done.64 = bf16[2,128,1536]{2,1,0:T(8,128)(2,1)S(1)} collective-permute-done((bf16[2,128,1536]{2,1,0:T(8,128)(2,1)S(1)}, bf16[2,128,1536]{2,1,0:T(8,128)(2,1)S(1)}, u32[]{:S(2)}, u32[]{:S(2)}) %collective-permute-start.64) | collective-permute-done | bytes 786464 | tf_op jit(solution)/shard_map/ppermute | solution.py:105
  458.1 12.8 %collective-permute-done.70 = bf16[2,128,1536]{2,1,0:T(8,128)(2,1)S(1)} collective-permute-done((bf16[2,128,1536]{2,1,0:T(8,128)(2,1)}, bf16[2,128,1536]{2,1,0:T(8,128)(2,1)S(1)}, u32[]{:S(2)}, u32[]{:S(2)}) %collective-permute-start.70) | collective-permute-done | bytes 786464 | tf_op jit(solution)/shard_map/ppermute | solution.py:105
  473.0 15.8 %collective-permute-done.71 = bf16[2,128,1536]{2,1,0:T(8,128)(2,1)S(1)} collective-permute-done((bf16[2,128,1536]{2,1,0:T(8,128)(2,1)S(1)}, bf16[2,128,1536]{2,1,0:T(8,128)(2,1)S(1)}, u32[]{:S(2)}, u32[]{:S(2)}) %collective-permute-start.71) | collective-permute-done | bytes 786464 | tf_op jit(solution)/shard_map/ppermute | solution.py:105
  492.1 5.7 %reduce-scatter.9.cloned.1.call-done = bf16[128,2048]{1,0:T(8,128)(2,1)} async-done(((bf16[512,2048]{1,0:T(8,128)(2,1)}), bf16[128,2048]{1,0:T(8,128)(2,1)}) %reduce-scatter.9.cloned.1.call-update) | async-done | bytes 524304 | tf_op jit(solution)/shard_map/reduce_scatter | solution.py:513
  (382 shorter events, 261.1 us)
Async XLA Ops:
  7.2 91.0 %reduce-scatter.5.cloned.1.call-start = ((), (), s32[]{:S(2)}) async-start(), calls=%async_computation.4 | async-start | bytes 2293760 | tf_op jit(solution)/shard_map/reduce_scatter | solution.py:391
  23.2 24.1 %collective-permute-start = (bf16[224,2048]{1,0:T(8,128)(2,1)S(1)}, bf16[224,2048]{1,0:T(8,128)(2,1)}, u32[]{:S(2)}, u32[]{:S(2)}) collective-permute-start(bf16[224,2048]{1,0:T(8,128)(2,1)S(1)} %get-tuple-element.282.refs_0_), channel_id=1, source_target_pairs={{0,4},{4,0},{8,12},{12,8},{16,20},{20,16},{24,28},{28,24},{1,5},{5... | collective-permute-start | bytes 2752520 | tf_op jit(solution)/shard_map/ppermute | solution.py:105
  59.0 130.5 %reduce-scatter.7.cloned.1.call-start = ((), (), s32[]{:S(2)}) async-start(), calls=%async_computation.5 | async-start | bytes 2293760 | tf_op jit(solution)/shard_map/reduce_scatter | solution.py:391
  59.7 24.5 %collective-permute-start.16 = (bf16[224,2048]{1,0:T(8,128)(2,1)S(1)}, bf16[224,2048]{1,0:T(8,128)(2,1)S(1)}, u32[]{:S(2)}, u32[]{:S(2)}) collective-permute-start(bf16[224,2048]{1,0:T(8,128)(2,1)S(1)} %get-tuple-element.138.refs_0_), channel_id=1, source_target_pairs={{0,8},{4,12},{8,0},{12,4},{16,24},{20,28},{24,16},{28,20},{1,9},{5... | collective-permute-start | bytes 2752520 | tf_op jit(solution)/shard_map/ppermute | solution.py:105
  62.9 39.0 %collective-permute-start.15 = (bf16[224,2048]{1,0:T(8,128)(2,1)S(1)}, bf16[224,2048]{1,0:T(8,128)(2,1)}, u32[]{:S(2)}, u32[]{:S(2)}) collective-permute-start(bf16[224,2048]{1,0:T(8,128)(2,1)S(1)} %get-tuple-element.138.refs_0_), channel_id=1, source_target_pairs={{0,4},{4,0},{8,12},{12,8},{16,20},{20,16},{24,28},{28,24},{1,5},{5... | collective-permute-start | bytes 2752520 | tf_op jit(solution)/shard_map/ppermute | solution.py:105
  122.6 26.3 %collective-permute-start.25 = (bf16[128,1792]{1,0:T(8,128)(2,1)}, bf16[128,1792]{1,0:T(8,128)(2,1)}, u32[]{:S(2)}, u32[]{:S(2)}) collective-permute-start(bf16[128,1792]{1,0:T(8,128)(2,1)} %collective-permute-done.24), channel_id=1, source_target_pairs={{2,3},{6,7},{10,11},{14,15},{18,19},{22,23},{26,27},{30,31}} | collective-permute-start | bytes 1376264 | tf_op jit(solution)/shard_map/ppermute | solution.py:115
  149.3 348.5 %reduce-scatter.9.cloned.1.call-start = ((), (), s32[]{:S(2)}) async-start(), calls=%async_computation.6 | async-start | bytes 2621440 | tf_op jit(solution)/shard_map/reduce_scatter | solution.py:513
  165.3 26.3 %collective-permute-start.30 = (bf16[4,128,1792]{2,1,0:T(8,128)(2,1)}, bf16[4,128,1792]{2,1,0:T(8,128)(2,1)}, u32[]{:S(2)}, u32[]{:S(2)}) collective-permute-start(bf16[4,128,1792]{2,1,0:T(8,128)(2,1)} %bitcast_dynamic-update-slice_fusion.4.refs_0_), channel_id=1, source_target_pairs={{0,4},{4,0},{8,12},{12,8},{16,20},{20,16},{24,28},{28,24},{1,5},{5... | collective-permute-start | bytes 5505032 | tf_op jit(solution)/shard_map/ppermute | solution.py:105
  165.4 42.8 %collective-permute-start.34 = (bf16[4,128,1792]{2,1,0:T(8,128)(2,1)}, bf16[4,128,1792]{2,1,0:T(8,128)(2,1)}, u32[]{:S(2)}, u32[]{:S(2)}) collective-permute-start(bf16[4,128,1792]{2,1,0:T(8,128)(2,1)} %bitcast_dynamic-update-slice_fusion.4.refs_0_), channel_id=1, source_target_pairs={{0,16},{4,20},{8,24},{12,28},{16,0},{20,4},{24,8},{28,12},{1,17},{... | collective-permute-start | bytes 5505032 | tf_op jit(solution)/shard_map/ppermute | solution.py:105
  166.8 42.5 %collective-permute-start.33 = (bf16[4,128,1792]{2,1,0:T(8,128)(2,1)}, bf16[4,128,1792]{2,1,0:T(8,128)(2,1)}, u32[]{:S(2)}, u32[]{:S(2)}) collective-permute-start(bf16[4,128,1792]{2,1,0:T(8,128)(2,1)} %bitcast_dynamic-update-slice_fusion.4.refs_0_), channel_id=1, source_target_pairs={{0,8},{4,12},{8,0},{12,4},{16,24},{20,28},{24,16},{28,20},{1,9},{5... | collective-permute-start | bytes 5505032 | tf_op jit(solution)/shard_map/ppermute | solution.py:105
  244.0 42.7 %collective-permute-start.42 = (bf16[4,128,1792]{2,1,0:T(8,128)(2,1)}, bf16[4,128,1792]{2,1,0:T(8,128)(2,1)}, u32[]{:S(2)}, u32[]{:S(2)}) collective-permute-start(bf16[4,128,1792]{2,1,0:T(8,128)(2,1)} %bitcast_dynamic-update-slice_fusion.refs_0_), channel_id=1, source_target_pairs={{0,16},{4,20},{8,24},{12,28},{16,0},{20,4},{24,8},{28,12},{1,17},{... | collective-permute-start | bytes 5505032 | tf_op jit(solution)/shard_map/ppermute | solution.py:105
  244.6 42.5 %collective-permute-start.41 = (bf16[4,128,1792]{2,1,0:T(8,128)(2,1)}, bf16[4,128,1792]{2,1,0:T(8,128)(2,1)}, u32[]{:S(2)}, u32[]{:S(2)}) collective-permute-start(bf16[4,128,1792]{2,1,0:T(8,128)(2,1)} %bitcast_dynamic-update-slice_fusion.refs_0_), channel_id=1, source_target_pairs={{0,8},{4,12},{8,0},{12,4},{16,24},{20,28},{24,16},{28,20},{1,9},{5... | collective-permute-start | bytes 5505032 | tf_op jit(solution)/shard_map/ppermute | solution.py:105
  292.0 28.9 %collective-permute-start.49 = (bf16[2,128,1792]{2,1,0:T(8,128)(2,1)}, bf16[2,128,1792]{2,1,0:T(8,128)(2,1)}, u32[]{:S(2)}, u32[]{:S(2)}) collective-permute-start(bf16[2,128,1792]{2,1,0:T(8,128)(2,1)} %slice.165), channel_id=1, source_target_pairs={{0,8},{4,12},{8,0},{12,4},{16,24},{20,28},{24,16},{28,20},{1,9},{5... | collective-permute-start | bytes 2752520 | tf_op jit(solution)/shard_map/ppermute | solution.py:105
  293.2 27.7 %collective-permute-start.48 = (bf16[2,128,1792]{2,1,0:T(8,128)(2,1)}, bf16[2,128,1792]{2,1,0:T(8,128)(2,1)}, u32[]{:S(2)}, u32[]{:S(2)}) collective-permute-start(bf16[2,128,1792]{2,1,0:T(8,128)(2,1)} %slice.164), channel_id=1, source_target_pairs={{0,16},{4,20},{8,24},{12,28},{16,0},{20,4},{24,8},{28,12},{1,17},{... | collective-permute-start | bytes 2752520 | tf_op jit(solution)/shard_map/ppermute | solution.py:105
  344.6 25.8 %collective-permute-start.56 = (bf16[2,128,2048]{2,1,0:T(8,128)(2,1)}, bf16[2,128,2048]{2,1,0:T(8,128)(2,1)}, u32[]{:S(2)}, u32[]{:S(2)}) collective-permute-start(bf16[2,128,2048]{2,1,0:T(8,128)(2,1)} %get-tuple-element.216), channel_id=1, source_target_pairs={{0,8},{4,12},{8,0},{12,4},{16,24},{20,28},{24,16},{28,20},{1,9},{5... | collective-permute-start | bytes 3145736 | tf_op jit(solution)/shard_map/ppermute | solution.py:105
  345.3 25.5 %collective-permute-start.57 = (bf16[2,128,2048]{2,1,0:T(8,128)(2,1)}, bf16[2,128,2048]{2,1,0:T(8,128)(2,1)}, u32[]{:S(2)}, u32[]{:S(2)}) collective-permute-start(bf16[2,128,2048]{2,1,0:T(8,128)(2,1)} %get-tuple-element.217), channel_id=1, source_target_pairs={{0,16},{4,20},{8,24},{12,28},{16,0},{20,4},{24,8},{28,12},{1,17},{... | collective-permute-start | bytes 3145736 | tf_op jit(solution)/shard_map/ppermute | solution.py:105
  377.1 26.5 %collective-permute-start.60 = (bf16[2,128,2048]{2,1,0:T(8,128)(2,1)}, bf16[2,128,2048]{2,1,0:T(8,128)(2,1)}, u32[]{:S(2)}, u32[]{:S(2)}) collective-permute-start(bf16[2,128,2048]{2,1,0:T(8,128)(2,1)} %get-tuple-element.271), channel_id=1, source_target_pairs={{0,16},{4,20},{8,24},{12,28},{16,0},{20,4},{24,8},{28,12},{1,17},{... | collective-permute-start | bytes 3145736 | tf_op jit(solution)/shard_map/ppermute | solution.py:105
  377.7 25.9 %collective-permute-start.59 = (bf16[2,128,2048]{2,1,0:T(8,128)(2,1)}, bf16[2,128,2048]{2,1,0:T(8,128)(2,1)}, u32[]{:S(2)}, u32[]{:S(2)}) collective-permute-start(bf16[2,128,2048]{2,1,0:T(8,128)(2,1)} %get-tuple-element.272), channel_id=1, source_target_pairs={{0,8},{4,12},{8,0},{12,4},{16,24},{20,28},{24,16},{28,20},{1,9},{5... | collective-permute-start | bytes 3145736 | tf_op jit(solution)/shard_map/ppermute | solution.py:105
  404.3 30.4 %collective-permute-start.67 = (bf16[4,128,2048]{2,1,0:T(8,128)(2,1)S(1)}, bf16[4,128,2048]{2,1,0:T(8,128)(2,1)S(1)}, u32[]{:S(2)}, u32[]{:S(2)}) collective-permute-start(bf16[4,128,2048]{2,1,0:T(8,128)(2,1)S(1)} %get-tuple-element.247), channel_id=1, source_target_pairs={{0,4},{4,0},{8,12},{12,8},{16,20},{20,16},{24,28},{28,24},{1,5},{5... | collective-permute-start | bytes 6291464 | tf_op jit(solution)/shard_map/ppermute | solution.py:105
  407.0 26.1 %collective-permute-start.68 = (bf16[2,128,2048]{2,1,0:T(8,128)(2,1)S(1)}, bf16[2,128,2048]{2,1,0:T(8,128)(2,1)S(1)}, u32[]{:S(2)}, u32[]{:S(2)}) collective-permute-start(bf16[2,128,2048]{2,1,0:T(8,128)(2,1)S(1)} %get-tuple-element.249), channel_id=1, source_target_pairs={{0,16},{4,20},{8,24},{12,28},{16,0},{20,4},{24,8},{28,12},{1,17},{... | collective-permute-start | bytes 3145736 | tf_op jit(solution)/shard_map/ppermute | solution.py:105
  408.7 26.1 %collective-permute-start.69 = (bf16[2,128,2048]{2,1,0:T(8,128)(2,1)S(1)}, bf16[2,128,2048]{2,1,0:T(8,128)(2,1)S(1)}, u32[]{:S(2)}, u32[]{:S(2)}) collective-permute-start(bf16[2,128,2048]{2,1,0:T(8,128)(2,1)S(1)} %get-tuple-element.250), channel_id=1, source_target_pairs={{0,8},{4,12},{8,0},{12,4},{16,24},{20,28},{24,16},{28,20},{1,9},{5... | collective-permute-start | bytes 3145736 | tf_op jit(solution)/shard_map/ppermute | solution.py:105
  411.8 38.5 %collective-permute-start.64 = (bf16[2,128,1536]{2,1,0:T(8,128)(2,1)S(1)}, bf16[2,128,1536]{2,1,0:T(8,128)(2,1)S(1)}, u32[]{:S(2)}, u32[]{:S(2)}) collective-permute-start(bf16[2,128,1536]{2,1,0:T(8,128)(2,1)S(1)} %add_convert_fusion.18), channel_id=1, source_target_pairs={{0,8},{4,12},{8,0},{12,4},{16,24},{20,28},{24,16},{28,20},{1,9},{5... | collective-permute-start | bytes 2359304 | tf_op jit(solution)/shard_map/ppermute | solution.py:105
  412.9 37.5 %collective-permute-start.66 = (bf16[2,128,1536]{2,1,0:T(8,128)(2,1)S(1)}, bf16[2,128,1536]{2,1,0:T(8,128)(2,1)S(1)}, u32[]{:S(2)}, u32[]{:S(2)}) collective-permute-start(bf16[2,128,1536]{2,1,0:T(8,128)(2,1)S(1)} %add_convert_fusion.17), channel_id=1, source_target_pairs={{0,16},{4,20},{8,24},{12,28},{16,0},{20,4},{24,8},{28,12},{1,17},{... | collective-permute-start | bytes 2359304 | tf_op jit(solution)/shard_map/ppermute | solution.py:105
  452.2 82.5 %reduce-scatter.11.cloned.1.call-start = ((), (), s32[]{:S(2)}) async-start(), calls=%async_computation.7 | async-start | bytes 1966080 | tf_op jit(solution)/shard_map/reduce_scatter | solution.py:528
  (122 other events, 1465.2 us)
Sparse Core Ops, SparseCore 0:
  59.1 38.9 reduce-scatter.4
  149.4 40.1 reduce-scatter.6
  452.3 45.4 reduce-scatter.8
  500.0 34.6 reduce-scatter.10
